TPU v7x, 32 devices: a whole 2x2x4 slice. The times are simulated.
32 devices in a mesh: fsdp: 4 (over y, x), tp: 2 (over core), ad: 4 (over z).
Axes of the slice: x: 2, y: 2, z: 4, core: 2. Of those that a mesh axis runs over, the one named last changes fastest.
Arguments:
- input_rows: bfloat16 [4096, 8192], P(('fsdp', 'ad')), may hold values from -6 to 6
- value_weight_frozen: bfloat16 [8192, 1024], P('fsdp', 'tp'), may hold values from -0.0625 to 0.0625
- adapter_down_weight: bfloat16 [32, 256, 8192], P('ad', None, 'tp'), may hold values from -0.0625 to 0.0625
- adapter_up_weight: bfloat16 [32, 256, 1024], P('ad', None, 'tp'), may hold values from -0.375 to 0.375
- layer_output_gradient: bfloat16 [4096, 1024], P(('fsdp', 'ad'), 'tp'), may hold values from -0.5 to 0.5
- domain: int32 [4096, 1], P(('fsdp', 'ad')), may hold values from 0 to 31; in each aligned block of 256 rows (0 to 255, 256 to 511, ...) at most 12 rows name the same one
Outputs:
- y_out: bfloat16 [4096, 1024], P(('fsdp', 'ad'), 'tp')
- grad_a: float32 [32, 256, 8192], P('ad', 'fsdp', 'tp')
- grad_b: float32 [32, 256, 1024], P('ad', 'fsdp', 'tp')
Inputs may be any that keep to these rules, and one draw needn't show every extreme that they name: In each aligned block of 256 rows (the tokens of one fsdp and ad index) no domain is named by more than 12 tokens, a bound that some block reaches.
All inputs are finite; a program needn't handle non-finite values.
Results may differ from a plain program's by a relative error of at most 0.004.
Values may be sent and summed in bfloat16 or wider, within the bound.
No kernel may reach another device: no remote copies, remote signals or barrier semaphores. Data moves between devices by JAX's collectives and lax.ppermute only.
A program may use at most 128 MiB of HBM per device.

v0:
```python
import jax
import jax.numpy as jnp
from jax import lax
from jax.sharding import PartitionSpec as P

CAPD = 12


adapter_scale = 0.5


def body(
    input_rows,
    value_weight_frozen,
    adapter_down_weight,
    adapter_up_weight,
    layer_output_gradient,
    domain,
):
    row_count = input_rows.shape[0]
    domain_local = adapter_down_weight.shape[0]
    width_local = adapter_down_weight.shape[2]
    value_width_local = adapter_up_weight.shape[2]
    ad_count = lax.axis_size("ad")
    dom_total = ad_count * domain_local
    slot_total = dom_total * CAPD
    dom_ids = domain[:, 0]
    onehot = (dom_ids[:, None] == jnp.arange(dom_total, dtype=jnp.int32)[None, :]).astype(
        jnp.float32
    )
    row_iota = jnp.arange(row_count, dtype=jnp.int32)
    earlier = (row_iota[:, None] > row_iota[None, :]).astype(jnp.float32)
    prior = jnp.dot(earlier, onehot, preferred_element_type=jnp.float32)
    position = jnp.sum(prior * onehot, axis=1).astype(jnp.int32)
    place = dom_ids * CAPD + position
    matches = place[None, :] == jnp.arange(slot_total, dtype=jnp.int32)[:, None]
    filled = jnp.any(matches, axis=1)
    source_row = jnp.sum(jnp.where(matches, row_iota[None, :], 0), axis=1)
    base = jnp.dot(
        input_rows,
        lax.all_gather(value_weight_frozen, "fsdp", axis=0, tiled=True),
        preferred_element_type=jnp.float32,
    )
    feature_cols = lax.dynamic_slice_in_dim(
        input_rows, lax.axis_index("tp") * width_local, width_local, 1
    )
    zero_value = jnp.zeros((), jnp.bfloat16)
    send_x = jnp.where(filled[:, None], feature_cols[source_row], zero_value)
    send_dy = jnp.where(filled[:, None], layer_output_gradient[source_row], zero_value)
    send_x = send_x.reshape(ad_count, domain_local * CAPD, width_local)
    send_dy = send_dy.reshape(ad_count, domain_local * CAPD, value_width_local)
    got_x = lax.all_to_all(send_x, "ad", split_axis=0, concat_axis=0, tiled=True)
    got_dy = lax.all_to_all(send_dy, "ad", split_axis=0, concat_axis=0, tiled=True)
    routed_input_rows = got_x.reshape(ad_count, domain_local, CAPD, width_local)
    routed_output_gradient = got_dy.reshape(ad_count, domain_local, CAPD, value_width_local)
    hidden_partial = jnp.einsum(
        "vqfj,qwj->vqfw", routed_input_rows, adapter_down_weight, preferred_element_type=jnp.float32
    )
    input_gradient_partial = jnp.einsum(
        "amgy,mzy->amgz",
        routed_output_gradient,
        adapter_up_weight,
        preferred_element_type=jnp.float32,
    )
    hidden_sum, input_gradient_total = lax.psum((hidden_partial, input_gradient_partial), "tp")
    hidden_lowrank = hidden_sum.astype(jnp.bfloat16)
    input_gradient_lowrank = (adapter_scale * input_gradient_total).astype(jnp.bfloat16)
    adapter_update = adapter_scale * jnp.einsum(
        "lokh,ohi->loki", hidden_lowrank, adapter_up_weight, preferred_element_type=jnp.float32
    )
    adapter_update = adapter_update.astype(jnp.bfloat16).reshape(
        ad_count, domain_local * CAPD, value_width_local
    )
    part_a = jnp.einsum(
        "sdcr,sdcx->drx",
        input_gradient_lowrank,
        routed_input_rows,
        preferred_element_type=jnp.float32,
    )
    up_weight_partial = adapter_scale * jnp.einsum(
        "sdcr,sdce->dre", hidden_lowrank, routed_output_gradient, preferred_element_type=jnp.float32
    )
    returned = lax.all_to_all(
        adapter_update, "ad", split_axis=0, concat_axis=0, tiled=True
    ).reshape(slot_total, value_width_local)
    y_out = (base + returned[place].astype(jnp.float32)).astype(jnp.bfloat16)
    grad_a, grad_b = (
        lax.psum_scatter(part_a, "fsdp", scatter_dimension=1, tiled=True),
        lax.psum_scatter(up_weight_partial, "fsdp", scatter_dimension=1, tiled=True),
    )
    return (y_out, grad_a, grad_b)


def solution(mesh):
    placed = (
        P(("fsdp", "ad"), None),
        P("fsdp", "tp"),
        P("ad", None, "tp"),
        P("ad", None, "tp"),
        P(("fsdp", "ad"), "tp"),
        P(("fsdp", "ad"), None),
    )
    return jax.shard_map(
        body,
        mesh=mesh,
        in_specs=placed,
        out_specs=(P(("fsdp", "ad"), "tp"), P("ad", "fsdp", "tp"), P("ad", "fsdp", "tp")),
        check_vma=False,
    )
```

profile of v0, /device:TPU:0, one launch (start us, length us, event | category | flops | bytes accessed | tf_op | source)
XLA Modules:
  0.0 497.4 jit_solution(6578952641937000454)
XLA Ops:
  8.0 0.0 copy-start
  8.0 0.0 all-reduce.3.cloned.1.call-start
  8.1 1.0 fusion.26
  9.1 0.7 multiply_add_fusion
  9.8 0.1 select_reduce_fusion
  9.9 0.2 fusion.29
  10.1 0.1 broadcast_in_dim.49
  10.2 3.1 gather_fusion.2
  13.3 0.1 broadcast_select_fusion.1
  13.4 17.8 %all_to_all.15 = bf16[4,96,512]{2,1,0:T(8,128)(2,1)S(1)} all-to-all(bf16[4,96,512]{2,1,0:T(8,128)(2,1)S(1)} %broadcast_select_fusion.1), channel_id=1, replica_groups=mesh['fsdp'=4,'tp'=2,'ad'=4] {'ad'}, dimensions={0} | all-to-all | bytes 786432 | tf_op jit(solution)/shard_map/all_to_all | solution.py:53
  31.2 0.3 copy.38
  31.5 0.0 copy-done
  31.5 1.6 fusion.22
  33.1 0.0 all-reduce.3.cloned.1.call-update
  33.1 0.0 all-gather.2.cloned.1.call-start
  33.2 0.5 all-gather.2.cloned.1.call-update
  33.7 0.0 reduce-scatter.5.cloned.1.call-start
  33.7 3.2 constant_dynamic-slice_fusion
  36.9 10.2 %gather_fusion = bf16[384,4096]{1,0:T(8,128)(2,1)} fusion(bf16[256,4096]{1,0:T(8,128)(2,1)} %constant_dynamic-slice_fusion, s32[1024]{0:T(1024)S(1)} %pad_clamp_fusion.1), kind=kCustom, calls=%fused_computation | custom fusion | bytes 6292992 | tf_op jit(solution)/shard_map/gather | solution.py:48
  47.1 2.2 broadcast_select_fusion
  49.4 73.0 %all_to_all.16 = bf16[4,96,4096]{2,1,0:T(8,128)(2,1)S(1)} all-to-all(bf16[4,96,4096]{2,1,0:T(8,128)(2,1)S(1)} %broadcast_select_fusion), channel_id=1, replica_groups=mesh['fsdp'=4,'tp'=2,'ad'=4] {'ad'}, dimensions={0} | all-to-all | bytes 6291456 | tf_op jit(solution)/shard_map/all_to_all | solution.py:52
  122.4 4.1 copy.34
  126.5 11.9 %fusion.14 = f32[4,8,12,256]{3,2,0,1:T(8,128)S(1)} fusion(bf16[8,256,4096]{2,1,0:T(8,128)(2,1)} %param.8, bf16[4,8,12,4096]{3,0,2,1:T(4,128)(2,1)} %bitcast.47), kind=kOutput, calls=%fused_computation.16 | convolution fusion | flops 805306368 | bytes 20316160 | tf_op jit(solution)/shard_map/vqfj,qwj->vqfw/dot_general | solution.py:56
  138.4 4.8 all-reduce.4
  143.3 2.7 bitcast_multiply_fusion
  146.0 0.0 reduce-scatter.5.cloned.1.call-update
  146.0 0.3 reduce-scatter.3.cloned.1.call-start
  146.3 0.0 all-reduce.3.cloned.1.call-done
  146.3 18.5 %convolution_bitcast_fusion = f32[8,256,4096]{2,1,0:T(8,128)} fusion(bf16[4,8,12,4096]{3,0,2,1:T(4,128)(2,1)} %bitcast.48, f32[4,8,12,256]{3,2,0,1:T(8,128)} %all-reduce.3.cloned.1.call-done), kind=kOutput, calls=%fused_computation.5 | convolution fusion | flops 805502976 | bytes 37093376 | tf_op jit(solution)/shard_map/sdcr,sdcx->drx/dot_general | solution.py:74
  164.8 0.0 reduce-scatter.3.cloned.1.call-update
  164.9 0.0 copy-start.1
  164.9 0.5 fusion.19
  165.4 0.3 copy.36
  165.7 0.8 copy.37
  166.5 3.5 all-to-all-start.1
  170.0 0.0 copy-done.1
  170.0 12.4 %all-to-all-done.1 = bf16[4,96,512]{2,1,0:T(8,128)(2,1)S(1)} async-done(((bf16[4,96,512]{2,1,0:T(8,128)(2,1)}), bf16[4,96,512]{2,1,0:T(8,128)(2,1)S(1)}, u32[]{:S(2)}, u32[]{:S(2)}) %all-to-all-start.1) | async-done | bytes 393248 | tf_op jit(solution)/shard_map/all_to_all | solution.py:83
  182.4 1.2 gather_fusion.1
  183.6 0.0 all-gather.2.cloned.1.call-done
  183.6 7.7 %fusion.25 = bf16[256,512]{1,0:T(8,128)(2,1)} fusion(bf16[256,8192]{1,0:T(8,128)(2,1)} %param.6, bf16[8192,512]{1,0:T(8,128)(2,1)} %all-gather.2.cloned.1.call-done, bf16[256,512]{1,0:T(8,128)(2,1)S(1)} %gather_fusion.1), kind=kOutput, calls=%fused_computation.20 | convolution fusion | flops 2147876864 | bytes 13107200 | tf_op jit(solution)/shard_map/dot_general | solution.py:39
  191.3 6.4 %reduce-scatter.5.cloned.1.call-done = f32[8,64,512]{2,1,0:T(8,128)} async-done(((f32[8,256,512]{2,1,0:T(8,128)}), f32[8,64,512]{2,1,0:T(8,128)}) %reduce-scatter.5.cloned.1.call-update) | async-done | bytes 1048592 | tf_op jit(solution)/shard_map/reduce_scatter | solution.py:89
  197.7 292.0 %reduce-scatter.3.cloned.1.call-done = f32[8,64,4096]{2,1,0:T(8,128)} async-done(((f32[8,256,4096]{2,1,0:T(8,128)}), f32[8,64,4096]{2,1,0:T(8,128)}) %reduce-scatter.3.cloned.1.call-update) | async-done | bytes 8388624 | tf_op jit(solution)/shard_map/reduce_scatter | solution.py:88
  (5 shorter events, 0.0 us)
Async XLA Ops:
  8.0 23.5 %copy-start = (bf16[8,256,512]{2,1,0:T(8,128)(2,1)S(1)}, bf16[8,256,512]{2,1,0:T(8,128)(2,1)}, u32[]{:S(2)}) copy-start(bf16[8,256,512]{2,1,0:T(8,128)(2,1)} %param.9) | copy-start | bytes 6291460
  8.0 138.3 %all-reduce.3.cloned.1.call-start = ((), (), s32[]{:S(2)}) async-start(), calls=%async_computation.6 | async-start | bytes 1048576 | tf_op jit(solution)/shard_map/psum | solution.py:65
  33.1 150.5 %all-gather.2.cloned.1.call-start = ((), (), s32[]{:S(2)}) async-start(), calls=%async_computation.5 | async-start | bytes 10485760 | tf_op jit(solution)/shard_map/all_gather | solution.py:41
  33.7 164.0 %reduce-scatter.5.cloned.1.call-start = ((), (), s32[]{:S(2)}) async-start(), calls=%async_computation.8 | async-start | bytes 5242880 | tf_op jit(solution)/shard_map/reduce_scatter | solution.py:89
  146.0 343.8 %reduce-scatter.3.cloned.1.call-start = ((), (), s32[]{:S(2)}) async-start(), calls=%async_computation.7 | async-start | bytes 41943040 | tf_op jit(solution)/shard_map/reduce_scatter | solution.py:88
  164.9 5.1 %copy-start.1 = (s32[256,1]{0,1:T(1,128)S(1)}, s32[256,1]{0,1:T(1,128)}, u32[]{:S(2)}) copy-start(s32[256,1]{0,1:T(1,128)} %param.11) | copy-start | bytes 3076
  166.5 15.9 %all-to-all-start.1 = ((bf16[4,96,512]{2,1,0:T(8,128)(2,1)}), bf16[4,96,512]{2,1,0:T(8,128)(2,1)S(1)}, u32[]{:S(2)}, u32[]{:S(2)}) async-start(bf16[4,96,512]{2,1,0:T(8,128)(2,1)} %copy.37), calls=%async_computation.1 | async-start | bytes 786432 | tf_op jit(solution)/shard_map/all_to_all | solution.py:83
Sparse Core Ops, SparseCore 0:
  33.2 17.8 all-reduce.2
Sparse Core Ops, SparseCore 1:
  35.4 86.5 all-gather.1
  146.1 51.6 reduce-scatter.4
  201.2 288.5 reduce-scatter.2
where the time goes:
time: 498 us; the launch traced here: 497 us
  waiting for transfers between devices  312 us (63%)
  blocking collectives  95.6 us (19%)
  matrix products  43.9 us (9%)
  local copies, waits for them, and re-layouts  23.3 us (5%)
  between operations  15.8 us (3%)
    reduce_scatter x1, waiting for transfers between devices, body(): lax.psum_scatter(part_a, 'fsdp', scatter_dimension=1, tiled=True)  292 us
    all_to_all x1, blocking collectives, body(): lax.all_to_all(send_x, 'ad', split_axis=0, concat_axis=0, tiled=True)  73 us
    dot_general x1, matrix products, body(): jnp.einsum('sdcr,sdcx->drx', input_gradient_lowrank, routed_input_rows, p...  18.5 us
    all_to_all x1, blocking collectives, body(): lax.all_to_all(send_dy, 'ad', split_axis=0, concat_axis=0, tiled=True)  17.8 us
    all_to_all x1, waiting for transfers between devices, body(): lax.all_to_all(adapter_update, 'ad', split_axis=0, concat_axis=0, tiled=T...  12.4 us
    dot_general x1, matrix products, body(): jnp.einsum('vqfj,qwj->vqfw', routed_input_rows, adapter_down_weight, pref...  11.9 us
    gather x1, local copies, waits for them, and re-layouts, body(): send_x = jnp.where(filled[:, None], feature_cols[source_row], zero_value)  10.2 us
  transfers between devices with their start and end apart: 5, of which 3 were waited for; matrix products, arithmetic and copies ran while one was open for 13% of the time, Pallas kernels for 0%

commit v1 on v0

v1 whole, which is shorter than its diff:
```python
import jax
import jax.numpy as jnp
from jax import lax
from jax.sharding import PartitionSpec as P

CAPD = 12
GROUP = 4
CHUNKS = 2

adapter_scale = 0.5


def slot_places(dom_ids, dom_total):
    row_count = dom_ids.shape[0]
    onehot = (dom_ids[:, None] == jnp.arange(dom_total, dtype=jnp.int32)[None, :]).astype(
        jnp.float32
    )
    row_iota = jnp.arange(row_count, dtype=jnp.int32)
    earlier = (row_iota[:, None] > row_iota[None, :]).astype(jnp.float32)
    prior = jnp.dot(earlier, onehot, preferred_element_type=jnp.float32)
    position = jnp.sum(prior * onehot, axis=1).astype(jnp.int32)
    return dom_ids * CAPD + position


def general_body(
    input_rows,
    value_weight_frozen,
    adapter_down_weight,
    adapter_up_weight,
    layer_output_gradient,
    domain,
):
    row_count = input_rows.shape[0]
    domain_local = adapter_down_weight.shape[0]
    width_local = adapter_down_weight.shape[2]
    value_width_local = adapter_up_weight.shape[2]
    ad_count = lax.axis_size("ad")
    slot_total = ad_count * domain_local * CAPD
    place = slot_places(domain[:, 0], ad_count * domain_local)
    row_iota = jnp.arange(row_count, dtype=jnp.int32)
    matches = place[None, :] == jnp.arange(slot_total, dtype=jnp.int32)[:, None]
    filled = jnp.any(matches, axis=1)
    source_row = jnp.sum(jnp.where(matches, row_iota[None, :], 0), axis=1)
    base = jnp.dot(
        input_rows,
        lax.all_gather(value_weight_frozen, "fsdp", axis=0, tiled=True),
        preferred_element_type=jnp.float32,
    )
    feature_cols = lax.dynamic_slice_in_dim(
        input_rows, lax.axis_index("tp") * width_local, width_local, 1
    )
    zero_value = jnp.zeros((), jnp.bfloat16)
    send_x = jnp.where(filled[:, None], feature_cols[source_row], zero_value)
    send_dy = jnp.where(filled[:, None], layer_output_gradient[source_row], zero_value)
    send_x = send_x.reshape(ad_count, domain_local * CAPD, width_local)
    send_dy = send_dy.reshape(ad_count, domain_local * CAPD, value_width_local)
    got_x = lax.all_to_all(send_x, "ad", split_axis=0, concat_axis=0, tiled=True)
    got_dy = lax.all_to_all(send_dy, "ad", split_axis=0, concat_axis=0, tiled=True)
    rows = got_x.reshape(ad_count, domain_local, CAPD, width_local)
    grads = got_dy.reshape(ad_count, domain_local, CAPD, value_width_local)
    f32 = dict(preferred_element_type=jnp.float32)
    hidden, back = lax.psum(
        (
            jnp.einsum("vqfj,qwj->vqfw", rows, adapter_down_weight, **f32),
            jnp.einsum("amgy,mzy->amgz", grads, adapter_up_weight, **f32),
        ),
        "tp",
    )
    hidden = hidden.astype(jnp.bfloat16)
    back = (adapter_scale * back).astype(jnp.bfloat16)
    delta = adapter_scale * jnp.einsum("lokh,ohi->loki", hidden, adapter_up_weight, **f32)
    delta = delta.astype(jnp.bfloat16).reshape(ad_count, domain_local * CAPD, value_width_local)
    part_a = jnp.einsum("sdcr,sdcx->drx", back, rows, **f32)
    part_b = adapter_scale * jnp.einsum("sdcr,sdce->dre", hidden, grads, **f32)
    returned = lax.all_to_all(delta, "ad", split_axis=0, concat_axis=0, tiled=True)
    returned = returned.reshape(slot_total, value_width_local)
    y_out = (base + returned[place].astype(jnp.float32)).astype(jnp.bfloat16)
    return (
        y_out,
        lax.psum_scatter(part_a, "fsdp", scatter_dimension=1, tiled=True),
        lax.psum_scatter(part_b, "fsdp", scatter_dimension=1, tiled=True),
    )


def column_body(
    input_rows,
    value_weight_frozen,
    adapter_down_weight,
    adapter_up_weight,
    layer_output_gradient,
    domain,
):
    f32 = dict(preferred_element_type=jnp.float32)
    bf16 = jnp.bfloat16
    fsdp, ad = lax.axis_size("fsdp"), lax.axis_size("ad")
    f, t, a = lax.axis_index("fsdp"), lax.axis_index("tp"), lax.axis_index("ad")
    fy, fx = f // 2, f % 2
    rows, width = input_rows.shape
    dloc, rank, half = adapter_down_weight.shape
    vloc = adapter_up_weight.shape[2]
    rloc = rank // fsdp
    kf_width = width // fsdp
    kt = kf_width // 2
    cw = kt // CHUNKS
    slots = dloc * CAPD
    ngroup = dloc // GROUP
    gslots = GROUP * CAPD

    def over_f(v, k):
        return lax.ppermute(v, "fsdp", [(i, i ^ k) for i in range(fsdp)])

    def over_a(v, k):
        return lax.ppermute(v, "ad", [(i, (i + k) % ad) for i in range(ad)])

    def swap(v):
        return lax.ppermute(v, "tp", [(0, 1), (1, 0)])

    def cut(v, start, size, axis):
        return lax.dynamic_slice_in_dim(v, start, size, axis)

    own_dom = lax.broadcasted_iota(jnp.int32, (gslots, GROUP, 1), 0) // CAPD
    own_dom = own_dom == lax.broadcasted_iota(jnp.int32, (gslots, GROUP, 1), 1)

    def spread(v):
        n = v.shape[-1]
        wide = jnp.where(own_dom, v[..., None, :], jnp.zeros((), v.dtype))
        return wide.reshape(*v.shape[:-1], GROUP * n)

    def pick(v):
        n = v.shape[-1] // GROUP
        total = jnp.where(own_dom[:, 0], v[..., :n], 0.0)
        for e in range(1, GROUP):
            total = total + jnp.where(own_dom[:, e], v[..., e * n : (e + 1) * n], 0.0)
        return total

    x_in = []
    for c in range(CHUNKS):
        piece = []
        for k in range(fsdp):
            block = cut(input_rows, (f ^ k) * kf_width + t * kt + c * cw, cw, 1)
            piece.append(over_f(block, k) if k else block)
        x_in.append(piece)
    place = slot_places(domain[:, 0], ad * dloc)
    places = [over_f(place, k) if k else place for k in range(fsdp)]

    slot_iota = lax.broadcasted_iota(jnp.int32, (slots, rows), 0)

    def onehot(kf, ka):
        return (places[kf][None, :] == slot_iota + ((a + ka) % ad) * slots).astype(bf16)

    own_hot = [onehot(0, ka) for ka in range(ad)]
    dy = []
    for ka in range(ad):
        block = jnp.dot(own_hot[ka], layer_output_gradient, **f32).astype(bf16)
        dy.append(over_a(block, ka) if ka else block)
    dy = jnp.stack(dy).reshape(ad, ngroup, gslots, vloc)
    up = adapter_up_weight.reshape(ngroup, GROUP * rank, vloc)
    back = pick(jnp.einsum("agkv,gjv->agkj", dy, up, **f32))
    back = (adapter_scale * (back + swap(back))).astype(bf16)
    backs = jnp.stack([over_f(back, k) if k else back for k in range(fsdp)], axis=1)
    dys = jnp.stack([over_f(dy, k) if k else dy for k in range(fsdp)])

    hots = jnp.stack(
        [jnp.stack([onehot(kf, ka) for kf in range(fsdp)]) for ka in range(ad)]
    )
    x_full = [jnp.stack(piece) for piece in x_in]
    x_routed = []
    for c in range(CHUNKS):
        piece = []
        for ka in range(ad):
            block = jnp.einsum("fin,fnw->fiw", hots[ka], x_full[c], **f32).astype(bf16)
            piece.append(over_a(block, ka) if ka else block)
        x_routed.append(jnp.stack(piece).reshape(ad, fsdp, ngroup, gslots, cw))

    holder = t == fy
    col0 = fx * kf_width
    down_mine = cut(adapter_down_weight, col0 + t * kt, kt, 2)
    down_other = cut(adapter_down_weight, col0 + (1 - t) * kt, kt, 2)
    pairs = [(i * 2 + i // 2, i * 2 + 1 - i // 2) for i in range(fsdp)]
    down_got = lax.ppermute(down_other, ("fsdp", "tp"), pairs)
    down = jnp.where(holder, down_mine, down_got).reshape(ngroup, GROUP * rank, kt)

    w_mine = cut(value_weight_frozen, t * kt, kt, 0)
    w_got = swap(cut(value_weight_frozen, (1 - t) * kt, kt, 0))
    x_cols = jnp.concatenate(x_full, axis=2)
    base_other = jnp.einsum("fnw,wv->fnv", x_cols, w_got, **f32)
    base = jnp.einsum("fnw,wv->fnv", x_cols, w_mine, **f32) + swap(base_other)
    base_sum = base[0]
    for k in range(1, fsdp):
        base_sum = base_sum + over_f(base[k], k)

    grad_a = jnp.zeros((dloc, rloc, half), jnp.float32)
    rounds = [(p, q) for p in range(2) for q in range(2)]
    masked = []
    for p, q in rounds:
        owner = (t ^ q) * 2 + (fx ^ p)
        masked.append(spread(cut(backs, owner * rloc, rloc, 4)))
    for c in range(CHUNKS):
        for (p, q), mb in zip(rounds, masked):
            block = jnp.einsum("abgkj,abgkw->gjw", mb, x_routed[c], **f32)
            block = block.astype(bf16).reshape(dloc, rloc, cw)
            perm = [
                ((y * 2 + x) * 2 + s, ((s ^ q) * 2 + (x ^ p)) * 2 + y)
                for y in range(2)
                for x in range(2)
                for s in range(2)
            ]
            got = lax.ppermute(block, ("fsdp", "tp"), perm)
            start = (fx ^ p) * kf_width + (fy ^ q) * kt + c * cw
            grad_a = lax.dynamic_update_slice_in_dim(grad_a, got.astype(jnp.float32), start, 2)

    hid = None
    for c in range(CHUNKS):
        part = jnp.einsum(
            "abgkw,gjw->abgkj", x_routed[c], down[:, :, c * cw : (c + 1) * cw], **f32
        )
        hid = pick(part) if hid is None else hid + pick(part)
    rhalf = rank // 2
    hid = cut(hid, t * rhalf, rhalf, 4) + swap(cut(hid, (1 - t) * rhalf, rhalf, 4))
    hid_sum = hid[:, 0]
    for k in range(1, fsdp):
        hid_sum = hid_sum + over_f(hid[:, k], k)
    hid_own = hid_sum.astype(bf16)
    hid_got = swap(hid_own)
    hidden = jnp.where(
        t == 0,
        jnp.concatenate([hid_own, hid_got], axis=3),
        jnp.concatenate([hid_got, hid_own], axis=3),
    )

    delta = adapter_scale * jnp.einsum("agkj,gjv->agkv", spread(hidden), up, **f32)
    delta = delta.astype(bf16).reshape(ad, slots, vloc)
    back_rows = [over_a(delta[ka], ad - ka) if ka else delta[ka] for ka in range(ad)]
    added = jnp.einsum("ain,aiv->nv", jnp.stack(own_hot), jnp.stack(back_rows), **f32)
    y_out = (base_sum + added).astype(bf16)

    hid_cols = []
    for k in range(fsdp):
        block = cut(hidden, (f ^ k) * rloc, rloc, 3)
        hid_cols.append(over_f(block, k) if k else block)
    hid_cols = spread(jnp.stack(hid_cols))
    grad_b = adapter_scale * jnp.einsum("fagkj,fagkv->gjv", hid_cols, dys, **f32)
    return y_out, grad_a, grad_b.reshape(dloc, rloc, vloc)


def solution(mesh):
    placed = (
        P(("fsdp", "ad"), None),
        P("fsdp", "tp"),
        P("ad", None, "tp"),
        P("ad", None, "tp"),
        P(("fsdp", "ad"), "tp"),
        P(("fsdp", "ad"), None),
    )
    square = mesh.shape["fsdp"] == 4 and mesh.shape["tp"] == 2
    return jax.shard_map(
        column_body if square else general_body,
        mesh=mesh,
        in_specs=placed,
        out_specs=(P(("fsdp", "ad"), "tp"), P("ad", "fsdp", "tp"), P("ad", "fsdp", "tp")),
        check_vma=False,
    )
```

time: 498 us -> 288 us (0.58)
  waiting for transfers between devices: 312 us -> 114 us
  blocking collectives: 95.6 us -> 0 us
  starting transfers between devices: 3.84 us -> 74.6 us
  local copies, waits for them, and re-layouts: 23.3 us -> 52.5 us
  between operations: 15.8 us -> 1.88 us
  matrix products: 43.9 us -> 30.3 us
  other arithmetic: 3.4 us -> 13.3 us
    reduce_scatter x2 -> x0, waiting for transfers between devices: 298 us -> none  [the longest x1 292 us: body(): lax.psum_scatter(part_a, 'fsdp', scatter_dimension=1, tiled=True)]
    ppermute x0 -> x50, waiting for transfers between devices: none -> 114 us  [the longest x12 62.1 us: over_a(): return lax.ppermute(v, 'ad', [(i, (i + k) % ad) for i in range(ad)])]
    all_to_all x2 -> x0, blocking collectives: 90.8 us -> none  [the longest x1 73 us: body(): lax.all_to_all(send_x, 'ad', split_axis=0, concat_axis=0, tiled=True)]
    ppermute x0 -> x50, starting transfers between devices: none -> 74.6 us  [the longest x24 25.5 us: over_f(): return lax.ppermute(v, 'fsdp', [(i, i ^ k) for i in range(fsdp)])]
    broadcast_in_dim x1 -> x16, local copies, waits for them, and re-layouts: 0.09 us -> 31.6 us  [the longest x15 30.6 us: spread(): wide = jnp.where(own_dom, v[..., None, :], jnp.zeros((), v.dtype))]
    gather x3 -> x0, local copies, waits for them, and re-layouts: 14.5 us -> none  [the longest x1 10.2 us: body(): send_x = jnp.where(filled[:, None], feature_cols[source_row], zero_value)]
    dot_general x7 -> x29, matrix products: 43.9 us -> 30.3 us  [the longest x8 4.95 us: column_body(): block = jnp.einsum('abgkj,abgkw->gjw', mb, x_routed[c], **f32)]
    all_to_all x1 -> x0, waiting for transfers between devices: 12.4 us -> none  [body(): lax.all_to_all(adapter_update, 'ad', split_axis=0, concat_axis=0, tiled=T...]
  transfers between devices with their start and end apart: 5 -> 50, of which waited for: 3 -> 20; matrix products, arithmetic and copies ran while one was open for 13% -> 31% of each run, Pallas kernels for 0% -> 0%
where the time goes in v1:
time: 288 us; the launch traced here: 287 us
  waiting for transfers between devices  114 us (40%)
  starting transfers between devices  74.6 us (26%)
  local copies, waits for them, and re-layouts  52.5 us (18%)
  matrix products  30.3 us (11%)
  other arithmetic  13.3 us (5%)
    ppermute x12, waiting for transfers between devices, over_a(): return lax.ppermute(v, 'ad', [(i, (i + k) % ad) for i in range(ad)])  62.1 us
    broadcast_in_dim x15, local copies, waits for them, and re-layouts, spread(): wide = jnp.where(own_dom, v[..., None, :], jnp.zeros((), v.dtype))  30.6 us
    ppermute x8, waiting for transfers between devices, column_body(): got = lax.ppermute(block, ('fsdp', 'tp'), perm)  27 us
    ppermute x24, starting transfers between devices, over_f(): return lax.ppermute(v, 'fsdp', [(i, i ^ k) for i in range(fsdp)])  25.5 us
    ppermute x24, waiting for transfers between devices, over_f(): return lax.ppermute(v, 'fsdp', [(i, i ^ k) for i in range(fsdp)])  25.2 us
    ppermute x12, starting transfers between devices, over_a(): return lax.ppermute(v, 'ad', [(i, (i + k) % ad) for i in range(ad)])  23.9 us
    ppermute x8, starting transfers between devices, column_body(): got = lax.ppermute(block, ('fsdp', 'tp'), perm)  18.8 us
    dynamic_slice x8, local copies, waits for them, and re-layouts, cut(): return lax.dynamic_slice_in_dim(v, start, size, axis)  10.4 us
  transfers between devices with their start and end apart: 50, of which 20 were waited for; matrix products, arithmetic and copies ran while one was open for 31% of the time, Pallas kernels for 0%

profile of v1, /device:TPU:0, one launch (start us, length us, event | category | flops | bytes accessed | tf_op | source)
XLA Modules:
  0.0 287.0 jit_solution(13482598962338035149)
XLA Ops:
  2.4 3.9 %collective-permute-start.14 = (s32[256]{0:T(256)S(1)}, s32[256]{0:T(256)S(1)}, u32[]{:S(2)}, u32[]{:S(2)}) collective-permute-start(s32[256]{0:T(256)S(1)} %convert_add_fusion), channel_id=1, source_target_pairs={{0,24},{8,16},{16,8},{24,0},{1,25},{9,17},{17,9},{25,1},{2,26},{10... | collective-permute-start | bytes 3080 | tf_op jit(solution)/shard_map/ppermute | solution.py:110
  6.8 1.3 constant_dynamic-slice_fusion.9
  8.2 4.6 %constant_dynamic-slice_fusion.8 = bf16[8,256,1024]{2,1,0:T(8,128)(2,1)} fusion(bf16[8,256,4096]{2,1,0:T(8,128)(2,1)} %param.8, s32[]{:T(128)S(6)} %select_n.303), kind=kLoop, calls=%fused_computation.197 | loop fusion | bytes 8388612 | tf_op jit(solution)/shard_map/dynamic_slice | solution.py:119
  12.9 4.4 %collective-permute-start.11 = (bf16[8,256,1024]{2,1,0:T(8,128)(2,1)}, bf16[8,256,1024]{2,1,0:T(8,128)(2,1)}, u32[]{:S(2)}, u32[]{:S(2)}) collective-permute-start(bf16[8,256,1024]{2,1,0:T(8,128)(2,1)} %constant_dynamic-slice_fusion.8), channel_id=1, source_target_pairs={{0,4},{8,12},{20,16},{28,24},{1,5},{9,13},{21,17},{29,25},{2,6},{1... | collective-permute-start | bytes 12582920 | tf_op jit(solution)/shard_map/ppermute | solution.py:180
  17.4 2.9 %dynamic-slice_bitcast_fusion.1 = (bf16[1,256,512]{2,1,0:T(8,128)(2,1)}, bf16[256,512]{1,0:T(8,128)(2,1)}, bf16[1,256,512]{2,1,0:T(8,128)(2,1)}, bf16[256,512]{1...) fusion(bf16[256,8192]{1,0:T(8,128)(2,1)} %param.6, ...), kind=kLoop, calls=%fused_computation.135 | loop fusion | bytes 4194336 | tf_op jit(solution)/shard_map/stack | solution.py:166
  23.2 4.1 %collective-permute-start.31 = (bf16[96,512]{1,0:T(8,128)(2,1)}, bf16[96,512]{1,0:T(8,128)(2,1)S(1)}, u32[]{:S(2)}, u32[]{:S(2)}) collective-permute-start(bf16[96,512]{1,0:T(8,128)(2,1)} %convolution_convert_fusion.8), channel_id=1, source_target_pairs={{0,3},{1,0},{2,1},{3,2},{4,7},{5,4},{6,5},{7,6},{8,11},{9,8},{10,9... | collective-permute-start | bytes 294920 | tf_op jit(solution)/shard_map/ppermute | solution.py:113
  29.9 4.7 %collective-permute-done.30 = bf16[96,512]{1,0:T(8,128)(2,1)S(1)} collective-permute-done((bf16[96,512]{1,0:T(8,128)(2,1)}, bf16[96,512]{1,0:T(8,128)(2,1)S(1)}, u32[]{:S(2)}, u32[]{:S(2)}) %collective-permute-start.30) | collective-permute-done | bytes 98336 | tf_op jit(solution)/shard_map/ppermute | solution.py:113
  34.5 1.3 collective-permute-start.4
  35.8 1.5 collective-permute-start.3
  38.2 1.3 collective-permute-done.5
  39.5 5.9 %collective-permute-done.4 = bf16[256,512]{1,0:T(8,128)(2,1)S(1)} collective-permute-done((bf16[256,512]{1,0:T(8,128)(2,1)}, bf16[256,512]{1,0:T(8,128)(2,1)S(1)}, u32[]{:S(2)}, u32[]{:S(2)}) %collective-permute-start.4) | collective-permute-done | bytes 262176 | tf_op jit(solution)/shard_map/ppermute | solution.py:110
  47.7 3.3 %collective-permute-done.2 = bf16[256,512]{1,0:T(8,128)(2,1)S(1)} collective-permute-done((bf16[256,512]{1,0:T(8,128)(2,1)S(1)}, bf16[256,512]{1,0:T(8,128)(2,1)S(1)}, u32[]{:S(2)}, u32[]{:S(2)}) %collective-permute-start.2) | collective-permute-done | bytes 262176 | tf_op jit(solution)/shard_map/ppermute | solution.py:110
  51.0 3.9 %collective-permute-start.20 = (bf16[4,96,512]{2,1,0:T(8,128)(2,1)S(1)}, bf16[4,96,512]{2,1,0:T(8,128)(2,1)S(1)}, u32[]{:S(2)}, u32[]{:S(2)}) collective-permute-start(bf16[4,96,512]{2,1,0:T(8,128)(2,1)S(1)} %convolution_convert_fusion), channel_id=1, source_target_pairs={{0,3},{1,0},{2,1},{3,2},{4,7},{5,4},{6,5},{7,6},{8,11},{9,8},{10,9... | collective-permute-start | bytes 1179656 | tf_op jit(solution)/shard_map/ppermute | solution.py:113
  56.1 2.9 %collective-permute-start.19 = (bf16[4,96,512]{2,1,0:T(8,128)(2,1)S(1)}, bf16[4,96,512]{2,1,0:T(8,128)(2,1)S(1)}, u32[]{:S(2)}, u32[]{:S(2)}) collective-permute-start(bf16[4,96,512]{2,1,0:T(8,128)(2,1)S(1)} %convolution_convert_fusion.1), channel_id=1, source_target_pairs={{0,2},{1,3},{2,0},{3,1},{4,6},{5,7},{6,4},{7,5},{8,10},{9,11},{10,... | collective-permute-start | bytes 1179656 | tf_op jit(solution)/shard_map/ppermute | solution.py:113
  59.0 1.6 collective-permute-start.18
  61.9 2.4 collective-permute-done.20
  64.4 4.3 %collective-permute-start.17 = (bf16[4,96,512]{2,1,0:T(8,128)(2,1)S(1)}, bf16[4,96,512]{2,1,0:T(8,128)(2,1)S(1)}, u32[]{:S(2)}, u32[]{:S(2)}) collective-permute-start(bf16[4,96,512]{2,1,0:T(8,128)(2,1)S(1)} %convolution_convert_fusion.4), channel_id=1, source_target_pairs={{0,3},{1,0},{2,1},{3,2},{4,7},{5,4},{6,5},{7,6},{8,11},{9,8},{10,9... | collective-permute-start | bytes 1179656 | tf_op jit(solution)/shard_map/ppermute | solution.py:113
  68.7 35.3 %collective-permute-done.19 = bf16[4,96,512]{2,1,0:T(8,128)(2,1)S(1)} collective-permute-done((bf16[4,96,512]{2,1,0:T(8,128)(2,1)S(1)}, bf16[4,96,512]{2,1,0:T(8,128)(2,1)S(1)}, u32[]{:S(2)}, u32[]{:S(2)}) %collective-permute-start.19) | collective-permute-done | bytes 393248 | tf_op jit(solution)/shard_map/ppermute | solution.py:113
  105.0 18.5 %collective-permute-done.16 = bf16[4,96,512]{2,1,0:T(8,128)(2,1)S(1)} collective-permute-done((bf16[4,96,512]{2,1,0:T(8,128)(2,1)S(1)}, bf16[4,96,512]{2,1,0:T(8,128)(2,1)S(1)}, u32[]{:S(2)}, u32[]{:S(2)}) %collective-permute-start.16) | collective-permute-done | bytes 393248 | tf_op jit(solution)/shard_map/ppermute | solution.py:113
  123.8 4.2 %fusion.28 = f32[4,256,512]{2,1,0:T(8,128)} fusion(bf16[1024,512]{1,0:T(8,128)(2,1)} %collective-permute-done.6, bf16[1,256,512]{2,1,0:T(8,128)(2,1)S(1)} %bitcast.278, bf16[1,256,512]{2,1,0:T(8,128)(2,1)S(1)} %bitcast.284, bf16[1,256,512]{2,1,0:T(8,128)(2,1)S(1)} %bitcast.290, bf16[1,256,512]{2,1,0:T(8,128)(2,1)S(1)} %copy-done.18, ...), kind=kOutput, calls=%fused_computation.68 | convolution fusion | flops 1090519040 | bytes 5242880 | tf_op jit(solution)/shard_map/fnw,wv->fnv/dot_general | solution.py:186
  128.0 4.3 %dynamic-slice_select_fusion = bf16[8,256,1024]{2,1,0:T(8,128)(2,1)S(1)} fusion(bf16[8,256,1024]{2,1,0:T(8,128)(2,1)} %collective-permute-done.11, bf16[8,256,4096]{2,1,0:T(8,128)(2,1)} %param.8, s32[]{:T(128)S(6)} %select_n.302, pred[]{:T(512)S(6)} %eq.341), kind=kLoop, calls=%fused_computation | loop fusion | flops 2097152 | bytes 12582917 | tf_op jit(solution)/shard_map/jit(_where)/select_n | solution.py:181
  132.3 1.8 convolution_bitcast_fusion
  134.1 1.8 convolution_bitcast_fusion.1
  138.2 1.8 collective-permute-start.21
  141.2 2.5 collective-permute-start.33
  145.9 3.1 %collective-permute-done.35 = bf16[4,2,48,256]{3,2,0,1:T(8,128)(2,1)S(1)} collective-permute-done((bf16[4,2,48,256]{3,2,0,1:T(8,128)(2,1)S(1)}, bf16[4,2,48,256]{3,2,0,1:T(8,128)(2,1)S(1)}, u32[]{:S(2)}, u32[]{:S(2)}) %collective-permute-start.35) | collective-permute-done | bytes 196640 | tf_op jit(solution)/shard_map/ppermute | solution.py:110
  149.0 2.5 collective-permute-done.34
  152.2 1.4 constant_dynamic-slice_fusion.3
  153.6 1.9 broadcast_in_dim.259
  155.5 2.8 broadcast_in_dim.260
  159.4 1.9 broadcast_in_dim.261
  161.2 3.6 %broadcast_in_dim.262 = bf16[4,4,2,48,256]{4,3,0,1,2:T(8,128)(2,1)} reshape(bf16[4,4,2,48,4,64]{5,4,3,0,1,2:T(4,128)(2,1)} %broadcast_in_dim.261) | data formatting | bytes 1572864 | tf_op jit(solution)/shard_map/jit(_where)/broadcast_in_dim | solution.py:126
  165.9 1.9 broadcast_in_dim.263
  167.7 3.6 %broadcast_in_dim.264 = bf16[4,4,2,48,256]{4,3,0,1,2:T(8,128)(2,1)} reshape(bf16[4,4,2,48,4,64]{5,4,3,0,1,2:T(4,128)(2,1)} %broadcast_in_dim.263) | data formatting | bytes 1572864 | tf_op jit(solution)/shard_map/jit(_where)/broadcast_in_dim | solution.py:126
  171.4 1.9 broadcast_in_dim.256
  173.2 3.6 %broadcast_in_dim.257 = bf16[4,4,2,48,256]{4,3,0,1,2:T(8,128)(2,1)} reshape(bf16[4,4,2,48,4,64]{5,4,3,0,1,2:T(4,128)(2,1)} %broadcast_in_dim.256) | data formatting | bytes 1572864 | tf_op jit(solution)/shard_map/jit(_where)/broadcast_in_dim | solution.py:126
  176.9 1.6 dynamic-slice_add_fusion
  178.5 2.0 collective-permute-start.24
  182.1 3.1 %convolution_add_fusion = f32[4,256,512]{2,1,0:T(8,128)S(1)} fusion(f32[4,256,512]{2,1,0:T(8,128)} %collective-permute-done.7, bf16[2048,512]{1,0:T(8,128)(2,1)S(1)} %copy-done.9, s32[]{:T(128)S(6)} %select_n.290, bf16[1,256,512]{2,1,0:T(8,128)(2,1)S(1)} %bitcast.279, bf16[1,256,512]{2,1,0:T(8,128)(2,1)S(1)} %bitcast.285, ...), kind=kOutput, calls=%fused_computation.28 | convolution fusion | flops 1091043328 | bytes 7340036 | tf_op jit(solution)/shard_map/fnw,wv->fnv/dot_general | solution.py:187
  185.3 1.8 collective-permute-done.24
  187.1 2.5 collective-permute-done.23
  192.3 2.6 broadcast_in_dim.245
  195.0 2.3 collective-permute-start.46
  198.6 1.7 fusion.26
  201.2 2.2 collective-permute-start.47
  203.3 1.6 collective-permute-start.10
  204.9 1.3 collective-permute-start.9
  206.4 1.9 broadcast_in_dim.265
  208.3 3.6 %broadcast_in_dim.266 = bf16[4,4,2,48,256]{4,3,0,1,2:T(8,128)(2,1)} reshape(bf16[4,4,2,48,4,64]{5,4,3,0,1,2:T(4,128)(2,1)} %broadcast_in_dim.265) | data formatting | bytes 1572864 | tf_op jit(solution)/shard_map/jit(_where)/broadcast_in_dim | solution.py:126
  211.9 2.2 broadcast_select_fusion
  220.2 3.2 %collective-permute-start.27 = (bf16[96,512]{1,0:T(8,128)(2,1)S(1)}, bf16[96,512]{1,0:T(8,128)(2,1)S(1)}, u32[]{:S(2)}, u32[]{:S(2)}) collective-permute-start(bf16[96,512]{1,0:T(8,128)(2,1)S(1)} %bitcast.258), channel_id=1, source_target_pairs={{0,2},{1,3},{2,0},{3,1},{4,6},{5,7},{6,4},{7,5},{8,10},{9,11},{10,... | collective-permute-start | bytes 294920 | tf_op jit(solution)/shard_map/ppermute | solution.py:113
  223.3 2.8 fusion.14
  227.4 1.7 collective-permute-start.26
  231.4 3.0 %collective-permute-done.8 = f32[256,512]{1,0:T(8,128)S(1)} collective-permute-done((f32[256,512]{1,0:T(8,128)S(1)}, f32[256,512]{1,0:T(8,128)S(1)}, u32[]{:S(2)}, u32[]{:S(2)}) %collective-permute-start.8) | collective-permute-done | bytes 524320 | tf_op jit(solution)/shard_map/ppermute | solution.py:110
  234.4 1.3 collective-permute-start.37
  235.7 1.4 collective-permute-start.38
  238.1 2.4 fusion.55
  240.5 9.6 %collective-permute-start.41 = (bf16[8,64,512]{2,1,0:T(8,128)(2,1)S(1)}, bf16[8,64,512]{2,1,0:T(8,128)(2,1)S(1)}, u32[]{:S(2)}, u32[]{:S(2)}) collective-permute-start(bf16[8,64,512]{2,1,0:T(8,128)(2,1)S(1)} %bitcast.266), channel_id=1, source_target_pairs={{0,16},{4,0},{8,24},{12,8},{16,20},{20,4},{24,28},{28,12},{1,17},{... | collective-permute-start | bytes 1572872 | tf_op jit(solution)/shard_map/ppermute | solution.py:208
  251.3 6.1 %collective-permute-done.37 = bf16[8,64,512]{2,1,0:T(8,128)(2,1)S(1)} collective-permute-done((bf16[8,64,512]{2,1,0:T(8,128)(2,1)S(1)}, bf16[8,64,512]{2,1,0:T(8,128)(2,1)S(1)}, u32[]{:S(2)}, u32[]{:S(2)}) %collective-permute-start.37) | collective-permute-done | bytes 524320 | tf_op jit(solution)/shard_map/ppermute | solution.py:208
  257.4 1.4 collective-permute-start.42
  259.0 3.0 %collective-permute-start.43 = (bf16[8,64,512]{2,1,0:T(8,128)(2,1)S(1)}, bf16[8,64,512]{2,1,0:T(8,128)(2,1)S(1)}, u32[]{:S(2)}, u32[]{:S(2)}) collective-permute-start(bf16[8,64,512]{2,1,0:T(8,128)(2,1)S(1)} %bitcast.271), channel_id=1, source_target_pairs={{0,24},{4,8},{8,16},{12,0},{16,28},{20,12},{24,20},{28,4},{1,25},{... | collective-permute-start | bytes 1572872 | tf_op jit(solution)/shard_map/ppermute | solution.py:208
  262.4 14.4 %collective-permute-done.41 = bf16[8,64,512]{2,1,0:T(8,128)(2,1)S(1)} collective-permute-done((bf16[8,64,512]{2,1,0:T(8,128)(2,1)S(1)}, bf16[8,64,512]{2,1,0:T(8,128)(2,1)S(1)}, u32[]{:S(2)}, u32[]{:S(2)}) %collective-permute-start.41) | collective-permute-done | bytes 524320 | tf_op jit(solution)/shard_map/ppermute | solution.py:208
  277.1 6.4 %collective-permute-done.43 = bf16[8,64,512]{2,1,0:T(8,128)(2,1)S(1)} collective-permute-done((bf16[8,64,512]{2,1,0:T(8,128)(2,1)S(1)}, bf16[8,64,512]{2,1,0:T(8,128)(2,1)S(1)}, u32[]{:S(2)}, u32[]{:S(2)}) %collective-permute-start.43) | collective-permute-done | bytes 524320 | tf_op jit(solution)/shard_map/ppermute | solution.py:208
  283.6 3.4 %copy-done.5 = f32[8,64,4096]{2,1,0:T(8,128)} copy-done((f32[8,64,4096]{2,1,0:T(8,128)}, f32[8,64,4096]{2,1,0:T(8,128)S(1)}, u32[]{:S(2)}) %copy-start.5) | copy-done | bytes 8388632
  (206 shorter events, 41.7 us)
Async XLA Ops:
  0.6 36.7 %copy-start = (bf16[8,256,512]{2,1,0:T(8,128)(2,1)S(1)}, bf16[8,256,512]{2,1,0:T(8,128)(2,1)}, u32[]{:S(2)}) copy-start(bf16[8,256,512]{2,1,0:T(8,128)(2,1)} %param.9) | copy-start | bytes 6291460
  2.4 20.8 %collective-permute-start.14 = (s32[256]{0:T(256)S(1)}, s32[256]{0:T(256)S(1)}, u32[]{:S(2)}, u32[]{:S(2)}) collective-permute-start(s32[256]{0:T(256)S(1)} %convert_add_fusion), channel_id=1, source_target_pairs={{0,24},{8,16},{16,8},{24,0},{1,25},{9,17},{17,9},{25,1},{2,26},{10... | collective-permute-start | bytes 3080 | tf_op jit(solution)/shard_map/ppermute | solution.py:110
  6.3 21.1 %collective-permute-start.13 = (s32[256]{0:T(256)S(1)}, s32[256]{0:T(256)S(1)}, u32[]{:S(2)}, u32[]{:S(2)}) collective-permute-start(s32[256]{0:T(256)S(1)} %convert_add_fusion), channel_id=1, source_target_pairs={{0,16},{8,24},{16,0},{24,8},{1,17},{9,25},{17,1},{25,9},{2,18},{10... | collective-permute-start | bytes 3080 | tf_op jit(solution)/shard_map/ppermute | solution.py:110
  6.8 20.6 %collective-permute-start.12 = (s32[256]{0:T(256)S(1)}, s32[256]{0:T(256)S(1)}, u32[]{:S(2)}, u32[]{:S(2)}) collective-permute-start(s32[256]{0:T(256)S(1)} %convert_add_fusion), channel_id=1, source_target_pairs={{0,8},{8,0},{16,24},{24,16},{1,9},{9,1},{17,25},{25,17},{2,10},{10... | collective-permute-start | bytes 3080 | tf_op jit(solution)/shard_map/ppermute | solution.py:110
  8.1 115.6 %collective-permute-start.6 = (bf16[1024,512]{1,0:T(8,128)(2,1)S(1)}, bf16[1024,512]{1,0:T(8,128)(2,1)}, u32[]{:S(2)}, u32[]{:S(2)}) collective-permute-start(bf16[1024,512]{1,0:T(8,128)(2,1)S(1)} %constant_dynamic-slice_fusion.9), channel_id=1, source_target_pairs={{0,4},{4,0},{1,5},{5,1},{2,6},{6,2},{3,7},{7,3},{8,12},{12,8},{9,1... | collective-permute-start | bytes 3145736 | tf_op jit(solution)/shard_map/ppermute | solution.py:116
  12.9 115.1 %collective-permute-start.11 = (bf16[8,256,1024]{2,1,0:T(8,128)(2,1)}, bf16[8,256,1024]{2,1,0:T(8,128)(2,1)}, u32[]{:S(2)}, u32[]{:S(2)}) collective-permute-start(bf16[8,256,1024]{2,1,0:T(8,128)(2,1)} %constant_dynamic-slice_fusion.8), channel_id=1, source_target_pairs={{0,4},{8,12},{20,16},{28,24},{1,5},{9,13},{21,17},{29,25},{2,6},{1... | collective-permute-start | bytes 12582920 | tf_op jit(solution)/shard_map/ppermute | solution.py:180
  23.2 6.7 %collective-permute-start.31 = (bf16[96,512]{1,0:T(8,128)(2,1)}, bf16[96,512]{1,0:T(8,128)(2,1)S(1)}, u32[]{:S(2)}, u32[]{:S(2)}) collective-permute-start(bf16[96,512]{1,0:T(8,128)(2,1)} %convolution_convert_fusion.8), channel_id=1, source_target_pairs={{0,3},{1,0},{2,1},{3,2},{4,7},{5,4},{6,5},{7,6},{8,11},{9,8},{10,9... | collective-permute-start | bytes 294920 | tf_op jit(solution)/shard_map/ppermute | solution.py:113
  27.3 7.2 %collective-permute-start.30 = (bf16[96,512]{1,0:T(8,128)(2,1)}, bf16[96,512]{1,0:T(8,128)(2,1)S(1)}, u32[]{:S(2)}, u32[]{:S(2)}) collective-permute-start(bf16[96,512]{1,0:T(8,128)(2,1)} %convolution_convert_fusion.9), channel_id=1, source_target_pairs={{0,2},{1,3},{2,0},{3,1},{4,6},{5,7},{6,4},{7,5},{8,10},{9,11},{10,... | collective-permute-start | bytes 294920 | tf_op jit(solution)/shard_map/ppermute | solution.py:113
  27.3 8.5 %collective-permute-start.29 = (bf16[96,512]{1,0:T(8,128)(2,1)}, bf16[96,512]{1,0:T(8,128)(2,1)S(1)}, u32[]{:S(2)}, u32[]{:S(2)}) collective-permute-start(bf16[96,512]{1,0:T(8,128)(2,1)} %convolution_convert_fusion.10), channel_id=1, source_target_pairs={{0,1},{1,2},{2,3},{3,0},{4,5},{5,6},{6,7},{7,4},{8,9},{9,10},{10,1... | collective-permute-start | bytes 294920 | tf_op jit(solution)/shard_map/ppermute | solution.py:113
  28.5 32.3 %copy-start.28 = (bf16[1,96,256]{2,1,0:T(8,128)(2,1)}, bf16[1,96,256]{2,1,0:T(8,128)(2,1)S(1)}, u32[]{:S(2)}) copy-start(bf16[1,96,256]{2,1,0:T(8,128)(2,1)S(1)} %get-tuple-element.77) | copy-start | bytes 147460
  28.6 32.6 %copy-start.26 = (bf16[1,96,256]{2,1,0:T(8,128)(2,1)}, bf16[1,96,256]{2,1,0:T(8,128)(2,1)S(1)}, u32[]{:S(2)}) copy-start(bf16[1,96,256]{2,1,0:T(8,128)(2,1)S(1)} %get-tuple-element.76) | copy-start | bytes 147460
  28.6 33.0 %copy-start.24 = (bf16[1,96,256]{2,1,0:T(8,128)(2,1)}, bf16[1,96,256]{2,1,0:T(8,128)(2,1)S(1)}, u32[]{:S(2)}) copy-start(bf16[1,96,256]{2,1,0:T(8,128)(2,1)S(1)} %get-tuple-element.63) | copy-start | bytes 147460
  28.6 17.3 %copy-start.20 = (bf16[256,512]{1,0:T(8,128)(2,1)S(1)}, bf16[256,512]{1,0:T(8,128)(2,1)}, u32[]{:S(2)}) copy-start(bf16[256,512]{1,0:T(8,128)(2,1)} %get-tuple-element.8) | copy-start | bytes 786436
  28.6 18.0 %copy-start.18 = (bf16[1,256,512]{2,1,0:T(8,128)(2,1)S(1)}, bf16[1,256,512]{2,1,0:T(8,128)(2,1)}, u32[]{:S(2)}) copy-start(bf16[1,256,512]{2,1,0:T(8,128)(2,1)} %get-tuple-element.5) | copy-start | bytes 786436
  29.9 9.6 %collective-permute-start.5 = (bf16[256,512]{1,0:T(8,128)(2,1)}, bf16[256,512]{1,0:T(8,128)(2,1)S(1)}, u32[]{:S(2)}, u32[]{:S(2)}) collective-permute-start(bf16[256,512]{1,0:T(8,128)(2,1)} %get-tuple-element.9), channel_id=1, source_target_pairs={{0,24},{8,16},{16,8},{24,0},{1,25},{9,17},{17,9},{25,1},{2,26},{10... | collective-permute-start | bytes 786440 | tf_op jit(solution)/shard_map/ppermute | solution.py:110
  34.5 110.5 %copy-start.11 = (bf16[96,512]{1,0:T(8,128)(2,1)}, bf16[96,512]{1,0:T(8,128)(2,1)S(1)}, u32[]{:S(2)}) copy-start(bf16[96,512]{1,0:T(8,128)(2,1)S(1)} %collective-permute-done.30) | copy-start | bytes 294916
  34.5 10.8 %collective-permute-start.4 = (bf16[256,512]{1,0:T(8,128)(2,1)}, bf16[256,512]{1,0:T(8,128)(2,1)S(1)}, u32[]{:S(2)}, u32[]{:S(2)}) collective-permute-start(bf16[256,512]{1,0:T(8,128)(2,1)} %get-tuple-element.10), channel_id=1, source_target_pairs={{0,16},{8,24},{16,0},{24,8},{1,17},{9,25},{17,1},{25,9},{2,18},{10... | collective-permute-start | bytes 786440 | tf_op jit(solution)/shard_map/ppermute | solution.py:110
  35.8 10.0 %collective-permute-start.3 = (bf16[256,512]{1,0:T(8,128)(2,1)}, bf16[256,512]{1,0:T(8,128)(2,1)S(1)}, u32[]{:S(2)}, u32[]{:S(2)}) collective-permute-start(bf16[256,512]{1,0:T(8,128)(2,1)} %get-tuple-element.4), channel_id=1, source_target_pairs={{0,8},{8,0},{16,24},{24,16},{1,9},{9,1},{17,25},{25,17},{2,10},{10... | collective-permute-start | bytes 786440 | tf_op jit(solution)/shard_map/ppermute | solution.py:110
  39.5 84.3 %copy-start.30 = (bf16[256,512]{1,0:T(8,128)(2,1)}, bf16[256,512]{1,0:T(8,128)(2,1)S(1)}, u32[]{:S(2)}) copy-start(bf16[256,512]{1,0:T(8,128)(2,1)S(1)} %collective-permute-done.5) | copy-start | bytes 786436
  39.5 11.5 %collective-permute-start.2 = (bf16[256,512]{1,0:T(8,128)(2,1)S(1)}, bf16[256,512]{1,0:T(8,128)(2,1)S(1)}, u32[]{:S(2)}, u32[]{:S(2)}) collective-permute-start(bf16[256,512]{1,0:T(8,128)(2,1)S(1)} %copy-done.22), channel_id=1, source_target_pairs={{0,24},{8,16},{16,8},{24,0},{1,25},{9,17},{17,9},{25,1},{2,26},{10... | collective-permute-start | bytes 786440 | tf_op jit(solution)/shard_map/ppermute | solution.py:110
  45.3 78.4 %copy-start.32 = (bf16[256,512]{1,0:T(8,128)(2,1)}, bf16[256,512]{1,0:T(8,128)(2,1)S(1)}, u32[]{:S(2)}) copy-start(bf16[256,512]{1,0:T(8,128)(2,1)S(1)} %collective-permute-done.4) | copy-start | bytes 786436
  45.4 10.7 %collective-permute-start.1 = (bf16[256,512]{1,0:T(8,128)(2,1)S(1)}, bf16[256,512]{1,0:T(8,128)(2,1)S(1)}, u32[]{:S(2)}, u32[]{:S(2)}) collective-permute-start(bf16[256,512]{1,0:T(8,128)(2,1)S(1)} %copy-done.21), channel_id=1, source_target_pairs={{0,16},{8,24},{16,0},{24,8},{1,17},{9,25},{17,1},{25,9},{2,18},{10... | collective-permute-start | bytes 786440 | tf_op jit(solution)/shard_map/ppermute | solution.py:110
  45.9 77.9 %copy-start.34 = (bf16[256,512]{1,0:T(8,128)(2,1)}, bf16[256,512]{1,0:T(8,128)(2,1)S(1)}, u32[]{:S(2)}) copy-start(bf16[256,512]{1,0:T(8,128)(2,1)S(1)} %collective-permute-done.3) | copy-start | bytes 786436
  45.9 13.2 %collective-permute-start = (bf16[256,512]{1,0:T(8,128)(2,1)S(1)}, bf16[256,512]{1,0:T(8,128)(2,1)S(1)}, u32[]{:S(2)}, u32[]{:S(2)}) collective-permute-start(bf16[256,512]{1,0:T(8,128)(2,1)S(1)} %copy-done.20), channel_id=1, source_target_pairs={{0,8},{8,0},{16,24},{24,16},{1,9},{9,1},{17,25},{25,17},{2,10},{10... | collective-permute-start | bytes 786440 | tf_op jit(solution)/shard_map/ppermute | solution.py:110
  51.0 72.8 %copy-start.36 = (bf16[256,512]{1,0:T(8,128)(2,1)}, bf16[256,512]{1,0:T(8,128)(2,1)S(1)}, u32[]{:S(2)}) copy-start(bf16[256,512]{1,0:T(8,128)(2,1)S(1)} %collective-permute-done.2) | copy-start | bytes 786436
  51.0 13.4 %collective-permute-start.20 = (bf16[4,96,512]{2,1,0:T(8,128)(2,1)S(1)}, bf16[4,96,512]{2,1,0:T(8,128)(2,1)S(1)}, u32[]{:S(2)}, u32[]{:S(2)}) collective-permute-start(bf16[4,96,512]{2,1,0:T(8,128)(2,1)S(1)} %convolution_convert_fusion), channel_id=1, source_target_pairs={{0,3},{1,0},{2,1},{3,2},{4,7},{5,4},{6,5},{7,6},{8,11},{9,8},{10,9... | collective-permute-start | bytes 1179656 | tf_op jit(solution)/shard_map/ppermute | solution.py:113
  56.1 67.7 %copy-start.37 = (bf16[256,512]{1,0:T(8,128)(2,1)}, bf16[256,512]{1,0:T(8,128)(2,1)S(1)}, u32[]{:S(2)}) copy-start(bf16[256,512]{1,0:T(8,128)(2,1)S(1)} %collective-permute-done.1) | copy-start | bytes 786436
  56.1 47.9 %collective-permute-start.19 = (bf16[4,96,512]{2,1,0:T(8,128)(2,1)S(1)}, bf16[4,96,512]{2,1,0:T(8,128)(2,1)S(1)}, u32[]{:S(2)}, u32[]{:S(2)}) collective-permute-start(bf16[4,96,512]{2,1,0:T(8,128)(2,1)S(1)} %convolution_convert_fusion.1), channel_id=1, source_target_pairs={{0,2},{1,3},{2,0},{3,1},{4,6},{5,7},{6,4},{7,5},{8,10},{9,11},{10,... | collective-permute-start | bytes 1179656 | tf_op jit(solution)/shard_map/ppermute | solution.py:113
  59.0 64.8 %copy-start.38 = (bf16[256,512]{1,0:T(8,128)(2,1)}, bf16[256,512]{1,0:T(8,128)(2,1)S(1)}, u32[]{:S(2)}) copy-start(bf16[256,512]{1,0:T(8,128)(2,1)S(1)} %collective-permute-done) | copy-start | bytes 786436
  59.0 45.0 %collective-permute-start.18 = (bf16[4,96,512]{2,1,0:T(8,128)(2,1)S(1)}, bf16[4,96,512]{2,1,0:T(8,128)(2,1)S(1)}, u32[]{:S(2)}, u32[]{:S(2)}) collective-permute-start(bf16[4,96,512]{2,1,0:T(8,128)(2,1)S(1)} %convolution_convert_fusion.2), channel_id=1, source_target_pairs={{0,1},{1,2},{2,3},{3,0},{4,5},{5,6},{6,7},{7,4},{8,9},{9,10},{10,1... | collective-permute-start | bytes 1179656 | tf_op jit(solution)/shard_map/ppermute | solution.py:113
  64.4 40.6 %collective-permute-start.17 = (bf16[4,96,512]{2,1,0:T(8,128)(2,1)S(1)}, bf16[4,96,512]{2,1,0:T(8,128)(2,1)S(1)}, u32[]{:S(2)}, u32[]{:S(2)}) collective-permute-start(bf16[4,96,512]{2,1,0:T(8,128)(2,1)S(1)} %convolution_convert_fusion.4), channel_id=1, source_target_pairs={{0,3},{1,0},{2,1},{3,2},{4,7},{5,4},{6,5},{7,6},{8,11},{9,8},{10,9... | collective-permute-start | bytes 1179656 | tf_op jit(solution)/shard_map/ppermute | solution.py:113
  104.0 19.5 %collective-permute-start.16 = (bf16[4,96,512]{2,1,0:T(8,128)(2,1)S(1)}, bf16[4,96,512]{2,1,0:T(8,128)(2,1)S(1)}, u32[]{:S(2)}, u32[]{:S(2)}) collective-permute-start(bf16[4,96,512]{2,1,0:T(8,128)(2,1)S(1)} %convolution_convert_fusion.5), channel_id=1, source_target_pairs={{0,2},{1,3},{2,0},{3,1},{4,6},{5,7},{6,4},{7,5},{8,10},{9,11},{10,... | collective-permute-start | bytes 1179656 | tf_op jit(solution)/shard_map/ppermute | solution.py:113
  104.0 19.5 %collective-permute-start.15 = (bf16[4,96,512]{2,1,0:T(8,128)(2,1)S(1)}, bf16[4,96,512]{2,1,0:T(8,128)(2,1)S(1)}, u32[]{:S(2)}, u32[]{:S(2)}) collective-permute-start(bf16[4,96,512]{2,1,0:T(8,128)(2,1)S(1)} %convolution_convert_fusion.6), channel_id=1, source_target_pairs={{0,1},{1,2},{2,3},{3,0},{4,5},{5,6},{6,7},{7,4},{8,9},{9,10},{10,1... | collective-permute-start | bytes 1179656 | tf_op jit(solution)/shard_map/ppermute | solution.py:113
  104.9 27.4 %copy-start.1 = (bf16[4,4,2,48,512]{4,3,2,1,0:T(8,128)(2,1)}, bf16[4,4,2,48,512]{4,3,2,1,0:T(8,128)(2,1)S(1)}, u32[]{:S(2)}) copy-start(bf16[4,4,2,48,512]{4,3,2,1,0:T(8,128)(2,1)S(1)} %pad_maximum_fusion.1) | copy-start | bytes 4718596
  104.9 35.0 %collective-permute-start.32 = (f32[4,2,48,256]{3,2,0,1:T(8,128)S(1)}, f32[4,2,48,256]{3,2,0,1:T(8,128)S(1)}, u32[]{:S(2)}, u32[]{:S(2)}) collective-permute-start(f32[4,2,48,256]{3,2,0,1:T(8,128)S(1)} %fusion.56), channel_id=1, source_target_pairs={{0,4},{4,0},{1,5},{5,1},{2,6},{6,2},{3,7},{7,3},{8,12},{12,8},{9,1... | collective-permute-start | bytes 1179656 | tf_op jit(solution)/shard_map/ppermute | solution.py:116
  128.0 53.7 %collective-permute-start.7 = (f32[4,256,512]{2,1,0:T(8,128)}, f32[4,256,512]{2,1,0:T(8,128)}, u32[]{:S(2)}, u32[]{:S(2)}) collective-permute-start(f32[4,256,512]{2,1,0:T(8,128)} %fusion.28), channel_id=1, source_target_pairs={{0,4},{4,0},{1,5},{5,1},{2,6},{6,2},{3,7},{7,3},{8,12},{12,8},{9,1... | collective-permute-start | bytes 6291464 | tf_op jit(solution)/shard_map/ppermute | solution.py:116
  138.2 38.7 %collective-permute-start.21 = (f32[4,4,2,48,128]{4,3,1,0,2:T(8,128)}, f32[4,4,2,48,128]{4,3,1,0,2:T(8,128)}, u32[]{:S(2)}, u32[]{:S(2)}) collective-permute-start(f32[4,4,2,48,128]{4,3,1,0,2:T(8,128)} %constant_dynamic-slice_fusion.7), channel_id=1, source_target_pairs={{0,4},{4,0},{1,5},{5,1},{2,6},{6,2},{3,7},{7,3},{8,12},{12,8},{9,1... | collective-permute-start | bytes 2359304 | tf_op jit(solution)/shard_map/ppermute | solution.py:116
  140.2 8.8 %collective-permute-start.35 = (bf16[4,2,48,256]{3,2,0,1:T(8,128)(2,1)S(1)}, bf16[4,2,48,256]{3,2,0,1:T(8,128)(2,1)S(1)}, u32[]{:S(2)}, u32[]{:S(2)}) collective-permute-start(bf16[4,2,48,256]{3,2,0,1:T(8,128)(2,1)S(1)} %multiply_convert_fusion), channel_id=1, source_target_pairs={{0,24},{8,16},{16,8},{24,0},{1,25},{9,17},{17,9},{25,1},{2,26},{10... | collective-permute-start | bytes 589832 | tf_op jit(solution)/shard_map/ppermute | solution.py:110
  140.3 11.2 %collective-permute-start.34 = (bf16[4,2,48,256]{3,2,0,1:T(8,128)(2,1)S(1)}, bf16[4,2,48,256]{3,2,0,1:T(8,128)(2,1)S(1)}, u32[]{:S(2)}, u32[]{:S(2)}) collective-permute-start(bf16[4,2,48,256]{3,2,0,1:T(8,128)(2,1)S(1)} %multiply_convert_fusion), channel_id=1, source_target_pairs={{0,16},{8,24},{16,0},{24,8},{1,17},{9,25},{17,1},{25,9},{2,18},{10... | collective-permute-start | bytes 589832 | tf_op jit(solution)/shard_map/ppermute | solution.py:110
  141.2 10.9 %collective-permute-start.33 = (bf16[4,2,48,256]{3,2,0,1:T(8,128)(2,1)S(1)}, bf16[4,2,48,256]{3,2,0,1:T(8,128)(2,1)S(1)}, u32[]{:S(2)}, u32[]{:S(2)}) collective-permute-start(bf16[4,2,48,256]{3,2,0,1:T(8,128)(2,1)S(1)} %multiply_convert_fusion), channel_id=1, source_target_pairs={{0,8},{8,0},{16,24},{24,16},{1,9},{9,1},{17,25},{25,17},{2,10},{10... | collective-permute-start | bytes 589832 | tf_op jit(solution)/shard_map/ppermute | solution.py:110
  149.0 69.2 %collective-permute-start.49 = (bf16[4,2,48,512]{3,2,0,1:T(8,128)(2,1)}, bf16[4,2,48,512]{3,2,0,1:T(8,128)(2,1)}, u32[]{:S(2)}, u32[]{:S(2)}) collective-permute-start(bf16[4,2,48,512]{3,2,0,1:T(8,128)(2,1)} %pad_maximum_fusion.6), channel_id=1, source_target_pairs={{0,24},{8,16},{16,8},{24,0},{1,25},{9,17},{17,9},{25,1},{2,26},{10... | collective-permute-start | bytes 1179656 | tf_op jit(solution)/shard_map/ppermute | solution.py:110
  151.5 67.7 %collective-permute-start.48 = (bf16[4,2,48,512]{3,2,0,1:T(8,128)(2,1)}, bf16[4,2,48,512]{3,2,0,1:T(8,128)(2,1)}, u32[]{:S(2)}, u32[]{:S(2)}) collective-permute-start(bf16[4,2,48,512]{3,2,0,1:T(8,128)(2,1)} %pad_maximum_fusion.6), channel_id=1, source_target_pairs={{0,16},{8,24},{16,0},{24,8},{1,17},{9,25},{17,1},{25,9},{2,18},{10... | collective-permute-start | bytes 1179656 | tf_op jit(solution)/shard_map/ppermute | solution.py:110
  178.5 8.6 %collective-permute-start.24 = (f32[4,2,48,128]{3,2,0,1:T(8,128)S(1)}, f32[4,2,48,128]{3,2,0,1:T(8,128)S(1)}, u32[]{:S(2)}, u32[]{:S(2)}) collective-permute-start(f32[4,2,48,128]{3,2,0,1:T(8,128)S(1)} %get-tuple-element.19), channel_id=1, source_target_pairs={{0,24},{8,16},{16,8},{24,0},{1,25},{9,17},{17,9},{25,1},{2,26},{10... | collective-permute-start | bytes 589832 | tf_op jit(solution)/shard_map/ppermute | solution.py:110
  180.6 9.0 %collective-permute-start.23 = (f32[4,2,48,128]{3,2,0,1:T(8,128)S(1)}, f32[4,2,48,128]{3,2,0,1:T(8,128)S(1)}, u32[]{:S(2)}, u32[]{:S(2)}) collective-permute-start(f32[4,2,48,128]{3,2,0,1:T(8,128)S(1)} %get-tuple-element.20), channel_id=1, source_target_pairs={{0,16},{8,24},{16,0},{24,8},{1,17},{9,25},{17,1},{25,9},{2,18},{10... | collective-permute-start | bytes 589832 | tf_op jit(solution)/shard_map/ppermute | solution.py:110
  181.6 8.0 %collective-permute-start.22 = (f32[4,2,48,128]{3,2,0,1:T(8,128)S(1)}, f32[4,2,48,128]{3,2,0,1:T(8,128)S(1)}, u32[]{:S(2)}, u32[]{:S(2)}) collective-permute-start(f32[4,2,48,128]{3,2,0,1:T(8,128)S(1)} %get-tuple-element.18), channel_id=1, source_target_pairs={{0,8},{8,0},{16,24},{24,16},{1,9},{9,1},{17,25},{25,17},{2,10},{10... | collective-permute-start | bytes 589832 | tf_op jit(solution)/shard_map/ppermute | solution.py:110
  189.7 1.4 collective-permute-start.25
  195.0 6.2 %collective-permute-start.46 = (bf16[4,2,48,64]{3,2,0,1:T(8,128)(2,1)S(1)}, bf16[4,2,48,64]{3,2,0,1:T(8,128)(2,1)S(1)}, u32[]{:S(2)}, u32[]{:S(2)}) collective-permute-start(bf16[4,2,48,64]{3,2,0,1:T(8,128)(2,1)S(1)} %get-tuple-element.26), channel_id=1, source_target_pairs={{0,24},{8,16},{16,8},{24,0},{1,25},{9,17},{17,9},{25,1},{2,26},{10... | collective-permute-start | bytes 147464 | tf_op jit(solution)/shard_map/ppermute | solution.py:110
  197.2 6.1 %collective-permute-start.45 = (bf16[4,2,48,64]{3,2,0,1:T(8,128)(2,1)S(1)}, bf16[4,2,48,64]{3,2,0,1:T(8,128)(2,1)S(1)}, u32[]{:S(2)}, u32[]{:S(2)}) collective-permute-start(bf16[4,2,48,64]{3,2,0,1:T(8,128)(2,1)S(1)} %get-tuple-element.27), channel_id=1, source_target_pairs={{0,16},{8,24},{16,0},{24,8},{1,17},{9,25},{17,1},{25,9},{2,18},{10... | collective-permute-start | bytes 147464 | tf_op jit(solution)/shard_map/ppermute | solution.py:110
  198.3 6.7 %collective-permute-start.44 = (bf16[4,2,48,64]{3,2,0,1:T(8,128)(2,1)S(1)}, bf16[4,2,48,64]{3,2,0,1:T(8,128)(2,1)S(1)}, u32[]{:S(2)}, u32[]{:S(2)}) collective-permute-start(bf16[4,2,48,64]{3,2,0,1:T(8,128)(2,1)S(1)} %get-tuple-element.28), channel_id=1, source_target_pairs={{0,8},{8,0},{16,24},{24,16},{1,9},{9,1},{17,25},{25,17},{2,10},{10... | collective-permute-start | bytes 147464 | tf_op jit(solution)/shard_map/ppermute | solution.py:110
  201.2 19.0 %collective-permute-start.47 = (bf16[4,2,48,512]{3,2,0,1:T(8,128)(2,1)}, bf16[4,2,48,512]{3,2,0,1:T(8,128)(2,1)}, u32[]{:S(2)}, u32[]{:S(2)}) collective-permute-start(bf16[4,2,48,512]{3,2,0,1:T(8,128)(2,1)} %pad_maximum_fusion.6), channel_id=1, source_target_pairs={{0,8},{8,0},{16,24},{24,16},{1,9},{9,1},{17,25},{25,17},{2,10},{10... | collective-permute-start | bytes 1179656 | tf_op jit(solution)/shard_map/ppermute | solution.py:110
  203.3 24.1 %collective-permute-start.10 = (f32[256,512]{1,0:T(8,128)}, f32[256,512]{1,0:T(8,128)}, u32[]{:S(2)}, u32[]{:S(2)}) collective-permute-start(f32[256,512]{1,0:T(8,128)} %get-tuple-element.12), channel_id=1, source_target_pairs={{0,24},{8,16},{16,8},{24,0},{1,25},{9,17},{17,9},{25,1},{2,26},{10... | collective-permute-start | bytes 1572872 | tf_op jit(solution)/shard_map/ppermute | solution.py:110
  204.9 24.7 %collective-permute-start.9 = (f32[256,512]{1,0:T(8,128)}, f32[256,512]{1,0:T(8,128)}, u32[]{:S(2)}, u32[]{:S(2)}) collective-permute-start(f32[256,512]{1,0:T(8,128)} %get-tuple-element.13), channel_id=1, source_target_pairs={{0,16},{8,24},{16,0},{24,8},{1,17},{9,25},{17,1},{25,9},{2,18},{10... | collective-permute-start | bytes 1572872 | tf_op jit(solution)/shard_map/ppermute | solution.py:110
  218.6 15.8 %collective-permute-start.8 = (f32[256,512]{1,0:T(8,128)S(1)}, f32[256,512]{1,0:T(8,128)S(1)}, u32[]{:S(2)}, u32[]{:S(2)}) collective-permute-start(f32[256,512]{1,0:T(8,128)S(1)} %copy-done.10), channel_id=1, source_target_pairs={{0,8},{8,0},{16,24},{24,16},{1,9},{9,1},{17,25},{25,17},{2,10},{10... | collective-permute-start | bytes 1572872 | tf_op jit(solution)/shard_map/ppermute | solution.py:110
  219.2 16.6 %collective-permute-start.28 = (bf16[96,512]{1,0:T(8,128)(2,1)S(1)}, bf16[96,512]{1,0:T(8,128)(2,1)S(1)}, u32[]{:S(2)}, u32[]{:S(2)}) collective-permute-start(bf16[96,512]{1,0:T(8,128)(2,1)S(1)} %bitcast.259), channel_id=1, source_target_pairs={{0,1},{1,2},{2,3},{3,0},{4,5},{5,6},{6,7},{7,4},{8,9},{9,10},{10,1... | collective-permute-start | bytes 294920 | tf_op jit(solution)/shard_map/ppermute | solution.py:113
  220.2 17.0 %collective-permute-start.27 = (bf16[96,512]{1,0:T(8,128)(2,1)S(1)}, bf16[96,512]{1,0:T(8,128)(2,1)S(1)}, u32[]{:S(2)}, u32[]{:S(2)}) collective-permute-start(bf16[96,512]{1,0:T(8,128)(2,1)S(1)} %bitcast.258), channel_id=1, source_target_pairs={{0,2},{1,3},{2,0},{3,1},{4,6},{5,7},{6,4},{7,5},{8,10},{9,11},{10,... | collective-permute-start | bytes 294920 | tf_op jit(solution)/shard_map/ppermute | solution.py:113
  227.4 10.0 %collective-permute-start.26 = (bf16[96,512]{1,0:T(8,128)(2,1)S(1)}, bf16[96,512]{1,0:T(8,128)(2,1)S(1)}, u32[]{:S(2)}, u32[]{:S(2)}) collective-permute-start(bf16[96,512]{1,0:T(8,128)(2,1)S(1)} %bitcast.257), channel_id=1, source_target_pairs={{0,3},{1,0},{2,1},{3,2},{4,7},{5,4},{6,5},{7,6},{8,11},{9,8},{10,9... | collective-permute-start | bytes 294920 | tf_op jit(solution)/shard_map/ppermute | solution.py:113
  229.6 10.9 %collective-permute-start.36 = (bf16[8,64,512]{2,1,0:T(8,128)(2,1)S(1)}, bf16[8,64,512]{2,1,0:T(8,128)(2,1)S(1)}, u32[]{:S(2)}, u32[]{:S(2)}) collective-permute-start(bf16[8,64,512]{2,1,0:T(8,128)(2,1)S(1)} %bitcast.272), channel_id=1, source_target_pairs={{0,0},{4,16},{8,8},{12,24},{16,4},{20,20},{24,12},{28,28},{1,1},{5... | collective-permute-start | bytes 1572872 | tf_op jit(solution)/shard_map/ppermute | solution.py:208
  234.4 23.0 %collective-permute-start.37 = (bf16[8,64,512]{2,1,0:T(8,128)(2,1)S(1)}, bf16[8,64,512]{2,1,0:T(8,128)(2,1)S(1)}, u32[]{:S(2)}, u32[]{:S(2)}) collective-permute-start(bf16[8,64,512]{2,1,0:T(8,128)(2,1)S(1)} %bitcast.270), channel_id=1, source_target_pairs={{0,16},{4,0},{8,24},{12,8},{16,20},{20,4},{24,28},{28,12},{1,17},{... | collective-permute-start | bytes 1572872 | tf_op jit(solution)/shard_map/ppermute | solution.py:208
  235.7 23.2 %collective-permute-start.38 = (bf16[8,64,512]{2,1,0:T(8,128)(2,1)S(1)}, bf16[8,64,512]{2,1,0:T(8,128)(2,1)S(1)}, u32[]{:S(2)}, u32[]{:S(2)}) collective-permute-start(bf16[8,64,512]{2,1,0:T(8,128)(2,1)S(1)} %bitcast.269), channel_id=1, source_target_pairs={{0,8},{4,24},{8,0},{12,16},{16,12},{20,28},{24,4},{28,20},{1,9},{5... | collective-permute-start | bytes 1572872 | tf_op jit(solution)/shard_map/ppermute | solution.py:208
  237.1 25.0 %collective-permute-start.39 = (bf16[8,64,512]{2,1,0:T(8,128)(2,1)S(1)}, bf16[8,64,512]{2,1,0:T(8,128)(2,1)S(1)}, u32[]{:S(2)}, u32[]{:S(2)}) collective-permute-start(bf16[8,64,512]{2,1,0:T(8,128)(2,1)S(1)} %bitcast.273), channel_id=1, source_target_pairs={{0,24},{4,8},{8,16},{12,0},{16,28},{20,12},{24,20},{28,4},{1,25},{... | collective-permute-start | bytes 1572872 | tf_op jit(solution)/shard_map/ppermute | solution.py:208
  237.4 24.8 %collective-permute-start.40 = (bf16[8,64,512]{2,1,0:T(8,128)(2,1)S(1)}, bf16[8,64,512]{2,1,0:T(8,128)(2,1)S(1)}, u32[]{:S(2)}, u32[]{:S(2)}) collective-permute-start(bf16[8,64,512]{2,1,0:T(8,128)(2,1)S(1)} %bitcast.267), channel_id=1, source_target_pairs={{0,0},{4,16},{8,8},{12,24},{16,4},{20,20},{24,12},{28,28},{1,1},{5... | collective-permute-start | bytes 1572872 | tf_op jit(solution)/shard_map/ppermute | solution.py:208
  240.5 36.3 %collective-permute-start.41 = (bf16[8,64,512]{2,1,0:T(8,128)(2,1)S(1)}, bf16[8,64,512]{2,1,0:T(8,128)(2,1)S(1)}, u32[]{:S(2)}, u32[]{:S(2)}) collective-permute-start(bf16[8,64,512]{2,1,0:T(8,128)(2,1)S(1)} %bitcast.266), channel_id=1, source_target_pairs={{0,16},{4,0},{8,24},{12,8},{16,20},{20,4},{24,28},{28,12},{1,17},{... | collective-permute-start | bytes 1572872 | tf_op jit(solution)/shard_map/ppermute | solution.py:208
  257.4 19.6 %collective-permute-start.42 = (bf16[8,64,512]{2,1,0:T(8,128)(2,1)S(1)}, bf16[8,64,512]{2,1,0:T(8,128)(2,1)S(1)}, u32[]{:S(2)}, u32[]{:S(2)}) collective-permute-start(bf16[8,64,512]{2,1,0:T(8,128)(2,1)S(1)} %bitcast.268), channel_id=1, source_target_pairs={{0,8},{4,24},{8,0},{12,16},{16,12},{20,28},{24,4},{28,20},{1,9},{5... | collective-permute-start | bytes 1572872 | tf_op jit(solution)/shard_map/ppermute | solution.py:208
  259.0 24.5 %collective-permute-start.43 = (bf16[8,64,512]{2,1,0:T(8,128)(2,1)S(1)}, bf16[8,64,512]{2,1,0:T(8,128)(2,1)S(1)}, u32[]{:S(2)}, u32[]{:S(2)}) collective-permute-start(bf16[8,64,512]{2,1,0:T(8,128)(2,1)S(1)} %bitcast.271), channel_id=1, source_target_pairs={{0,24},{4,8},{8,16},{12,0},{16,28},{20,12},{24,20},{28,4},{1,25},{... | collective-permute-start | bytes 1572872 | tf_op jit(solution)/shard_map/ppermute | solution.py:208
  (25 other events, 160.8 us)

commit v2 on v1

--- a/solution.py
+++ b/solution.py
@@ -1,6 +1,8 @@
 import jax
 import jax.numpy as jnp
 from jax import lax
+from jax.experimental import pallas as pl
+from jax.experimental.pallas import tpu as pltpu
 from jax.sharding import PartitionSpec as P
 
 CAPD = 12
@@ -82,6 +84,24 @@
     )
 
 
+def base_kernel(order, *refs):
+    out = refs[-1]
+    w_refs, x_refs = refs[-3:-1], refs[:-3]
+    chunks = len(x_refs) // (out.shape[0] // 2)
+    cw = x_refs[0].shape[1]
+    for k in range(out.shape[0] // 2):
+        for side in range(2):
+            total = None
+            for c in range(chunks):
+                term = jnp.dot(
+                    x_refs[k * chunks + c][...],
+                    w_refs[side][c * cw : (c + 1) * cw, :],
+                    preferred_element_type=jnp.float32,
+                )
+                total = term if total is None else total + term
+            out[order[2 * k + side]] = total
+
+
 def column_body(
     input_rows,
     value_weight_frozen,
@@ -118,19 +138,20 @@
     def cut(v, start, size, axis):
         return lax.dynamic_slice_in_dim(v, start, size, axis)
 
-    own_dom = lax.broadcasted_iota(jnp.int32, (gslots, GROUP, 1), 0) // CAPD
-    own_dom = own_dom == lax.broadcasted_iota(jnp.int32, (gslots, GROUP, 1), 1)
+    def own_lanes(n):
+        slot = lax.broadcasted_iota(jnp.int32, (gslots, GROUP * n), 0) // CAPD
+        return slot == lax.broadcasted_iota(jnp.int32, (gslots, GROUP * n), 1) // n
 
     def spread(v):
-        n = v.shape[-1]
-        wide = jnp.where(own_dom, v[..., None, :], jnp.zeros((), v.dtype))
-        return wide.reshape(*v.shape[:-1], GROUP * n)
+        wide = jnp.concatenate([v] * GROUP, axis=-1)
+        return jnp.where(own_lanes(v.shape[-1]), wide, jnp.zeros((), v.dtype))
 
     def pick(v):
         n = v.shape[-1] // GROUP
-        total = jnp.where(own_dom[:, 0], v[..., :n], 0.0)
+        slot = lax.broadcasted_iota(jnp.int32, (gslots, n), 0) // CAPD
+        total = v[..., :n]
         for e in range(1, GROUP):
-            total = total + jnp.where(own_dom[:, e], v[..., e * n : (e + 1) * n], 0.0)
+            total = jnp.where(slot == e, v[..., e * n : (e + 1) * n], total)
         return total
 
     x_in = []
@@ -138,10 +159,14 @@
         piece = []
         for k in range(fsdp):
             block = cut(input_rows, (f ^ k) * kf_width + t * kt + c * cw, cw, 1)
+            if c == 0:
+                dom_row = jnp.pad(domain.T.astype(bf16), ((0, 15), (0, cw - rows)))
+                block = jnp.concatenate([block, dom_row], axis=0)
             piece.append(over_f(block, k) if k else block)
         x_in.append(piece)
-    place = slot_places(domain[:, 0], ad * dloc)
-    places = [over_f(place, k) if k else place for k in range(fsdp)]
+    doms = [v[rows, :rows].astype(jnp.int32) for v in x_in[0]]
+    x_in[0] = [v[:rows] for v in x_in[0]]
+    places = [slot_places(v, ad * dloc) for v in [domain[:, 0]] + doms[1:]]
 
     slot_iota = lax.broadcasted_iota(jnp.int32, (slots, rows), 0)
 
@@ -153,70 +178,86 @@
     for ka in range(ad):
         block = jnp.dot(own_hot[ka], layer_output_gradient, **f32).astype(bf16)
         dy.append(over_a(block, ka) if ka else block)
+
+    hots = jnp.stack(
+        [jnp.stack([onehot(kf, ka) for kf in range(fsdp)]) for ka in range(ad)]
+    )
+    x_routed = []
+    for c in range(CHUNKS):
+        piece = []
+        for ka in range(ad):
+            block = jnp.einsum("fin,fnw->fiw", hots[ka], jnp.stack(x_in[c]), **f32)
+            block = block.astype(bf16)
+            if c == 0 and ka == ad - 1:
+                block, dn_held, w_held = lax.optimization_barrier(
+                    (block, adapter_down_weight, value_weight_frozen)
+                )
+            piece.append(over_a(block, ka) if ka else block)
+        x_routed.append(jnp.stack(piece).reshape(ad, fsdp, ngroup, gslots, cw))
+
     dy = jnp.stack(dy).reshape(ad, ngroup, gslots, vloc)
     up = adapter_up_weight.reshape(ngroup, GROUP * rank, vloc)
     back = pick(jnp.einsum("agkv,gjv->agkj", dy, up, **f32))
     back = (adapter_scale * (back + swap(back))).astype(bf16)
-    backs = jnp.stack([over_f(back, k) if k else back for k in range(fsdp)], axis=1)
-    dys = jnp.stack([over_f(dy, k) if k else dy for k in range(fsdp)])
-
-    hots = jnp.stack(
-        [jnp.stack([onehot(kf, ka) for kf in range(fsdp)]) for ka in range(ad)]
-    )
-    x_full = [jnp.stack(piece) for piece in x_in]
-    x_routed = []
-    for c in range(CHUNKS):
-        piece = []
-        for ka in range(ad):
-            block = jnp.einsum("fin,fnw->fiw", hots[ka], x_full[c], **f32).astype(bf16)
-            piece.append(over_a(block, ka) if ka else block)
-        x_routed.append(jnp.stack(piece).reshape(ad, fsdp, ngroup, gslots, cw))
+    back_all = lax.all_gather(back, "fsdp")
+    dy_all = lax.all_gather(dy, "fsdp")
 
     holder = t == fy
     col0 = fx * kf_width
-    down_mine = cut(adapter_down_weight, col0 + t * kt, kt, 2)
-    down_other = cut(adapter_down_weight, col0 + (1 - t) * kt, kt, 2)
+    down_mine = cut(dn_held, col0 + t * kt, kt, 2)
+    down_other = cut(dn_held, col0 + (1 - t) * kt, kt, 2)
     pairs = [(i * 2 + i // 2, i * 2 + 1 - i // 2) for i in range(fsdp)]
     down_got = lax.ppermute(down_other, ("fsdp", "tp"), pairs)
     down = jnp.where(holder, down_mine, down_got).reshape(ngroup, GROUP * rank, kt)
 
-    w_mine = cut(value_weight_frozen, t * kt, kt, 0)
-    w_got = swap(cut(value_weight_frozen, (1 - t) * kt, kt, 0))
-    x_cols = jnp.concatenate(x_full, axis=2)
-    base_other = jnp.einsum("fnw,wv->fnv", x_cols, w_got, **f32)
-    base = jnp.einsum("fnw,wv->fnv", x_cols, w_mine, **f32) + swap(base_other)
-    base_sum = base[0]
-    for k in range(1, fsdp):
-        base_sum = base_sum + over_f(base[k], k)
+    w_mine = cut(w_held, t * kt, kt, 0)
+    w_got = swap(cut(w_held, (1 - t) * kt, kt, 0))
+    order = jnp.stack([(f ^ k) * 2 + (t ^ s) for k in range(fsdp) for s in range(2)])
+    vmem = pl.BlockSpec(memory_space=pltpu.VMEM)
+    base = pl.pallas_call(
+        base_kernel,
+        out_shape=jax.ShapeDtypeStruct((2 * fsdp, rows, vloc), jnp.float32),
+        in_specs=[pl.BlockSpec(memory_space=pltpu.SMEM)] + [vmem] * (fsdp * CHUNKS + 2),
+        out_specs=vmem,
+        compiler_params=pltpu.CompilerParams(vmem_limit_bytes=32 << 20),
+        cost_estimate=pl.CostEstimate(
+            flops=4 * fsdp * rows * kt * vloc, bytes_accessed=10 << 20, transcendentals=0
+        ),
+    )(order, *[x_in[c][k] for k in range(fsdp) for c in range(CHUNKS)], w_mine, w_got)
+    base = lax.psum_scatter(base, ("fsdp", "tp"), scatter_dimension=0)
+
+    backs = jnp.stack([cut(back_all, f ^ k, 1, 0)[0] for k in range(fsdp)], axis=1)
+    parts = jnp.split(backs, fsdp, axis=-1)
+    parts = [jnp.where(fx == 1, parts[i ^ 1], parts[i]) for i in range(fsdp)]
+    parts = [jnp.where(t == 1, parts[i ^ 2], parts[i]) for i in range(fsdp)]
+    masked = spread(jnp.concatenate(parts, axis=-1))
 
     grad_a = jnp.zeros((dloc, rloc, half), jnp.float32)
-    rounds = [(p, q) for p in range(2) for q in range(2)]
-    masked = []
-    for p, q in rounds:
-        owner = (t ^ q) * 2 + (fx ^ p)
-        masked.append(spread(cut(backs, owner * rloc, rloc, 4)))
+    rhalf = rank // 2
+    hid = None
     for c in range(CHUNKS):
-        for (p, q), mb in zip(rounds, masked):
-            block = jnp.einsum("abgkj,abgkw->gjw", mb, x_routed[c], **f32)
-            block = block.astype(bf16).reshape(dloc, rloc, cw)
+        part = jnp.einsum(
+            "abgkw,gjw->abgkj", x_routed[c], down[:, :, c * cw : (c + 1) * cw], **f32
+        )
+        hid = pick(part) if hid is None else hid + pick(part)
+        if c == CHUNKS - 1:
+            hid = cut(hid, t * rhalf, rhalf, 4) + swap(cut(hid, (1 - t) * rhalf, rhalf, 4))
+        hid, masked = lax.optimization_barrier((hid, masked))
+
+        sums = jnp.einsum("abgkj,abgkw->gjw", masked, x_routed[c], **f32)
+        sums = sums.astype(bf16).reshape(dloc, fsdp, rloc, cw)
+        for r in range(fsdp):
+            p, q = r % 2, r // 2
             perm = [
                 ((y * 2 + x) * 2 + s, ((s ^ q) * 2 + (x ^ p)) * 2 + y)
                 for y in range(2)
                 for x in range(2)
                 for s in range(2)
             ]
-            got = lax.ppermute(block, ("fsdp", "tp"), perm)
+            got = lax.ppermute(sums[:, r], ("fsdp", "tp"), perm)
             start = (fx ^ p) * kf_width + (fy ^ q) * kt + c * cw
             grad_a = lax.dynamic_update_slice_in_dim(grad_a, got.astype(jnp.float32), start, 2)
 
-    hid = None
-    for c in range(CHUNKS):
-        part = jnp.einsum(
-            "abgkw,gjw->abgkj", x_routed[c], down[:, :, c * cw : (c + 1) * cw], **f32
-        )
-        hid = pick(part) if hid is None else hid + pick(part)
-    rhalf = rank // 2
-    hid = cut(hid, t * rhalf, rhalf, 4) + swap(cut(hid, (1 - t) * rhalf, rhalf, 4))
     hid_sum = hid[:, 0]
     for k in range(1, fsdp):
         hid_sum = hid_sum + over_f(hid[:, k], k)
@@ -232,13 +273,14 @@
     delta = delta.astype(bf16).reshape(ad, slots, vloc)
     back_rows = [over_a(delta[ka], ad - ka) if ka else delta[ka] for ka in range(ad)]
     added = jnp.einsum("ain,aiv->nv", jnp.stack(own_hot), jnp.stack(back_rows), **f32)
-    y_out = (base_sum + added).astype(bf16)
+    y_out = (base + added).astype(bf16)
 
     hid_cols = []
     for k in range(fsdp):
         block = cut(hidden, (f ^ k) * rloc, rloc, 3)
         hid_cols.append(over_f(block, k) if k else block)
     hid_cols = spread(jnp.stack(hid_cols))
+    dys = jnp.stack([cut(dy_all, f ^ k, 1, 0)[0] for k in range(fsdp)])
     grad_b = adapter_scale * jnp.einsum("fagkj,fagkv->gjv", hid_cols, dys, **f32)
     return y_out, grad_a, grad_b.reshape(dloc, rloc, vloc)
 

time: 288 us -> 253 us (0.88)
  waiting for transfers between devices: 114 us -> 59.3 us
  starting transfers between devices: 74.6 us -> 51.9 us
  other arithmetic: 13.3 us -> 32.7 us
  local copies, waits for them, and re-layouts: 52.5 us -> 37.8 us
  between operations: 1.88 us -> 16.3 us
  blocking collectives: 0 us -> 13.5 us
  matrix products: 30.3 us -> 35.9 us
  Pallas kernels: 0 us -> 3.82 us
    ppermute x12, waiting for transfers between devices: 62.1 us -> 9.43 us  [over_a(): return lax.ppermute(v, 'ad', [(i, (i + k) % ad) for i in range(ad)])]
    broadcast_in_dim x15 -> x0, local copies, waits for them, and re-layouts: 30.6 us -> none  [spread(): wide = jnp.where(own_dom, v[..., None, :], jnp.zeros((), v.dtype))]
    all_gather x0 -> x1, blocking collectives: none -> 13.5 us  [column_body(): back_all = lax.all_gather(back, 'fsdp')]
    ppermute x8, starting transfers between devices: 18.8 us -> 7.06 us  [column_body(): got = lax.ppermute(sums[:, r], ('fsdp', 'tp'), perm)]
    ppermute x8, waiting for transfers between devices: 27 us -> 15.6 us  [column_body(): got = lax.ppermute(sums[:, r], ('fsdp', 'tp'), perm)]
    concatenate x0 -> x1, local copies, waits for them, and re-layouts: none -> 10.2 us  [spread(): wide = jnp.concatenate([v] * GROUP, axis=-1)]
    ppermute x24 -> x12, waiting for transfers between devices: 25.2 us -> 34.1 us  [over_f(): return lax.ppermute(v, 'fsdp', [(i, i ^ k) for i in range(fsdp)])]
    dynamic_update_slice x8, other arithmetic: 0.98 us -> 8.8 us  [column_body(): lax.dynamic_update_slice_in_dim(grad_a, got.astype(jnp.float32), start, 2)]
  transfers between devices with their start and end apart: 50 -> 39, of which waited for: 20 -> 11; matrix products, arithmetic and copies ran while one was open for 31% -> 38% of each run, Pallas kernels for 0% -> 2%
where the time goes in v2:
time: 253 us; the launch traced here: 251 us
  waiting for transfers between devices  59.3 us (23%)
  starting transfers between devices  51.9 us (21%)
  local copies, waits for them, and re-layouts  37.8 us (15%)
  matrix products  35.9 us (14%)
  other arithmetic  32.7 us (13%)
  between operations  16.3 us (6%)
  blocking collectives  13.5 us (5%)
  Pallas kernels  3.82 us (2%)
    ppermute x12, waiting for transfers between devices, over_f(): return lax.ppermute(v, 'fsdp', [(i, i ^ k) for i in range(fsdp)])  34.1 us
    ppermute x12, starting transfers between devices, over_f(): return lax.ppermute(v, 'fsdp', [(i, i ^ k) for i in range(fsdp)])  20.6 us
    ppermute x12, starting transfers between devices, over_a(): return lax.ppermute(v, 'ad', [(i, (i + k) % ad) for i in range(ad)])  20.2 us
    ppermute x8, waiting for transfers between devices, column_body(): got = lax.ppermute(sums[:, r], ('fsdp', 'tp'), perm)  15.6 us
    dot_general x8, matrix products, column_body(): block = jnp.einsum('fin,fnw->fiw', hots[ka], jnp.stack(x_in[c]), **f32)  13.5 us
    all_gather x1, blocking collectives, column_body(): back_all = lax.all_gather(back, 'fsdp')  13.5 us
    dynamic_slice x5, local copies, waits for them, and re-layouts, cut(): return lax.dynamic_slice_in_dim(v, start, size, axis)  11.4 us
    concatenate x1, local copies, waits for them, and re-layouts, spread(): wide = jnp.concatenate([v] * GROUP, axis=-1)  10.2 us
  transfers between devices with their start and end apart: 39, of which 11 were waited for; matrix products, arithmetic and copies ran while one was open for 38% of the time, Pallas kernels for 2%

profile of v2, /device:TPU:0, one launch (start us, length us, event | category | flops | bytes accessed | tf_op | source)
XLA Modules:
  0.0 251.2 jit_solution(3506776838819297214)
XLA Ops:
  8.9 2.5 constant_dynamic-slice_fusion.11
  12.3 2.9 %collective-permute-start = (bf16[272,512]{1,0:T(8,128)(2,1)S(1)}, bf16[272,512]{1,0:T(8,128)(2,1)}, u32[]{:S(2)}, u32[]{:S(2)}) collective-permute-start(bf16[272,512]{1,0:T(8,128)(2,1)S(1)} %get-tuple-element.108), channel_id=1, source_target_pairs={{0,8},{8,0},{16,24},{24,16},{1,9},{9,1},{17,25},{25,17},{2,10},{10... | collective-permute-start | bytes 835592 | tf_op jit(solution)/shard_map/ppermute | solution.py:130
  15.2 2.0 collective-permute-start.2
  17.3 1.4 collective-permute-start.4
  19.8 3.6 %collective-permute-start.13 = (bf16[96,512]{1,0:T(8,128)(2,1)}, bf16[96,512]{1,0:T(8,128)(2,1)S(1)}, u32[]{:S(2)}, u32[]{:S(2)}) collective-permute-start(bf16[96,512]{1,0:T(8,128)(2,1)} %convolution_convert_fusion.8), channel_id=1, source_target_pairs={{0,3},{1,0},{2,1},{3,2},{4,7},{5,4},{6,5},{7,6},{8,11},{9,8},{10,9... | collective-permute-start | bytes 294920 | tf_op jit(solution)/shard_map/ppermute | solution.py:133
  27.3 7.4 %collective-permute-done.4 = bf16[272,512]{1,0:T(8,128)(2,1)} collective-permute-done((bf16[272,512]{1,0:T(8,128)(2,1)}, bf16[272,512]{1,0:T(8,128)(2,1)}, u32[]{:S(2)}, u32[]{:S(2)}) %collective-permute-start.4) | collective-permute-done | bytes 278560 | tf_op jit(solution)/shard_map/ppermute | solution.py:130
  34.8 2.6 %collective-permute-start.12 = (bf16[96,512]{1,0:T(8,128)(2,1)}, bf16[96,512]{1,0:T(8,128)(2,1)S(1)}, u32[]{:S(2)}, u32[]{:S(2)}) collective-permute-start(bf16[96,512]{1,0:T(8,128)(2,1)} %convolution_convert_fusion.9), channel_id=1, source_target_pairs={{0,2},{1,3},{2,0},{3,1},{4,6},{5,7},{6,4},{7,5},{8,10},{9,11},{10,... | collective-permute-start | bytes 294920 | tf_op jit(solution)/shard_map/ppermute | solution.py:133
  38.3 1.6 collective-permute-start.11
  44.8 1.8 slice_bitcast_fusion.18
  46.5 1.8 slice_bitcast_fusion.17
  48.3 1.8 slice_bitcast_fusion.16
  50.9 1.1 convolution_convert_fusion.7
  52.0 4.6 %constant_dynamic-slice_fusion.8 = bf16[8,256,1024]{2,1,0:T(8,128)(2,1)} fusion(bf16[8,256,4096]{2,1,0:T(8,128)(2,1)} %param.8, s32[]{:T(128)S(6)} %select_n.313), kind=kLoop, calls=%fused_computation.227 | loop fusion | bytes 8388612 | tf_op jit(solution)/shard_map/dynamic_slice | solution.py:139
  56.7 3.3 %collective-permute-start.7 = (bf16[8,256,1024]{2,1,0:T(8,128)(2,1)}, bf16[8,256,1024]{2,1,0:T(8,128)(2,1)}, u32[]{:S(2)}, u32[]{:S(2)}) collective-permute-start(bf16[8,256,1024]{2,1,0:T(8,128)(2,1)} %constant_dynamic-slice_fusion.8), channel_id=1, source_target_pairs={{0,4},{8,12},{20,16},{28,24},{1,5},{9,13},{21,17},{29,25},{2,6},{1... | collective-permute-start | bytes 12582920 | tf_op jit(solution)/shard_map/ppermute | solution.py:210
  61.3 2.9 %collective-permute-start.5 = (bf16[256,512]{1,0:T(8,128)(2,1)}, bf16[256,512]{1,0:T(8,128)(2,1)}, u32[]{:S(2)}, u32[]{:S(2)}) collective-permute-start(bf16[256,512]{1,0:T(8,128)(2,1)} %get-tuple-element.17), channel_id=1, source_target_pairs={{0,24},{8,16},{16,8},{24,0},{1,25},{9,17},{17,9},{25,1},{2,26},{10... | collective-permute-start | bytes 786440 | tf_op jit(solution)/shard_map/ppermute | solution.py:130
  65.1 1.2 copy-done.8
  68.1 2.7 %constant_dynamic-slice_fusion.9 = (bf16[1024,512]{1,0:T(8,128)(2,1)}, bf16[1024,512]{1,0:T(8,128)(2,1)S(1)}) fusion(bf16[2048,512]{1,0:T(8,128)(2,1)} %param.7, s32[]{:T(128)S(6)} %select_n.301, s32[]{:T(128)S(6)} %select_n.300), kind=kLoop, calls=%fused_computation.228 | loop fusion | bytes 4194312 | tf_op jit(solution)/shard_map/dynamic_slice | solution.py:139
  70.9 1.1 convolution_convert_fusion.4
  72.6 2.7 %collective-permute-done.3.refs_5_ = bf16[256,512]{1,0:T(8,128)(2,1)} collective-permute-done((bf16[256,512]{1,0:T(8,128)(2,1)}, bf16[256,512]{1,0:T(8,128)(2,1)}, u32[]{:S(2)}, u32[]{:S(2)}) %collective-permute-start.3) | collective-permute-done | bytes 262176 | tf_op jit(solution)/shard_map/ppermute | solution.py:130
  75.3 2.2 collective-permute-start.10
  77.6 2.2 convolution_convert_fusion
  79.8 2.2 convolution_convert_fusion.1
  82.1 1.1 convolution_convert_fusion.5
  83.2 2.2 convolution_convert_fusion.2
  85.5 1.1 convolution_convert_fusion.6
  86.6 2.3 convolution_convert_fusion.3
  89.5 1.1 multiply_convert_fusion
  90.6 13.5 %all-gather = bf16[16,2,48,256]{3,2,0,1:T(8,128)(2,1)S(1)} all-gather(bf16[4,2,48,256]{3,2,0,1:T(8,128)(2,1)S(1)} %multiply_convert_fusion), channel_id=2, replica_groups=mesh['fsdp'=4,'tp'=2,'ad'=4] {'fsdp'}, dimensions={0}, use_global_device_ids=true | all-gather | bytes 983040 | tf_op jit(solution)/shard_map/all_gather | solution.py:202
  104.3 1.5 broadcast_select_fusion.5
  105.8 10.2 %concatenate.33 = bf16[4,4,2,48,1024]{4,3,1,0,2:T(8,128)(2,1)} concatenate(bf16[4,4,2,48,64]{4,3,1,0,2:T(8,128)(2,1)} %get-tuple-element.44, bf16[4,4,2,48,64]{4,3,1,0,2:T(8,128)(2,1)} %get-tuple-element.42, bf16[4,4,2,48,64]{4,3,1,0,2:T(8,128)(2,1)} %get-tuple-element.43, bf16[4,4,2,48,64]{4,3,1,0,2:T(8,128)(2,1)} %get-tuple-element.41, ...), dimensions={4} | concatenate | bytes 6291456 | tf_op jit(solution)/shard_map/concatenate | solution.py:146
  116.0 3.9 %broadcast_select_fusion = bf16[4,4,2,48,1024]{4,3,1,0,2:T(8,128)(2,1)} fusion(bf16[4,4,2,48,1024]{4,3,1,0,2:T(8,128)(2,1)} %concatenate.33, pred[48,1024]{1,0:T(8,128)(4,1)S(1)} %select_compare_fusion), kind=kLoop, calls=%fused_computation.7 | loop fusion | flops 1572864 | bytes 6340608 | tf_op jit(solution)/shard_map/jit(_where)/select_n | solution.py:147
  119.9 3.4 %collective-permute-start.17 = (bf16[4,96,512]{2,1,0:T(8,128)(2,1)}, bf16[4,96,512]{2,1,0:T(8,128)(2,1)}, u32[]{:S(2)}, u32[]{:S(2)}) collective-permute-start(bf16[4,96,512]{2,1,0:T(8,128)(2,1)} %convolution_convert_fusion), channel_id=1, source_target_pairs={{0,3},{1,0},{2,1},{3,2},{4,7},{5,4},{6,5},{7,6},{8,11},{9,8},{10,9... | collective-permute-start | bytes 1179656 | tf_op jit(solution)/shard_map/ppermute | solution.py:133
  123.3 3.8 %shard_map.85 = f32[8,256,512]{2,1,0:T(8,128)S(1)} custom-call(s32[8]{0:T(128)S(1)} %stack.218.order, bf16[256,512]{1,0:T(8,128)(2,1)S(1)} %copy-done.4, bf16[256,512]{1,0:T(8,128)(2,1)S(1)} %get-tuple-element.22.refs_1_, bf16[256,512]{1,0:T(8,128)(2,1)S(1)} %copy-done.5, bf16[256,512]{1,0:T(8,128)(2,1)} %collective-permute-done.1.refs_3_, ...), custom_call_target="tpu_custom_call" | custom-call | flops 2147483648 | bytes 10485760 | tf_op jit(solution)/shard_map/pallas_call | solution.py:217
  127.1 2.0 copy-done.1
  129.2 1.5 constant_dynamic-slice_fusion.3
  131.0 4.6 %dynamic-slice_select_fusion = bf16[8,256,1024]{2,1,0:T(8,128)(2,1)S(1)} fusion(bf16[8,256,1024]{2,1,0:T(8,128)(2,1)} %collective-permute-done.7, bf16[8,256,4096]{2,1,0:T(8,128)(2,1)} %param.8, s32[]{:T(128)S(6)} %select_n.312, pred[]{:T(512)S(6)} %eq.405), kind=kLoop, calls=%fused_computation.2 | loop fusion | flops 2097152 | bytes 12582917 | tf_op jit(solution)/shard_map/jit(_where)/select_n | solution.py:211
  136.5 3.2 %convolution_bitcast_fusion.1 = f32[4,4,2,48,1024]{4,3,1,0,2:T(8,128)S(1)} fusion(bf16[2,1024,1024]{2,1,0:T(8,128)(2,1)S(1)} %bitcast.197, bf16[1,4,2,48,512]{4,3,2,1,0:T(8,128)(2,1)} %bitcast.30, bf16[1,4,2,48,512]{4,3,2,1,0:T(8,128)(2,1)} %bitcast.29, bf16[1,4,2,48,512]{4,3,2,1,0:T(8,128)(2,1)} %bitcast.28, bf16[1,4,2,48,512]{4,3,2,1,0:T(8,128)(2,1)S(1)} %bitcast.238), kind=kOutput, calls=%fused_computation.9 | convolution fusion | flops 1612972032 | bytes 9961472 | tf_op jit(solution)/shard_map/abgkw,gjw->abgkj/dot_general | solution.py:239
  140.2 1.5 copy-done.11
  141.7 3.1 %bitcast_convert_fusion.1 = bf16[2,1024,512]{2,1,0:T(8,128)(2,1)S(1)} fusion(bf16[4,4,2,48,1024]{4,3,1,0,2:T(8,128)(2,1)S(1)} %copy-done.11, bf16[1,4,2,48,512]{4,3,2,1,0:T(8,128)(2,1)} %bitcast.30, bf16[1,4,2,48,512]{4,3,2,1,0:T(8,128)(2,1)} %bitcast.29, bf16[1,4,2,48,512]{4,3,2,1,0:T(8,128)(2,1)} %bitcast.28, bf16[1,4,2,48,512]{4,3,2,1,0:T(8,128)(2,1)S(1)} %bitcast.239), kind=kOutput, calls=%fused_computation.1 | convolution fusion | flops 1614020608 | bytes 6815744 | tf_op jit(solution)/shard_map/abgkj,abgkw->gjw/dot_general | solution.py:247
  145.7 1.3 collective-permute-start.27
  147.0 9.2 %collective-permute-done.16 = bf16[4,96,512]{2,1,0:T(8,128)(2,1)S(1)} collective-permute-done((bf16[4,96,512]{2,1,0:T(8,128)(2,1)S(1)}, bf16[4,96,512]{2,1,0:T(8,128)(2,1)S(1)}, u32[]{:S(2)}, u32[]{:S(2)}) %collective-permute-start.16) | collective-permute-done | bytes 393248 | tf_op jit(solution)/shard_map/ppermute | solution.py:133
  156.2 2.8 %convolution_bitcast_fusion = f32[4,4,2,48,1024]{4,3,1,0,2:T(8,128)S(1)} fusion(bf16[2,1024,1024]{2,1,0:T(8,128)(2,1)S(1)} %bitcast.198, bf16[1,4,2,48,512]{4,3,2,1,0:T(8,128)(2,1)} %bitcast.58, bf16[1,4,2,48,512]{4,3,2,1,0:T(8,128)(2,1)S(1)} %bitcast.225, bf16[1,4,2,48,512]{4,3,2,1,0:T(8,128)(2,1)S(1)} %bitcast.227, ...), kind=kOutput, calls=%fused_computation.8 | convolution fusion | flops 1612972032 | bytes 9961472 | tf_op jit(solution)/shard_map/abgkw,gjw->abgkj/dot_general | solution.py:239
  159.8 2.4 collective-permute-start.28
  162.3 4.4 %broadcast_in_dim.101 = f32[8,64,4096]{2,1,0:T(8,128)} broadcast(f32[]{:T(128)} %constant.176.clone.1), dimensions={} | broadcast | bytes 8388612 | tf_op jit(solution)/shard_map/broadcast_in_dim | solution.py:235
  166.7 1.1 convert_dynamic-update-slice_fusion.7
  169.5 13.0 %collective-permute-done.28 = bf16[8,64,512]{2,1,0:T(8,128)(2,1)S(1)} collective-permute-done((bf16[8,64,512]{2,1,0:T(8,128)(2,1)S(1)}, bf16[8,64,512]{2,1,0:T(8,128)(2,1)S(1)}, u32[]{:S(2)}, u32[]{:S(2)}) %collective-permute-start.28) | collective-permute-done | bytes 524320 | tf_op jit(solution)/shard_map/ppermute | solution.py:257
  182.4 1.1 convert_dynamic-update-slice_fusion.5
  183.5 1.1 convert_dynamic-update-slice_fusion.4
  184.8 5.6 %collective-permute-start.21 = (f32[4,2,48,128]{3,2,0,1:T(8,128)S(1)}, f32[4,2,48,128]{3,2,0,1:T(8,128)S(1)}, u32[]{:S(2)}, u32[]{:S(2)}) collective-permute-start(f32[4,2,48,128]{3,2,0,1:T(8,128)S(1)} %slice_bitcast_fusion.15), channel_id=1, source_target_pairs={{0,24},{8,16},{16,8},{24,0},{1,25},{9,17},{17,9},{25,1},{2,26},{10... | collective-permute-start | bytes 589832 | tf_op jit(solution)/shard_map/ppermute | solution.py:130
  191.5 2.8 %bitcast_convert_fusion = bf16[2,1024,512]{2,1,0:T(8,128)(2,1)S(1)} fusion(bf16[4,4,2,48,1024]{4,3,1,0,2:T(8,128)(2,1)S(1)} %copy-done.11, bf16[1,4,2,48,512]{4,3,2,1,0:T(8,128)(2,1)} %bitcast.58, bf16[1,4,2,48,512]{4,3,2,1,0:T(8,128)(2,1)S(1)} %bitcast.226, bf16[1,4,2,48,512]{4,3,2,1,0:T(8,128)(2,1)S(1)} %bitcast.228, ...), kind=kOutput, calls=%fused_computation | convolution fusion | flops 1614020608 | bytes 6815744 | tf_op jit(solution)/shard_map/abgkj,abgkw->gjw/dot_general | solution.py:247
  194.4 4.9 %collective-permute-done.21 = f32[4,2,48,128]{3,2,0,1:T(8,128)S(1)} collective-permute-done((f32[4,2,48,128]{3,2,0,1:T(8,128)S(1)}, f32[4,2,48,128]{3,2,0,1:T(8,128)S(1)}, u32[]{:S(2)}, u32[]{:S(2)}) %collective-permute-start.21) | collective-permute-done | bytes 196640 | tf_op jit(solution)/shard_map/ppermute | solution.py:130
  199.3 5.6 %collective-permute-done.20 = f32[4,2,48,128]{3,2,0,1:T(8,128)S(1)} collective-permute-done((f32[4,2,48,128]{3,2,0,1:T(8,128)S(1)}, f32[4,2,48,128]{3,2,0,1:T(8,128)S(1)}, u32[]{:S(2)}, u32[]{:S(2)}) %collective-permute-start.20) | collective-permute-done | bytes 196640 | tf_op jit(solution)/shard_map/ppermute | solution.py:130
  205.9 1.6 collective-permute-start.31
  207.7 3.7 %collective-permute-start.36 = (bf16[4,2,48,64]{3,2,0,1:T(8,128)(2,1)S(1)}, bf16[4,2,48,64]{3,2,0,1:T(8,128)(2,1)S(1)}, u32[]{:S(2)}, u32[]{:S(2)}) collective-permute-start(bf16[4,2,48,64]{3,2,0,1:T(8,128)(2,1)S(1)} %get-tuple-element.60), channel_id=1, source_target_pairs={{0,24},{8,16},{16,8},{24,0},{1,25},{9,17},{17,9},{25,1},{2,26},{10... | collective-permute-start | bytes 147464 | tf_op jit(solution)/shard_map/ppermute | solution.py:130
  212.7 11.1 %collective-permute-done.36 = bf16[4,2,48,64]{3,2,0,1:T(8,128)(2,1)S(1)} collective-permute-done((bf16[4,2,48,64]{3,2,0,1:T(8,128)(2,1)S(1)}, bf16[4,2,48,64]{3,2,0,1:T(8,128)(2,1)S(1)}, u32[]{:S(2)}, u32[]{:S(2)}) %collective-permute-start.36) | collective-permute-done | bytes 49184 | tf_op jit(solution)/shard_map/ppermute | solution.py:130
  223.7 2.4 collective-permute-done.35
  226.5 1.6 collective-permute-start.25
  228.1 3.3 %fusion.22 = f32[2,256,512]{2,1,0:T(8,128)} fusion(bf16[1,4,2,48,64]{4,3,1,2,0:T(8,128)(2,1)S(1)} %bitcast.231, bf16[1,4,2,48,64]{4,3,1,2,0:T(8,128)(2,1)S(1)} %bitcast.232, bf16[1,4,2,48,64]{4,3,1,2,0:T(8,128)(2,1)S(1)} %bitcast.233, bf16[1,4,2,48,64]{4,3,1,2,0:T(8,128)(2,1)S(1)} %get-tuple-element.59, pred[48,256]{1,0:T(8,128)(4,1)S(1)} %copy-done.40, ...), kind=kOutput, calls=%fused_computation.30 | convolution fusion | flops 418250752 | bytes 2830336 | tf_op jit(solution)/shard_map/fagkj,fagkv->gjv/dot_general | solution.py:284
  231.4 2.4 collective-permute-start.24
  234.9 1.1 collective-permute-start.23
  237.1 1.1 convert_dynamic-update-slice_fusion.1
  238.3 2.1 collective-permute-done.33
  240.3 1.1 convert_dynamic-update-slice_fusion
  241.6 2.1 fusion.70
  (211 shorter events, 29.9 us)
Async XLA Ops:
  8.0 56.2 %copy-start = (bf16[8,256,512]{2,1,0:T(8,128)(2,1)S(1)}, bf16[8,256,512]{2,1,0:T(8,128)(2,1)}, u32[]{:S(2)}) copy-start(bf16[8,256,512]{2,1,0:T(8,128)(2,1)} %param.9) | copy-start | bytes 6291460
  8.0 121.2 %all-gather.3.cloned.1.call-start = ((), (), s32[]{:S(2)}) async-start(), calls=%async_computation.2 | async-start | bytes 1966080 | tf_op jit(solution)/shard_map/all_gather | solution.py:203
  11.4 38.7 %copy-start.2 = (bf16[256,512]{1,0:T(8,128)(2,1)}, bf16[256,512]{1,0:T(8,128)(2,1)S(1)}, u32[]{:S(2)}) copy-start(bf16[256,512]{1,0:T(8,128)(2,1)S(1)} %get-tuple-element.23.refs_0_) | copy-start | bytes 786436
  11.4 7.3 %copy-start.41 = (s32[256,1]{0,1:T(1,128)S(1)}, s32[256,1]{0,1:T(1,128)}, u32[]{:S(2)}) copy-start(s32[256,1]{0,1:T(1,128)} %param.11) | copy-start | bytes 3076
  11.4 7.6 %copy-start.10 = (bf16[256,512]{1,0:T(8,128)(2,1)S(1)}, bf16[256,512]{1,0:T(8,128)(2,1)}, u32[]{:S(2)}) copy-start(bf16[256,512]{1,0:T(8,128)(2,1)} %param.10) | copy-start | bytes 786436
  12.3 28.5 %collective-permute-start = (bf16[272,512]{1,0:T(8,128)(2,1)S(1)}, bf16[272,512]{1,0:T(8,128)(2,1)}, u32[]{:S(2)}, u32[]{:S(2)}) collective-permute-start(bf16[272,512]{1,0:T(8,128)(2,1)S(1)} %get-tuple-element.108), channel_id=1, source_target_pairs={{0,8},{8,0},{16,24},{24,16},{1,9},{9,1},{17,25},{25,17},{2,10},{10... | collective-permute-start | bytes 835592 | tf_op jit(solution)/shard_map/ppermute | solution.py:130
  15.2 56.8 %collective-permute-start.1 = (bf16[256,512]{1,0:T(8,128)(2,1)}, bf16[256,512]{1,0:T(8,128)(2,1)}, u32[]{:S(2)}, u32[]{:S(2)}) collective-permute-start(bf16[256,512]{1,0:T(8,128)(2,1)} %get-tuple-element.20), channel_id=1, source_target_pairs={{0,8},{8,0},{16,24},{24,16},{1,9},{9,1},{17,25},{25,17},{2,10},{10... | collective-permute-start | bytes 786440 | tf_op jit(solution)/shard_map/ppermute | solution.py:130
  15.2 23.0 %collective-permute-start.2 = (bf16[272,512]{1,0:T(8,128)(2,1)}, bf16[272,512]{1,0:T(8,128)(2,1)}, u32[]{:S(2)}, u32[]{:S(2)}) collective-permute-start(bf16[272,512]{1,0:T(8,128)(2,1)} %get-tuple-element.109), channel_id=1, source_target_pairs={{0,16},{8,24},{16,0},{24,8},{1,17},{9,25},{17,1},{25,9},{2,18},{10... | collective-permute-start | bytes 835592 | tf_op jit(solution)/shard_map/ppermute | solution.py:130
  17.3 17.5 %collective-permute-start.4 = (bf16[272,512]{1,0:T(8,128)(2,1)}, bf16[272,512]{1,0:T(8,128)(2,1)}, u32[]{:S(2)}, u32[]{:S(2)}) collective-permute-start(bf16[272,512]{1,0:T(8,128)(2,1)} %get-tuple-element.107), channel_id=1, source_target_pairs={{0,24},{8,16},{16,8},{24,0},{1,25},{9,17},{17,9},{25,1},{2,26},{10... | collective-permute-start | bytes 835592 | tf_op jit(solution)/shard_map/ppermute | solution.py:130
  19.8 41.4 %collective-permute-start.13 = (bf16[96,512]{1,0:T(8,128)(2,1)}, bf16[96,512]{1,0:T(8,128)(2,1)S(1)}, u32[]{:S(2)}, u32[]{:S(2)}) collective-permute-start(bf16[96,512]{1,0:T(8,128)(2,1)} %convolution_convert_fusion.8), channel_id=1, source_target_pairs={{0,3},{1,0},{2,1},{3,2},{4,7},{5,4},{6,5},{7,6},{8,11},{9,8},{10,9... | collective-permute-start | bytes 294920 | tf_op jit(solution)/shard_map/ppermute | solution.py:133
  25.6 22.8 %copy-start.43 = (s32[96]{0:T(128)}, s32[96]{0:T(128)S(1)}, u32[]{:S(2)}) copy-start(s32[96]{0:T(128)S(1)} %iota_add_fusion.2) | copy-start | bytes 1156
  34.8 26.5 %collective-permute-start.12 = (bf16[96,512]{1,0:T(8,128)(2,1)}, bf16[96,512]{1,0:T(8,128)(2,1)S(1)}, u32[]{:S(2)}, u32[]{:S(2)}) collective-permute-start(bf16[96,512]{1,0:T(8,128)(2,1)} %convolution_convert_fusion.9), channel_id=1, source_target_pairs={{0,2},{1,3},{2,0},{3,1},{4,6},{5,7},{6,4},{7,5},{8,10},{9,11},{10,... | collective-permute-start | bytes 294920 | tf_op jit(solution)/shard_map/ppermute | solution.py:133
  38.3 26.0 %collective-permute-start.11 = (bf16[96,512]{1,0:T(8,128)(2,1)}, bf16[96,512]{1,0:T(8,128)(2,1)S(1)}, u32[]{:S(2)}, u32[]{:S(2)}) collective-permute-start(bf16[96,512]{1,0:T(8,128)(2,1)} %convolution_convert_fusion.10), channel_id=1, source_target_pairs={{0,1},{1,2},{2,3},{3,0},{4,5},{5,6},{6,7},{7,4},{8,9},{9,10},{10,1... | collective-permute-start | bytes 294920 | tf_op jit(solution)/shard_map/ppermute | solution.py:133
  44.7 7.2 %copy-start.22 = (bf16[1,96,256]{2,1,0:T(8,128)(2,1)}, bf16[1,96,256]{2,1,0:T(8,128)(2,1)S(1)}, u32[]{:S(2)}) copy-start(bf16[1,96,256]{2,1,0:T(8,128)(2,1)S(1)} %get-tuple-element.106) | copy-start | bytes 147460
  44.7 7.2 %copy-start.34 = (bf16[1,96,256]{2,1,0:T(8,128)(2,1)}, bf16[1,96,256]{2,1,0:T(8,128)(2,1)S(1)}, u32[]{:S(2)}) copy-start(bf16[1,96,256]{2,1,0:T(8,128)(2,1)S(1)} %get-tuple-element.93) | copy-start | bytes 147460
  44.7 7.2 %copy-start.36 = (bf16[1,96,256]{2,1,0:T(8,128)(2,1)}, bf16[1,96,256]{2,1,0:T(8,128)(2,1)S(1)}, u32[]{:S(2)}) copy-start(bf16[1,96,256]{2,1,0:T(8,128)(2,1)S(1)} %get-tuple-element.97) | copy-start | bytes 147460
  44.8 7.2 %copy-start.38 = (bf16[1,96,256]{2,1,0:T(8,128)(2,1)}, bf16[1,96,256]{2,1,0:T(8,128)(2,1)S(1)}, u32[]{:S(2)}) copy-start(bf16[1,96,256]{2,1,0:T(8,128)(2,1)S(1)} %get-tuple-element.102) | copy-start | bytes 147460
  52.0 8.0 %copy-start.45 = (s32[48]{0:T(128)S(1)}, s32[48]{0:T(128)}, u32[]{:S(2)}) copy-start(s32[48]{0:T(128)} %get-tuple-element.112) | copy-start | bytes 580
  52.0 8.0 %copy-start.46 = (s32[48]{0:T(128)S(1)}, s32[48]{0:T(128)}, u32[]{:S(2)}) copy-start(s32[48]{0:T(128)} %get-tuple-element.113) | copy-start | bytes 580
  52.0 8.0 %copy-start.47 = (pred[48]{0:T(512)(128)(4,1)S(1)}, pred[48]{0:T(512)(128)(4,1)}, u32[]{:S(2)}) copy-start(pred[48]{0:T(512)(128)(4,1)} %compare_and_fusion.1) | copy-start | bytes 148
  52.0 8.0 %copy-start.48 = (pred[1024]{0:T(1024)(128)(4,1)S(1)}, pred[1024]{0:T(1024)(128)(4,1)}, u32[]{:S(2)}) copy-start(pred[1024]{0:T(1024)(128)(4,1)} %fusion.126) | copy-start | bytes 3076
  52.0 8.1 %copy-start.44 = (s32[96]{0:T(128)S(1)}, s32[96]{0:T(128)}, u32[]{:S(2)}) copy-start(s32[96]{0:T(128)} %copy-done.43) | copy-start | bytes 1156
  52.0 8.4 %copy-start.42 = (s32[256]{0:T(256)S(1)}, s32[256]{0:T(256)}, u32[]{:S(2)}) copy-start(s32[256]{0:T(256)} %get-tuple-element.111) | copy-start | bytes 3076
  56.7 74.0 %collective-permute-start.7 = (bf16[8,256,1024]{2,1,0:T(8,128)(2,1)}, bf16[8,256,1024]{2,1,0:T(8,128)(2,1)}, u32[]{:S(2)}, u32[]{:S(2)}) collective-permute-start(bf16[8,256,1024]{2,1,0:T(8,128)(2,1)} %constant_dynamic-slice_fusion.8), channel_id=1, source_target_pairs={{0,4},{8,12},{20,16},{28,24},{1,5},{9,13},{21,17},{29,25},{2,6},{1... | collective-permute-start | bytes 12582920 | tf_op jit(solution)/shard_map/ppermute | solution.py:210
  61.2 14.1 %collective-permute-start.3 = (bf16[256,512]{1,0:T(8,128)(2,1)}, bf16[256,512]{1,0:T(8,128)(2,1)}, u32[]{:S(2)}, u32[]{:S(2)}) collective-permute-start(bf16[256,512]{1,0:T(8,128)(2,1)} %get-tuple-element.18), channel_id=1, source_target_pairs={{0,16},{8,24},{16,0},{24,8},{1,17},{9,25},{17,1},{25,9},{2,18},{10... | collective-permute-start | bytes 786440 | tf_op jit(solution)/shard_map/ppermute | solution.py:130
  61.3 16.3 %collective-permute-start.5 = (bf16[256,512]{1,0:T(8,128)(2,1)}, bf16[256,512]{1,0:T(8,128)(2,1)}, u32[]{:S(2)}, u32[]{:S(2)}) collective-permute-start(bf16[256,512]{1,0:T(8,128)(2,1)} %get-tuple-element.17), channel_id=1, source_target_pairs={{0,24},{8,16},{16,8},{24,0},{1,25},{9,17},{17,9},{25,1},{2,26},{10... | collective-permute-start | bytes 786440 | tf_op jit(solution)/shard_map/ppermute | solution.py:130
  67.1 21.8 %collective-permute-start.14 = (f32[4,2,48,256]{3,2,0,1:T(8,128)}, f32[4,2,48,256]{3,2,0,1:T(8,128)}, u32[]{:S(2)}, u32[]{:S(2)}) collective-permute-start(f32[4,2,48,256]{3,2,0,1:T(8,128)} %fusion.72), channel_id=1, source_target_pairs={{0,4},{4,0},{1,5},{5,1},{2,6},{6,2},{3,7},{7,3},{8,12},{12,8},{9,1... | collective-permute-start | bytes 1179656 | tf_op jit(solution)/shard_map/ppermute | solution.py:136
  68.0 173.7 %reduce-scatter.2.cloned.1.call-start = ((), (), s32[]{:S(2)}) async-start(), calls=%async_computation.1 | async-start | bytes 4718592 | tf_op jit(solution)/shard_map/reduce_scatter | solution.py:227
  70.9 6.7 %copy-start.23 = (bf16[1,96,256]{2,1,0:T(8,128)(2,1)S(1)}, bf16[1,96,256]{2,1,0:T(8,128)(2,1)}, u32[]{:S(2)}) copy-start(bf16[1,96,256]{2,1,0:T(8,128)(2,1)} %copy-done.22) | copy-start | bytes 147460
  70.9 6.7 %copy-start.35 = (bf16[1,96,256]{2,1,0:T(8,128)(2,1)S(1)}, bf16[1,96,256]{2,1,0:T(8,128)(2,1)}, u32[]{:S(2)}) copy-start(bf16[1,96,256]{2,1,0:T(8,128)(2,1)} %copy-done.34) | copy-start | bytes 147460
  70.9 6.7 %copy-start.37 = (bf16[1,96,256]{2,1,0:T(8,128)(2,1)S(1)}, bf16[1,96,256]{2,1,0:T(8,128)(2,1)}, u32[]{:S(2)}) copy-start(bf16[1,96,256]{2,1,0:T(8,128)(2,1)} %copy-done.36) | copy-start | bytes 147460
  70.9 6.7 %copy-start.39 = (bf16[1,96,256]{2,1,0:T(8,128)(2,1)S(1)}, bf16[1,96,256]{2,1,0:T(8,128)(2,1)}, u32[]{:S(2)}) copy-start(bf16[1,96,256]{2,1,0:T(8,128)(2,1)} %copy-done.38) | copy-start | bytes 147460
  72.0 47.8 %collective-permute-start.6 = (bf16[1024,512]{1,0:T(8,128)(2,1)}, bf16[1024,512]{1,0:T(8,128)(2,1)}, u32[]{:S(2)}, u32[]{:S(2)}) collective-permute-start(bf16[1024,512]{1,0:T(8,128)(2,1)} %get-tuple-element.33), channel_id=1, source_target_pairs={{0,4},{4,0},{1,5},{5,1},{2,6},{6,2},{3,7},{7,3},{8,12},{12,8},{9,1... | collective-permute-start | bytes 3145736 | tf_op jit(solution)/shard_map/ppermute | solution.py:136
  75.3 60.4 %collective-permute-start.10 = (bf16[4,96,512]{2,1,0:T(8,128)(2,1)}, bf16[4,96,512]{2,1,0:T(8,128)(2,1)}, u32[]{:S(2)}, u32[]{:S(2)}) collective-permute-start(bf16[4,96,512]{2,1,0:T(8,128)(2,1)} %convolution_convert_fusion.7), channel_id=1, source_target_pairs={{0,3},{1,0},{2,1},{3,2},{4,7},{5,4},{6,5},{7,6},{8,11},{9,8},{10,9... | collective-permute-start | bytes 1179656 | tf_op jit(solution)/shard_map/ppermute | solution.py:133
  77.5 59.0 %collective-permute-start.9 = (bf16[4,96,512]{2,1,0:T(8,128)(2,1)}, bf16[4,96,512]{2,1,0:T(8,128)(2,1)}, u32[]{:S(2)}, u32[]{:S(2)}) collective-permute-start(bf16[4,96,512]{2,1,0:T(8,128)(2,1)} %convolution_convert_fusion.4), channel_id=1, source_target_pairs={{0,2},{1,3},{2,0},{3,1},{4,6},{5,7},{6,4},{7,5},{8,10},{9,11},{10,... | collective-permute-start | bytes 1179656 | tf_op jit(solution)/shard_map/ppermute | solution.py:133
  88.9 47.6 %collective-permute-start.8 = (bf16[4,96,512]{2,1,0:T(8,128)(2,1)}, bf16[4,96,512]{2,1,0:T(8,128)(2,1)}, u32[]{:S(2)}, u32[]{:S(2)}) collective-permute-start(bf16[4,96,512]{2,1,0:T(8,128)(2,1)} %convolution_convert_fusion.5), channel_id=1, source_target_pairs={{0,1},{1,2},{2,3},{3,0},{4,5},{5,6},{6,7},{7,4},{8,9},{9,10},{10,1... | collective-permute-start | bytes 1179656 | tf_op jit(solution)/shard_map/ppermute | solution.py:133
  116.0 7.3 %copy-start.4 = (bf16[256,512]{1,0:T(8,128)(2,1)S(1)}, bf16[256,512]{1,0:T(8,128)(2,1)}, u32[]{:S(2)}) copy-start(bf16[256,512]{1,0:T(8,128)(2,1)} %copy-done.2) | copy-start | bytes 786436
  116.0 7.3 %copy-start.5 = (bf16[256,512]{1,0:T(8,128)(2,1)S(1)}, bf16[256,512]{1,0:T(8,128)(2,1)}, u32[]{:S(2)}) copy-start(bf16[256,512]{1,0:T(8,128)(2,1)} %get-tuple-element.54.refs_2_) | copy-start | bytes 786436
  116.0 7.3 %copy-start.6 = (bf16[256,512]{1,0:T(8,128)(2,1)S(1)}, bf16[256,512]{1,0:T(8,128)(2,1)}, u32[]{:S(2)}) copy-start(bf16[256,512]{1,0:T(8,128)(2,1)} %get-tuple-element.56.refs_4_) | copy-start | bytes 786436
  116.0 7.3 %copy-start.7 = (bf16[256,512]{1,0:T(8,128)(2,1)S(1)}, bf16[256,512]{1,0:T(8,128)(2,1)}, u32[]{:S(2)}) copy-start(bf16[256,512]{1,0:T(8,128)(2,1)} %get-tuple-element.58.refs_6_) | copy-start | bytes 786436
  119.9 27.1 %collective-permute-start.17 = (bf16[4,96,512]{2,1,0:T(8,128)(2,1)}, bf16[4,96,512]{2,1,0:T(8,128)(2,1)}, u32[]{:S(2)}, u32[]{:S(2)}) collective-permute-start(bf16[4,96,512]{2,1,0:T(8,128)(2,1)} %convolution_convert_fusion), channel_id=1, source_target_pairs={{0,3},{1,0},{2,1},{3,2},{4,7},{5,4},{6,5},{7,6},{8,11},{9,8},{10,9... | collective-permute-start | bytes 1179656 | tf_op jit(solution)/shard_map/ppermute | solution.py:133
  130.7 25.5 %collective-permute-start.16 = (bf16[4,96,512]{2,1,0:T(8,128)(2,1)S(1)}, bf16[4,96,512]{2,1,0:T(8,128)(2,1)S(1)}, u32[]{:S(2)}, u32[]{:S(2)}) collective-permute-start(bf16[4,96,512]{2,1,0:T(8,128)(2,1)S(1)} %copy-done.49), channel_id=1, source_target_pairs={{0,2},{1,3},{2,0},{3,1},{4,6},{5,7},{6,4},{7,5},{8,10},{9,11},{10,... | collective-permute-start | bytes 1179656 | tf_op jit(solution)/shard_map/ppermute | solution.py:133
  135.7 20.5 %collective-permute-start.15 = (bf16[4,96,512]{2,1,0:T(8,128)(2,1)S(1)}, bf16[4,96,512]{2,1,0:T(8,128)(2,1)S(1)}, u32[]{:S(2)}, u32[]{:S(2)}) collective-permute-start(bf16[4,96,512]{2,1,0:T(8,128)(2,1)S(1)} %copy-done.50), channel_id=1, source_target_pairs={{0,1},{1,2},{2,3},{3,0},{4,5},{5,6},{6,7},{7,4},{8,9},{9,10},{10,1... | collective-permute-start | bytes 1179656 | tf_op jit(solution)/shard_map/ppermute | solution.py:133
  144.8 11.4 %copy-start.51 = (bf16[4,96,512]{2,1,0:T(8,128)(2,1)S(1)}, bf16[4,96,512]{2,1,0:T(8,128)(2,1)}, u32[]{:S(2)}) copy-start(bf16[4,96,512]{2,1,0:T(8,128)(2,1)} %convolution_convert_fusion.3) | copy-start | bytes 1179652
  145.0 17.3 %collective-permute-start.26 = (bf16[8,64,512]{2,1,0:T(8,128)(2,1)S(1)}, bf16[8,64,512]{2,1,0:T(8,128)(2,1)S(1)}, u32[]{:S(2)}, u32[]{:S(2)}) collective-permute-start(bf16[8,64,512]{2,1,0:T(8,128)(2,1)S(1)} %get-tuple-element.32), channel_id=1, source_target_pairs={{0,0},{4,16},{8,8},{12,24},{16,4},{20,20},{24,12},{28,28},{1,1},{5... | collective-permute-start | bytes 1572872 | tf_op jit(solution)/shard_map/ppermute | solution.py:257
  145.7 22.7 %collective-permute-start.27 = (bf16[8,64,512]{2,1,0:T(8,128)(2,1)S(1)}, bf16[8,64,512]{2,1,0:T(8,128)(2,1)S(1)}, u32[]{:S(2)}, u32[]{:S(2)}) collective-permute-start(bf16[8,64,512]{2,1,0:T(8,128)(2,1)S(1)} %get-tuple-element.31), channel_id=1, source_target_pairs={{0,8},{4,24},{8,0},{12,16},{16,12},{20,28},{24,4},{28,20},{1,9},{5... | collective-permute-start | bytes 1572872 | tf_op jit(solution)/shard_map/ppermute | solution.py:257
  159.6 25.0 %collective-permute-start.18 = (f32[4,4,2,48,128]{4,3,1,0,2:T(8,128)S(1)}, f32[4,4,2,48,128]{4,3,1,0,2:T(8,128)S(1)}, u32[]{:S(2)}, u32[]{:S(2)}) collective-permute-start(f32[4,4,2,48,128]{4,3,1,0,2:T(8,128)S(1)} %constant_dynamic-slice_fusion.7), channel_id=1, source_target_pairs={{0,4},{4,0},{1,5},{5,1},{2,6},{6,2},{3,7},{7,3},{8,12},{12,8},{9,1... | collective-permute-start | bytes 2359304 | tf_op jit(solution)/shard_map/ppermute | solution.py:136
  159.8 22.6 %collective-permute-start.28 = (bf16[8,64,512]{2,1,0:T(8,128)(2,1)S(1)}, bf16[8,64,512]{2,1,0:T(8,128)(2,1)S(1)}, u32[]{:S(2)}, u32[]{:S(2)}) collective-permute-start(bf16[8,64,512]{2,1,0:T(8,128)(2,1)S(1)} %get-tuple-element.30), channel_id=1, source_target_pairs={{0,16},{4,0},{8,24},{12,8},{16,20},{20,4},{24,28},{28,12},{1,17},{... | collective-permute-start | bytes 1572872 | tf_op jit(solution)/shard_map/ppermute | solution.py:257
  162.2 21.3 %collective-permute-start.29 = (bf16[8,64,512]{2,1,0:T(8,128)(2,1)S(1)}, bf16[8,64,512]{2,1,0:T(8,128)(2,1)S(1)}, u32[]{:S(2)}, u32[]{:S(2)}) collective-permute-start(bf16[8,64,512]{2,1,0:T(8,128)(2,1)S(1)} %get-tuple-element.29), channel_id=1, source_target_pairs={{0,24},{4,8},{8,16},{12,0},{16,28},{20,12},{24,20},{28,4},{1,25},{... | collective-permute-start | bytes 1572872 | tf_op jit(solution)/shard_map/ppermute | solution.py:257
  184.8 14.5 %collective-permute-start.21 = (f32[4,2,48,128]{3,2,0,1:T(8,128)S(1)}, f32[4,2,48,128]{3,2,0,1:T(8,128)S(1)}, u32[]{:S(2)}, u32[]{:S(2)}) collective-permute-start(f32[4,2,48,128]{3,2,0,1:T(8,128)S(1)} %slice_bitcast_fusion.15), channel_id=1, source_target_pairs={{0,24},{8,16},{16,8},{24,0},{1,25},{9,17},{17,9},{25,1},{2,26},{10... | collective-permute-start | bytes 589832 | tf_op jit(solution)/shard_map/ppermute | solution.py:130
  190.4 14.5 %collective-permute-start.20 = (f32[4,2,48,128]{3,2,0,1:T(8,128)S(1)}, f32[4,2,48,128]{3,2,0,1:T(8,128)S(1)}, u32[]{:S(2)}, u32[]{:S(2)}) collective-permute-start(f32[4,2,48,128]{3,2,0,1:T(8,128)S(1)} %get-tuple-element.40), channel_id=1, source_target_pairs={{0,16},{8,24},{16,0},{24,8},{1,17},{9,25},{17,1},{25,9},{2,18},{10... | collective-permute-start | bytes 589832 | tf_op jit(solution)/shard_map/ppermute | solution.py:130
  190.5 14.4 %collective-permute-start.19 = (f32[4,2,48,128]{3,2,0,1:T(8,128)S(1)}, f32[4,2,48,128]{3,2,0,1:T(8,128)S(1)}, u32[]{:S(2)}, u32[]{:S(2)}) collective-permute-start(f32[4,2,48,128]{3,2,0,1:T(8,128)S(1)} %get-tuple-element.39), channel_id=1, source_target_pairs={{0,8},{8,0},{16,24},{24,16},{1,9},{9,1},{17,25},{25,17},{2,10},{10... | collective-permute-start | bytes 589832 | tf_op jit(solution)/shard_map/ppermute | solution.py:130
  204.9 2.5 %collective-permute-start.22 = (bf16[4,2,48,128]{3,2,0,1:T(8,128)(2,1)S(1)}, bf16[4,2,48,128]{3,2,0,1:T(8,128)(2,1)S(1)}, u32[]{:S(2)}, u32[]{:S(2)}) collective-permute-start(bf16[4,2,48,128]{3,2,0,1:T(8,128)(2,1)S(1)} %fusion.102), channel_id=1, source_target_pairs={{0,4},{4,0},{1,5},{5,1},{2,6},{6,2},{3,7},{7,3},{8,12},{12,8},{9,1... | collective-permute-start | bytes 294920 | tf_op jit(solution)/shard_map/ppermute | solution.py:136
  205.2 26.3 %collective-permute-start.30 = (bf16[8,64,512]{2,1,0:T(8,128)(2,1)S(1)}, bf16[8,64,512]{2,1,0:T(8,128)(2,1)S(1)}, u32[]{:S(2)}, u32[]{:S(2)}) collective-permute-start(bf16[8,64,512]{2,1,0:T(8,128)(2,1)S(1)} %get-tuple-element.28), channel_id=1, source_target_pairs={{0,0},{4,16},{8,8},{12,24},{16,4},{20,20},{24,12},{28,28},{1,1},{5... | collective-permute-start | bytes 1572872 | tf_op jit(solution)/shard_map/ppermute | solution.py:257
  205.9 29.1 %collective-permute-start.31 = (bf16[8,64,512]{2,1,0:T(8,128)(2,1)S(1)}, bf16[8,64,512]{2,1,0:T(8,128)(2,1)S(1)}, u32[]{:S(2)}, u32[]{:S(2)}) collective-permute-start(bf16[8,64,512]{2,1,0:T(8,128)(2,1)S(1)} %get-tuple-element.27), channel_id=1, source_target_pairs={{0,8},{4,24},{8,0},{12,16},{16,12},{20,28},{24,4},{28,20},{1,9},{5... | collective-permute-start | bytes 1572872 | tf_op jit(solution)/shard_map/ppermute | solution.py:257
  207.7 16.1 %collective-permute-start.36 = (bf16[4,2,48,64]{3,2,0,1:T(8,128)(2,1)S(1)}, bf16[4,2,48,64]{3,2,0,1:T(8,128)(2,1)S(1)}, u32[]{:S(2)}, u32[]{:S(2)}) collective-permute-start(bf16[4,2,48,64]{3,2,0,1:T(8,128)(2,1)S(1)} %get-tuple-element.60), channel_id=1, source_target_pairs={{0,24},{8,16},{16,8},{24,0},{1,25},{9,17},{17,9},{25,1},{2,26},{10... | collective-permute-start | bytes 147464 | tf_op jit(solution)/shard_map/ppermute | solution.py:130
  211.4 14.8 %collective-permute-start.35 = (bf16[4,2,48,64]{3,2,0,1:T(8,128)(2,1)S(1)}, bf16[4,2,48,64]{3,2,0,1:T(8,128)(2,1)S(1)}, u32[]{:S(2)}, u32[]{:S(2)}) collective-permute-start(bf16[4,2,48,64]{3,2,0,1:T(8,128)(2,1)S(1)} %get-tuple-element.61), channel_id=1, source_target_pairs={{0,16},{8,24},{16,0},{24,8},{1,17},{9,25},{17,1},{25,9},{2,18},{10... | collective-permute-start | bytes 147464 | tf_op jit(solution)/shard_map/ppermute | solution.py:130
  211.4 16.7 %copy-start.40 = (pred[48,256]{1,0:T(8,128)(4,1)S(1)}, pred[48,256]{1,0:T(8,128)(4,1)}, u32[]{:S(2)}) copy-start(pred[48,256]{1,0:T(8,128)(4,1)} %get-tuple-element.63) | copy-start | bytes 36868
  211.4 15.1 %collective-permute-start.34 = (bf16[4,2,48,64]{3,2,0,1:T(8,128)(2,1)S(1)}, bf16[4,2,48,64]{3,2,0,1:T(8,128)(2,1)S(1)}, u32[]{:S(2)}, u32[]{:S(2)}) collective-permute-start(bf16[4,2,48,64]{3,2,0,1:T(8,128)(2,1)S(1)} %get-tuple-element.62), channel_id=1, source_target_pairs={{0,8},{8,0},{16,24},{24,16},{1,9},{9,1},{17,25},{25,17},{2,10},{10... | collective-permute-start | bytes 147464 | tf_op jit(solution)/shard_map/ppermute | solution.py:130
  223.7 13.4 %collective-permute-start.32 = (bf16[8,64,512]{2,1,0:T(8,128)(2,1)S(1)}, bf16[8,64,512]{2,1,0:T(8,128)(2,1)S(1)}, u32[]{:S(2)}, u32[]{:S(2)}) collective-permute-start(bf16[8,64,512]{2,1,0:T(8,128)(2,1)S(1)} %get-tuple-element.26), channel_id=1, source_target_pairs={{0,16},{4,0},{8,24},{12,8},{16,20},{20,4},{24,28},{28,12},{1,17},{... | collective-permute-start | bytes 1572872 | tf_op jit(solution)/shard_map/ppermute | solution.py:257
  226.2 14.2 %collective-permute-start.33 = (bf16[8,64,512]{2,1,0:T(8,128)(2,1)S(1)}, bf16[8,64,512]{2,1,0:T(8,128)(2,1)S(1)}, u32[]{:S(2)}, u32[]{:S(2)}) collective-permute-start(bf16[8,64,512]{2,1,0:T(8,128)(2,1)S(1)} %get-tuple-element.25), channel_id=1, source_target_pairs={{0,24},{4,8},{8,16},{12,0},{16,28},{20,12},{24,20},{28,4},{1,25},{... | collective-permute-start | bytes 1572872 | tf_op jit(solution)/shard_map/ppermute | solution.py:257
  226.5 14.9 %collective-permute-start.25 = (bf16[96,512]{1,0:T(8,128)(2,1)S(1)}, bf16[96,512]{1,0:T(8,128)(2,1)S(1)}, u32[]{:S(2)}, u32[]{:S(2)}) collective-permute-start(bf16[96,512]{1,0:T(8,128)(2,1)S(1)} %bitcast.213), channel_id=1, source_target_pairs={{0,1},{1,2},{2,3},{3,0},{4,5},{5,6},{6,7},{7,4},{8,9},{9,10},{10,1... | collective-permute-start | bytes 294920 | tf_op jit(solution)/shard_map/ppermute | solution.py:133
  231.4 10.0 %collective-permute-start.24 = (bf16[96,512]{1,0:T(8,128)(2,1)S(1)}, bf16[96,512]{1,0:T(8,128)(2,1)S(1)}, u32[]{:S(2)}, u32[]{:S(2)}) collective-permute-start(bf16[96,512]{1,0:T(8,128)(2,1)S(1)} %bitcast.212), channel_id=1, source_target_pairs={{0,2},{1,3},{2,0},{3,1},{4,6},{5,7},{6,4},{7,5},{8,10},{9,11},{10,... | collective-permute-start | bytes 294920 | tf_op jit(solution)/shard_map/ppermute | solution.py:133
  234.9 6.7 %collective-permute-start.23 = (bf16[96,512]{1,0:T(8,128)(2,1)S(1)}, bf16[96,512]{1,0:T(8,128)(2,1)S(1)}, u32[]{:S(2)}, u32[]{:S(2)}) collective-permute-start(bf16[96,512]{1,0:T(8,128)(2,1)S(1)} %bitcast.211), channel_id=1, source_target_pairs={{0,3},{1,0},{2,1},{3,2},{4,7},{5,4},{6,5},{7,6},{8,11},{9,8},{10,9... | collective-permute-start | bytes 294920 | tf_op jit(solution)/shard_map/ppermute | solution.py:133
  (28 other events, 78.2 us)
Sparse Core Ops, SparseCore 0:
  68.1 31.5 all-gather.2
Sparse Core Ops, SparseCore 1:
  129.2 76.3 reduce-scatter.1

commit v3 on v0

v3 whole, which is shorter than its diff:
```python
import functools

import jax
import jax.numpy as jnp
from jax import lax
from jax.experimental import pallas as pl
from jax.experimental.pallas import tpu as pltpu
from jax.sharding import PartitionSpec as P

CAPD = 12
GROUP = 4
CHUNKS = 1

adapter_scale = 0.5


def slot_places(dom_ids, dom_total):
    row_count = dom_ids.shape[0]
    onehot = (dom_ids[:, None] == jnp.arange(dom_total, dtype=jnp.int32)[None, :]).astype(
        jnp.float32
    )
    row_iota = jnp.arange(row_count, dtype=jnp.int32)
    earlier = (row_iota[:, None] > row_iota[None, :]).astype(jnp.float32)
    prior = jnp.dot(earlier, onehot, preferred_element_type=jnp.float32)
    position = jnp.sum(prior * onehot, axis=1).astype(jnp.int32)
    return dom_ids * CAPD + position


def general_body(
    input_rows,
    value_weight_frozen,
    adapter_down_weight,
    adapter_up_weight,
    layer_output_gradient,
    domain,
):
    row_count = input_rows.shape[0]
    domain_local = adapter_down_weight.shape[0]
    width_local = adapter_down_weight.shape[2]
    value_width_local = adapter_up_weight.shape[2]
    ad_count = lax.axis_size("ad")
    slot_total = ad_count * domain_local * CAPD
    place = slot_places(domain[:, 0], ad_count * domain_local)
    row_iota = jnp.arange(row_count, dtype=jnp.int32)
    matches = place[None, :] == jnp.arange(slot_total, dtype=jnp.int32)[:, None]
    filled = jnp.any(matches, axis=1)
    source_row = jnp.sum(jnp.where(matches, row_iota[None, :], 0), axis=1)
    base = jnp.dot(
        input_rows,
        lax.all_gather(value_weight_frozen, "fsdp", axis=0, tiled=True),
        preferred_element_type=jnp.float32,
    )
    feature_cols = lax.dynamic_slice_in_dim(
        input_rows, lax.axis_index("tp") * width_local, width_local, 1
    )
    zero_value = jnp.zeros((), jnp.bfloat16)
    send_x = jnp.where(filled[:, None], feature_cols[source_row], zero_value)
    send_dy = jnp.where(filled[:, None], layer_output_gradient[source_row], zero_value)
    send_x = send_x.reshape(ad_count, domain_local * CAPD, width_local)
    send_dy = send_dy.reshape(ad_count, domain_local * CAPD, value_width_local)
    got_x = lax.all_to_all(send_x, "ad", split_axis=0, concat_axis=0, tiled=True)
    got_dy = lax.all_to_all(send_dy, "ad", split_axis=0, concat_axis=0, tiled=True)
    rows = got_x.reshape(ad_count, domain_local, CAPD, width_local)
    grads = got_dy.reshape(ad_count, domain_local, CAPD, value_width_local)
    f32 = dict(preferred_element_type=jnp.float32)
    hidden, back = lax.psum(
        (
            jnp.einsum("vqfj,qwj->vqfw", rows, adapter_down_weight, **f32),
            jnp.einsum("amgy,mzy->amgz", grads, adapter_up_weight, **f32),
        ),
        "tp",
    )
    hidden = hidden.astype(jnp.bfloat16)
    back = (adapter_scale * back).astype(jnp.bfloat16)
    delta = adapter_scale * jnp.einsum("lokh,ohi->loki", hidden, adapter_up_weight, **f32)
    delta = delta.astype(jnp.bfloat16).reshape(ad_count, domain_local * CAPD, value_width_local)
    part_a = jnp.einsum("sdcr,sdcx->drx", back, rows, **f32)
    part_b = adapter_scale * jnp.einsum("sdcr,sdce->dre", hidden, grads, **f32)
    returned = lax.all_to_all(delta, "ad", split_axis=0, concat_axis=0, tiled=True)
    returned = returned.reshape(slot_total, value_width_local)
    y_out = (base + returned[place].astype(jnp.float32)).astype(jnp.bfloat16)
    return (
        y_out,
        lax.psum_scatter(part_a, "fsdp", scatter_dimension=1, tiled=True),
        lax.psum_scatter(part_b, "fsdp", scatter_dimension=1, tiled=True),
    )


BF16, F32 = jnp.bfloat16, jnp.float32
VMEM = pl.BlockSpec(memory_space=pltpu.VMEM)
SMEM = pl.BlockSpec(memory_space=pltpu.SMEM)
ANY = pl.BlockSpec(memory_space=pl.ANY)


def dot(lhs, rhs, dims):
    return lax.dot_general(lhs, rhs, (dims, ((), ())), preferred_element_type=F32)


def call(kernel, out_shape, args, in_specs=None, **kwargs):
    outs = [jax.ShapeDtypeStruct(shape, dtype) for shape, dtype in out_shape]
    kwargs.setdefault("out_specs", [VMEM] * len(outs))
    return pl.pallas_call(
        kernel,
        out_shape=outs,
        in_specs=in_specs or [VMEM] * len(args),
        compiler_params=pltpu.CompilerParams(vmem_limit_bytes=48 << 20),
        cost_estimate=pl.CostEstimate(flops=1, bytes_accessed=1, transcendentals=0),
        **kwargs,
    )(*args)


def slot_domain(count, lanes, gslots):
    slot = lax.broadcasted_iota(jnp.int32, (count, lanes), 0)
    return lax.rem(slot, gslots) // CAPD


def widen(v, gslots):
    domain = slot_domain(*v.shape, gslots)
    parts = [jnp.where(domain == e, v.astype(F32), 0.0).astype(v.dtype) for e in range(GROUP)]
    return jnp.concatenate(parts, axis=1)


def narrow(v, gslots):
    n = v.shape[1] // GROUP
    domain = slot_domain(v.shape[0], n, gslots)
    total = v[:, :n]
    for e in range(1, GROUP):
        total = jnp.where(domain == e, v[:, e * n : (e + 1) * n], total)
    return total


def group_rows(refs, g, gslots):
    rows = pl.ds(g * gslots, gslots)
    parts = []
    for r in refs:
        if len(r.shape) == 2:
            parts.append(r[rows, :])
        else:
            parts.extend(r[i, rows, :] for i in range(r.shape[0]))
    return jnp.concatenate(parts, axis=0)


def pack_kernel(at, down, weight, down_out, w_out, sems):
    kt, rows = down_out.shape[2], w_out.shape[0]
    copies = []
    for d in range(down_out.shape[0]):
        columns = pl.ds(pl.multiple_of(at[0] * kt, kt), kt)
        copies.append((down.at[d, :, columns], down_out.at[d]))
    copies.append((weight.at[pl.ds(pl.multiple_of(at[1] * rows, rows), rows), :], w_out))
    copies = [pltpu.make_async_copy(*c, sems.at[i]) for i, c in enumerate(copies)]
    for c in copies:
        c.start()
    for c in copies:
        c.wait()


def one_hot(dom, first, slots, ad, dom_total):
    rows = dom.shape[1]
    names = lax.broadcasted_iota(jnp.int32, (dom_total, rows), 0)
    is_dom = (names == dom).astype(F32)
    before = lax.broadcasted_iota(jnp.int32, (rows, rows), 0) < lax.broadcasted_iota(
        jnp.int32, (rows, rows), 1
    )
    prior = dot(is_dom.astype(BF16), before.astype(F32).astype(BF16), ((1,), (0,)))
    position = jnp.sum(prior * is_dom, axis=0, keepdims=True).astype(jnp.int32)
    slot = lax.broadcasted_iota(jnp.int32, (ad * slots, rows), 0)
    slot = lax.rem(slot + first * slots, ad * slots)
    return (slot == dom * CAPD + position).astype(F32).astype(BF16)


def own_kernel(ad, slots, dom_total, at, dom, x, dy, hot_ref, *outs):
    hot = one_hot(dom[...], at[0], slots, ad, dom_total)
    hot_ref[...] = hot
    width = x.shape[1]
    moved = dot(hot, x[...], ((1,), (0,))).astype(BF16)
    moved_dy = dot(hot, dy[...], ((1,), (0,))).astype(BF16)
    for ka in range(ad):
        outs[ka][:, :width] = moved[ka * slots : (ka + 1) * slots]
        outs[ka][:, width:] = moved_dy[ka * slots : (ka + 1) * slots]


def others_kernel(fsdp, ad, slots, dom_total, at, *refs):
    x_refs, outs = refs[: fsdp - 1], refs[fsdp - 1 :]
    for kf in range(fsdp - 1):
        rows = x_refs[kf].shape[0] - 16
        dom = x_refs[kf][rows:, :rows].astype(F32).astype(jnp.int32)[:1]
        hot = one_hot(dom, at[0], slots, ad, dom_total)
        moved = dot(hot, x_refs[kf][:rows, :], ((1,), (0,))).astype(BF16)
        for c in range(CHUNKS):
            for ka in range(ad):
                cw = outs[c * ad + ka].shape[2]
                part = moved[ka * slots : (ka + 1) * slots, c * cw : (c + 1) * cw]
                outs[c * ad + ka][kf] = part


def back_kernel(ad, gslots, *refs):
    dy_refs, up, out = refs[:ad], refs[ad], refs[ad + 1]
    for g in range(up.shape[0] // GROUP):
        rows = pl.ds(g * gslots, gslots)
        dy = jnp.concatenate([r[rows, :] for r in dy_refs], axis=0)
        weights = up[g * GROUP : (g + 1) * GROUP].reshape(-1, up.shape[2])
        part = narrow(dot(dy, weights, ((1,), (1,))), gslots)
        for ka in range(ad):
            out[ka, rows, :] = part[ka * gslots : (ka + 1) * gslots]


def both_kernel(ad, mine, got, *refs):
    dy_refs, out = refs[:ad], refs[ad]
    width = dy_refs[0].shape[1]
    for ka in range(ad):
        out[ka, :, :width] = dy_refs[ka][...]
        out[ka, :, width:] = (adapter_scale * (mine[ka] + got[ka])).astype(BF16)


def hidden_kernel(fsdp, ad, gslots, start, last, at, *refs):
    own_refs, x_refs, down, down_got = refs[:ad], refs[ad : 2 * ad], refs[2 * ad], refs[2 * ad + 1]
    outs = refs[2 * ad + 2 : -2]
    earlier = None
    if start:
        earlier, outs = outs[0], outs[1:]
    held, sem = refs[-2:]
    cw = held.shape[2]

    @pl.when(at[0] == 1)
    def _():
        columns = pl.ds(pl.multiple_of(at[1], 128), cw)
        copy = pltpu.make_async_copy(down.at[:, :, columns], held, sem)
        copy.start()
        copy.wait()

    @pl.when(at[0] != 1)
    def _():
        copy = pltpu.make_async_copy(down_got.at[:, :, pl.ds(start, cw)], held, sem)
        copy.start()
        copy.wait()

    for g in range(held.shape[0] // GROUP):
        weights = held[g * GROUP : (g + 1) * GROUP].reshape(-1, cw)
        rows = pl.ds(g * gslots, gslots)
        for ka in range(ad):
            x = group_rows((own_refs[ka], x_refs[ka]), g, gslots)
            part = narrow(dot(x, weights, ((1,), (1,))), gslots)
            for kf in range(fsdp):
                new = part[kf * gslots : (kf + 1) * gslots]
                if earlier is not None:
                    new = new + earlier[kf, ka, rows, :]
                if not last:
                    outs[0][kf, ka, rows, :] = new
                else:
                    n = new.shape[1] // 2
                    second = at[2] == 1
                    outs[0][kf, ka, rows, :] = jnp.where(second, new[:, n:], new[:, :n])
                    outs[1][kf, ka, rows, :] = jnp.where(second, new[:, :n], new[:, n:])


def down_grad_kernel(fsdp, ad, gslots, at, *refs):
    own_refs, x_refs, back_refs = refs[:ad], refs[ad : 2 * ad], refs[2 * ad : 2 * ad + fsdp]
    outs, total = refs[2 * ad + fsdp : -1], refs[-1]
    rloc = outs[0].shape[1]
    rank = back_refs[0].shape[2]
    for g in range(outs[0].shape[0] // GROUP):
        rows = pl.ds(g * gslots, gslots)
        x = group_rows([r for pair in zip(own_refs, x_refs) for r in pair], g, gslots)
        back = [back_refs[kf][ka, rows, :] for ka in range(ad) for kf in range(fsdp)]
        back = widen(jnp.concatenate(back, axis=0), gslots)
        total[...] = dot(back, x, ((0,), (0,)))
        for r in range(fsdp):
            for e in range(GROUP):
                first = pl.multiple_of(e * rank + at[r] * rloc, rloc)
                outs[r][g * GROUP + e] = total[pl.ds(first, rloc), :].astype(BF16)


def place_kernel(fsdp, at, *refs):
    for r in range(fsdp):

        @pl.when(pl.program_id(0) == r)
        def _():
            refs[-1][...] = refs[r][...].astype(F32)


def delta_kernel(fsdp, ad, gslots, at, own, got, up, *outs):
    for g in range(up.shape[0] // GROUP):
        rows = pl.ds(g * gslots, gslots)
        mine = jnp.concatenate([own[ka, rows, :] for ka in range(ad)], axis=0)
        other = jnp.concatenate([got[ka, rows, :] for ka in range(ad)], axis=0)
        second = at[0] == 1
        low = jnp.where(second, other.astype(F32), mine.astype(F32))
        high = jnp.where(second, mine.astype(F32), other.astype(F32))
        hidden = jnp.concatenate([low, high], axis=1)
        weights = up[g * GROUP : (g + 1) * GROUP].reshape(-1, up.shape[2])
        delta = dot(widen(hidden.astype(BF16), gslots), weights, ((1,), (0,)))
        delta = (adapter_scale * delta).astype(BF16)
        rloc = hidden.shape[1] // fsdp
        for ka in range(ad):
            outs[ka][rows, :] = delta[ka * gslots : (ka + 1) * gslots]
        for kf in range(fsdp):
            part = hidden[:, :rloc]
            for i in range(1, fsdp):
                part = jnp.where(at[1 + kf] == i, hidden[:, i * rloc : (i + 1) * rloc], part)
            part = part.astype(BF16)
            for ka in range(ad):
                outs[ad + kf][ka, rows, :] = part[ka * gslots : (ka + 1) * gslots]


def up_grad_kernel(fsdp, ad, gslots, *refs):
    hid_refs, dy_refs, out = refs[:fsdp], refs[fsdp:-1], refs[-1]
    rloc = hid_refs[0].shape[2]
    for g in range(out.shape[0] // GROUP):
        hid = group_rows(hid_refs, g, gslots)
        dy = group_rows(dy_refs, g, gslots)
        domain = slot_domain(hid.shape[0], rloc, gslots)
        wide = [jnp.where(domain == e, hid.astype(F32), 0.0) for e in range(GROUP)]
        wide = jnp.concatenate(wide, axis=1).astype(BF16)
        total = adapter_scale * dot(wide, dy, ((0,), (0,)))
        for e in range(GROUP):
            out[g * GROUP + e] = total[e * rloc : (e + 1) * rloc]


def output_kernel(fsdp, ad, *refs):
    base, hot, rows, out = refs[:fsdp], refs[fsdp], refs[fsdp + 1 : -1], refs[-1]
    total = base[0][...]
    for k in range(1, fsdp):
        total = total + base[k][...]
    delta = jnp.concatenate([r[...] for r in rows], axis=0)
    out[...] = (total + dot(hot[...], delta, ((0,), (0,)))).astype(BF16)


def base_kernel(fsdp, rows, at, *refs):
    mine, other, weight, w_got, x_refs = refs[-2], refs[-1], refs[-4], refs[-3], refs[:-4]
    kt = w_got.shape[0]
    for k in range(fsdp):
        x = x_refs[k][:rows, :]
        own = weight[pl.ds(pl.multiple_of(at[0] * kt, kt), kt), :]
        mine[k] = dot(x, own, ((1,), (0,)))
        other[k] = dot(x, w_got[...], ((1,), (0,)))


def column_body(
    input_rows,
    value_weight_frozen,
    adapter_down_weight,
    adapter_up_weight,
    layer_output_gradient,
    domain,
):
    fsdp, ad = lax.axis_size("fsdp"), lax.axis_size("ad")
    f, t, a = lax.axis_index("fsdp"), lax.axis_index("tp"), lax.axis_index("ad")
    fy, fx = f // 2, f % 2
    rows, width = input_rows.shape
    dloc, rank, half = adapter_down_weight.shape
    vloc = adapter_up_weight.shape[2]
    rloc = rank // fsdp
    kf_width = width // fsdp
    kt = kf_width // 2
    slots = dloc * CAPD
    gslots = GROUP * CAPD
    cw = kt // CHUNKS

    def over_f(v, k):
        return lax.ppermute(v, "fsdp", [(i, i ^ k) for i in range(fsdp)]) if k else v

    def over_a(v, k):
        return lax.ppermute(v, "ad", [(i, (i + k) % ad) for i in range(ad)]) if k else v

    def swap(v):
        return lax.ppermute(v, "tp", [(0, 1), (1, 0)])

    def numbers(*values):
        return jnp.stack([jnp.asarray(v, jnp.int32) for v in values])

    def after(v, *others):
        return lax.optimization_barrier((v, others))[0]

    x_in = []
    for k in range(fsdp):
        block = lax.dynamic_slice_in_dim(input_rows, (f ^ k) * kf_width + t * kt, kt, 1)
        if k:
            dom_row = jnp.pad(domain.T.astype(BF16), ((0, 15), (0, kt - rows)))
            block = jnp.concatenate([block, dom_row], axis=0)
        x_in.append(block)
    x_in = lax.optimization_barrier(x_in)
    x_in = [over_f(v, k) for k, v in enumerate(x_in)]

    hot, *sends = call(
        functools.partial(own_kernel, ad, slots, ad * dloc),
        [((ad * slots, rows), BF16)] + [((slots, kt + vloc), BF16)] * ad,
        [numbers(a), domain.T, x_in[0], layer_output_gradient],
        [SMEM] + [VMEM] * 3,
    )
    sends[-1] = after(sends[-1], x_in[1])
    own = [over_a(v, ka) for ka, v in enumerate(sends)]

    down_other, w_other = call(
        pack_kernel,
        [((dloc, rank, kt), BF16), ((kt, vloc), BF16)],
        [
            numbers(fx * 2 + 1 - t, 1 - t),
            after(adapter_down_weight, *sends[:-1]),
            value_weight_frozen,
        ],
        [SMEM, ANY, ANY],
        out_specs=[ANY, ANY],
        scratch_shapes=[pltpu.SemaphoreType.DMA((dloc + 1,))],
    )

    sends = call(
        functools.partial(others_kernel, fsdp, ad, slots, ad * dloc),
        [((fsdp - 1, slots, cw), BF16)] * (CHUNKS * ad),
        [numbers(a), *lax.optimization_barrier((x_in[1:], own[1:]))[0]],
        [SMEM] + [VMEM] * (fsdp - 1),
    )
    x_routed = [[over_a(v, ka) for ka, v in enumerate(sends[:ad])]]

    own = after(own, *sends)

    dy_specs = [pl.BlockSpec((slots, vloc), lambda i: (0, kt // vloc))] * ad
    (back,) = call(
        functools.partial(back_kernel, ad, gslots),
        [((ad, slots, rank), F32)],
        [*own, adapter_up_weight],
        dy_specs + [pl.BlockSpec((dloc, rank, vloc), lambda i: (0, 0, 0))],
        grid=(1,),
    )
    pairs = [(i * 2 + i // 2, i * 2 + 1 - i // 2) for i in range(fsdp)]
    w_got = swap(after(w_other, back))
    back_spec = pl.BlockSpec((ad, slots, rank), lambda i: (0, 0, 0))
    (both,) = call(
        functools.partial(both_kernel, ad),
        [((ad, slots, vloc + rank), BF16)],
        [back, swap(back), *own],
        [back_spec] * 2 + dy_specs,
        grid=(1,),
    )
    w_got = after(w_got, both)
    both = [over_f(both, k) for k in range(fsdp)]
    down_got = lax.ppermute(after(down_other, w_got), ("fsdp", "tp"), pairs)
    for c in range(1, CHUNKS):
        chunk = [after(v, *x_routed[c - 1], *both) for v in sends[c * ad : (c + 1) * ad]]
        x_routed.append([over_a(v, ka) for ka, v in enumerate(chunk)])

    mine, other = call(
        functools.partial(base_kernel, fsdp, rows),
        [((fsdp, rows, vloc), F32)] * 2,
        [numbers(t), *x_in, value_weight_frozen, w_got],
        [SMEM] + [VMEM] * (fsdp + 2),
    )
    base = mine + swap(after(other, down_got))
    base = [over_f(base[k], k) for k in range(fsdp)]

    def chunk_specs(c):
        specs = [pl.BlockSpec((slots, cw), lambda i: (0, c))] * ad
        return specs + [pl.BlockSpec((fsdp - 1, slots, cw), lambda i: (0, 0, 0))] * ad

    def hidden(c, earlier, routed):
        last = c == CHUNKS - 1
        return call(
            functools.partial(hidden_kernel, fsdp, ad, gslots, c * cw, last),
            [((fsdp, ad, slots, rank // 2 if last else rank), F32)] * (2 if last else 1),
            [
                numbers(t == fy, fx * kf_width + t * kt + c * cw, t),
                *own,
                *routed,
                adapter_down_weight,
                down_got,
                *earlier,
            ],
            [SMEM] + chunk_specs(c) + [ANY, ANY] + [VMEM] * len(earlier),
            grid=(1,),
            scratch_shapes=[pltpu.VMEM((dloc, rank, cw), BF16), pltpu.SemaphoreType.DMA],
        )

    grad_a = None
    hid = []
    for c in range(CHUNKS):
        last = c == CHUNKS - 1
        if last:
            hid = hidden(c, hid, after(x_routed[c], *both, *base))
            hid = hid[0] + swap(hid[1])
            hid, both = lax.optimization_barrier((hid, both))
        sums = call(
            functools.partial(down_grad_kernel, fsdp, ad, gslots),
            [((dloc, rloc, cw), BF16)] * fsdp,
            [
                numbers(*[(t ^ (r // 2)) * 2 + (fx ^ (r % 2)) for r in range(fsdp)]),
                *own,
                *x_routed[c],
                *both,
            ],
            [SMEM]
            + chunk_specs(c)
            + [pl.BlockSpec((ad, slots, rank), lambda i: (0, 0, vloc // rank))] * fsdp,
            grid=(1,),
            scratch_shapes=[pltpu.VMEM((GROUP * rank, cw), F32)],
        )
        got = []
        for r in range(fsdp):
            p, q = r % 2, r // 2
            perm = [
                ((y * 2 + x) * 2 + s, ((s ^ q) * 2 + (x ^ p)) * 2 + y)
                for y in range(2)
                for x in range(2)
                for s in range(2)
            ]
            got.append(lax.ppermute(sums[r], ("fsdp", "tp"), perm))
        if not last:
            hid = hidden(c, hid, after(x_routed[c], *sums))
            x_routed[c + 1] = after(x_routed[c + 1], *got[:2])
        at = [
            ((fx ^ (r % 2)) * kf_width + (fy ^ (r // 2)) * kt + c * cw) // cw
            for r in range(fsdp)
        ]
        args = got if grad_a is None else [*got, grad_a]
        grad_a = pl.pallas_call(
            functools.partial(place_kernel, fsdp),
            out_shape=jax.ShapeDtypeStruct((dloc, rloc, half), F32),
            grid_spec=pltpu.PrefetchScalarGridSpec(
                num_scalar_prefetch=1,
                grid=(fsdp,),
                in_specs=[VMEM] * fsdp + [ANY] * (len(args) - fsdp),
                out_specs=pl.BlockSpec((dloc, rloc, cw), lambda i, at: (0, 0, at[i])),
            ),
            input_output_aliases={} if grad_a is None else {fsdp + 1: 0},
            cost_estimate=pl.CostEstimate(flops=1, bytes_accessed=1, transcendentals=0),
        )(numbers(*at), *args)

    hid = [over_f(hid[k], k) for k in range(fsdp)]
    hid_own = (hid[0] + hid[1] + hid[2] + hid[3]).astype(BF16)
    outs = call(
        functools.partial(delta_kernel, fsdp, ad, gslots),
        [((slots, vloc), BF16)] * ad + [((ad, slots, rloc), BF16)] * fsdp,
        [numbers(t, *[f ^ k for k in range(fsdp)]), hid_own, swap(hid_own), adapter_up_weight],
        [SMEM] + [VMEM] * 3,
    )
    returned = [over_a(v, (ad - ka) % ad) for ka, v in enumerate(outs[:ad])]
    hid_cols = [over_f(v, k) for k, v in enumerate(outs[ad:])]

    (y_out,) = call(
        functools.partial(output_kernel, fsdp, ad),
        [((rows, vloc), BF16)],
        [*base, hot, *returned],
    )
    (grad_b,) = call(
        functools.partial(up_grad_kernel, fsdp, ad, gslots),
        [((dloc, rloc, vloc), F32)],
        [*hid_cols, *both],
        [pl.BlockSpec((ad, slots, rloc), lambda i: (0, 0, 0))] * fsdp
        + [pl.BlockSpec((ad, slots, vloc), lambda i: (0, 0, 0))] * fsdp,
        grid=(1,),
    )
    return y_out, grad_a, grad_b


def solution(mesh):
    placed = (
        P(("fsdp", "ad"), None),
        P("fsdp", "tp"),
        P("ad", None, "tp"),
        P("ad", None, "tp"),
        P(("fsdp", "ad"), "tp"),
        P(("fsdp", "ad"), None),
    )
    square = mesh.shape["fsdp"] == 4 and mesh.shape["tp"] == 2
    return jax.shard_map(
        column_body if square else general_body,
        mesh=mesh,
        in_specs=placed,
        out_specs=(P(("fsdp", "ad"), "tp"), P("ad", "fsdp", "tp"), P("ad", "fsdp", "tp")),
        check_vma=False,
    )
```

time: 498 us -> 397 us (0.80)
  waiting for transfers between devices: 312 us -> 123 us
  Pallas kernels: 0 us -> 169 us
  blocking collectives: 95.6 us -> 0 us
  starting transfers between devices: 3.84 us -> 68.4 us
  matrix products: 43.9 us -> 0 us
  between operations: 15.8 us -> 0.99 us
  local copies, waits for them, and re-layouts: 23.3 us -> 29.5 us
    reduce_scatter x2 -> x0, waiting for transfers between devices: 298 us -> none  [the longest x1 292 us: body(): lax.psum_scatter(part_a, 'fsdp', scatter_dimension=1, tiled=True)]
    pallas_call x0 -> x12, Pallas kernels: none -> 169 us  [the longest x11 163 us: call(): pl.pallas_call(kernel, out_shape=outs, in_specs=in_specs or [VMEM] * len(...]
    ppermute x0 -> x34, waiting for transfers between devices: none -> 123 us  [the longest x15 79.6 us: over_f(): lax.ppermute(v, 'fsdp', [(i, i ^ k) for i in range(fsdp)])]
    all_to_all x2 -> x0, blocking collectives: 90.8 us -> none  [the longest x1 73 us: body(): lax.all_to_all(send_x, 'ad', split_axis=0, concat_axis=0, tiled=True)]
    ppermute x0 -> x34, starting transfers between devices: none -> 68.4 us  [the longest x9 31.7 us: over_a(): lax.ppermute(v, 'ad', [(i, (i + k) % ad) for i in range(ad)])]
    dot_general x7 -> x0, matrix products: 43.9 us -> none  [the longest x1 18.5 us: body(): jnp.einsum('sdcr,sdcx->drx', input_gradient_lowrank, routed_input_rows, p...]
    unnamed x4 -> x82, local copies, waits for them, and re-layouts: 0.02 us -> 25.5 us
    gather x3 -> x0, local copies, waits for them, and re-layouts: 14.5 us -> none  [the longest x1 10.2 us: body(): send_x = jnp.where(filled[:, None], feature_cols[source_row], zero_value)]
  transfers between devices with their start and end apart: 5 -> 34, of which waited for: 3 -> 15; matrix products, arithmetic and copies ran while one was open for 13% -> 1% of each run, Pallas kernels for 0% -> 38%
where the time goes in v3:
time: 397 us; the launch traced here: 396 us
  Pallas kernels  169 us (43%)
  waiting for transfers between devices  123 us (31%)
  starting transfers between devices  68.4 us (17%)
  local copies, waits for them, and re-layouts  29.5 us (7%)
  other arithmetic  4.37 us (1%)
    pallas_call x11, Pallas kernels, call(): pl.pallas_call(kernel, out_shape=outs, in_specs=in_specs or [VMEM] * len(...  163 us
    ppermute x15, waiting for transfers between devices, over_f(): lax.ppermute(v, 'fsdp', [(i, i ^ k) for i in range(fsdp)])  79.6 us
    ppermute x9, waiting for transfers between devices, over_a(): lax.ppermute(v, 'ad', [(i, (i + k) % ad) for i in range(ad)])  36.8 us
    ppermute x9, starting transfers between devices, over_a(): lax.ppermute(v, 'ad', [(i, (i + k) % ad) for i in range(ad)])  31.7 us
    unnamed x82, local copies, waits for them, and re-layouts  25.5 us
    ppermute x15, starting transfers between devices, over_f(): lax.ppermute(v, 'fsdp', [(i, i ^ k) for i in range(fsdp)])  20.4 us
    ppermute x4, starting transfers between devices, column_body(): got.append(lax.ppermute(sums[r], ('fsdp', 'tp'), perm))  11.1 us
  transfers between devices with their start and end apart: 34, of which 15 were waited for; matrix products, arithmetic and copies ran while one was open for 1% of the time, Pallas kernels for 38%

profile of v3, /device:TPU:0, one launch (start us, length us, event | category | flops | bytes accessed | tf_op | source)
XLA Modules:
  0.0 395.6 jit_solution(5448461025192046081)
XLA Ops:
  1.3 1.7 constant_dynamic-slice_fusion
  3.1 1.1 fusion.3
  4.2 2.9 collective-permute-start
  7.2 1.5 collective-permute-start.1
  8.7 1.5 shard_map.85
  10.9 2.0 collective-permute-start.3
  12.9 2.6 collective-permute-start.4
  15.5 5.1 %collective-permute-done.refs_0_.refs_1_ = bf16[272,1024]{1,0:T(8,128)(2,1)S(1)} collective-permute-done((bf16[272,1024]{1,0:T(8,128)(2,1)S(1)}, bf16[272,1024]{1,0:T(8,128)(2,1)S(1)}, u32[]{:S(2)}, u32[]{:S(2)}) %collective-permute-start) | collective-permute-done | bytes 557088 | tf_op jit(solution)/shard_map/ppermute | solution.py:360
  21.4 4.2 %collective-permute-start.5 = (bf16[96,1536]{1,0:T(8,128)(2,1)}, bf16[96,1536]{1,0:T(8,128)(2,1)S(1)}, u32[]{:S(2)}, u32[]{:S(2)}) collective-permute-start(bf16[96,1536]{1,0:T(8,128)(2,1)} %get-tuple-element.66), channel_id=1, source_target_pairs={{0,3},{1,0},{2,1},{3,2},{4,7},{5,4},{6,5},{7,6},{8,11},{9,8},{10,9... | collective-permute-start | bytes 884744 | tf_op jit(solution)/shard_map/ppermute | solution.py:363
  25.7 1.6 copy-done.1
  27.3 128.8 %shard_map.86 = (bf16[8,256,1024]{2,1,0:T(8,128)(2,1)}, bf16[1024,512]{1,0:T(8,128)(2,1)S(1)}) custom-call(s32[2]{0:T(128)S(1)} %pad_add_fusion.at, bf16[8,256,4096]{2,1,0:T(8,128)(2,1)} %refs_8_.1, bf16[2048,512]{1,0:T(8,128)(2,1)S(1)} %copy-done.1), custom_call_target="tpu_custom_call" | custom-call | flops 1 | bytes 1 | tf_op jit(solution)/shard_map/pallas_call | solution.py:102
  156.2 2.6 shard_map.87
  160.3 2.7 collective-permute-done.7.got
  163.0 1.0 copy-done.3
  165.0 2.3 collective-permute-start.8
  167.3 5.6 %shard_map.90 = (f32[4,256,512]{2,1,0:T(8,128)S(1)}, f32[4,256,512]{2,1,0:T(8,128)}) custom-call(s32[1]{0:T(128)} %bitcast.at, bf16[256,1024]{1,0:T(8,128)(2,1)S(1)} %copy-done.11, bf16[272,1024]{1,0:T(8,128)(2,1)S(1)} %copy-done.28, bf16[272,1024]{1,0:T(8,128)(2,1)} %collective-permute-done.1.refs_1_.refs_2_, ...), custom_call_target="tpu_custom_call" | custom-call | flops 1 | bytes 1 | tf_op jit(solution)/shard_map/pallas_call | solution.py:102
  172.9 1.1 collective-permute-done.8.refs_9_
  174.4 1.0 collective-permute-start.14
  175.4 2.8 collective-permute-start.15
  178.2 1.5 collective-permute-start.16
  179.7 1.5 collective-permute-start.17
  181.7 10.8 %collective-permute-done.13.refs_5_ = bf16[3,96,1024]{2,1,0:T(8,128)(2,1)S(1)} collective-permute-done((bf16[3,96,1024]{2,1,0:T(8,128)(2,1)S(1)}, bf16[3,96,1024]{2,1,0:T(8,128)(2,1)S(1)}, u32[]{:S(2)}, u32[]{:S(2)}) %collective-permute-start.13) | collective-permute-done | bytes 589856 | tf_op jit(solution)/shard_map/ppermute | solution.py:363
  192.5 2.4 collective-permute-start.18
  194.9 1.4 slice_bitcast_fusion
  196.3 20.5 %collective-permute-done.14.refs_6_ = bf16[3,96,1024]{2,1,0:T(8,128)(2,1)S(1)} collective-permute-done((bf16[3,96,1024]{2,1,0:T(8,128)(2,1)S(1)}, bf16[3,96,1024]{2,1,0:T(8,128)(2,1)S(1)}, u32[]{:S(2)}, u32[]{:S(2)}) %collective-permute-start.14) | collective-permute-done | bytes 589856 | tf_op jit(solution)/shard_map/ppermute | solution.py:363
  217.6 1.5 collective-permute-start.10
  219.9 1.5 collective-permute-start.11
  222.8 10.0 %collective-permute-done.10.refs_1_ = f32[256,512]{1,0:T(8,128)} collective-permute-done((f32[256,512]{1,0:T(8,128)}, f32[256,512]{1,0:T(8,128)}, u32[]{:S(2)}, u32[]{:S(2)}) %collective-permute-start.10) | collective-permute-done | bytes 524320 | tf_op jit(solution)/shard_map/ppermute | solution.py:360
  232.8 11.0 %collective-permute-done.11.refs_2_ = f32[256,512]{1,0:T(8,128)} collective-permute-done((f32[256,512]{1,0:T(8,128)}, f32[256,512]{1,0:T(8,128)}, u32[]{:S(2)}, u32[]{:S(2)}) %collective-permute-start.11) | collective-permute-done | bytes 524320 | tf_op jit(solution)/shard_map/ppermute | solution.py:360
  243.8 1.0 copy-done.4
  244.8 1.0 copy-done.8
  245.7 1.1 copy-done.13
  246.8 1.1 copy-done.16
  247.8 1.1 copy-done.19
  248.9 1.1 copy-done.22
  250.0 8.3 %shard_map.91 = (f32[4,4,96,128]{3,2,1,0:T(8,128)S(1)}, f32[4,4,96,128]{3,2,1,0:T(8,128)S(1)}) custom-call(s32[3]{0:T(128)S(1)} %pad_add_fusion.1.at, bf16[96,1536]{1,0:T(8,128)(2,1)S(1)} %get-tuple-element.74.refs_0_, bf16[96,1536]{1,0:T(8,128)(2,1)S(1)} %collective-permute-done.3.refs_1_, bf16[96,1536]{1,0:T(8,128)(2,1)S(1)} %copy-done.4, ...), custom_call_target="tpu_custom_call" | custom-call | flops 1 | bytes 1 | tf_op jit(solution)/shard_map/pallas_call | solution.py:102
  258.4 2.3 collective-permute-done.19
  263.1 1.7 collective-permute-start.21
  264.8 1.0 copy-done.5
  266.7 1.1 copy-done.14
  267.8 1.1 copy-done.17
  268.9 1.1 copy-done.20
  269.9 1.1 copy-done.23
  271.0 1.1 copy-done.25
  272.0 7.0 %shard_map.94 = (bf16[8,64,1024]{2,1,0:T(8,128)(2,1)}, bf16[8,64,1024]{2,1,0:T(8,128)(2,1)}, bf16[8,64,1024]{2,1,0:T(8,128)(2,1)}, bf16[8,64,1024]{2,1,0:T(8,128)(2,1)}) custom-call(s32[4]{0:T(128)S(1)} %pad_add_fusion.3.at, bf16[96,1536]{1,0:T(8,128)(2,1)S(1)} %get-tuple-element.74.refs_0_, bf16[96,1536]{1,0:T(8,128)(2,1)S(1)} %collective-permute-done.3.refs_1_, ...), custom_call_target="tpu_custom_call" | custom-call | flops 1 | bytes 1 | tf_op jit(solution)/shard_map/pallas_call | solution.py:102
  279.0 9.6 %collective-permute-start.27 = (bf16[8,64,1024]{2,1,0:T(8,128)(2,1)}, bf16[8,64,1024]{2,1,0:T(8,128)(2,1)}, u32[]{:S(2)}, u32[]{:S(2)}) collective-permute-start(bf16[8,64,1024]{2,1,0:T(8,128)(2,1)} %get-tuple-element.101), channel_id=1, source_target_pairs={{0,0},{4,16},{8,8},{12,24},{16,4},{20,20},{24,12},{28,28},{1,1},{5... | collective-permute-start | bytes 3145736 | tf_op jit(solution)/shard_map/ppermute | solution.py:504
  288.6 1.5 collective-permute-start.28
  290.8 42.4 %collective-permute-done.22 = f32[4,96,128]{2,1,0:T(8,128)S(1)} collective-permute-done((f32[4,96,128]{2,1,0:T(8,128)S(1)}, f32[4,96,128]{2,1,0:T(8,128)S(1)}, u32[]{:S(2)}, u32[]{:S(2)}) %collective-permute-start.22) | collective-permute-done | bytes 196640 | tf_op jit(solution)/shard_map/ppermute | solution.py:360
  333.2 1.2 fusion.6.own
  334.4 1.8 collective-permute-start.23
  338.6 2.1 shard_map.92
  342.0 1.4 collective-permute-start.31
  343.4 3.6 collective-permute-done.31.refs_1_
  348.0 3.7 collective-permute-done.32.refs_2_
  351.7 1.8 collective-permute-start.33
  353.5 3.7 collective-permute-done.33.refs_3_
  357.2 12.0 %collective-permute-start.24 = (bf16[96,512]{1,0:T(8,128)(2,1)S(1)}, bf16[96,512]{1,0:T(8,128)(2,1)S(1)}, u32[]{:S(2)}, u32[]{:S(2)}) collective-permute-start(bf16[96,512]{1,0:T(8,128)(2,1)S(1)} %get-tuple-element.94), channel_id=1, source_target_pairs={{0,3},{1,0},{2,1},{3,2},{4,7},{5,4},{6,5},{7,6},{8,11},{9,8},{10,9... | collective-permute-start | bytes 294920 | tf_op jit(solution)/shard_map/ppermute | solution.py:363
  369.2 2.6 collective-permute-done.24.refs_6_
  371.8 2.8 collective-permute-start.25
  374.6 2.9 collective-permute-done.25.refs_7_
  377.6 4.3 %collective-permute-start.26 = (bf16[96,512]{1,0:T(8,128)(2,1)}, bf16[96,512]{1,0:T(8,128)(2,1)S(1)}, u32[]{:S(2)}, u32[]{:S(2)}) collective-permute-start(bf16[96,512]{1,0:T(8,128)(2,1)} %copy-done.38), channel_id=1, source_target_pairs={{0,1},{1,2},{2,3},{3,0},{4,5},{5,6},{6,7},{7,4},{8,9},{9,10},{10,1... | collective-permute-start | bytes 294920 | tf_op jit(solution)/shard_map/ppermute | solution.py:363
  383.3 3.4 shard_map.96
  386.8 2.4 shard_map.93
  389.2 6.5 %shard_map.95 = f32[8,64,4096]{2,1,0:T(8,128)} custom-call(s32[4]{0:T(128)} %pad_add_fusion.2.at, bf16[8,64,1024]{2,1,0:T(8,128)(2,1)} %collective-permute-done.27.refs_0_, bf16[8,64,1024]{2,1,0:T(8,128)(2,1)} %collective-permute-done.28.refs_1_, bf16[8,64,1024]{2,1,0:T(8,128)(2,1)} %collective-permute-done.29.refs_2_, ...), custom_call_target="tpu_custom_call" | custom-call | flops 1 | bytes 1 | tf_op jit(solution)/shard_map/pallas_call | solution.py:513
  (111 shorter events, 18.9 us)
Async XLA Ops:
  3.1 22.5 %copy-start.10 = (bf16[256,1024]{1,0:T(8,128)(2,1)}, bf16[256,1024]{1,0:T(8,128)(2,1)S(1)}, u32[]{:S(2)}) copy-start(bf16[256,1024]{1,0:T(8,128)(2,1)S(1)} %get-tuple-element.56.x.refs_0_) | copy-start | bytes 1572868
  3.1 5.6 %copy-start.30 = (bf16[256,512]{1,0:T(8,128)(2,1)S(1)}, bf16[256,512]{1,0:T(8,128)(2,1)}, u32[]{:S(2)}) copy-start(bf16[256,512]{1,0:T(8,128)(2,1)} %dy.1) | copy-start | bytes 786436
  3.1 5.6 %copy-start.37 = (s32[256,1]{0,1:T(1,128)S(1)}, s32[256,1]{0,1:T(1,128)}, u32[]{:S(2)}) copy-start(s32[256,1]{0,1:T(1,128)} %param.11) | copy-start | bytes 3076
  4.2 16.4 %collective-permute-start = (bf16[272,1024]{1,0:T(8,128)(2,1)S(1)}, bf16[272,1024]{1,0:T(8,128)(2,1)S(1)}, u32[]{:S(2)}, u32[]{:S(2)}) collective-permute-start(bf16[272,1024]{1,0:T(8,128)(2,1)S(1)} %get-tuple-element.57), channel_id=1, source_target_pairs={{0,8},{8,0},{16,24},{24,16},{1,9},{9,1},{17,25},{25,17},{2,10},{10... | collective-permute-start | bytes 1671176 | tf_op jit(solution)/shard_map/ppermute | solution.py:360
  7.2 148.9 %collective-permute-start.1 = (bf16[272,1024]{1,0:T(8,128)(2,1)}, bf16[272,1024]{1,0:T(8,128)(2,1)}, u32[]{:S(2)}, u32[]{:S(2)}) collective-permute-start(bf16[272,1024]{1,0:T(8,128)(2,1)} %get-tuple-element.58), channel_id=1, source_target_pairs={{0,16},{8,24},{16,0},{24,8},{1,17},{9,25},{17,1},{25,9},{2,18},{10... | collective-permute-start | bytes 1671176 | tf_op jit(solution)/shard_map/ppermute | solution.py:360
  8.7 147.4 %collective-permute-start.2 = (bf16[272,1024]{1,0:T(8,128)(2,1)}, bf16[272,1024]{1,0:T(8,128)(2,1)}, u32[]{:S(2)}, u32[]{:S(2)}) collective-permute-start(bf16[272,1024]{1,0:T(8,128)(2,1)} %get-tuple-element.59), channel_id=1, source_target_pairs={{0,24},{8,16},{16,8},{24,0},{1,25},{9,17},{17,9},{25,1},{2,26},{10... | collective-permute-start | bytes 1671176 | tf_op jit(solution)/shard_map/ppermute | solution.py:360
  10.9 145.2 %collective-permute-start.3 = (bf16[96,1536]{1,0:T(8,128)(2,1)}, bf16[96,1536]{1,0:T(8,128)(2,1)S(1)}, u32[]{:S(2)}, u32[]{:S(2)}) collective-permute-start(bf16[96,1536]{1,0:T(8,128)(2,1)} %get-tuple-element.61), channel_id=1, source_target_pairs={{0,1},{1,2},{2,3},{3,0},{4,5},{5,6},{6,7},{7,4},{8,9},{9,10},{10,1... | collective-permute-start | bytes 884744 | tf_op jit(solution)/shard_map/ppermute | solution.py:363
  12.9 143.1 %collective-permute-start.4 = (bf16[96,1536]{1,0:T(8,128)(2,1)}, bf16[96,1536]{1,0:T(8,128)(2,1)S(1)}, u32[]{:S(2)}, u32[]{:S(2)}) collective-permute-start(bf16[96,1536]{1,0:T(8,128)(2,1)} %get-tuple-element.62), channel_id=1, source_target_pairs={{0,2},{1,3},{2,0},{3,1},{4,6},{5,7},{6,4},{7,5},{8,10},{9,11},{10,... | collective-permute-start | bytes 884744 | tf_op jit(solution)/shard_map/ppermute | solution.py:363
  21.4 134.7 %collective-permute-start.5 = (bf16[96,1536]{1,0:T(8,128)(2,1)}, bf16[96,1536]{1,0:T(8,128)(2,1)S(1)}, u32[]{:S(2)}, u32[]{:S(2)}) collective-permute-start(bf16[96,1536]{1,0:T(8,128)(2,1)} %get-tuple-element.66), channel_id=1, source_target_pairs={{0,3},{1,0},{2,1},{3,2},{4,7},{5,4},{6,5},{7,6},{8,11},{9,8},{10,9... | collective-permute-start | bytes 884744 | tf_op jit(solution)/shard_map/ppermute | solution.py:363
  25.7 1.6 copy-start.1
  27.3 128.9 %copy-start.28 = (bf16[272,1024]{1,0:T(8,128)(2,1)S(1)}, bf16[272,1024]{1,0:T(8,128)(2,1)}, u32[]{:S(2)}) copy-start(bf16[272,1024]{1,0:T(8,128)(2,1)} %copy-done.27) | copy-start | bytes 1671172
  27.3 131.5 %copy-start = (bf16[8,256,512]{2,1,0:T(8,128)(2,1)S(1)}, bf16[8,256,512]{2,1,0:T(8,128)(2,1)}, u32[]{:S(2)}) copy-start(bf16[8,256,512]{2,1,0:T(8,128)(2,1)} %up.1) | copy-start | bytes 6291460
  156.1 3.6 copy-start.2
  156.1 3.5 copy-start.6
  158.8 1.5 copy-start.12
  158.8 8.5 %copy-start.11 = (bf16[256,1024]{1,0:T(8,128)(2,1)S(1)}, bf16[256,1024]{1,0:T(8,128)(2,1)}, u32[]{:S(2)}) copy-start(bf16[256,1024]{1,0:T(8,128)(2,1)} %copy-done.10) | copy-start | bytes 1572868
  159.7 5.3 %collective-permute-start.6 = (bf16[1024,512]{1,0:T(8,128)(2,1)S(1)}, bf16[1024,512]{1,0:T(8,128)(2,1)S(1)}, u32[]{:S(2)}, u32[]{:S(2)}) collective-permute-start(bf16[1024,512]{1,0:T(8,128)(2,1)S(1)} %get-tuple-element.78), channel_id=1, source_target_pairs={{0,4},{4,0},{1,5},{5,1},{2,6},{6,2},{3,7},{7,3},{8,12},{12,8},{9,1... | collective-permute-start | bytes 3145736 | tf_op jit(solution)/shard_map/ppermute | solution.py:366
  159.8 3.2 collective-permute-start.7
  163.0 1.0 copy-start.3
  163.9 1.0 copy-start.7
  165.0 9.0 %collective-permute-start.8 = (bf16[8,256,1024]{2,1,0:T(8,128)(2,1)}, bf16[8,256,1024]{2,1,0:T(8,128)(2,1)S(1)}, u32[]{:S(2)}, u32[]{:S(2)}) collective-permute-start(bf16[8,256,1024]{2,1,0:T(8,128)(2,1)} %get-tuple-element.83), channel_id=1, source_target_pairs={{0,4},{8,12},{20,16},{28,24},{1,5},{9,13},{21,17},{29,25},{2,6},{1... | collective-permute-start | bytes 12582920 | tf_op jit(solution)/shard_map/ppermute | solution.py:436
  174.0 7.7 %copy-start.39 = (bf16[8,256,1024]{2,1,0:T(8,128)(2,1)}, bf16[8,256,1024]{2,1,0:T(8,128)(2,1)S(1)}, u32[]{:S(2)}) copy-start(bf16[8,256,1024]{2,1,0:T(8,128)(2,1)S(1)} %collective-permute-done.8.refs_9_) | copy-start | bytes 12582916
  174.0 5.7 %collective-permute-start.9 = (f32[4,256,512]{2,1,0:T(8,128)}, f32[4,256,512]{2,1,0:T(8,128)S(1)}, u32[]{:S(2)}, u32[]{:S(2)}) collective-permute-start(f32[4,256,512]{2,1,0:T(8,128)} %get-tuple-element.84), channel_id=1, source_target_pairs={{0,4},{4,0},{1,5},{5,1},{2,6},{6,2},{3,7},{7,3},{8,12},{12,8},{9,1... | collective-permute-start | bytes 6291464 | tf_op jit(solution)/shard_map/ppermute | solution.py:366
  174.4 18.1 %collective-permute-start.13 = (bf16[3,96,1024]{2,1,0:T(8,128)(2,1)S(1)}, bf16[3,96,1024]{2,1,0:T(8,128)(2,1)S(1)}, u32[]{:S(2)}, u32[]{:S(2)}) collective-permute-start(bf16[3,96,1024]{2,1,0:T(8,128)(2,1)S(1)} %get-tuple-element.71), channel_id=1, source_target_pairs={{0,1},{1,2},{2,3},{3,0},{4,5},{5,6},{6,7},{7,4},{8,9},{9,10},{10,1... | collective-permute-start | bytes 1769480 | tf_op jit(solution)/shard_map/ppermute | solution.py:363
  174.4 42.4 %collective-permute-start.14 = (bf16[3,96,1024]{2,1,0:T(8,128)(2,1)S(1)}, bf16[3,96,1024]{2,1,0:T(8,128)(2,1)S(1)}, u32[]{:S(2)}, u32[]{:S(2)}) collective-permute-start(bf16[3,96,1024]{2,1,0:T(8,128)(2,1)S(1)} %get-tuple-element.72), channel_id=1, source_target_pairs={{0,2},{1,3},{2,0},{3,1},{4,6},{5,7},{6,4},{7,5},{8,10},{9,11},{10,... | collective-permute-start | bytes 1769480 | tf_op jit(solution)/shard_map/ppermute | solution.py:363
  175.4 43.7 %collective-permute-start.15 = (bf16[3,96,1024]{2,1,0:T(8,128)(2,1)S(1)}, bf16[3,96,1024]{2,1,0:T(8,128)(2,1)S(1)}, u32[]{:S(2)}, u32[]{:S(2)}) collective-permute-start(bf16[3,96,1024]{2,1,0:T(8,128)(2,1)S(1)} %get-tuple-element.73), channel_id=1, source_target_pairs={{0,3},{1,0},{2,1},{3,2},{4,7},{5,4},{6,5},{7,6},{8,11},{9,8},{10,9... | collective-permute-start | bytes 1769480 | tf_op jit(solution)/shard_map/ppermute | solution.py:363
  178.2 43.2 %collective-permute-start.16 = (bf16[4,96,768]{2,1,0:T(8,128)(2,1)S(1)}, bf16[4,96,768]{2,1,0:T(8,128)(2,1)S(1)}, u32[]{:S(2)}, u32[]{:S(2)}) collective-permute-start(bf16[4,96,768]{2,1,0:T(8,128)(2,1)S(1)} %shard_map.89.refs_8_.refs_4_), channel_id=1, source_target_pairs={{0,8},{8,0},{16,24},{24,16},{1,9},{9,1},{17,25},{25,17},{2,10},{10... | collective-permute-start | bytes 1769480 | tf_op jit(solution)/shard_map/ppermute | solution.py:360
  179.7 43.1 %collective-permute-start.17 = (bf16[4,96,768]{2,1,0:T(8,128)(2,1)S(1)}, bf16[4,96,768]{2,1,0:T(8,128)(2,1)}, u32[]{:S(2)}, u32[]{:S(2)}) collective-permute-start(bf16[4,96,768]{2,1,0:T(8,128)(2,1)S(1)} %shard_map.89.refs_8_.refs_4_), channel_id=1, source_target_pairs={{0,16},{8,24},{16,0},{24,8},{1,17},{9,25},{17,1},{25,9},{2,18},{10... | collective-permute-start | bytes 1769480 | tf_op jit(solution)/shard_map/ppermute | solution.py:360
  192.5 3.8 copy-start.15
  192.5 30.3 %collective-permute-start.18 = (bf16[4,96,768]{2,1,0:T(8,128)(2,1)S(1)}, bf16[4,96,768]{2,1,0:T(8,128)(2,1)}, u32[]{:S(2)}, u32[]{:S(2)}) collective-permute-start(bf16[4,96,768]{2,1,0:T(8,128)(2,1)S(1)} %shard_map.89.refs_8_.refs_4_), channel_id=1, source_target_pairs={{0,24},{8,16},{16,8},{24,0},{1,25},{9,17},{17,9},{25,1},{2,26},{10... | collective-permute-start | bytes 1769480 | tf_op jit(solution)/shard_map/ppermute | solution.py:360
  217.6 15.2 %collective-permute-start.10 = (f32[256,512]{1,0:T(8,128)}, f32[256,512]{1,0:T(8,128)}, u32[]{:S(2)}, u32[]{:S(2)}) collective-permute-start(f32[256,512]{1,0:T(8,128)} %get-tuple-element.115), channel_id=1, source_target_pairs={{0,8},{8,0},{16,24},{24,16},{1,9},{9,1},{17,25},{25,17},{2,10},{10... | collective-permute-start | bytes 1572872 | tf_op jit(solution)/shard_map/ppermute | solution.py:360
  219.9 23.9 %collective-permute-start.11 = (f32[256,512]{1,0:T(8,128)}, f32[256,512]{1,0:T(8,128)}, u32[]{:S(2)}, u32[]{:S(2)}) collective-permute-start(f32[256,512]{1,0:T(8,128)} %get-tuple-element.114), channel_id=1, source_target_pairs={{0,16},{8,24},{16,0},{24,8},{1,17},{9,25},{17,1},{25,9},{2,18},{10... | collective-permute-start | bytes 1572872 | tf_op jit(solution)/shard_map/ppermute | solution.py:360
  222.2 21.6 %collective-permute-start.12 = (f32[256,512]{1,0:T(8,128)}, f32[256,512]{1,0:T(8,128)}, u32[]{:S(2)}, u32[]{:S(2)}) collective-permute-start(f32[256,512]{1,0:T(8,128)} %get-tuple-element.113), channel_id=1, source_target_pairs={{0,24},{8,16},{16,8},{24,0},{1,25},{9,17},{17,9},{25,1},{2,26},{10... | collective-permute-start | bytes 1572872 | tf_op jit(solution)/shard_map/ppermute | solution.py:360
  243.8 1.0 copy-start.4
  244.8 1.0 copy-start.8
  245.7 1.1 copy-start.13
  246.8 1.1 copy-start.16
  247.8 1.1 copy-start.19
  248.9 1.1 copy-start.22
  258.3 2.4 collective-permute-start.19
  262.4 27.7 %collective-permute-start.20 = (f32[4,96,128]{2,1,0:T(8,128)}, f32[4,96,128]{2,1,0:T(8,128)}, u32[]{:S(2)}, u32[]{:S(2)}) collective-permute-start(f32[4,96,128]{2,1,0:T(8,128)} %get-tuple-element.117), channel_id=1, source_target_pairs={{0,8},{8,0},{16,24},{24,16},{1,9},{9,1},{17,25},{25,17},{2,10},{10... | collective-permute-start | bytes 589832 | tf_op jit(solution)/shard_map/ppermute | solution.py:360
  263.1 27.1 %collective-permute-start.21 = (f32[4,96,128]{2,1,0:T(8,128)}, f32[4,96,128]{2,1,0:T(8,128)}, u32[]{:S(2)}, u32[]{:S(2)}) collective-permute-start(f32[4,96,128]{2,1,0:T(8,128)} %get-tuple-element.119), channel_id=1, source_target_pairs={{0,16},{8,24},{16,0},{24,8},{1,17},{9,25},{17,1},{25,9},{2,18},{10... | collective-permute-start | bytes 589832 | tf_op jit(solution)/shard_map/ppermute | solution.py:360
  264.8 1.0 copy-start.5
  265.8 1.0 copy-start.9
  266.7 1.1 copy-start.14
  267.8 1.1 copy-start.17
  268.9 1.1 copy-start.20
  269.9 1.1 copy-start.23
  271.0 1.1 copy-start.25
  279.0 103.4 %copy-start.26 = (bf16[4,96,768]{2,1,0:T(8,128)(2,1)S(1)}, bf16[4,96,768]{2,1,0:T(8,128)(2,1)}, u32[]{:S(2)}) copy-start(bf16[4,96,768]{2,1,0:T(8,128)(2,1)} %copy-done.24) | copy-start | bytes 1769476
  279.0 110.1 %collective-permute-start.27 = (bf16[8,64,1024]{2,1,0:T(8,128)(2,1)}, bf16[8,64,1024]{2,1,0:T(8,128)(2,1)}, u32[]{:S(2)}, u32[]{:S(2)}) collective-permute-start(bf16[8,64,1024]{2,1,0:T(8,128)(2,1)} %get-tuple-element.101), channel_id=1, source_target_pairs={{0,0},{4,16},{8,8},{12,24},{16,4},{20,20},{24,12},{28,28},{1,1},{5... | collective-permute-start | bytes 3145736 | tf_op jit(solution)/shard_map/ppermute | solution.py:504
  288.6 100.5 %collective-permute-start.28 = (bf16[8,64,1024]{2,1,0:T(8,128)(2,1)}, bf16[8,64,1024]{2,1,0:T(8,128)(2,1)}, u32[]{:S(2)}, u32[]{:S(2)}) collective-permute-start(bf16[8,64,1024]{2,1,0:T(8,128)(2,1)} %get-tuple-element.102), channel_id=1, source_target_pairs={{0,8},{4,24},{8,0},{12,16},{16,12},{20,28},{24,4},{28,20},{1,9},{5... | collective-permute-start | bytes 3145736 | tf_op jit(solution)/shard_map/ppermute | solution.py:504
  290.1 99.0 %collective-permute-start.29 = (bf16[8,64,1024]{2,1,0:T(8,128)(2,1)}, bf16[8,64,1024]{2,1,0:T(8,128)(2,1)}, u32[]{:S(2)}, u32[]{:S(2)}) collective-permute-start(bf16[8,64,1024]{2,1,0:T(8,128)(2,1)} %get-tuple-element.103), channel_id=1, source_target_pairs={{0,16},{4,0},{8,24},{12,8},{16,20},{20,4},{24,28},{28,12},{1,17},{... | collective-permute-start | bytes 3145736 | tf_op jit(solution)/shard_map/ppermute | solution.py:504
  290.1 99.0 %collective-permute-start.30 = (bf16[8,64,1024]{2,1,0:T(8,128)(2,1)}, bf16[8,64,1024]{2,1,0:T(8,128)(2,1)}, u32[]{:S(2)}, u32[]{:S(2)}) collective-permute-start(bf16[8,64,1024]{2,1,0:T(8,128)(2,1)} %get-tuple-element.104), channel_id=1, source_target_pairs={{0,24},{4,8},{8,16},{12,0},{16,28},{20,12},{24,20},{28,4},{1,25},{... | collective-permute-start | bytes 3145736 | tf_op jit(solution)/shard_map/ppermute | solution.py:504
  290.1 43.0 %collective-permute-start.22 = (f32[4,96,128]{2,1,0:T(8,128)S(1)}, f32[4,96,128]{2,1,0:T(8,128)S(1)}, u32[]{:S(2)}, u32[]{:S(2)}) collective-permute-start(f32[4,96,128]{2,1,0:T(8,128)S(1)} %get-tuple-element.118), channel_id=1, source_target_pairs={{0,24},{8,16},{16,8},{24,0},{1,25},{9,17},{17,9},{25,1},{2,26},{10... | collective-permute-start | bytes 589832 | tf_op jit(solution)/shard_map/ppermute | solution.py:360
  334.4 2.7 collective-permute-start.23
  342.0 44.7 %copy-start.29 = (f32[256,512]{1,0:T(8,128)S(1)}, f32[256,512]{1,0:T(8,128)}, u32[]{:S(2)}) copy-start(f32[256,512]{1,0:T(8,128)} %get-tuple-element.116.refs_0_) | copy-start | bytes 1572868
  342.0 44.7 %copy-start.32 = (bf16[384,256]{1,0:T(8,128)(2,1)S(1)}, bf16[384,256]{1,0:T(8,128)(2,1)}, u32[]{:S(2)}) copy-start(bf16[384,256]{1,0:T(8,128)(2,1)} %copy-done.31) | copy-start | bytes 589828
  342.0 5.1 %collective-permute-start.31 = (bf16[4,96,64]{2,1,0:T(8,128)(2,1)S(1)}, bf16[4,96,64]{2,1,0:T(8,128)(2,1)S(1)}, u32[]{:S(2)}, u32[]{:S(2)}) collective-permute-start(bf16[4,96,64]{2,1,0:T(8,128)(2,1)S(1)} %get-tuple-element.106), channel_id=1, source_target_pairs={{0,8},{8,0},{16,24},{24,16},{1,9},{9,1},{17,25},{25,17},{2,10},{10... | collective-permute-start | bytes 147464 | tf_op jit(solution)/shard_map/ppermute | solution.py:360
  347.1 4.6 %collective-permute-start.32 = (bf16[4,96,64]{2,1,0:T(8,128)(2,1)S(1)}, bf16[4,96,64]{2,1,0:T(8,128)(2,1)S(1)}, u32[]{:S(2)}, u32[]{:S(2)}) collective-permute-start(bf16[4,96,64]{2,1,0:T(8,128)(2,1)S(1)} %get-tuple-element.107), channel_id=1, source_target_pairs={{0,16},{8,24},{16,0},{24,8},{1,17},{9,25},{17,1},{25,9},{2,18},{10... | collective-permute-start | bytes 147464 | tf_op jit(solution)/shard_map/ppermute | solution.py:360
  351.7 5.5 %collective-permute-start.33 = (bf16[4,96,64]{2,1,0:T(8,128)(2,1)S(1)}, bf16[4,96,64]{2,1,0:T(8,128)(2,1)S(1)}, u32[]{:S(2)}, u32[]{:S(2)}) collective-permute-start(bf16[4,96,64]{2,1,0:T(8,128)(2,1)S(1)} %get-tuple-element.108), channel_id=1, source_target_pairs={{0,24},{8,16},{16,8},{24,0},{1,25},{9,17},{17,9},{25,1},{2,26},{10... | collective-permute-start | bytes 147464 | tf_op jit(solution)/shard_map/ppermute | solution.py:360
  357.2 14.6 %collective-permute-start.24 = (bf16[96,512]{1,0:T(8,128)(2,1)S(1)}, bf16[96,512]{1,0:T(8,128)(2,1)S(1)}, u32[]{:S(2)}, u32[]{:S(2)}) collective-permute-start(bf16[96,512]{1,0:T(8,128)(2,1)S(1)} %get-tuple-element.94), channel_id=1, source_target_pairs={{0,3},{1,0},{2,1},{3,2},{4,7},{5,4},{6,5},{7,6},{8,11},{9,8},{10,9... | collective-permute-start | bytes 294920 | tf_op jit(solution)/shard_map/ppermute | solution.py:363
  371.8 5.7 %collective-permute-start.25 = (bf16[96,512]{1,0:T(8,128)(2,1)}, bf16[96,512]{1,0:T(8,128)(2,1)S(1)}, u32[]{:S(2)}, u32[]{:S(2)}) collective-permute-start(bf16[96,512]{1,0:T(8,128)(2,1)} %get-tuple-element.95), channel_id=1, source_target_pairs={{0,2},{1,3},{2,0},{3,1},{4,6},{5,7},{6,4},{7,5},{8,10},{9,11},{10,... | collective-permute-start | bytes 294920 | tf_op jit(solution)/shard_map/ppermute | solution.py:363
  377.6 9.2 %collective-permute-start.26 = (bf16[96,512]{1,0:T(8,128)(2,1)}, bf16[96,512]{1,0:T(8,128)(2,1)S(1)}, u32[]{:S(2)}, u32[]{:S(2)}) collective-permute-start(bf16[96,512]{1,0:T(8,128)(2,1)} %copy-done.38), channel_id=1, source_target_pairs={{0,1},{1,2},{2,3},{3,0},{4,5},{5,6},{6,7},{7,4},{8,9},{9,10},{10,1... | collective-permute-start | bytes 294920 | tf_op jit(solution)/shard_map/ppermute | solution.py:363
  (11 other events, 8.5 us)

commit v4 on v3

--- a/solution.py
+++ b/solution.py
@@ -9,7 +9,7 @@
 
 CAPD = 12
 GROUP = 4
-CHUNKS = 1
+CHUNKS = 2
 
 adapter_scale = 0.5
 
@@ -96,17 +96,39 @@
     return lax.dot_general(lhs, rhs, (dims, ((), ())), preferred_element_type=F32)
 
 
-def call(kernel, out_shape, args, in_specs=None, **kwargs):
-    outs = [jax.ShapeDtypeStruct(shape, dtype) for shape, dtype in out_shape]
-    kwargs.setdefault("out_specs", [VMEM] * len(outs))
+def call(kernel, out_shape, fetched, plain=(), at=None, scratch=()):
+    nf, n_out = len(fetched), len(out_shape)
+    shapes = [v.shape[:-1] + (v.shape[-1] if w is None else w[1],) for v, w in fetched]
+
+    def body(*refs):
+        refs = list(refs)
+        head = [refs.pop(0)] if at is not None else []
+        sources, refs = refs[:nf], refs[nf:]
+        rest, buffers = refs[: len(plain) + n_out], refs[len(plain) + n_out :]
+        buffers, sems, extra = buffers[:nf], buffers[nf], buffers[nf + 1 :]
+        copies = []
+        for i, (source, (_, columns)) in enumerate(zip(sources, fetched)):
+            if columns is not None:
+                lead = (slice(None),) * (len(source.shape) - 1)
+                source = source.at[lead + (pl.ds(*columns),)]
+            copies.append(pltpu.make_async_copy(source, buffers[i], sems.at[i]))
+        for c in copies:
+            c.start()
+        for c in copies:
+            c.wait()
+        kernel(*head, *buffers, *rest, *extra)
+
     return pl.pallas_call(
-        kernel,
-        out_shape=outs,
-        in_specs=in_specs or [VMEM] * len(args),
+        body,
+        out_shape=[jax.ShapeDtypeStruct(shape, dtype) for shape, dtype in out_shape],
+        in_specs=[SMEM] * (at is not None) + [ANY] * nf + [VMEM] * len(plain),
+        out_specs=[VMEM] * n_out,
+        scratch_shapes=[pltpu.VMEM(shape, v.dtype) for shape, (v, _) in zip(shapes, fetched)]
+        + [pltpu.SemaphoreType.DMA((max(nf, 1),))]
+        + list(scratch),
         compiler_params=pltpu.CompilerParams(vmem_limit_bytes=48 << 20),
         cost_estimate=pl.CostEstimate(flops=1, bytes_accessed=1, transcendentals=0),
-        **kwargs,
-    )(*args)
+    )(*([at] if at is not None else []), *[v for v, _ in fetched], *plain)
 
 
 def slot_domain(count, lanes, gslots):
@@ -140,20 +162,6 @@
     return jnp.concatenate(parts, axis=0)
 
 
-def pack_kernel(at, down, weight, down_out, w_out, sems):
-    kt, rows = down_out.shape[2], w_out.shape[0]
-    copies = []
-    for d in range(down_out.shape[0]):
-        columns = pl.ds(pl.multiple_of(at[0] * kt, kt), kt)
-        copies.append((down.at[d, :, columns], down_out.at[d]))
-    copies.append((weight.at[pl.ds(pl.multiple_of(at[1] * rows, rows), rows), :], w_out))
-    copies = [pltpu.make_async_copy(*c, sems.at[i]) for i, c in enumerate(copies)]
-    for c in copies:
-        c.start()
-    for c in copies:
-        c.wait()
-
-
 def one_hot(dom, first, slots, ad, dom_total):
     rows = dom.shape[1]
     names = lax.broadcasted_iota(jnp.int32, (dom_total, rows), 0)
@@ -171,18 +179,18 @@
 def own_kernel(ad, slots, dom_total, at, dom, x, dy, hot_ref, *outs):
     hot = one_hot(dom[...], at[0], slots, ad, dom_total)
     hot_ref[...] = hot
-    width = x.shape[1]
+    moved_dy = dot(hot, dy[...], ((1,), (0,))).astype(BF16)
     moved = dot(hot, x[...], ((1,), (0,))).astype(BF16)
-    moved_dy = dot(hot, dy[...], ((1,), (0,))).astype(BF16)
     for ka in range(ad):
-        outs[ka][:, :width] = moved[ka * slots : (ka + 1) * slots]
-        outs[ka][:, width:] = moved_dy[ka * slots : (ka + 1) * slots]
+        outs[ka][...] = moved_dy[ka * slots : (ka + 1) * slots]
+        outs[ad + ka][...] = moved[ka * slots : (ka + 1) * slots]
 
 
 def others_kernel(fsdp, ad, slots, dom_total, at, *refs):
-    x_refs, outs = refs[: fsdp - 1], refs[fsdp - 1 :]
+    x_refs, outs, plain = refs[: fsdp - 1], refs[fsdp - 1 : -1], refs[-1]
     for kf in range(fsdp - 1):
         rows = x_refs[kf].shape[0] - 16
+        plain[kf] = x_refs[kf][:rows, :]
         dom = x_refs[kf][rows:, :rows].astype(F32).astype(jnp.int32)[:1]
         hot = one_hot(dom, at[0], slots, ad, dom_total)
         moved = dot(hot, x_refs[kf][:rows, :], ((1,), (0,))).astype(BF16)
@@ -212,28 +220,13 @@
         out[ka, :, width:] = (adapter_scale * (mine[ka] + got[ka])).astype(BF16)
 
 
-def hidden_kernel(fsdp, ad, gslots, start, last, at, *refs):
-    own_refs, x_refs, down, down_got = refs[:ad], refs[ad : 2 * ad], refs[2 * ad], refs[2 * ad + 1]
-    outs = refs[2 * ad + 2 : -2]
+def hidden_kernel(fsdp, ad, gslots, first, last, at, *refs):
+    own_refs, x_refs, held = refs[:ad], refs[ad : 2 * ad], refs[2 * ad]
+    outs = refs[2 * ad + 1 :]
     earlier = None
-    if start:
+    if not first:
         earlier, outs = outs[0], outs[1:]
-    held, sem = refs[-2:]
     cw = held.shape[2]
-
-    @pl.when(at[0] == 1)
-    def _():
-        columns = pl.ds(pl.multiple_of(at[1], 128), cw)
-        copy = pltpu.make_async_copy(down.at[:, :, columns], held, sem)
-        copy.start()
-        copy.wait()
-
-    @pl.when(at[0] != 1)
-    def _():
-        copy = pltpu.make_async_copy(down_got.at[:, :, pl.ds(start, cw)], held, sem)
-        copy.start()
-        copy.wait()
-
     for g in range(held.shape[0] // GROUP):
         weights = held[g * GROUP : (g + 1) * GROUP].reshape(-1, cw)
         rows = pl.ds(g * gslots, gslots)
@@ -248,7 +241,7 @@
                     outs[0][kf, ka, rows, :] = new
                 else:
                     n = new.shape[1] // 2
-                    second = at[2] == 1
+                    second = at[0] == 1
                     outs[0][kf, ka, rows, :] = jnp.where(second, new[:, n:], new[:, :n])
                     outs[1][kf, ka, rows, :] = jnp.where(second, new[:, :n], new[:, n:])
 
@@ -325,14 +318,14 @@
     out[...] = (total + dot(hot[...], delta, ((0,), (0,)))).astype(BF16)
 
 
-def base_kernel(fsdp, rows, at, *refs):
-    mine, other, weight, w_got, x_refs = refs[-2], refs[-1], refs[-4], refs[-3], refs[:-4]
-    kt = w_got.shape[0]
-    for k in range(fsdp):
-        x = x_refs[k][:rows, :]
-        own = weight[pl.ds(pl.multiple_of(at[0] * kt, kt), kt), :]
-        mine[k] = dot(x, own, ((1,), (0,)))
-        other[k] = dot(x, w_got[...], ((1,), (0,)))
+def base_kernel(fsdp, at, own, mine, got, weight, *outs):
+    kt = mine.shape[2]
+    outs[0][...] = dot(own[...], weight[...], ((1,), (0,)))
+    w_mine = weight[pl.ds(pl.multiple_of(at[0] * kt, kt), kt), :]
+    w_got = weight[pl.ds(pl.multiple_of((1 - at[0]) * kt, kt), kt), :]
+    for k in range(1, fsdp):
+        total = dot(mine[k - 1], w_mine, ((1,), (0,)))
+        outs[k][...] = total + dot(got[k - 1], w_got, ((1,), (0,)))
 
 
 def column_body(
@@ -379,94 +372,76 @@
             block = jnp.concatenate([block, dom_row], axis=0)
         x_in.append(block)
     x_in = lax.optimization_barrier(x_in)
-    x_in = [over_f(v, k) for k, v in enumerate(x_in)]
+    x_in[1], x_in[2] = over_f(x_in[1], 1), over_f(x_in[2], 2)
+    x_in[3] = over_f(x_in[3], 3)
 
     hot, *sends = call(
         functools.partial(own_kernel, ad, slots, ad * dloc),
-        [((ad * slots, rows), BF16)] + [((slots, kt + vloc), BF16)] * ad,
-        [numbers(a), domain.T, x_in[0], layer_output_gradient],
-        [SMEM] + [VMEM] * 3,
-    )
-    sends[-1] = after(sends[-1], x_in[1])
-    own = [over_a(v, ka) for ka, v in enumerate(sends)]
-
-    down_other, w_other = call(
-        pack_kernel,
-        [((dloc, rank, kt), BF16), ((kt, vloc), BF16)],
-        [
-            numbers(fx * 2 + 1 - t, 1 - t),
-            after(adapter_down_weight, *sends[:-1]),
-            value_weight_frozen,
-        ],
-        [SMEM, ANY, ANY],
-        out_specs=[ANY, ANY],
-        scratch_shapes=[pltpu.SemaphoreType.DMA((dloc + 1,))],
-    )
-
-    sends = call(
-        functools.partial(others_kernel, fsdp, ad, slots, ad * dloc),
-        [((fsdp - 1, slots, cw), BF16)] * (CHUNKS * ad),
-        [numbers(a), *lax.optimization_barrier((x_in[1:], own[1:]))[0]],
-        [SMEM] + [VMEM] * (fsdp - 1),
-    )
-    x_routed = [[over_a(v, ka) for ka, v in enumerate(sends[:ad])]]
-
-    own = after(own, *sends)
-
-    dy_specs = [pl.BlockSpec((slots, vloc), lambda i: (0, kt // vloc))] * ad
+        [((ad * slots, rows), BF16)]
+        + [((slots, vloc), BF16)] * ad
+        + [((slots, kt), BF16)] * ad,
+        [(v, None) for v in (domain.T, x_in[0], layer_output_gradient)],
+        at=numbers(a),
+    )
+    dy = [over_a(v, ka) for ka, v in enumerate(sends[:ad])]
+    own = [over_a(after(v, *dy), ka) for ka, v in enumerate(sends[ad:-1])]
+    own.append(over_a(after(sends[-1], *dy, x_in[1]), ad - 1))
+
     (back,) = call(
         functools.partial(back_kernel, ad, gslots),
         [((ad, slots, rank), F32)],
-        [*own, adapter_up_weight],
-        dy_specs + [pl.BlockSpec((dloc, rank, vloc), lambda i: (0, 0, 0))],
-        grid=(1,),
-    )
-    pairs = [(i * 2 + i // 2, i * 2 + 1 - i // 2) for i in range(fsdp)]
-    w_got = swap(after(w_other, back))
-    back_spec = pl.BlockSpec((ad, slots, rank), lambda i: (0, 0, 0))
+        [(v, None) for v in after(dy, x_in[1], x_in[2])] + [(adapter_up_weight, None)],
+    )
     (both,) = call(
         functools.partial(both_kernel, ad),
         [((ad, slots, vloc + rank), BF16)],
-        [back, swap(back), *own],
-        [back_spec] * 2 + dy_specs,
-        grid=(1,),
-    )
-    w_got = after(w_got, both)
-    both = [over_f(both, k) for k in range(fsdp)]
-    down_got = lax.ppermute(after(down_other, w_got), ("fsdp", "tp"), pairs)
+        [(back, None), (swap(back), None)] + [(v, None) for v in dy],
+    )
+
+    ready = after(x_in[1:], *own, both)
+    *sends, x_plain = call(
+        functools.partial(others_kernel, fsdp, ad, slots, ad * dloc),
+        [((fsdp - 1, slots, cw), BF16)] * (CHUNKS * ad) + [((fsdp - 1, rows, kt), BF16)],
+        [(v, None) for v in ready],
+        at=numbers(a),
+    )
+    x_routed = [[over_a(v, ka) for ka, v in enumerate(sends[:ad])]]
+
+    x_chip = lax.dynamic_slice_in_dim(input_rows, f * kf_width, kf_width, 1)
+    base = call(
+        functools.partial(base_kernel, fsdp),
+        [((rows, vloc), F32)] * fsdp,
+        [(v, None) for v in (x_chip, x_plain, swap(x_plain), value_weight_frozen)],
+        at=numbers(t),
+    )
+    base_plain = base[0]
+
+    both = [after(both, x_plain)] * fsdp
+    both[1], both[2] = over_f(both[1], 1), over_f(both[2], 2)
+    both[3] = over_f(after(both[3], base_plain), 3)
+    held = after(adapter_down_weight, x_plain)
+    down_other = lax.dynamic_slice_in_dim(held, (fx * 2 + 1 - t) * kt, kt, 2)
+    pairs = [(i * 2 + i // 2, i * 2 + 1 - i // 2) for i in range(fsdp)]
+    down_got = lax.ppermute(after(down_other, x_routed[0], both), ("fsdp", "tp"), pairs)
+
     for c in range(1, CHUNKS):
         chunk = [after(v, *x_routed[c - 1], *both) for v in sends[c * ad : (c + 1) * ad]]
         x_routed.append([over_a(v, ka) for ka, v in enumerate(chunk)])
 
-    mine, other = call(
-        functools.partial(base_kernel, fsdp, rows),
-        [((fsdp, rows, vloc), F32)] * 2,
-        [numbers(t), *x_in, value_weight_frozen, w_got],
-        [SMEM] + [VMEM] * (fsdp + 2),
-    )
-    base = mine + swap(after(other, down_got))
-    base = [over_f(base[k], k) for k in range(fsdp)]
-
-    def chunk_specs(c):
-        specs = [pl.BlockSpec((slots, cw), lambda i: (0, c))] * ad
-        return specs + [pl.BlockSpec((fsdp - 1, slots, cw), lambda i: (0, 0, 0))] * ad
+
+    down_mine = lax.dynamic_slice_in_dim(adapter_down_weight, (fx * 2 + t) * kt, kt, 2)
+    down = jnp.where(t == fy, down_mine, down_got)
+
+    def chunk_of(c, routed):
+        return [(v, (c * cw, cw)) for v in own] + [(v, None) for v in routed]
 
     def hidden(c, earlier, routed):
         last = c == CHUNKS - 1
         return call(
-            functools.partial(hidden_kernel, fsdp, ad, gslots, c * cw, last),
+            functools.partial(hidden_kernel, fsdp, ad, gslots, c == 0, last),
             [((fsdp, ad, slots, rank // 2 if last else rank), F32)] * (2 if last else 1),
-            [
-                numbers(t == fy, fx * kf_width + t * kt + c * cw, t),
-                *own,
-                *routed,
-                adapter_down_weight,
-                down_got,
-                *earlier,
-            ],
-            [SMEM] + chunk_specs(c) + [ANY, ANY] + [VMEM] * len(earlier),
-            grid=(1,),
-            scratch_shapes=[pltpu.VMEM((dloc, rank, cw), BF16), pltpu.SemaphoreType.DMA],
+            [*chunk_of(c, routed), (down, (c * cw, cw)), *[(v, None) for v in earlier]],
+            at=numbers(t),
         )
 
     grad_a = None
@@ -474,25 +449,21 @@
     for c in range(CHUNKS):
         last = c == CHUNKS - 1
         if last:
-            hid = hidden(c, hid, after(x_routed[c], *both, *base))
+            hid = hidden(c, hid, x_routed[c])
             hid = hid[0] + swap(hid[1])
+            hid = [over_f(hid[k], k) for k in range(fsdp)]
             hid, both = lax.optimization_barrier((hid, both))
         sums = call(
             functools.partial(down_grad_kernel, fsdp, ad, gslots),
             [((dloc, rloc, cw), BF16)] * fsdp,
-            [
-                numbers(*[(t ^ (r // 2)) * 2 + (fx ^ (r % 2)) for r in range(fsdp)]),
-                *own,
-                *x_routed[c],
-                *both,
-            ],
-            [SMEM]
-            + chunk_specs(c)
-            + [pl.BlockSpec((ad, slots, rank), lambda i: (0, 0, vloc // rank))] * fsdp,
-            grid=(1,),
-            scratch_shapes=[pltpu.VMEM((GROUP * rank, cw), F32)],
+            [*chunk_of(c, x_routed[c]), *[(v, (vloc, rank)) for v in both]],
+            at=numbers(*[(t ^ (r // 2)) * 2 + (fx ^ (r % 2)) for r in range(fsdp)]),
+            scratch=[pltpu.VMEM((GROUP * rank, cw), F32)],
         )
         got = []
+        if not last:
+            hid = hidden(c, hid, after(x_routed[c], *sums))
+            sums = [*sums[:2], *after(sums[2:], hid)]
         for r in range(fsdp):
             p, q = r % 2, r // 2
             perm = [
@@ -503,33 +474,36 @@
             ]
             got.append(lax.ppermute(sums[r], ("fsdp", "tp"), perm))
         if not last:
-            hid = hidden(c, hid, after(x_routed[c], *sums))
-            x_routed[c + 1] = after(x_routed[c + 1], *got[:2])
+            x_routed[c + 1] = after(x_routed[c + 1], *got)
+            base = [over_f(after(v, *got), k) for k, v in enumerate(base)]
         at = [
             ((fx ^ (r % 2)) * kf_width + (fy ^ (r // 2)) * kt + c * cw) // cw
             for r in range(fsdp)
         ]
-        args = got if grad_a is None else [*got, grad_a]
-        grad_a = pl.pallas_call(
-            functools.partial(place_kernel, fsdp),
-            out_shape=jax.ShapeDtypeStruct((dloc, rloc, half), F32),
-            grid_spec=pltpu.PrefetchScalarGridSpec(
-                num_scalar_prefetch=1,
-                grid=(fsdp,),
-                in_specs=[VMEM] * fsdp + [ANY] * (len(args) - fsdp),
-                out_specs=pl.BlockSpec((dloc, rloc, cw), lambda i, at: (0, 0, at[i])),
-            ),
-            input_output_aliases={} if grad_a is None else {fsdp + 1: 0},
-            cost_estimate=pl.CostEstimate(flops=1, bytes_accessed=1, transcendentals=0),
-        )(numbers(*at), *args)
-
-    hid = [over_f(hid[k], k) for k in range(fsdp)]
+        if c == 0:
+            grad_a = pl.pallas_call(
+                functools.partial(place_kernel, fsdp),
+                out_shape=jax.ShapeDtypeStruct((dloc, rloc, half), F32),
+                grid_spec=pltpu.PrefetchScalarGridSpec(
+                    num_scalar_prefetch=1,
+                    grid=(fsdp,),
+                    in_specs=[VMEM] * fsdp,
+                    out_specs=pl.BlockSpec((dloc, rloc, cw), lambda i, at: (0, 0, at[i])),
+                ),
+                cost_estimate=pl.CostEstimate(flops=1, bytes_accessed=1, transcendentals=0),
+            )(numbers(*at), *got)
+        else:
+            for v, column in zip(got, at):
+                grad_a = lax.dynamic_update_slice_in_dim(
+                    grad_a, v.astype(F32), column * cw, 2
+                )
+
     hid_own = (hid[0] + hid[1] + hid[2] + hid[3]).astype(BF16)
     outs = call(
         functools.partial(delta_kernel, fsdp, ad, gslots),
         [((slots, vloc), BF16)] * ad + [((ad, slots, rloc), BF16)] * fsdp,
-        [numbers(t, *[f ^ k for k in range(fsdp)]), hid_own, swap(hid_own), adapter_up_weight],
-        [SMEM] + [VMEM] * 3,
+        [(v, None) for v in (hid_own, swap(hid_own), adapter_up_weight)],
+        at=numbers(t, *[f ^ k for k in range(fsdp)]),
     )
     returned = [over_a(v, (ad - ka) % ad) for ka, v in enumerate(outs[:ad])]
     hid_cols = [over_f(v, k) for k, v in enumerate(outs[ad:])]
@@ -537,15 +511,12 @@
     (y_out,) = call(
         functools.partial(output_kernel, fsdp, ad),
         [((rows, vloc), BF16)],
-        [*base, hot, *returned],
+        [(v, None) for v in (*base, hot, *returned)],
     )
     (grad_b,) = call(
         functools.partial(up_grad_kernel, fsdp, ad, gslots),
         [((dloc, rloc, vloc), F32)],
-        [*hid_cols, *both],
-        [pl.BlockSpec((ad, slots, rloc), lambda i: (0, 0, 0))] * fsdp
-        + [pl.BlockSpec((ad, slots, vloc), lambda i: (0, 0, 0))] * fsdp,
-        grid=(1,),
+        [(v, None) for v in hid_cols] + [(v, (0, vloc)) for v in both],
     )
     return y_out, grad_a, grad_b
 

time: 397 us -> 231 us (0.58)
  Pallas kernels: 169 us -> 45.8 us
  waiting for transfers between devices: 123 us -> 74.2 us
  other arithmetic: 4.37 us -> 16 us
  local copies, waits for them, and re-layouts: 29.5 us -> 25.4 us
    pallas_call x11 -> x12, Pallas kernels: 163 us -> 41 us  [call(): pl.pallas_call(body, out_shape=[jax.ShapeDtypeStruct(shape, dtype) for sh...]
    ppermute x15, waiting for transfers between devices: 79.6 us -> 27 us  [over_f(): lax.ppermute(v, 'fsdp', [(i, i ^ k) for i in range(fsdp)])]
    ppermute x4 -> x8, waiting for transfers between devices: 0.01 us -> 8.83 us  [column_body(): got.append(lax.ppermute(sums[r], ('fsdp', 'tp'), perm))]
    unnamed x82 -> x80, local copies, waits for them, and re-layouts: 25.5 us -> 17.5 us
    select_n x0 -> x1, other arithmetic: none -> 6.5 us  [column_body(): down = jnp.where(t == fy, down_mine, down_got)]
    dynamic_update_slice x0 -> x4, other arithmetic: none -> 6.49 us  [column_body(): lax.dynamic_update_slice_in_dim(grad_a, v.astype(F32), column * cw, 2)]
    dynamic_slice x0 -> x2, local copies, waits for them, and re-layouts: none -> 5.97 us  [the longest x1 4.64 us: column_body(): down_other = lax.dynamic_slice_in_dim(held, (fx * 2 + 1 - t) * kt, kt, 2)]
    ppermute x9 -> x15, waiting for transfers between devices: 36.8 us -> 34.8 us  [over_a(): lax.ppermute(v, 'ad', [(i, (i + k) % ad) for i in range(ad)])]
  transfers between devices with their start and end apart: 34 -> 43, of which waited for: 15 -> 20; matrix products, arithmetic and copies ran while one was open for 1% -> 8% of each run, Pallas kernels for 38% -> 16%
where the time goes in v4:
time: 231 us; the launch traced here: 230 us
  waiting for transfers between devices  74.2 us (32%)
  starting transfers between devices  67.3 us (29%)
  Pallas kernels  45.8 us (20%)
  local copies, waits for them, and re-layouts  25.4 us (11%)
  other arithmetic  16 us (7%)
    pallas_call x12, Pallas kernels, call(): pl.pallas_call(body, out_shape=[jax.ShapeDtypeStruct(shape, dtype) for sh...  41 us
    ppermute x15, waiting for transfers between devices, over_a(): lax.ppermute(v, 'ad', [(i, (i + k) % ad) for i in range(ad)])  34.8 us
    ppermute x15, starting transfers between devices, over_a(): lax.ppermute(v, 'ad', [(i, (i + k) % ad) for i in range(ad)])  30.1 us
    ppermute x15, waiting for transfers between devices, over_f(): lax.ppermute(v, 'fsdp', [(i, i ^ k) for i in range(fsdp)])  27 us
    ppermute x15, starting transfers between devices, over_f(): lax.ppermute(v, 'fsdp', [(i, i ^ k) for i in range(fsdp)])  20.9 us
    unnamed x80, local copies, waits for them, and re-layouts  17.5 us
    ppermute x8, starting transfers between devices, column_body(): got.append(lax.ppermute(sums[r], ('fsdp', 'tp'), perm))  12.8 us
    ppermute x8, waiting for transfers between devices, column_body(): got.append(lax.ppermute(sums[r], ('fsdp', 'tp'), perm))  8.83 us
  transfers between devices with their start and end apart: 43, of which 20 were waited for; matrix products, arithmetic and copies ran while one was open for 8% of the time, Pallas kernels for 16%

profile of v4, /device:TPU:0, one launch (start us, length us, event | category | flops | bytes accessed | tf_op | source)
XLA Modules:
  0.0 229.7 jit_solution(5268998674971497681)
XLA Ops:
  1.5 1.7 constant_dynamic-slice_fusion.1
  3.2 1.3 fusion.3
  4.5 2.9 %collective-permute-start = (bf16[272,1024]{1,0:T(8,128)(2,1)}, bf16[272,1024]{1,0:T(8,128)(2,1)S(1)}, u32[]{:S(2)}, u32[]{:S(2)}) collective-permute-start(bf16[272,1024]{1,0:T(8,128)(2,1)} %get-tuple-element.88), channel_id=1, source_target_pairs={{0,8},{8,0},{16,24},{24,16},{1,9},{9,1},{17,25},{25,17},{2,10},{10... | collective-permute-start | bytes 1671176 | tf_op jit(solution)/shard_map/ppermute | solution.py:353
  7.4 1.5 collective-permute-start.1
  11.3 1.6 collective-permute-start.3
  13.4 2.6 %collective-permute-start.4 = (bf16[96,512]{1,0:T(8,128)(2,1)S(1)}, bf16[96,512]{1,0:T(8,128)(2,1)S(1)}, u32[]{:S(2)}, u32[]{:S(2)}) collective-permute-start(bf16[96,512]{1,0:T(8,128)(2,1)S(1)} %get-tuple-element.95), channel_id=1, source_target_pairs={{0,2},{1,3},{2,0},{3,1},{4,6},{5,7},{6,4},{7,5},{8,10},{9,11},{10,... | collective-permute-start | bytes 294920 | tf_op jit(solution)/shard_map/ppermute | solution.py:356
  16.0 2.8 %collective-permute-done.3.refs_1_.refs_3_ = bf16[96,512]{1,0:T(8,128)(2,1)S(1)} collective-permute-done((bf16[96,512]{1,0:T(8,128)(2,1)S(1)}, bf16[96,512]{1,0:T(8,128)(2,1)S(1)}, u32[]{:S(2)}, u32[]{:S(2)}) %collective-permute-start.3) | collective-permute-done | bytes 98336 | tf_op jit(solution)/shard_map/ppermute | solution.py:356
  18.8 1.1 collective-permute-start.5
  20.0 2.0 collective-permute-done.4.refs_2_.refs_4_
  21.9 1.5 collective-permute-done.5.refs_3_.refs_5_
  23.4 10.3 %collective-permute-done.1.refs_2_ = bf16[272,1024]{1,0:T(8,128)(2,1)} collective-permute-done((bf16[272,1024]{1,0:T(8,128)(2,1)}, bf16[272,1024]{1,0:T(8,128)(2,1)}, u32[]{:S(2)}, u32[]{:S(2)}) %collective-permute-start.1) | collective-permute-done | bytes 557088 | tf_op jit(solution)/shard_map/ppermute | solution.py:353
  33.8 1.5 shard_map.86.refs_0_
  35.4 1.6 collective-permute-start.6
  37.0 2.6 %collective-permute-start.7 = (bf16[96,1024]{1,0:T(8,128)(2,1)S(1)}, bf16[96,1024]{1,0:T(8,128)(2,1)S(1)}, u32[]{:S(2)}, u32[]{:S(2)}) collective-permute-start(bf16[96,1024]{1,0:T(8,128)(2,1)S(1)} %get-tuple-element.101), channel_id=1, source_target_pairs={{0,2},{1,3},{2,0},{3,1},{4,6},{5,7},{6,4},{7,5},{8,10},{9,11},{10,... | collective-permute-start | bytes 589832 | tf_op jit(solution)/shard_map/ppermute | solution.py:356
  39.6 1.3 collective-permute-start.8
  42.0 3.1 %collective-permute-done.6.refs_2_ = bf16[96,1024]{1,0:T(8,128)(2,1)S(1)} collective-permute-done((bf16[96,1024]{1,0:T(8,128)(2,1)S(1)}, bf16[96,1024]{1,0:T(8,128)(2,1)S(1)}, u32[]{:S(2)}, u32[]{:S(2)}) %collective-permute-start.6) | collective-permute-done | bytes 196640 | tf_op jit(solution)/shard_map/ppermute | solution.py:356
  45.1 8.0 %collective-permute-done.7.refs_3_ = bf16[96,1024]{1,0:T(8,128)(2,1)S(1)} collective-permute-done((bf16[96,1024]{1,0:T(8,128)(2,1)S(1)}, bf16[96,1024]{1,0:T(8,128)(2,1)S(1)}, u32[]{:S(2)}, u32[]{:S(2)}) %collective-permute-start.7) | collective-permute-done | bytes 196640 | tf_op jit(solution)/shard_map/ppermute | solution.py:356
  53.1 1.1 copy-done.15
  54.2 3.7 %shard_map.88 = (bf16[3,96,512]{2,1,0:T(8,128)(2,1)S(1)}, bf16[3,96,512]{2,1,0:T(8,128)(2,1)S(1)}, bf16[3,96,512]{2,1,0:T(8,128)(2,1)}, bf16[3,96,512]{2,1,0:T(8...) custom-call(s32[1]{0:T(128)} %bitcast.1.refs_0_, ...), custom_call_target="tpu_custom_call" | custom-call | flops 1 | bytes 1 | tf_op jit(solution)/shard_map/pallas_call | solution.py:121
  61.7 1.3 constant_dynamic-slice_fusion.5.refs_1_
  63.0 1.6 collective-permute-start.15
  65.1 4.7 %collective-permute-start.11 = (bf16[3,96,512]{2,1,0:T(8,128)(2,1)}, bf16[3,96,512]{2,1,0:T(8,128)(2,1)S(1)}, u32[]{:S(2)}, u32[]{:S(2)}) collective-permute-start(bf16[3,96,512]{2,1,0:T(8,128)(2,1)} %copy-done.33), channel_id=1, source_target_pairs={{0,1},{1,2},{2,3},{3,0},{4,5},{5,6},{6,7},{7,4},{8,9},{9,10},{10,1... | collective-permute-start | bytes 884744 | tf_op jit(solution)/shard_map/ppermute | solution.py:356
  69.8 5.8 %shard_map.89 = (f32[256,512]{1,0:T(8,128)S(1)}, f32[256,512]{1,0:T(8,128)}, f32[256,512]{1,0:T(8,128)}, f32[256,512]{1,0:T(8,128)}) custom-call(s32[1]{0:T(128)} %bitcast.refs_0_, bf16[256,2048]{1,0:T(8,128)(2,1)S(1)} %constant_dynamic-slice_fusion.5.refs_1_, bf16[3,256,1024]{2,1,0:T(8,128)(2,1)} %get-tuple-element.111.refs_2_, ...), custom_call_target="tpu_custom_call" | custom-call | flops 1 | bytes 1 | tf_op jit(solution)/shard_map/pallas_call | solution.py:121
  76.4 1.4 collective-permute-start.16
  77.8 1.6 collective-permute-start.12
  80.1 1.0 collective-permute-start.13
  81.2 4.6 %constant_dynamic-slice_fusion = bf16[8,256,1024]{2,1,0:T(8,128)(2,1)} fusion(bf16[8,256,4096]{2,1,0:T(8,128)(2,1)} %param.8, s32[]{:T(128)S(6)} %select_n.85), kind=kLoop, calls=%fused_computation.15 | loop fusion | bytes 8388612 | tf_op jit(solution)/shard_map/dynamic_slice | solution.py:423
  85.8 8.2 %collective-permute-done.12.refs_7_ = bf16[3,96,512]{2,1,0:T(8,128)(2,1)} collective-permute-done((bf16[3,96,512]{2,1,0:T(8,128)(2,1)}, bf16[3,96,512]{2,1,0:T(8,128)(2,1)}, u32[]{:S(2)}, u32[]{:S(2)}) %collective-permute-start.12) | collective-permute-done | bytes 294944 | tf_op jit(solution)/shard_map/ppermute | solution.py:356
  94.4 3.3 %collective-permute-start.19 = (bf16[8,256,1024]{2,1,0:T(8,128)(2,1)}, bf16[8,256,1024]{2,1,0:T(8,128)(2,1)}, u32[]{:S(2)}, u32[]{:S(2)}) collective-permute-start(bf16[8,256,1024]{2,1,0:T(8,128)(2,1)} %constant_dynamic-slice_fusion), channel_id=1, source_target_pairs={{0,4},{8,12},{20,16},{28,24},{1,5},{9,13},{21,17},{29,25},{2,6},{1... | collective-permute-start | bytes 12582920 | tf_op jit(solution)/shard_map/ppermute | solution.py:425
  97.9 6.5 %collective-permute-start.25 = (bf16[3,96,512]{2,1,0:T(8,128)(2,1)}, bf16[3,96,512]{2,1,0:T(8,128)(2,1)S(1)}, u32[]{:S(2)}, u32[]{:S(2)}) collective-permute-start(bf16[3,96,512]{2,1,0:T(8,128)(2,1)} %copy-done.32), channel_id=1, source_target_pairs={{0,1},{1,2},{2,3},{3,0},{4,5},{5,6},{6,7},{7,4},{8,9},{9,10},{10,1... | collective-permute-start | bytes 884744 | tf_op jit(solution)/shard_map/ppermute | solution.py:356
  104.3 1.5 collective-permute-start.26
  110.5 4.3 %shard_map.90 = (bf16[8,64,512]{2,1,0:T(8,128)(2,1)S(1)}, bf16[8,64,512]{2,1,0:T(8,128)(2,1)S(1)}, bf16[8,64,512]{2,1,0:T(8,128)(2,1)S(1)}, bf16[8,64,512]{2,1,0:T(8,128)(2,1)S(1)}) custom-call(s32[4]{0:T(128)S(1)} %pad_add_fusion.refs_0_, bf16[96,1024]{1,0:T(8,128)(2,1)S(1)} %get-tuple-element.97.refs_1_, bf16[96,1024]{1,0:T(8,128)(2,1)S(1)} %copy-done.2, ...), custom_call_target="tpu_custom_call" | custom-call | flops 1 | bytes 1 | tf_op jit(solution)/shard_map/pallas_call | solution.py:121
  115.7 1.7 collective-permute-start.18
  117.4 6.5 %dynamic-slice_select_fusion.refs_9_ = bf16[8,256,1024]{2,1,0:T(8,128)(2,1)} fusion(bf16[8,256,1024]{2,1,0:T(8,128)(2,1)} %collective-permute-done.19, bf16[8,256,4096]{2,1,0:T(8,128)(2,1)} %param.8, s32[]{:T(128)S(6)} %select_n.84, pred[]{:T(512)S(6)} %eq.5), kind=kLoop, calls=%fused_computation | loop fusion | flops 2097152 | bytes 12582917 | tf_op jit(solution)/shard_map/jit(_where)/select_n | solution.py:433
  123.9 4.9 %shard_map.91.refs_10_ = f32[4,4,96,256]{3,2,1,0:T(8,128)S(1)} custom-call(s32[1]{0:T(128)} %bitcast.refs_0_, bf16[96,1024]{1,0:T(8,128)(2,1)S(1)} %get-tuple-element.97.refs_1_, bf16[96,1024]{1,0:T(8,128)(2,1)S(1)} %copy-done.3, bf16[96,1024]{1,0:T(8,128)(2,1)S(1)} %copy-done.5, bf16[96,1024]{1,0:T(8,128)(2,1)S(1)} %copy-done.7, ...), custom_call_target="tpu_custom_call" | custom-call | flops 1 | bytes 1 | tf_op jit(solution)/shard_map/pallas_call | solution.py:121
  128.8 2.0 collective-permute-start.20
  132.2 8.7 %collective-permute-done.27.refs_8_ = bf16[3,96,512]{2,1,0:T(8,128)(2,1)S(1)} collective-permute-done((bf16[3,96,512]{2,1,0:T(8,128)(2,1)S(1)}, bf16[3,96,512]{2,1,0:T(8,128)(2,1)S(1)}, u32[]{:S(2)}, u32[]{:S(2)}) %collective-permute-start.27) | collective-permute-done | bytes 294944 | tf_op jit(solution)/shard_map/ppermute | solution.py:356
  140.9 1.1 collective-permute-done.20.refs_2_
  142.8 2.3 collective-permute-done.21.refs_3_
  145.1 4.8 %shard_map.92 = (f32[4,4,96,128]{3,2,1,0:T(8,128)S(1)}, f32[4,4,96,128]{3,2,1,0:T(8,128)S(1)}) custom-call(s32[1]{0:T(128)} %bitcast.refs_0_, bf16[96,1024]{1,0:T(8,128)(2,1)S(1)} %get-tuple-element.97.refs_1_, bf16[96,1024]{1,0:T(8,128)(2,1)S(1)} %copy-done.3, bf16[96,1024]{1,0:T(8,128)(2,1)S(1)} %copy-done.5, bf16[96,1024]{1,0:T(8,128)(2,1)S(1)} %copy-done.7, ...), custom_call_target="tpu_custom_call" | custom-call | flops 1 | bytes 1 | tf_op jit(solution)/shard_map/pallas_call | solution.py:121
  150.0 2.3 collective-permute-done.28
  152.5 2.1 collective-permute-start.31
  157.0 1.6 collective-permute-start.23
  158.6 2.6 %collective-permute-done.31 = f32[4,96,128]{2,1,0:T(8,128)S(1)} collective-permute-done((f32[4,96,128]{2,1,0:T(8,128)S(1)}, f32[4,96,128]{2,1,0:T(8,128)S(1)}, u32[]{:S(2)}, u32[]{:S(2)}) %collective-permute-start.31) | collective-permute-done | bytes 196640 | tf_op jit(solution)/shard_map/ppermute | solution.py:353
  161.2 2.0 collective-permute-start.24
  163.2 1.4 collective-permute-done.30
  165.5 5.2 %shard_map.96 = (bf16[8,64,512]{2,1,0:T(8,128)(2,1)}, bf16[8,64,512]{2,1,0:T(8,128)(2,1)}, bf16[8,64,512]{2,1,0:T(8,128)(2,1)S(1)}, bf16[8,64,512]{2,1,0:T(8,128)(2,1)S(1)}) custom-call(s32[4]{0:T(128)S(1)} %pad_add_fusion.refs_0_, bf16[96,1024]{1,0:T(8,128)(2,1)S(1)} %get-tuple-element.97.refs_1_, bf16[96,1024]{1,0:T(8,128)(2,1)S(1)} %copy-done.3, ...), custom_call_target="tpu_custom_call" | custom-call | flops 1 | bytes 1 | tf_op jit(solution)/shard_map/pallas_call | solution.py:121
  170.7 5.4 %collective-permute-start.36 = (bf16[8,64,512]{2,1,0:T(8,128)(2,1)}, bf16[8,64,512]{2,1,0:T(8,128)(2,1)}, u32[]{:S(2)}, u32[]{:S(2)}) collective-permute-start(bf16[8,64,512]{2,1,0:T(8,128)(2,1)} %get-tuple-element.165), channel_id=1, source_target_pairs={{0,0},{4,16},{8,8},{12,24},{16,4},{20,20},{24,12},{28,28},{1,1},{5... | collective-permute-start | bytes 1572872 | tf_op jit(solution)/shard_map/ppermute | solution.py:475
  176.2 1.3 collective-permute-done.32.refs_2_
  178.2 1.0 collective-permute-start.37
  180.2 2.7 %shard_map.93 = (bf16[96,512]{1,0:T(8,128)(2,1)S(1)}, bf16[96,512]{1,0:T(8,128)(2,1)S(1)}, bf16[96,512]{1,0:T(8,128)(2,1)S(1)}, bf16[96,512]{1,0:T(8,128)(2,1)S(...) custom-call(s32[5]{0:T(128)S(1)} %stack.71.refs_0_, ...), custom_call_target="tpu_custom_call" | custom-call | flops 1 | bytes 1 | tf_op jit(solution)/shard_map/pallas_call | solution.py:121
  186.4 1.2 collective-permute-start.41
  188.1 2.1 collective-permute-start.42
  190.1 11.3 %collective-permute-done.40.refs_1_ = bf16[4,96,64]{2,1,0:T(8,128)(2,1)S(1)} collective-permute-done((bf16[4,96,64]{2,1,0:T(8,128)(2,1)}, bf16[4,96,64]{2,1,0:T(8,128)(2,1)S(1)}, u32[]{:S(2)}, u32[]{:S(2)}) %collective-permute-start.40) | collective-permute-done | bytes 49184 | tf_op jit(solution)/shard_map/ppermute | solution.py:353
  202.9 1.6 collective-permute-start.35
  205.2 4.8 %shard_map.95 = f32[8,64,4096]{2,1,0:T(8,128)} custom-call(s32[4]{0:T(128)} %pad_add_fusion.1.at, bf16[8,64,512]{2,1,0:T(8,128)(2,1)} %copy-done.37, bf16[8,64,512]{2,1,0:T(8,128)(2,1)} %copy-done.38, bf16[8,64,512]{2,1,0:T(8,128)(2,1)} %copy-done.39, bf16[8,64,512]{2,1,0:T(8,128)(2,1)} %collective-permute-done.21.refs_3_), custom_call_target="tpu_custom_call" | custom-call | flops 1 | bytes 1 | tf_op jit(solution)/shard_map/pallas_call | solution.py:484
  210.0 4.0 %shard_map.97 = f32[8,64,512]{2,1,0:T(8,128)} custom-call(bf16[4,96,64]{2,1,0:T(8,128)(2,1)S(1)} %copy-done.24, bf16[4,96,64]{2,1,0:T(8,128)(2,1)S(1)} %collective-permute-done.40.refs_1_, bf16[4,96,64]{2,1,0:T(8,128)(2,1)S(1)} %collective-permute-done.41.refs_2_, bf16[4,96,64]{2,1,0:T(8,128)(2,1)S(1)} %collective-permute-done.42.refs_3_, ...), custom_call_target="tpu_custom_call" | custom-call | flops 1 | bytes 1 | tf_op jit(solution)/shard_map/pallas_call | solution.py:121
  215.2 2.5 %shard_map.94 = bf16[256,512]{1,0:T(8,128)(2,1)} custom-call(f32[256,512]{1,0:T(8,128)S(1)} %copy-done.17, f32[256,512]{1,0:T(8,128)} %collective-permute-done.22.refs_1_, f32[256,512]{1,0:T(8,128)} %collective-permute-done.23.refs_2_, f32[256,512]{1,0:T(8,128)} %collective-permute-done.24.refs_3_, bf16[384,256]{1,0:T(8,128)(2,1)S(1)} %copy-done.20, ...), custom_call_target="tpu_custom_call" | custom-call | flops 1 | bytes 1 | tf_op jit(solution)/shard_map/pallas_call | solution.py:121
  217.7 2.1 convert_dynamic-update-slice_fusion.3
  219.9 2.1 convert_dynamic-update-slice_fusion.2
  222.0 4.1 %collective-permute-done.38 = bf16[8,64,512]{2,1,0:T(8,128)(2,1)S(1)} collective-permute-done((bf16[8,64,512]{2,1,0:T(8,128)(2,1)}, bf16[8,64,512]{2,1,0:T(8,128)(2,1)S(1)}, u32[]{:S(2)}, u32[]{:S(2)}) %collective-permute-start.38) | collective-permute-done | bytes 524320 | tf_op jit(solution)/shard_map/ppermute | solution.py:475
  226.1 1.1 convert_dynamic-update-slice_fusion.1
  227.2 1.3 collective-permute-done.39
  228.6 1.1 convert_dynamic-update-slice_fusion
  (131 shorter events, 31.5 us)
Async XLA Ops:
  0.6 8.3 %copy-start.25 = (s32[256,1]{0,1:T(1,128)S(1)}, s32[256,1]{0,1:T(1,128)}, u32[]{:S(2)}) copy-start(s32[256,1]{0,1:T(1,128)} %param.11) | copy-start | bytes 3076
  0.6 33.1 %copy-start = (bf16[8,256,512]{2,1,0:T(8,128)(2,1)S(1)}, bf16[8,256,512]{2,1,0:T(8,128)(2,1)}, u32[]{:S(2)}) copy-start(bf16[8,256,512]{2,1,0:T(8,128)(2,1)} %refs_3_.3) | copy-start | bytes 6291460
  4.5 18.9 %collective-permute-start = (bf16[272,1024]{1,0:T(8,128)(2,1)}, bf16[272,1024]{1,0:T(8,128)(2,1)S(1)}, u32[]{:S(2)}, u32[]{:S(2)}) collective-permute-start(bf16[272,1024]{1,0:T(8,128)(2,1)} %get-tuple-element.88), channel_id=1, source_target_pairs={{0,8},{8,0},{16,24},{24,16},{1,9},{9,1},{17,25},{25,17},{2,10},{10... | collective-permute-start | bytes 1671176 | tf_op jit(solution)/shard_map/ppermute | solution.py:353
  7.4 26.3 %collective-permute-start.1 = (bf16[272,1024]{1,0:T(8,128)(2,1)}, bf16[272,1024]{1,0:T(8,128)(2,1)}, u32[]{:S(2)}, u32[]{:S(2)}) collective-permute-start(bf16[272,1024]{1,0:T(8,128)(2,1)} %get-tuple-element.89), channel_id=1, source_target_pairs={{0,16},{8,24},{16,0},{24,8},{1,17},{9,25},{17,1},{25,9},{2,18},{10... | collective-permute-start | bytes 1671176 | tf_op jit(solution)/shard_map/ppermute | solution.py:353
  9.0 1.0 copy-start.18
  11.3 7.5 %collective-permute-start.3 = (bf16[96,512]{1,0:T(8,128)(2,1)S(1)}, bf16[96,512]{1,0:T(8,128)(2,1)S(1)}, u32[]{:S(2)}, u32[]{:S(2)}) collective-permute-start(bf16[96,512]{1,0:T(8,128)(2,1)S(1)} %get-tuple-element.94), channel_id=1, source_target_pairs={{0,1},{1,2},{2,3},{3,0},{4,5},{5,6},{6,7},{7,4},{8,9},{9,10},{10,1... | collective-permute-start | bytes 294920 | tf_op jit(solution)/shard_map/ppermute | solution.py:356
  12.9 40.2 %collective-permute-start.2 = (bf16[272,1024]{1,0:T(8,128)(2,1)}, bf16[272,1024]{1,0:T(8,128)(2,1)S(1)}, u32[]{:S(2)}, u32[]{:S(2)}) collective-permute-start(bf16[272,1024]{1,0:T(8,128)(2,1)} %get-tuple-element.90), channel_id=1, source_target_pairs={{0,24},{8,16},{16,8},{24,0},{1,25},{9,17},{17,9},{25,1},{2,26},{10... | collective-permute-start | bytes 1671176 | tf_op jit(solution)/shard_map/ppermute | solution.py:353
  13.4 8.5 %collective-permute-start.4 = (bf16[96,512]{1,0:T(8,128)(2,1)S(1)}, bf16[96,512]{1,0:T(8,128)(2,1)S(1)}, u32[]{:S(2)}, u32[]{:S(2)}) collective-permute-start(bf16[96,512]{1,0:T(8,128)(2,1)S(1)} %get-tuple-element.95), channel_id=1, source_target_pairs={{0,2},{1,3},{2,0},{3,1},{4,6},{5,7},{6,4},{7,5},{8,10},{9,11},{10,... | collective-permute-start | bytes 294920 | tf_op jit(solution)/shard_map/ppermute | solution.py:356
  18.8 4.6 %collective-permute-start.5 = (bf16[96,512]{1,0:T(8,128)(2,1)S(1)}, bf16[96,512]{1,0:T(8,128)(2,1)S(1)}, u32[]{:S(2)}, u32[]{:S(2)}) collective-permute-start(bf16[96,512]{1,0:T(8,128)(2,1)S(1)} %get-tuple-element.96), channel_id=1, source_target_pairs={{0,3},{1,0},{2,1},{3,2},{4,7},{5,4},{6,5},{7,6},{8,11},{9,8},{10,9... | collective-permute-start | bytes 294920 | tf_op jit(solution)/shard_map/ppermute | solution.py:356
  23.4 11.9 %copy-start.14 = (bf16[272,1024]{1,0:T(8,128)(2,1)}, bf16[272,1024]{1,0:T(8,128)(2,1)S(1)}, u32[]{:S(2)}) copy-start(bf16[272,1024]{1,0:T(8,128)(2,1)S(1)} %collective-permute-done.refs_1_) | copy-start | bytes 1671172
  35.3 5.7 %collective-permute-start.9 = (f32[4,96,256]{2,1,0:T(8,128)S(1)}, f32[4,96,256]{2,1,0:T(8,128)S(1)}, u32[]{:S(2)}, u32[]{:S(2)}) collective-permute-start(f32[4,96,256]{2,1,0:T(8,128)S(1)} %shard_map.86.refs_0_), channel_id=1, source_target_pairs={{0,4},{4,0},{1,5},{5,1},{2,6},{6,2},{3,7},{7,3},{8,12},{12,8},{9,1... | collective-permute-start | bytes 1179656 | tf_op jit(solution)/shard_map/ppermute | solution.py:359
  35.4 9.7 %collective-permute-start.6 = (bf16[96,1024]{1,0:T(8,128)(2,1)S(1)}, bf16[96,1024]{1,0:T(8,128)(2,1)S(1)}, u32[]{:S(2)}, u32[]{:S(2)}) collective-permute-start(bf16[96,1024]{1,0:T(8,128)(2,1)S(1)} %get-tuple-element.99), channel_id=1, source_target_pairs={{0,1},{1,2},{2,3},{3,0},{4,5},{5,6},{6,7},{7,4},{8,9},{9,10},{10,1... | collective-permute-start | bytes 589832 | tf_op jit(solution)/shard_map/ppermute | solution.py:356
  37.0 16.1 %collective-permute-start.7 = (bf16[96,1024]{1,0:T(8,128)(2,1)S(1)}, bf16[96,1024]{1,0:T(8,128)(2,1)S(1)}, u32[]{:S(2)}, u32[]{:S(2)}) collective-permute-start(bf16[96,1024]{1,0:T(8,128)(2,1)S(1)} %get-tuple-element.101), channel_id=1, source_target_pairs={{0,2},{1,3},{2,0},{3,1},{4,6},{5,7},{6,4},{7,5},{8,10},{9,11},{10,... | collective-permute-start | bytes 589832 | tf_op jit(solution)/shard_map/ppermute | solution.py:356
  39.6 13.5 %collective-permute-start.8 = (bf16[96,1024]{1,0:T(8,128)(2,1)S(1)}, bf16[96,1024]{1,0:T(8,128)(2,1)S(1)}, u32[]{:S(2)}, u32[]{:S(2)}) collective-permute-start(bf16[96,1024]{1,0:T(8,128)(2,1)S(1)} %get-tuple-element.103), channel_id=1, source_target_pairs={{0,3},{1,0},{2,1},{3,2},{4,7},{5,4},{6,5},{7,6},{8,11},{9,8},{10,9... | collective-permute-start | bytes 589832 | tf_op jit(solution)/shard_map/ppermute | solution.py:356
  45.1 16.6 %copy-start.1 = (bf16[96,1024]{1,0:T(8,128)(2,1)}, bf16[96,1024]{1,0:T(8,128)(2,1)S(1)}, u32[]{:S(2)}) copy-start(bf16[96,1024]{1,0:T(8,128)(2,1)S(1)} %collective-permute-done.6.refs_2_) | copy-start | bytes 589828
  53.1 8.6 %copy-start.4 = (bf16[96,1024]{1,0:T(8,128)(2,1)}, bf16[96,1024]{1,0:T(8,128)(2,1)S(1)}, u32[]{:S(2)}) copy-start(bf16[96,1024]{1,0:T(8,128)(2,1)S(1)} %collective-permute-done.7.refs_3_) | copy-start | bytes 589828
  53.1 1.1 copy-start.15
  54.2 7.4 %copy-start.6 = (bf16[96,1024]{1,0:T(8,128)(2,1)}, bf16[96,1024]{1,0:T(8,128)(2,1)S(1)}, u32[]{:S(2)}) copy-start(bf16[96,1024]{1,0:T(8,128)(2,1)S(1)} %collective-permute-done.8.refs_4_) | copy-start | bytes 589828
  61.7 8.1 %collective-permute-start.10 = (bf16[3,256,1024]{2,1,0:T(8,128)(2,1)}, bf16[3,256,1024]{2,1,0:T(8,128)(2,1)}, u32[]{:S(2)}, u32[]{:S(2)}) collective-permute-start(bf16[3,256,1024]{2,1,0:T(8,128)(2,1)} %get-tuple-element.111.refs_2_), channel_id=1, source_target_pairs={{0,4},{4,0},{1,5},{5,1},{2,6},{6,2},{3,7},{7,3},{8,12},{12,8},{9,1... | collective-permute-start | bytes 4718600 | tf_op jit(solution)/shard_map/ppermute | solution.py:359
  63.0 31.4 %collective-permute-start.15 = (bf16[4,96,768]{2,1,0:T(8,128)(2,1)S(1)}, bf16[4,96,768]{2,1,0:T(8,128)(2,1)S(1)}, u32[]{:S(2)}, u32[]{:S(2)}) collective-permute-start(bf16[4,96,768]{2,1,0:T(8,128)(2,1)S(1)} %shard_map.87.refs_9_.refs_4_), channel_id=1, source_target_pairs={{0,16},{8,24},{16,0},{24,8},{1,17},{9,25},{17,1},{25,9},{2,18},{10... | collective-permute-start | bytes 1769480 | tf_op jit(solution)/shard_map/ppermute | solution.py:353
  64.6 29.8 %collective-permute-start.14 = (bf16[4,96,768]{2,1,0:T(8,128)(2,1)S(1)}, bf16[4,96,768]{2,1,0:T(8,128)(2,1)}, u32[]{:S(2)}, u32[]{:S(2)}) collective-permute-start(bf16[4,96,768]{2,1,0:T(8,128)(2,1)S(1)} %shard_map.87.refs_9_.refs_4_), channel_id=1, source_target_pairs={{0,8},{8,0},{16,24},{24,16},{1,9},{9,1},{17,25},{25,17},{2,10},{10... | collective-permute-start | bytes 1769480 | tf_op jit(solution)/shard_map/ppermute | solution.py:353
  65.1 14.3 %collective-permute-start.11 = (bf16[3,96,512]{2,1,0:T(8,128)(2,1)}, bf16[3,96,512]{2,1,0:T(8,128)(2,1)S(1)}, u32[]{:S(2)}, u32[]{:S(2)}) collective-permute-start(bf16[3,96,512]{2,1,0:T(8,128)(2,1)} %copy-done.33), channel_id=1, source_target_pairs={{0,1},{1,2},{2,3},{3,0},{4,5},{5,6},{6,7},{7,4},{8,9},{9,10},{10,1... | collective-permute-start | bytes 884744 | tf_op jit(solution)/shard_map/ppermute | solution.py:356
  76.4 18.1 %collective-permute-start.16 = (bf16[4,96,768]{2,1,0:T(8,128)(2,1)S(1)}, bf16[4,96,768]{2,1,0:T(8,128)(2,1)}, u32[]{:S(2)}, u32[]{:S(2)}) collective-permute-start(bf16[4,96,768]{2,1,0:T(8,128)(2,1)S(1)} %shard_map.87.refs_9_.refs_4_), channel_id=1, source_target_pairs={{0,24},{8,16},{16,8},{24,0},{1,25},{9,17},{17,9},{25,1},{2,26},{10... | collective-permute-start | bytes 1769480 | tf_op jit(solution)/shard_map/ppermute | solution.py:353
  77.8 16.2 %collective-permute-start.12 = (bf16[3,96,512]{2,1,0:T(8,128)(2,1)}, bf16[3,96,512]{2,1,0:T(8,128)(2,1)}, u32[]{:S(2)}, u32[]{:S(2)}) collective-permute-start(bf16[3,96,512]{2,1,0:T(8,128)(2,1)} %get-tuple-element.115), channel_id=1, source_target_pairs={{0,2},{1,3},{2,0},{3,1},{4,6},{5,7},{6,4},{7,5},{8,10},{9,11},{10,... | collective-permute-start | bytes 884744 | tf_op jit(solution)/shard_map/ppermute | solution.py:356
  80.1 14.3 %collective-permute-start.13 = (bf16[3,96,512]{2,1,0:T(8,128)(2,1)}, bf16[3,96,512]{2,1,0:T(8,128)(2,1)}, u32[]{:S(2)}, u32[]{:S(2)}) collective-permute-start(bf16[3,96,512]{2,1,0:T(8,128)(2,1)} %get-tuple-element.116), channel_id=1, source_target_pairs={{0,3},{1,0},{2,1},{3,2},{4,7},{5,4},{6,5},{7,6},{8,11},{9,8},{10,9... | collective-permute-start | bytes 884744 | tf_op jit(solution)/shard_map/ppermute | solution.py:356
  94.4 23.0 %collective-permute-start.19 = (bf16[8,256,1024]{2,1,0:T(8,128)(2,1)}, bf16[8,256,1024]{2,1,0:T(8,128)(2,1)}, u32[]{:S(2)}, u32[]{:S(2)}) collective-permute-start(bf16[8,256,1024]{2,1,0:T(8,128)(2,1)} %constant_dynamic-slice_fusion), channel_id=1, source_target_pairs={{0,4},{8,12},{20,16},{28,24},{1,5},{9,13},{21,17},{29,25},{2,6},{1... | collective-permute-start | bytes 12582920 | tf_op jit(solution)/shard_map/ppermute | solution.py:425
  97.9 33.0 %collective-permute-start.25 = (bf16[3,96,512]{2,1,0:T(8,128)(2,1)}, bf16[3,96,512]{2,1,0:T(8,128)(2,1)S(1)}, u32[]{:S(2)}, u32[]{:S(2)}) collective-permute-start(bf16[3,96,512]{2,1,0:T(8,128)(2,1)} %copy-done.32), channel_id=1, source_target_pairs={{0,1},{1,2},{2,3},{3,0},{4,5},{5,6},{6,7},{7,4},{8,9},{9,10},{10,1... | collective-permute-start | bytes 884744 | tf_op jit(solution)/shard_map/ppermute | solution.py:356
  104.3 27.1 %collective-permute-start.26 = (bf16[3,96,512]{2,1,0:T(8,128)(2,1)}, bf16[3,96,512]{2,1,0:T(8,128)(2,1)S(1)}, u32[]{:S(2)}, u32[]{:S(2)}) collective-permute-start(bf16[3,96,512]{2,1,0:T(8,128)(2,1)} %copy-done.31), channel_id=1, source_target_pairs={{0,2},{1,3},{2,0},{3,1},{4,6},{5,7},{6,4},{7,5},{8,10},{9,11},{10,... | collective-permute-start | bytes 884744 | tf_op jit(solution)/shard_map/ppermute | solution.py:356
  108.6 1.0 copy-start.11
  109.5 1.0 copy-start.13
  114.8 26.1 %collective-permute-start.17 = (bf16[8,64,512]{2,1,0:T(8,128)(2,1)S(1)}, bf16[8,64,512]{2,1,0:T(8,128)(2,1)S(1)}, u32[]{:S(2)}, u32[]{:S(2)}) collective-permute-start(bf16[8,64,512]{2,1,0:T(8,128)(2,1)S(1)} %get-tuple-element.119), channel_id=1, source_target_pairs={{0,0},{4,16},{8,8},{12,24},{16,4},{20,20},{24,12},{28,28},{1,1},{5... | collective-permute-start | bytes 1572872 | tf_op jit(solution)/shard_map/ppermute | solution.py:475
  115.7 25.2 %collective-permute-start.18 = (bf16[8,64,512]{2,1,0:T(8,128)(2,1)S(1)}, bf16[8,64,512]{2,1,0:T(8,128)(2,1)S(1)}, u32[]{:S(2)}, u32[]{:S(2)}) collective-permute-start(bf16[8,64,512]{2,1,0:T(8,128)(2,1)S(1)} %get-tuple-element.120), channel_id=1, source_target_pairs={{0,8},{4,24},{8,0},{12,16},{16,12},{20,28},{24,4},{28,20},{1,9},{5... | collective-permute-start | bytes 1572872 | tf_op jit(solution)/shard_map/ppermute | solution.py:475
  117.4 6.5 %copy-start.3 = (bf16[96,1024]{1,0:T(8,128)(2,1)S(1)}, bf16[96,1024]{1,0:T(8,128)(2,1)}, u32[]{:S(2)}) copy-start(bf16[96,1024]{1,0:T(8,128)(2,1)} %copy-done.1) | copy-start | bytes 589828
  123.9 7.5 %copy-start.30 = (bf16[3,96,512]{2,1,0:T(8,128)(2,1)S(1)}, bf16[3,96,512]{2,1,0:T(8,128)(2,1)}, u32[]{:S(2)}) copy-start(bf16[3,96,512]{2,1,0:T(8,128)(2,1)} %copy-done.29) | copy-start | bytes 884740
  123.9 21.2 %copy-start.9 = (bf16[3,96,512]{2,1,0:T(8,128)(2,1)S(1)}, bf16[3,96,512]{2,1,0:T(8,128)(2,1)}, u32[]{:S(2)}) copy-start(bf16[3,96,512]{2,1,0:T(8,128)(2,1)} %copy-done.8) | copy-start | bytes 884740
  128.8 13.2 %collective-permute-start.20 = (bf16[8,64,512]{2,1,0:T(8,128)(2,1)S(1)}, bf16[8,64,512]{2,1,0:T(8,128)(2,1)S(1)}, u32[]{:S(2)}, u32[]{:S(2)}) collective-permute-start(bf16[8,64,512]{2,1,0:T(8,128)(2,1)S(1)} %get-tuple-element.129), channel_id=1, source_target_pairs={{0,16},{4,0},{8,24},{12,8},{16,20},{20,4},{24,28},{28,12},{1,17},{... | collective-permute-start | bytes 1572872 | tf_op jit(solution)/shard_map/ppermute | solution.py:475
  130.8 14.2 %collective-permute-start.21 = (bf16[8,64,512]{2,1,0:T(8,128)(2,1)S(1)}, bf16[8,64,512]{2,1,0:T(8,128)(2,1)}, u32[]{:S(2)}, u32[]{:S(2)}) collective-permute-start(bf16[8,64,512]{2,1,0:T(8,128)(2,1)S(1)} %get-tuple-element.130), channel_id=1, source_target_pairs={{0,24},{4,8},{8,16},{12,0},{16,28},{20,12},{24,20},{28,4},{1,25},{... | collective-permute-start | bytes 1572872 | tf_op jit(solution)/shard_map/ppermute | solution.py:475
  131.4 9.5 %collective-permute-start.27 = (bf16[3,96,512]{2,1,0:T(8,128)(2,1)S(1)}, bf16[3,96,512]{2,1,0:T(8,128)(2,1)S(1)}, u32[]{:S(2)}, u32[]{:S(2)}) collective-permute-start(bf16[3,96,512]{2,1,0:T(8,128)(2,1)S(1)} %copy-done.30), channel_id=1, source_target_pairs={{0,3},{1,0},{2,1},{3,2},{4,7},{5,4},{6,5},{7,6},{8,11},{9,8},{10,9... | collective-permute-start | bytes 884744 | tf_op jit(solution)/shard_map/ppermute | solution.py:356
  140.9 1.1 copy-start.37
  140.9 11.5 %copy-start.38 = (bf16[8,64,512]{2,1,0:T(8,128)(2,1)}, bf16[8,64,512]{2,1,0:T(8,128)(2,1)S(1)}, u32[]{:S(2)}) copy-start(bf16[8,64,512]{2,1,0:T(8,128)(2,1)S(1)} %collective-permute-done.18.refs_1_) | copy-start | bytes 1572868
  149.9 2.4 %collective-permute-start.28 = (f32[4,4,96,128]{3,2,1,0:T(8,128)S(1)}, f32[4,4,96,128]{3,2,1,0:T(8,128)S(1)}, u32[]{:S(2)}, u32[]{:S(2)}) collective-permute-start(f32[4,4,96,128]{3,2,1,0:T(8,128)S(1)} %get-tuple-element.152), channel_id=1, source_target_pairs={{0,4},{4,0},{1,5},{5,1},{2,6},{6,2},{3,7},{7,3},{8,12},{12,8},{9,1... | collective-permute-start | bytes 2359304 | tf_op jit(solution)/shard_map/ppermute | solution.py:359
  152.5 8.8 %collective-permute-start.31 = (f32[4,96,128]{2,1,0:T(8,128)S(1)}, f32[4,96,128]{2,1,0:T(8,128)S(1)}, u32[]{:S(2)}, u32[]{:S(2)}) collective-permute-start(f32[4,96,128]{2,1,0:T(8,128)S(1)} %get-tuple-element.177), channel_id=1, source_target_pairs={{0,24},{8,16},{16,8},{24,0},{1,25},{9,17},{17,9},{25,1},{2,26},{10... | collective-permute-start | bytes 589832 | tf_op jit(solution)/shard_map/ppermute | solution.py:353
  154.5 10.1 %collective-permute-start.30 = (f32[4,96,128]{2,1,0:T(8,128)S(1)}, f32[4,96,128]{2,1,0:T(8,128)S(1)}, u32[]{:S(2)}, u32[]{:S(2)}) collective-permute-start(f32[4,96,128]{2,1,0:T(8,128)S(1)} %get-tuple-element.178), channel_id=1, source_target_pairs={{0,16},{8,24},{16,0},{24,8},{1,17},{9,25},{17,1},{25,9},{2,18},{10... | collective-permute-start | bytes 589832 | tf_op jit(solution)/shard_map/ppermute | solution.py:353
  155.0 10.5 %collective-permute-start.29 = (f32[4,96,128]{2,1,0:T(8,128)S(1)}, f32[4,96,128]{2,1,0:T(8,128)S(1)}, u32[]{:S(2)}, u32[]{:S(2)}) collective-permute-start(f32[4,96,128]{2,1,0:T(8,128)S(1)} %get-tuple-element.179), channel_id=1, source_target_pairs={{0,8},{8,0},{16,24},{24,16},{1,9},{9,1},{17,25},{25,17},{2,10},{10... | collective-permute-start | bytes 589832 | tf_op jit(solution)/shard_map/ppermute | solution.py:353
  156.0 29.3 %collective-permute-start.22 = (f32[256,512]{1,0:T(8,128)}, f32[256,512]{1,0:T(8,128)}, u32[]{:S(2)}, u32[]{:S(2)}) collective-permute-start(f32[256,512]{1,0:T(8,128)} %get-tuple-element.133), channel_id=1, source_target_pairs={{0,8},{8,0},{16,24},{24,16},{1,9},{9,1},{17,25},{25,17},{2,10},{10... | collective-permute-start | bytes 1572872 | tf_op jit(solution)/shard_map/ppermute | solution.py:353
  157.0 29.3 %collective-permute-start.23 = (f32[256,512]{1,0:T(8,128)}, f32[256,512]{1,0:T(8,128)}, u32[]{:S(2)}, u32[]{:S(2)}) collective-permute-start(f32[256,512]{1,0:T(8,128)} %get-tuple-element.135), channel_id=1, source_target_pairs={{0,16},{8,24},{16,0},{24,8},{1,17},{9,25},{17,1},{25,9},{2,18},{10... | collective-permute-start | bytes 1572872 | tf_op jit(solution)/shard_map/ppermute | solution.py:353
  161.2 26.8 %collective-permute-start.24 = (f32[256,512]{1,0:T(8,128)}, f32[256,512]{1,0:T(8,128)}, u32[]{:S(2)}, u32[]{:S(2)}) collective-permute-start(f32[256,512]{1,0:T(8,128)} %get-tuple-element.137), channel_id=1, source_target_pairs={{0,24},{8,16},{16,8},{24,0},{1,25},{9,17},{17,9},{25,1},{2,26},{10... | collective-permute-start | bytes 1572872 | tf_op jit(solution)/shard_map/ppermute | solution.py:353
  170.7 8.5 %copy-start.26 = (bf16[8,64,512]{2,1,0:T(8,128)(2,1)}, bf16[8,64,512]{2,1,0:T(8,128)(2,1)S(1)}, u32[]{:S(2)}) copy-start(bf16[8,64,512]{2,1,0:T(8,128)(2,1)S(1)} %get-tuple-element.168) | copy-start | bytes 1572868
  170.7 8.5 %copy-start.28 = (bf16[8,64,512]{2,1,0:T(8,128)(2,1)}, bf16[8,64,512]{2,1,0:T(8,128)(2,1)S(1)}, u32[]{:S(2)}) copy-start(bf16[8,64,512]{2,1,0:T(8,128)(2,1)S(1)} %get-tuple-element.167) | copy-start | bytes 1572868
  170.7 47.0 %collective-permute-start.36 = (bf16[8,64,512]{2,1,0:T(8,128)(2,1)}, bf16[8,64,512]{2,1,0:T(8,128)(2,1)}, u32[]{:S(2)}, u32[]{:S(2)}) collective-permute-start(bf16[8,64,512]{2,1,0:T(8,128)(2,1)} %get-tuple-element.165), channel_id=1, source_target_pairs={{0,0},{4,16},{8,8},{12,24},{16,4},{20,20},{24,12},{28,28},{1,1},{5... | collective-permute-start | bytes 1572872 | tf_op jit(solution)/shard_map/ppermute | solution.py:475
  176.2 1.4 collective-permute-start.32
  178.2 41.7 %collective-permute-start.37 = (bf16[8,64,512]{2,1,0:T(8,128)(2,1)}, bf16[8,64,512]{2,1,0:T(8,128)(2,1)}, u32[]{:S(2)}, u32[]{:S(2)}) collective-permute-start(bf16[8,64,512]{2,1,0:T(8,128)(2,1)} %get-tuple-element.166), channel_id=1, source_target_pairs={{0,8},{4,24},{8,0},{12,16},{16,12},{20,28},{24,4},{28,20},{1,9},{5... | collective-permute-start | bytes 1572872 | tf_op jit(solution)/shard_map/ppermute | solution.py:475
  185.4 16.0 %collective-permute-start.40 = (bf16[4,96,64]{2,1,0:T(8,128)(2,1)}, bf16[4,96,64]{2,1,0:T(8,128)(2,1)S(1)}, u32[]{:S(2)}, u32[]{:S(2)}) collective-permute-start(bf16[4,96,64]{2,1,0:T(8,128)(2,1)} %get-tuple-element.170), channel_id=1, source_target_pairs={{0,8},{8,0},{16,24},{24,16},{1,9},{9,1},{17,25},{25,17},{2,10},{10... | collective-permute-start | bytes 147464 | tf_op jit(solution)/shard_map/ppermute | solution.py:353
  186.4 15.6 %collective-permute-start.41 = (bf16[4,96,64]{2,1,0:T(8,128)(2,1)}, bf16[4,96,64]{2,1,0:T(8,128)(2,1)S(1)}, u32[]{:S(2)}, u32[]{:S(2)}) collective-permute-start(bf16[4,96,64]{2,1,0:T(8,128)(2,1)} %get-tuple-element.171), channel_id=1, source_target_pairs={{0,16},{8,24},{16,0},{24,8},{1,17},{9,25},{17,1},{25,9},{2,18},{10... | collective-permute-start | bytes 147464 | tf_op jit(solution)/shard_map/ppermute | solution.py:353
  188.1 14.9 %collective-permute-start.42 = (bf16[4,96,64]{2,1,0:T(8,128)(2,1)}, bf16[4,96,64]{2,1,0:T(8,128)(2,1)S(1)}, u32[]{:S(2)}, u32[]{:S(2)}) collective-permute-start(bf16[4,96,64]{2,1,0:T(8,128)(2,1)} %get-tuple-element.172), channel_id=1, source_target_pairs={{0,24},{8,16},{16,8},{24,0},{1,25},{9,17},{17,9},{25,1},{2,26},{10... | collective-permute-start | bytes 147464 | tf_op jit(solution)/shard_map/ppermute | solution.py:353
  201.4 12.6 %collective-permute-start.33 = (bf16[96,512]{1,0:T(8,128)(2,1)}, bf16[96,512]{1,0:T(8,128)(2,1)S(1)}, u32[]{:S(2)}, u32[]{:S(2)}) collective-permute-start(bf16[96,512]{1,0:T(8,128)(2,1)} %copy-done.36), channel_id=1, source_target_pairs={{0,3},{1,0},{2,1},{3,2},{4,7},{5,4},{6,5},{7,6},{8,11},{9,8},{10,9... | collective-permute-start | bytes 294920 | tf_op jit(solution)/shard_map/ppermute | solution.py:356
  202.0 12.4 %collective-permute-start.34 = (bf16[96,512]{1,0:T(8,128)(2,1)}, bf16[96,512]{1,0:T(8,128)(2,1)S(1)}, u32[]{:S(2)}, u32[]{:S(2)}) collective-permute-start(bf16[96,512]{1,0:T(8,128)(2,1)} %copy-done.35), channel_id=1, source_target_pairs={{0,2},{1,3},{2,0},{3,1},{4,6},{5,7},{6,4},{7,5},{8,10},{9,11},{10,... | collective-permute-start | bytes 294920 | tf_op jit(solution)/shard_map/ppermute | solution.py:356
  202.9 12.2 %collective-permute-start.35 = (bf16[96,512]{1,0:T(8,128)(2,1)}, bf16[96,512]{1,0:T(8,128)(2,1)S(1)}, u32[]{:S(2)}, u32[]{:S(2)}) collective-permute-start(bf16[96,512]{1,0:T(8,128)(2,1)} %copy-done.34), channel_id=1, source_target_pairs={{0,1},{1,2},{2,3},{3,0},{4,5},{5,6},{6,7},{7,4},{8,9},{9,10},{10,1... | collective-permute-start | bytes 294920 | tf_op jit(solution)/shard_map/ppermute | solution.py:356
  205.2 4.8 %copy-start.24 = (bf16[4,96,64]{2,1,0:T(8,128)(2,1)S(1)}, bf16[4,96,64]{2,1,0:T(8,128)(2,1)}, u32[]{:S(2)}) copy-start(bf16[4,96,64]{2,1,0:T(8,128)(2,1)} %copy-done.23) | copy-start | bytes 147460
  205.2 9.3 %copy-start.27 = (bf16[8,64,512]{2,1,0:T(8,128)(2,1)S(1)}, bf16[8,64,512]{2,1,0:T(8,128)(2,1)}, u32[]{:S(2)}) copy-start(bf16[8,64,512]{2,1,0:T(8,128)(2,1)} %copy-done.26) | copy-start | bytes 1572868
  205.2 10.0 %copy-start.17 = (f32[256,512]{1,0:T(8,128)S(1)}, f32[256,512]{1,0:T(8,128)}, u32[]{:S(2)}) copy-start(f32[256,512]{1,0:T(8,128)} %copy-done.16) | copy-start | bytes 1572868
  205.2 10.0 %copy-start.20 = (bf16[384,256]{1,0:T(8,128)(2,1)S(1)}, bf16[384,256]{1,0:T(8,128)(2,1)}, u32[]{:S(2)}) copy-start(bf16[384,256]{1,0:T(8,128)(2,1)} %copy-done.19) | copy-start | bytes 589828
  214.0 12.2 %collective-permute-start.38 = (bf16[8,64,512]{2,1,0:T(8,128)(2,1)}, bf16[8,64,512]{2,1,0:T(8,128)(2,1)S(1)}, u32[]{:S(2)}, u32[]{:S(2)}) collective-permute-start(bf16[8,64,512]{2,1,0:T(8,128)(2,1)} %copy-done.28), channel_id=1, source_target_pairs={{0,16},{4,0},{8,24},{12,8},{16,20},{20,4},{24,28},{28,12},{1,17},{... | collective-permute-start | bytes 1572872 | tf_op jit(solution)/shard_map/ppermute | solution.py:475
  214.4 14.1 %collective-permute-start.39 = (bf16[8,64,512]{2,1,0:T(8,128)(2,1)S(1)}, bf16[8,64,512]{2,1,0:T(8,128)(2,1)S(1)}, u32[]{:S(2)}, u32[]{:S(2)}) collective-permute-start(bf16[8,64,512]{2,1,0:T(8,128)(2,1)S(1)} %copy-done.27), channel_id=1, source_target_pairs={{0,24},{4,8},{8,16},{12,0},{16,28},{20,12},{24,20},{28,4},{1,25},{... | collective-permute-start | bytes 1572872 | tf_op jit(solution)/shard_map/ppermute | solution.py:475
  (19 other events, 14.2 us)

commit v5 on v4

--- a/solution.py
+++ b/solution.py
@@ -87,6 +87,7 @@
 
 
 BF16, F32 = jnp.bfloat16, jnp.float32
+VMEM_BYTES = 58 << 20
 VMEM = pl.BlockSpec(memory_space=pltpu.VMEM)
 SMEM = pl.BlockSpec(memory_space=pltpu.SMEM)
 ANY = pl.BlockSpec(memory_space=pl.ANY)
@@ -96,39 +97,69 @@
     return lax.dot_general(lhs, rhs, (dims, ((), ())), preferred_element_type=F32)
 
 
-def call(kernel, out_shape, fetched, plain=(), at=None, scratch=()):
+def call(kernel, out_shape, fetched, at=None, scratch=(), either=None, flops=1):
     nf, n_out = len(fetched), len(out_shape)
     shapes = [v.shape[:-1] + (v.shape[-1] if w is None else w[1],) for v, w in fetched]
+    sources = [v for v, _ in fetched] + ([] if either is None else list(either[:2]))
+    buffers = [pltpu.VMEM(shape, v.dtype) for shape, (v, _) in zip(shapes, fetched)]
+    if either is not None:
+        lead, width = either[0].shape[:-1], either[2][1]
+        buffers.append(pltpu.VMEM(lead + (width,), either[0].dtype))
+        buffers.append(pltpu.SemaphoreType.DMA((lead[0],)))
 
     def body(*refs):
         refs = list(refs)
         head = [refs.pop(0)] if at is not None else []
-        sources, refs = refs[:nf], refs[nf:]
-        rest, buffers = refs[: len(plain) + n_out], refs[len(plain) + n_out :]
-        buffers, sems, extra = buffers[:nf], buffers[nf], buffers[nf + 1 :]
+        froms, refs = refs[: len(sources)], refs[len(sources) :]
+        outs, refs = refs[:n_out], refs[n_out:]
+        sems, held, extra = refs[0], refs[1 : 1 + len(buffers)], refs[1 + len(buffers) :]
         copies = []
-        for i, (source, (_, columns)) in enumerate(zip(sources, fetched)):
+        for i, (source, (_, columns)) in enumerate(zip(froms, fetched)):
             if columns is not None:
-                lead = (slice(None),) * (len(source.shape) - 1)
-                source = source.at[lead + (pl.ds(*columns),)]
-            copies.append(pltpu.make_async_copy(source, buffers[i], sems.at[i]))
+                first = (slice(None),) * (len(source.shape) - 1)
+                source = source.at[first + (pl.ds(*columns),)]
+            copies.append(pltpu.make_async_copy(source, held[i], sems.at[i]))
         for c in copies:
             c.start()
+        if either is not None:
+            one, other = froms[nf:]
+            buffer, more = held[nf], held.pop()
+            start = pl.multiple_of(head[0][1], 128)
+            parts = [
+                pltpu.make_async_copy(one.at[d, :, pl.ds(start, width)], buffer.at[d], more.at[d])
+                for d in range(lead[0])
+            ]
+            others = [
+                pltpu.make_async_copy(
+                    other.at[d, :, pl.ds(*either[2])], buffer.at[d], more.at[d]
+                )
+                for d in range(lead[0])
+            ]
+
+            @pl.when(head[0][0] == 1)
+            def _():
+                for c in parts:
+                    c.start()
+
+            @pl.when(head[0][0] != 1)
+            def _():
+                for c in others:
+                    c.start()
+
+            copies.extend(others)
         for c in copies:
             c.wait()
-        kernel(*head, *buffers, *rest, *extra)
+        kernel(*head, *held[:nf], *outs, *held[nf:], *extra)
 
     return pl.pallas_call(
         body,
         out_shape=[jax.ShapeDtypeStruct(shape, dtype) for shape, dtype in out_shape],
-        in_specs=[SMEM] * (at is not None) + [ANY] * nf + [VMEM] * len(plain),
+        in_specs=[SMEM] * (at is not None) + [ANY] * len(sources),
         out_specs=[VMEM] * n_out,
-        scratch_shapes=[pltpu.VMEM(shape, v.dtype) for shape, (v, _) in zip(shapes, fetched)]
-        + [pltpu.SemaphoreType.DMA((max(nf, 1),))]
-        + list(scratch),
-        compiler_params=pltpu.CompilerParams(vmem_limit_bytes=48 << 20),
-        cost_estimate=pl.CostEstimate(flops=1, bytes_accessed=1, transcendentals=0),
-    )(*([at] if at is not None else []), *[v for v, _ in fetched], *plain)
+        scratch_shapes=[pltpu.SemaphoreType.DMA((nf,)), *buffers, *scratch],
+        compiler_params=pltpu.CompilerParams(vmem_limit_bytes=VMEM_BYTES),
+        cost_estimate=pl.CostEstimate(flops=flops, bytes_accessed=1, transcendentals=0),
+    )(*([at] if at is not None else []), *sources)
 
 
 def slot_domain(count, lanes, gslots):
@@ -179,11 +210,12 @@
 def own_kernel(ad, slots, dom_total, at, dom, x, dy, hot_ref, *outs):
     hot = one_hot(dom[...], at[0], slots, ad, dom_total)
     hot_ref[...] = hot
+    width = x.shape[1]
+    moved = dot(hot, x[...], ((1,), (0,))).astype(BF16)
     moved_dy = dot(hot, dy[...], ((1,), (0,))).astype(BF16)
-    moved = dot(hot, x[...], ((1,), (0,))).astype(BF16)
     for ka in range(ad):
-        outs[ka][...] = moved_dy[ka * slots : (ka + 1) * slots]
-        outs[ad + ka][...] = moved[ka * slots : (ka + 1) * slots]
+        outs[ka][:, :width] = moved[ka * slots : (ka + 1) * slots]
+        outs[ka][:, width:] = moved_dy[ka * slots : (ka + 1) * slots]
 
 
 def others_kernel(fsdp, ad, slots, dom_total, at, *refs):
@@ -221,8 +253,7 @@
 
 
 def hidden_kernel(fsdp, ad, gslots, first, last, at, *refs):
-    own_refs, x_refs, held = refs[:ad], refs[ad : 2 * ad], refs[2 * ad]
-    outs = refs[2 * ad + 1 :]
+    own_refs, x_refs, outs, held = refs[:ad], refs[ad : 2 * ad], refs[2 * ad : -1], refs[-1]
     earlier = None
     if not first:
         earlier, outs = outs[0], outs[1:]
@@ -241,7 +272,7 @@
                     outs[0][kf, ka, rows, :] = new
                 else:
                     n = new.shape[1] // 2
-                    second = at[0] == 1
+                    second = at[2] == 1
                     outs[0][kf, ka, rows, :] = jnp.where(second, new[:, n:], new[:, :n])
                     outs[1][kf, ka, rows, :] = jnp.where(second, new[:, :n], new[:, n:])
 
@@ -377,28 +408,18 @@
 
     hot, *sends = call(
         functools.partial(own_kernel, ad, slots, ad * dloc),
-        [((ad * slots, rows), BF16)]
-        + [((slots, vloc), BF16)] * ad
-        + [((slots, kt), BF16)] * ad,
+        [((ad * slots, rows), BF16)] + [((slots, kt + vloc), BF16)] * ad,
         [(v, None) for v in (domain.T, x_in[0], layer_output_gradient)],
         at=numbers(a),
     )
-    dy = [over_a(v, ka) for ka, v in enumerate(sends[:ad])]
-    own = [over_a(after(v, *dy), ka) for ka, v in enumerate(sends[ad:-1])]
-    own.append(over_a(after(sends[-1], *dy, x_in[1]), ad - 1))
-
-    (back,) = call(
-        functools.partial(back_kernel, ad, gslots),
-        [((ad, slots, rank), F32)],
-        [(v, None) for v in after(dy, x_in[1], x_in[2])] + [(adapter_up_weight, None)],
-    )
-    (both,) = call(
-        functools.partial(both_kernel, ad),
-        [((ad, slots, vloc + rank), BF16)],
-        [(back, None), (swap(back), None)] + [(v, None) for v in dy],
-    )
-
-    ready = after(x_in[1:], *own, both)
+    held = after(adapter_down_weight, *sends)
+    sends[-1] = after(sends[-1], x_in[1])
+    own = [over_a(v, ka) for ka, v in enumerate(sends)]
+
+    down_other = lax.dynamic_slice_in_dim(held, (fx * 2 + 1 - t) * kt, kt, 2)
+    pairs = [(i * 2 + i // 2, i * 2 + 1 - i // 2) for i in range(fsdp)]
+
+    ready, own, down_other = lax.optimization_barrier((x_in[1:], own, down_other))
     *sends, x_plain = call(
         functools.partial(others_kernel, fsdp, ad, slots, ad * dloc),
         [((fsdp - 1, slots, cw), BF16)] * (CHUNKS * ad) + [((fsdp - 1, rows, kt), BF16)],
@@ -407,30 +428,38 @@
     )
     x_routed = [[over_a(v, ka) for ka, v in enumerate(sends[:ad])]]
 
+    dy = [(v, (kt, vloc)) for v in after(own, x_plain)]
+    (back,) = call(
+        functools.partial(back_kernel, ad, gslots),
+        [((ad, slots, rank), F32)],
+        [*dy, (adapter_up_weight, None)],
+    )
+    (both,) = call(
+        functools.partial(both_kernel, ad),
+        [((ad, slots, vloc + rank), BF16)],
+        [(back, None), (swap(back), None), *dy],
+    )
+
+    down_got = lax.ppermute(after(down_other, both), ("fsdp", "tp"), pairs)
+
     x_chip = lax.dynamic_slice_in_dim(input_rows, f * kf_width, kf_width, 1)
+    x_other = after(swap(x_plain), both, down_got)
     base = call(
         functools.partial(base_kernel, fsdp),
         [((rows, vloc), F32)] * fsdp,
-        [(v, None) for v in (x_chip, x_plain, swap(x_plain), value_weight_frozen)],
+        [(v, None) for v in (x_chip, x_plain, x_other, value_weight_frozen)],
         at=numbers(t),
+        flops=20 * fsdp * rows * kt * vloc,
     )
     base_plain = base[0]
 
-    both = [after(both, x_plain)] * fsdp
+    both = [both] * fsdp
     both[1], both[2] = over_f(both[1], 1), over_f(both[2], 2)
-    both[3] = over_f(after(both[3], base_plain), 3)
-    held = after(adapter_down_weight, x_plain)
-    down_other = lax.dynamic_slice_in_dim(held, (fx * 2 + 1 - t) * kt, kt, 2)
-    pairs = [(i * 2 + i // 2, i * 2 + 1 - i // 2) for i in range(fsdp)]
-    down_got = lax.ppermute(after(down_other, x_routed[0], both), ("fsdp", "tp"), pairs)
-
+    both[3] = over_f(both[3], 3)
+    base = [over_f(v, k) for k, v in enumerate(base)]
     for c in range(1, CHUNKS):
-        chunk = [after(v, *x_routed[c - 1], *both) for v in sends[c * ad : (c + 1) * ad]]
+        chunk = [after(v, *x_routed[c - 1], *both, base_plain) for v in sends[c * ad : (c + 1) * ad]]
         x_routed.append([over_a(v, ka) for ka, v in enumerate(chunk)])
-
-
-    down_mine = lax.dynamic_slice_in_dim(adapter_down_weight, (fx * 2 + t) * kt, kt, 2)
-    down = jnp.where(t == fy, down_mine, down_got)
 
     def chunk_of(c, routed):
         return [(v, (c * cw, cw)) for v in own] + [(v, None) for v in routed]
@@ -440,8 +469,9 @@
         return call(
             functools.partial(hidden_kernel, fsdp, ad, gslots, c == 0, last),
             [((fsdp, ad, slots, rank // 2 if last else rank), F32)] * (2 if last else 1),
-            [*chunk_of(c, routed), (down, (c * cw, cw)), *[(v, None) for v in earlier]],
-            at=numbers(t),
+            [*chunk_of(c, routed), *[(v, None) for v in earlier]],
+            at=numbers(t == fy, fx * kf_width + t * kt + c * cw, t),
+            either=(adapter_down_weight, down_got, (c * cw, cw)),
         )
 
     grad_a = None
@@ -451,8 +481,8 @@
         if last:
             hid = hidden(c, hid, x_routed[c])
             hid = hid[0] + swap(hid[1])
+            hid, both = lax.optimization_barrier((hid, both))
             hid = [over_f(hid[k], k) for k in range(fsdp)]
-            hid, both = lax.optimization_barrier((hid, both))
         sums = call(
             functools.partial(down_grad_kernel, fsdp, ad, gslots),
             [((dloc, rloc, cw), BF16)] * fsdp,
@@ -462,7 +492,7 @@
         )
         got = []
         if not last:
-            hid = hidden(c, hid, after(x_routed[c], *sums))
+            hid = hidden(c, hid, after(x_routed[c], x_routed[c + 1][2], *sums))
             sums = [*sums[:2], *after(sums[2:], hid)]
         for r in range(fsdp):
             p, q = r % 2, r // 2
@@ -473,9 +503,6 @@
                 for s in range(2)
             ]
             got.append(lax.ppermute(sums[r], ("fsdp", "tp"), perm))
-        if not last:
-            x_routed[c + 1] = after(x_routed[c + 1], *got)
-            base = [over_f(after(v, *got), k) for k, v in enumerate(base)]
         at = [
             ((fx ^ (r % 2)) * kf_width + (fy ^ (r // 2)) * kt + c * cw) // cw
             for r in range(fsdp)
@@ -491,7 +518,8 @@
                     out_specs=pl.BlockSpec((dloc, rloc, cw), lambda i, at: (0, 0, at[i])),
                 ),
                 cost_estimate=pl.CostEstimate(flops=1, bytes_accessed=1, transcendentals=0),
-            )(numbers(*at), *got)
+            )(numbers(*at), *after(got, x_routed[1][1]))
+            x_routed[c + 1] = after(x_routed[c + 1], grad_a, *base)
         else:
             for v, column in zip(got, at):
                 grad_a = lax.dynamic_update_slice_in_dim(
@@ -506,7 +534,7 @@
         at=numbers(t, *[f ^ k for k in range(fsdp)]),
     )
     returned = [over_a(v, (ad - ka) % ad) for ka, v in enumerate(outs[:ad])]
-    hid_cols = [over_f(v, k) for k, v in enumerate(outs[ad:])]
+    hid_cols = [over_f(after(v, got[0], got[1]), k) for k, v in enumerate(outs[ad:])]
 
     (y_out,) = call(
         functools.partial(output_kernel, fsdp, ad),

time: 231 us -> 222 us (0.961)
  Pallas kernels: 45.8 us -> 60.7 us
  local copies, waits for them, and re-layouts: 25.4 us -> 14.1 us
  waiting for transfers between devices: 74.2 us -> 67.2 us
  other arithmetic: 16 us -> 9.91 us
    pallas_call x12, Pallas kernels: 41 us -> 56 us  [call(): pl.pallas_call(body, out_shape=[jax.ShapeDtypeStruct(shape, dtype) for sh...]
    unnamed x80 -> x74, local copies, waits for them, and re-layouts: 17.5 us -> 3.88 us
    ppermute x15 -> x12, waiting for transfers between devices: 34.8 us -> 27.2 us  [over_a(): lax.ppermute(v, 'ad', [(i, (i + k) % ad) for i in range(ad)])]
    select_n x1 -> x0, other arithmetic: 6.5 us -> none  [column_body(): down = jnp.where(t == fy, down_mine, down_got)]
    ppermute x8, waiting for transfers between devices: 8.83 us -> 4.58 us  [column_body(): got.append(lax.ppermute(sums[r], ('fsdp', 'tp'), perm))]
    ppermute x15, waiting for transfers between devices: 27 us -> 30.8 us  [over_f(): lax.ppermute(v, 'fsdp', [(i, i ^ k) for i in range(fsdp)])]
    ppermute x15 -> x12, starting transfers between devices: 30.1 us -> 30.1 us  [over_a(): lax.ppermute(v, 'ad', [(i, (i + k) % ad) for i in range(ad)])]
  transfers between devices with their start and end apart: 43 -> 40, of which waited for: 20 -> 21; matrix products, arithmetic and copies ran while one was open for 8% -> 7% of each run, Pallas kernels for 16% -> 18%
where the time goes in v5:
time: 222 us
  starting transfers between devices  68.6 us (31%)
  waiting for transfers between devices  67.2 us (30%)
  Pallas kernels  60.7 us (27%)
  local copies, waits for them, and re-layouts  14.1 us (6%)
  other arithmetic  9.91 us (4%)
    pallas_call x12, Pallas kernels, call(): pl.pallas_call(body, out_shape=[jax.ShapeDtypeStruct(shape, dtype) for sh...  56 us
    ppermute x15, waiting for transfers between devices, over_f(): lax.ppermute(v, 'fsdp', [(i, i ^ k) for i in range(fsdp)])  30.8 us
    ppermute x12, starting transfers between devices, over_a(): lax.ppermute(v, 'ad', [(i, (i + k) % ad) for i in range(ad)])  30.1 us
    ppermute x12, waiting for transfers between devices, over_a(): lax.ppermute(v, 'ad', [(i, (i + k) % ad) for i in range(ad)])  27.2 us
    ppermute x15, starting transfers between devices, over_f(): lax.ppermute(v, 'fsdp', [(i, i ^ k) for i in range(fsdp)])  20.6 us
    ppermute x8, starting transfers between devices, column_body(): got.append(lax.ppermute(sums[r], ('fsdp', 'tp'), perm))  11.8 us
    ppermute x4, waiting for transfers between devices, swap(): return lax.ppermute(v, 'tp', [(0, 1), (1, 0)])  4.68 us
    pallas_call x1, Pallas kernels, column_body(): pl.pallas_call(functools.partial(place_kernel, fsdp), out_shape=jax.Shape...  4.65 us
  transfers between devices with their start and end apart: 40, of which 21 were waited for; matrix products, arithmetic and copies ran while one was open for 7% of the time, Pallas kernels for 18%

profile of v5, /device:TPU:0, one launch (start us, length us, event | category | flops | bytes accessed | tf_op | source)
XLA Modules:
  0.0 221.6 jit_solution(2103071095010360283)
XLA Ops:
  1.3 2.5 %constant_dynamic-slice_fusion.1 = (bf16[256,1024]{1,0:T(8,128)(2,1)S(1)}, bf16[256,1024]{1,0:T(8,128)(2,1)S(1)}, bf16[256,1024]{1,0:T(8,128)(2,1)}, bf16[256,1024]{1,0:T(8,128)(2,1)S(1)}) fusion(bf16[256,8192]{1,0:T(8,128)(2,1)} %param.6, s32[]{:T(128)S(6)} %select_n.69, s32[]{:T(128)S(6)} %select_n.67, s32[]{:T(128)S(6)} %select_n.66, s32[]{:T(128)S(6)} %select_n.68), kind=kLoop, calls=%fused_computation.17 | loop fusion | bytes 4194320 | tf_op jit(solution)/shard_map/dynamic_slice | solution.py:400
  3.9 1.1 fusion.3
  5.0 2.9 %collective-permute-start = (bf16[272,1024]{1,0:T(8,128)(2,1)}, bf16[272,1024]{1,0:T(8,128)(2,1)S(1)}, u32[]{:S(2)}, u32[]{:S(2)}) collective-permute-start(bf16[272,1024]{1,0:T(8,128)(2,1)} %get-tuple-element.86), channel_id=1, source_target_pairs={{0,8},{8,0},{16,24},{24,16},{1,9},{9,1},{17,25},{25,17},{2,10},{10... | collective-permute-start | bytes 1671176 | tf_op jit(solution)/shard_map/ppermute | solution.py:384
  7.9 1.5 collective-permute-start.1
  9.5 2.8 %shard_map.85 = (bf16[384,256]{1,0:T(8,128)(2,1)}, bf16[96,1536]{1,0:T(8,128)(2,1)}, bf16[96,1536]{1,0:T(8,128)(2,1)}, bf16[96,1536]{1,0:T(8,128)(2,1)}, bf16[96,1536]{1,0:T(8,128)(2,1)}) custom-call(s32[1]{0:T(128)} %bitcast.1.refs_0_, s32[1,256]{1,0:T(1,128)} %bitcast.33, bf16[256,1024]{1,0:T(8,128)(2,1)} %get-tuple-element.89.refs_2_, ...), custom_call_target="tpu_custom_call" | custom-call | flops 1 | bytes 1 | tf_op jit(solution)/shard_map/pallas_call | solution.py:154
  12.2 2.1 collective-permute-start.3
  14.3 2.6 %collective-permute-start.4 = (bf16[96,1536]{1,0:T(8,128)(2,1)}, bf16[96,1536]{1,0:T(8,128)(2,1)S(1)}, u32[]{:S(2)}, u32[]{:S(2)}) collective-permute-start(bf16[96,1536]{1,0:T(8,128)(2,1)} %get-tuple-element.92), channel_id=1, source_target_pairs={{0,2},{1,3},{2,0},{3,1},{4,6},{5,7},{6,4},{7,5},{8,10},{9,11},{10,... | collective-permute-start | bytes 884744 | tf_op jit(solution)/shard_map/ppermute | solution.py:387
  16.9 4.7 %collective-permute-done.refs_1_ = bf16[272,1024]{1,0:T(8,128)(2,1)S(1)} collective-permute-done((bf16[272,1024]{1,0:T(8,128)(2,1)}, bf16[272,1024]{1,0:T(8,128)(2,1)S(1)}, u32[]{:S(2)}, u32[]{:S(2)}) %collective-permute-start) | collective-permute-done | bytes 557088 | tf_op jit(solution)/shard_map/ppermute | solution.py:384
  21.6 4.2 %collective-permute-start.5 = (bf16[96,1536]{1,0:T(8,128)(2,1)}, bf16[96,1536]{1,0:T(8,128)(2,1)S(1)}, u32[]{:S(2)}, u32[]{:S(2)}) collective-permute-start(bf16[96,1536]{1,0:T(8,128)(2,1)} %get-tuple-element.94), channel_id=1, source_target_pairs={{0,3},{1,0},{2,1},{3,2},{4,7},{5,4},{6,5},{7,6},{8,11},{9,8},{10,9... | collective-permute-start | bytes 884744 | tf_op jit(solution)/shard_map/ppermute | solution.py:387
  25.8 4.6 %constant_dynamic-slice_fusion = bf16[8,256,1024]{2,1,0:T(8,128)(2,1)} fusion(bf16[8,256,4096]{2,1,0:T(8,128)(2,1)} %refs_10_.1, s32[]{:T(128)S(6)} %select_n.71), kind=kLoop, calls=%fused_computation.16 | loop fusion | bytes 8388612 | tf_op jit(solution)/shard_map/dynamic_slice | solution.py:419
  30.4 5.1 %collective-permute-done.4.refs_2_.refs_4_.refs_3_ = bf16[96,1536]{1,0:T(8,128)(2,1)S(1)} collective-permute-done((bf16[96,1536]{1,0:T(8,128)(2,1)}, bf16[96,1536]{1,0:T(8,128)(2,1)S(1)}, u32[]{:S(2)}, u32[]{:S(2)}) %collective-permute-start.4) | collective-permute-done | bytes 294944 | tf_op jit(solution)/shard_map/ppermute | solution.py:387
  36.5 4.5 %shard_map.86 = (bf16[3,96,512]{2,1,0:T(8,128)(2,1)}, bf16[3,96,512]{2,1,0:T(8,128)(2,1)}, bf16[3,96,512]{2,1,0:T(8,128)(2,1)}, bf16[3,96,512]{2,1,0:T(8,128)(2,...) custom-call(s32[1]{0:T(128)} %bitcast.1.refs_0_, ...), custom_call_target="tpu_custom_call" | custom-call | flops 1 | bytes 1 | tf_op jit(solution)/shard_map/pallas_call | solution.py:154
  41.1 3.6 %shard_map.87.refs_0_ = f32[4,96,256]{2,1,0:T(8,128)} custom-call(bf16[96,1536]{1,0:T(8,128)(2,1)} %get-tuple-element.104.refs_0_.refs_2_.refs_1_, bf16[96,1536]{1,0:T(8,128)(2,1)} %copy-done, bf16[96,1536]{1,0:T(8,128)(2,1)} %copy-done.1, bf16[96,1536]{1,0:T(8,128)(2,1)} %copy-done.2, bf16[8,256,512]{2,1,0:T(8,128)(2,1)} %refs_3_.3), custom_call_target="tpu_custom_call" | custom-call | flops 1 | bytes 1 | tf_op jit(solution)/shard_map/pallas_call | solution.py:154
  44.8 1.9 collective-permute-done.7.refs_1_
  47.4 2.2 shard_map.88.refs_9_.refs_4_
  49.6 4.1 %collective-permute-start.8 = (bf16[8,256,1024]{2,1,0:T(8,128)(2,1)}, bf16[8,256,1024]{2,1,0:T(8,128)(2,1)}, u32[]{:S(2)}, u32[]{:S(2)}) collective-permute-start(bf16[8,256,1024]{2,1,0:T(8,128)(2,1)} %constant_dynamic-slice_fusion), channel_id=1, source_target_pairs={{0,4},{8,12},{20,16},{28,24},{1,5},{9,13},{21,17},{29,25},{2,6},{1... | collective-permute-start | bytes 12582920 | tf_op jit(solution)/shard_map/ppermute | solution.py:443
  53.7 5.8 %collective-permute-start.12 = (bf16[3,96,512]{2,1,0:T(8,128)(2,1)}, bf16[3,96,512]{2,1,0:T(8,128)(2,1)S(1)}, u32[]{:S(2)}, u32[]{:S(2)}) collective-permute-start(bf16[3,96,512]{2,1,0:T(8,128)(2,1)} %get-tuple-element.118), channel_id=1, source_target_pairs={{0,1},{1,2},{2,3},{3,0},{4,5},{5,6},{6,7},{7,4},{8,9},{9,10},{10,1... | collective-permute-start | bytes 884744 | tf_op jit(solution)/shard_map/ppermute | solution.py:387
  59.4 2.3 %constant_dynamic-slice_fusion.5.refs_1_ = bf16[256,2048]{1,0:T(8,128)(2,1)} fusion(bf16[256,8192]{1,0:T(8,128)(2,1)} %param.6, s32[]{:T(128)S(6)} %select_n.65), kind=kLoop, calls=%fused_computation.21 | loop fusion | bytes 2097156 | tf_op jit(solution)/shard_map/dynamic_slice | solution.py:445
  61.8 2.6 %collective-permute-start.13 = (bf16[3,96,512]{2,1,0:T(8,128)(2,1)S(1)}, bf16[3,96,512]{2,1,0:T(8,128)(2,1)S(1)}, u32[]{:S(2)}, u32[]{:S(2)}) collective-permute-start(bf16[3,96,512]{2,1,0:T(8,128)(2,1)S(1)} %copy-done.36), channel_id=1, source_target_pairs={{0,2},{1,3},{2,0},{3,1},{4,6},{5,7},{6,4},{7,5},{8,10},{9,11},{10,... | collective-permute-start | bytes 884744 | tf_op jit(solution)/shard_map/ppermute | solution.py:387
  64.4 1.6 collective-permute-start.15
  65.9 1.9 collective-permute-start.16
  67.8 1.9 collective-permute-done.12.refs_6_
  69.7 2.8 %collective-permute-start.17 = (bf16[4,96,768]{2,1,0:T(8,128)(2,1)}, bf16[4,96,768]{2,1,0:T(8,128)(2,1)S(1)}, u32[]{:S(2)}, u32[]{:S(2)}) collective-permute-start(bf16[4,96,768]{2,1,0:T(8,128)(2,1)} %shard_map.88.refs_9_.refs_4_), channel_id=1, source_target_pairs={{0,24},{8,16},{16,8},{24,0},{1,25},{9,17},{17,9},{25,1},{2,26},{10... | collective-permute-start | bytes 1769480 | tf_op jit(solution)/shard_map/ppermute | solution.py:384
  72.5 6.1 %shard_map.89 = (f32[256,512]{1,0:T(8,128)}, f32[256,512]{1,0:T(8,128)}, f32[256,512]{1,0:T(8,128)}, f32[256,512]{1,0:T(8,128)}) custom-call(s32[1]{0:T(128)} %bitcast.refs_0_, bf16[256,2048]{1,0:T(8,128)(2,1)} %constant_dynamic-slice_fusion.5.refs_1_, bf16[3,256,1024]{2,1,0:T(8,128)(2,1)} %get-tuple-element.99.refs_2_, ...), custom_call_target="tpu_custom_call" | custom-call | flops 10737418240 | bytes 1 | tf_op jit(solution)/shard_map/pallas_call | solution.py:154
  78.6 3.5 %collective-permute-done.13.refs_7_ = bf16[3,96,512]{2,1,0:T(8,128)(2,1)S(1)} collective-permute-done((bf16[3,96,512]{2,1,0:T(8,128)(2,1)S(1)}, bf16[3,96,512]{2,1,0:T(8,128)(2,1)S(1)}, u32[]{:S(2)}, u32[]{:S(2)}) %collective-permute-start.13) | collective-permute-done | bytes 294944 | tf_op jit(solution)/shard_map/ppermute | solution.py:387
  82.2 11.5 %collective-permute-done.16.refs_11_.refs_6_ = bf16[4,96,768]{2,1,0:T(8,128)(2,1)S(1)} collective-permute-done((bf16[4,96,768]{2,1,0:T(8,128)(2,1)}, bf16[4,96,768]{2,1,0:T(8,128)(2,1)S(1)}, u32[]{:S(2)}, u32[]{:S(2)}) %collective-permute-start.16) | collective-permute-done | bytes 589856 | tf_op jit(solution)/shard_map/ppermute | solution.py:384
  93.7 1.7 collective-permute-start.19
  96.0 5.9 %shard_map.90 = (bf16[8,64,512]{2,1,0:T(8,128)(2,1)}, bf16[8,64,512]{2,1,0:T(8,128)(2,1)}, bf16[8,64,512]{2,1,0:T(8,128)(2,1)}, bf16[8,64,512]{2,1,0:T(8,128)(2,1)}) custom-call(s32[4]{0:T(128)} %pad_add_fusion.1.refs_0_, bf16[96,1536]{1,0:T(8,128)(2,1)} %get-tuple-element.104.refs_0_.refs_2_.refs_1_, bf16[96,1536]{1,0:T(8,128)(2,1)} %copy-done, ...), custom_call_target="tpu_custom_call" | custom-call | flops 1 | bytes 1 | tf_op jit(solution)/shard_map/pallas_call | solution.py:154
  101.9 1.7 collective-permute-start.21
  103.6 1.2 collective-permute-start.22
  105.5 2.5 %collective-permute-done.19.refs_7_ = bf16[3,96,512]{2,1,0:T(8,128)(2,1)S(1)} collective-permute-done((bf16[3,96,512]{2,1,0:T(8,128)(2,1)S(1)}, bf16[3,96,512]{2,1,0:T(8,128)(2,1)S(1)}, u32[]{:S(2)}, u32[]{:S(2)}) %collective-permute-start.19) | collective-permute-done | bytes 294944 | tf_op jit(solution)/shard_map/ppermute | solution.py:387
  108.0 7.0 %shard_map.91.refs_9_ = f32[4,4,96,256]{3,2,1,0:T(8,128)} custom-call(s32[3]{0:T(128)} %add_add_fusion.1.refs_0_, bf16[96,1536]{1,0:T(8,128)(2,1)} %get-tuple-element.104.refs_0_.refs_2_.refs_1_, bf16[96,1536]{1,0:T(8,128)(2,1)} %copy-done, bf16[96,1536]{1,0:T(8,128)(2,1)} %copy-done.1, bf16[96,1536]{1,0:T(8,128)(2,1)} %copy-done.2, ...), custom_call_target="tpu_custom_call" | custom-call | flops 1 | bytes 1 | tf_op jit(solution)/shard_map/pallas_call | solution.py:154
  115.0 1.2 collective-permute-start.23
  116.3 2.1 collective-permute-start.18
  120.2 6.1 %collective-permute-done.18.refs_6_ = bf16[3,96,512]{2,1,0:T(8,128)(2,1)S(1)} collective-permute-done((bf16[3,96,512]{2,1,0:T(8,128)(2,1)S(1)}, bf16[3,96,512]{2,1,0:T(8,128)(2,1)S(1)}, u32[]{:S(2)}, u32[]{:S(2)}) %collective-permute-start.18) | collective-permute-done | bytes 294944 | tf_op jit(solution)/shard_map/ppermute | solution.py:387
  126.3 1.7 collective-permute-start.11
  128.0 2.2 collective-permute-done.23.refs_2_
  131.0 5.8 %collective-permute-start.20 = (bf16[3,96,512]{2,1,0:T(8,128)(2,1)S(1)}, bf16[3,96,512]{2,1,0:T(8,128)(2,1)S(1)}, u32[]{:S(2)}, u32[]{:S(2)}) collective-permute-start(bf16[3,96,512]{2,1,0:T(8,128)(2,1)S(1)} %copy-done.32), channel_id=1, source_target_pairs={{0,3},{1,0},{2,1},{3,2},{4,7},{5,4},{6,5},{7,6},{8,11},{9,8},{10,9... | collective-permute-start | bytes 884744 | tf_op jit(solution)/shard_map/ppermute | solution.py:387
  137.9 4.6 %shard_map.92 = f32[8,64,4096]{2,1,0:T(8,128)} custom-call(s32[4]{0:T(128)} %pad_add_fusion.at, bf16[8,64,512]{2,1,0:T(8,128)(2,1)} %copy-done.18, bf16[8,64,512]{2,1,0:T(8,128)(2,1)} %copy-done.19, bf16[8,64,512]{2,1,0:T(8,128)(2,1)} %copy-done.20, bf16[8,64,512]{2,1,0:T(8,128)(2,1)} %collective-permute-done.24.refs_3_), custom_call_target="tpu_custom_call" | custom-call | flops 1 | bytes 1 | tf_op jit(solution)/shard_map/pallas_call | solution.py:511
  144.2 10.3 %collective-permute-done.11.refs_3_ = f32[256,512]{1,0:T(8,128)S(1)} collective-permute-done((f32[256,512]{1,0:T(8,128)}, f32[256,512]{1,0:T(8,128)S(1)}, u32[]{:S(2)}, u32[]{:S(2)}) %collective-permute-start.11) | collective-permute-done | bytes 524320 | tf_op jit(solution)/shard_map/ppermute | solution.py:384
  154.4 7.4 %shard_map.93 = (f32[4,4,96,128]{3,2,1,0:T(8,128)}, f32[4,4,96,128]{3,2,1,0:T(8,128)}) custom-call(s32[3]{0:T(128)} %add_add_fusion.refs_0_, bf16[96,1536]{1,0:T(8,128)(2,1)} %get-tuple-element.104.refs_0_.refs_2_.refs_1_, bf16[96,1536]{1,0:T(8,128)(2,1)} %copy-done, bf16[96,1536]{1,0:T(8,128)(2,1)} %copy-done.1, bf16[96,1536]{1,0:T(8,128)(2,1)} %copy-done.2, ...), custom_call_target="tpu_custom_call" | custom-call | flops 1 | bytes 1 | tf_op jit(solution)/shard_map/pallas_call | solution.py:154
  161.9 2.5 %collective-permute-done.25 = f32[4,4,96,128]{3,2,1,0:T(8,128)S(1)} collective-permute-done((f32[4,4,96,128]{3,2,1,0:T(8,128)}, f32[4,4,96,128]{3,2,1,0:T(8,128)S(1)}, u32[]{:S(2)}, u32[]{:S(2)}) %collective-permute-start.25) | collective-permute-done | bytes 786464 | tf_op jit(solution)/shard_map/ppermute | solution.py:390
  164.4 1.2 add.145
  165.7 3.3 %collective-permute-start.28 = (f32[4,96,128]{2,1,0:T(8,128)S(1)}, f32[4,96,128]{2,1,0:T(8,128)S(1)}, u32[]{:S(2)}, u32[]{:S(2)}) collective-permute-start(f32[4,96,128]{2,1,0:T(8,128)S(1)} %get-tuple-element.174), channel_id=1, source_target_pairs={{0,24},{8,16},{16,8},{24,0},{1,25},{9,17},{17,9},{25,1},{2,26},{10... | collective-permute-start | bytes 589832 | tf_op jit(solution)/shard_map/ppermute | solution.py:384
  169.7 5.9 %shard_map.96 = (bf16[8,64,512]{2,1,0:T(8,128)(2,1)}, bf16[8,64,512]{2,1,0:T(8,128)(2,1)}, bf16[8,64,512]{2,1,0:T(8,128)(2,1)}, bf16[8,64,512]{2,1,0:T(8,128)(2,1)}) custom-call(s32[4]{0:T(128)} %pad_add_fusion.1.refs_0_, bf16[96,1536]{1,0:T(8,128)(2,1)} %get-tuple-element.104.refs_0_.refs_2_.refs_1_, bf16[96,1536]{1,0:T(8,128)(2,1)} %copy-done, ...), custom_call_target="tpu_custom_call" | custom-call | flops 1 | bytes 1 | tf_op jit(solution)/shard_map/pallas_call | solution.py:154
  175.5 1.7 collective-permute-start.33
  177.2 1.4 collective-permute-start.34
  178.8 1.9 collective-permute-start.29
  182.2 4.1 %shard_map.94 = (bf16[96,512]{1,0:T(8,128)(2,1)}, bf16[96,512]{1,0:T(8,128)(2,1)}, bf16[96,512]{1,0:T(8,128)(2,1)}, bf16[96,512]{1,0:T(8,128)(2,1)}, bf16[4,96,6...) custom-call(s32[5]{0:T(128)} %stack.85.refs_0_, ...), custom_call_target="tpu_custom_call" | custom-call | flops 1 | bytes 1 | tf_op jit(solution)/shard_map/pallas_call | solution.py:154
  186.4 1.8 collective-permute-start.30
  188.1 1.5 collective-permute-start.32
  189.7 2.0 collective-permute-done.30.refs_6_
  191.7 1.9 collective-permute-start.35
  193.6 4.5 %collective-permute-done.31.refs_7_ = bf16[96,512]{1,0:T(8,128)(2,1)S(1)} collective-permute-done((bf16[96,512]{1,0:T(8,128)(2,1)}, bf16[96,512]{1,0:T(8,128)(2,1)S(1)}, u32[]{:S(2)}, u32[]{:S(2)}) %collective-permute-start.31) | collective-permute-done | bytes 98336 | tf_op jit(solution)/shard_map/ppermute | solution.py:387
  198.1 1.7 collective-permute-start.36
  200.5 2.8 %shard_map.95 = bf16[256,512]{1,0:T(8,128)(2,1)} custom-call(f32[256,512]{1,0:T(8,128)} %get-tuple-element.111.refs_0_, f32[256,512]{1,0:T(8,128)} %copy-done.15, f32[256,512]{1,0:T(8,128)} %copy-done.16, f32[256,512]{1,0:T(8,128)} %copy-done.17, bf16[384,256]{1,0:T(8,128)(2,1)} %get-tuple-element.115.refs_4_, bf16[96,512]{1,0:T(8,128)(2,1)} %get-tuple-element.149.refs_5_, ...), custom_call_target="tpu_custom_call" | custom-call | flops 1 | bytes 1 | tf_op jit(solution)/shard_map/pallas_call | solution.py:154
  203.3 1.6 collective-permute-start.37
  204.8 2.0 collective-permute-start.39
  206.8 1.1 convert_dynamic-update-slice_fusion.3
  209.0 1.1 convert_dynamic-update-slice_fusion.1
  210.1 2.4 %collective-permute-done.36 = bf16[8,64,512]{2,1,0:T(8,128)(2,1)S(1)} collective-permute-done((bf16[8,64,512]{2,1,0:T(8,128)(2,1)}, bf16[8,64,512]{2,1,0:T(8,128)(2,1)S(1)}, u32[]{:S(2)}, u32[]{:S(2)}) %collective-permute-start.36) | collective-permute-done | bytes 524320 | tf_op jit(solution)/shard_map/ppermute | solution.py:505
  213.6 2.1 collective-permute-done.37.refs_1_
  215.7 1.2 collective-permute-done.39.refs_3_
  217.6 3.9 %shard_map.97 = f32[8,64,512]{2,1,0:T(8,128)} custom-call(bf16[4,96,64]{2,1,0:T(8,128)(2,1)} %get-tuple-element.162.refs_0_, bf16[4,96,64]{2,1,0:T(8,128)(2,1)} %copy-done.27, bf16[4,96,64]{2,1,0:T(8,128)(2,1)} %copy-done.28, bf16[4,96,64]{2,1,0:T(8,128)(2,1)} %copy-done.29, bf16[4,96,768]{2,1,0:T(8,128)(2,1)} %shard_map.88.refs_9_.refs_4_, ...), custom_call_target="tpu_custom_call" | custom-call | flops 1 | bytes 1 | tf_op jit(solution)/shard_map/pallas_call | solution.py:154
  (120 shorter events, 15.2 us)
Async XLA Ops:
  5.0 16.6 %collective-permute-start = (bf16[272,1024]{1,0:T(8,128)(2,1)}, bf16[272,1024]{1,0:T(8,128)(2,1)S(1)}, u32[]{:S(2)}, u32[]{:S(2)}) collective-permute-start(bf16[272,1024]{1,0:T(8,128)(2,1)} %get-tuple-element.86), channel_id=1, source_target_pairs={{0,8},{8,0},{16,24},{24,16},{1,9},{9,1},{17,25},{25,17},{2,10},{10... | collective-permute-start | bytes 1671176 | tf_op jit(solution)/shard_map/ppermute | solution.py:384
  7.9 27.6 %collective-permute-start.1 = (bf16[272,1024]{1,0:T(8,128)(2,1)}, bf16[272,1024]{1,0:T(8,128)(2,1)S(1)}, u32[]{:S(2)}, u32[]{:S(2)}) collective-permute-start(bf16[272,1024]{1,0:T(8,128)(2,1)} %get-tuple-element.87), channel_id=1, source_target_pairs={{0,16},{8,24},{16,0},{24,8},{1,17},{9,25},{17,1},{25,9},{2,18},{10... | collective-permute-start | bytes 1671176 | tf_op jit(solution)/shard_map/ppermute | solution.py:384
  9.5 26.1 %collective-permute-start.2 = (bf16[272,1024]{1,0:T(8,128)(2,1)S(1)}, bf16[272,1024]{1,0:T(8,128)(2,1)S(1)}, u32[]{:S(2)}, u32[]{:S(2)}) collective-permute-start(bf16[272,1024]{1,0:T(8,128)(2,1)S(1)} %get-tuple-element.88), channel_id=1, source_target_pairs={{0,24},{8,16},{16,8},{24,0},{1,25},{9,17},{17,9},{25,1},{2,26},{10... | collective-permute-start | bytes 1671176 | tf_op jit(solution)/shard_map/ppermute | solution.py:384
  12.2 18.2 %collective-permute-start.3 = (bf16[96,1536]{1,0:T(8,128)(2,1)}, bf16[96,1536]{1,0:T(8,128)(2,1)S(1)}, u32[]{:S(2)}, u32[]{:S(2)}) collective-permute-start(bf16[96,1536]{1,0:T(8,128)(2,1)} %get-tuple-element.91), channel_id=1, source_target_pairs={{0,1},{1,2},{2,3},{3,0},{4,5},{5,6},{6,7},{7,4},{8,9},{9,10},{10,1... | collective-permute-start | bytes 884744 | tf_op jit(solution)/shard_map/ppermute | solution.py:387
  14.3 21.2 %collective-permute-start.4 = (bf16[96,1536]{1,0:T(8,128)(2,1)}, bf16[96,1536]{1,0:T(8,128)(2,1)S(1)}, u32[]{:S(2)}, u32[]{:S(2)}) collective-permute-start(bf16[96,1536]{1,0:T(8,128)(2,1)} %get-tuple-element.92), channel_id=1, source_target_pairs={{0,2},{1,3},{2,0},{3,1},{4,6},{5,7},{6,4},{7,5},{8,10},{9,11},{10,... | collective-permute-start | bytes 884744 | tf_op jit(solution)/shard_map/ppermute | solution.py:387
  21.6 8.8 %copy-start.12 = (bf16[272,1024]{1,0:T(8,128)(2,1)}, bf16[272,1024]{1,0:T(8,128)(2,1)S(1)}, u32[]{:S(2)}) copy-start(bf16[272,1024]{1,0:T(8,128)(2,1)S(1)} %collective-permute-done.refs_1_) | copy-start | bytes 1671172
  21.6 14.7 %collective-permute-start.5 = (bf16[96,1536]{1,0:T(8,128)(2,1)}, bf16[96,1536]{1,0:T(8,128)(2,1)S(1)}, u32[]{:S(2)}, u32[]{:S(2)}) collective-permute-start(bf16[96,1536]{1,0:T(8,128)(2,1)} %get-tuple-element.94), channel_id=1, source_target_pairs={{0,3},{1,0},{2,1},{3,2},{4,7},{5,4},{6,5},{7,6},{8,11},{9,8},{10,9... | collective-permute-start | bytes 884744 | tf_op jit(solution)/shard_map/ppermute | solution.py:387
  30.4 10.7 %copy-start = (bf16[96,1536]{1,0:T(8,128)(2,1)}, bf16[96,1536]{1,0:T(8,128)(2,1)S(1)}, u32[]{:S(2)}) copy-start(bf16[96,1536]{1,0:T(8,128)(2,1)S(1)} %collective-permute-done.3.refs_1_.refs_3_.refs_2_) | copy-start | bytes 884740
  35.5 5.6 %copy-start.1 = (bf16[96,1536]{1,0:T(8,128)(2,1)}, bf16[96,1536]{1,0:T(8,128)(2,1)S(1)}, u32[]{:S(2)}) copy-start(bf16[96,1536]{1,0:T(8,128)(2,1)S(1)} %collective-permute-done.4.refs_2_.refs_4_.refs_3_) | copy-start | bytes 884740
  36.5 4.6 %copy-start.2 = (bf16[96,1536]{1,0:T(8,128)(2,1)}, bf16[96,1536]{1,0:T(8,128)(2,1)S(1)}, u32[]{:S(2)}) copy-start(bf16[96,1536]{1,0:T(8,128)(2,1)S(1)} %collective-permute-done.5.refs_3_.refs_5_.refs_4_) | copy-start | bytes 884740
  41.1 12.6 %copy-start.30 = (bf16[3,256,1024]{2,1,0:T(8,128)(2,1)S(1)}, bf16[3,256,1024]{2,1,0:T(8,128)(2,1)}, u32[]{:S(2)}) copy-start(bf16[3,256,1024]{2,1,0:T(8,128)(2,1)} %get-tuple-element.99.refs_2_) | copy-start | bytes 4718596
  41.1 20.7 %copy-start.36 = (bf16[3,96,512]{2,1,0:T(8,128)(2,1)S(1)}, bf16[3,96,512]{2,1,0:T(8,128)(2,1)}, u32[]{:S(2)}) copy-start(bf16[3,96,512]{2,1,0:T(8,128)(2,1)} %get-tuple-element.119) | copy-start | bytes 884740
  41.1 23.3 %copy-start.35 = (bf16[3,96,512]{2,1,0:T(8,128)(2,1)S(1)}, bf16[3,96,512]{2,1,0:T(8,128)(2,1)}, u32[]{:S(2)}) copy-start(bf16[3,96,512]{2,1,0:T(8,128)(2,1)} %get-tuple-element.120) | copy-start | bytes 884740
  44.7 2.0 collective-permute-start.7
  49.6 16.3 %collective-permute-start.8 = (bf16[8,256,1024]{2,1,0:T(8,128)(2,1)}, bf16[8,256,1024]{2,1,0:T(8,128)(2,1)}, u32[]{:S(2)}, u32[]{:S(2)}) collective-permute-start(bf16[8,256,1024]{2,1,0:T(8,128)(2,1)} %constant_dynamic-slice_fusion), channel_id=1, source_target_pairs={{0,4},{8,12},{20,16},{28,24},{1,5},{9,13},{21,17},{29,25},{2,6},{1... | collective-permute-start | bytes 12582920 | tf_op jit(solution)/shard_map/ppermute | solution.py:443
  53.7 10.7 %collective-permute-start.6 = (bf16[3,256,1024]{2,1,0:T(8,128)(2,1)S(1)}, bf16[3,256,1024]{2,1,0:T(8,128)(2,1)}, u32[]{:S(2)}, u32[]{:S(2)}) collective-permute-start(bf16[3,256,1024]{2,1,0:T(8,128)(2,1)S(1)} %copy-done.30), channel_id=1, source_target_pairs={{0,4},{4,0},{1,5},{5,1},{2,6},{6,2},{3,7},{7,3},{8,12},{12,8},{9,1... | collective-permute-start | bytes 4718600 | tf_op jit(solution)/shard_map/ppermute | solution.py:390
  53.7 16.0 %collective-permute-start.12 = (bf16[3,96,512]{2,1,0:T(8,128)(2,1)}, bf16[3,96,512]{2,1,0:T(8,128)(2,1)S(1)}, u32[]{:S(2)}, u32[]{:S(2)}) collective-permute-start(bf16[3,96,512]{2,1,0:T(8,128)(2,1)} %get-tuple-element.118), channel_id=1, source_target_pairs={{0,1},{1,2},{2,3},{3,0},{4,5},{5,6},{6,7},{7,4},{8,9},{9,10},{10,1... | collective-permute-start | bytes 884744 | tf_op jit(solution)/shard_map/ppermute | solution.py:387
  61.8 20.4 %collective-permute-start.13 = (bf16[3,96,512]{2,1,0:T(8,128)(2,1)S(1)}, bf16[3,96,512]{2,1,0:T(8,128)(2,1)S(1)}, u32[]{:S(2)}, u32[]{:S(2)}) collective-permute-start(bf16[3,96,512]{2,1,0:T(8,128)(2,1)S(1)} %copy-done.36), channel_id=1, source_target_pairs={{0,2},{1,3},{2,0},{3,1},{4,6},{5,7},{6,4},{7,5},{8,10},{9,11},{10,... | collective-permute-start | bytes 884744 | tf_op jit(solution)/shard_map/ppermute | solution.py:387
  64.4 17.8 %collective-permute-start.14 = (bf16[3,96,512]{2,1,0:T(8,128)(2,1)S(1)}, bf16[3,96,512]{2,1,0:T(8,128)(2,1)S(1)}, u32[]{:S(2)}, u32[]{:S(2)}) collective-permute-start(bf16[3,96,512]{2,1,0:T(8,128)(2,1)S(1)} %copy-done.35), channel_id=1, source_target_pairs={{0,3},{1,0},{2,1},{3,2},{4,7},{5,4},{6,5},{7,6},{8,11},{9,8},{10,9... | collective-permute-start | bytes 884744 | tf_op jit(solution)/shard_map/ppermute | solution.py:387
  64.4 17.8 %collective-permute-start.15 = (bf16[4,96,768]{2,1,0:T(8,128)(2,1)}, bf16[4,96,768]{2,1,0:T(8,128)(2,1)S(1)}, u32[]{:S(2)}, u32[]{:S(2)}) collective-permute-start(bf16[4,96,768]{2,1,0:T(8,128)(2,1)} %shard_map.88.refs_9_.refs_4_), channel_id=1, source_target_pairs={{0,8},{8,0},{16,24},{24,16},{1,9},{9,1},{17,25},{25,17},{2,10},{10... | collective-permute-start | bytes 1769480 | tf_op jit(solution)/shard_map/ppermute | solution.py:384
  65.9 27.8 %collective-permute-start.16 = (bf16[4,96,768]{2,1,0:T(8,128)(2,1)}, bf16[4,96,768]{2,1,0:T(8,128)(2,1)S(1)}, u32[]{:S(2)}, u32[]{:S(2)}) collective-permute-start(bf16[4,96,768]{2,1,0:T(8,128)(2,1)} %shard_map.88.refs_9_.refs_4_), channel_id=1, source_target_pairs={{0,16},{8,24},{16,0},{24,8},{1,17},{9,25},{17,1},{25,9},{2,18},{10... | collective-permute-start | bytes 1769480 | tf_op jit(solution)/shard_map/ppermute | solution.py:384
  69.7 8.9 %copy-start.9 = (bf16[3,96,512]{2,1,0:T(8,128)(2,1)}, bf16[3,96,512]{2,1,0:T(8,128)(2,1)S(1)}, u32[]{:S(2)}) copy-start(bf16[3,96,512]{2,1,0:T(8,128)(2,1)S(1)} %collective-permute-done.12.refs_6_) | copy-start | bytes 884740
  69.7 24.0 %collective-permute-start.17 = (bf16[4,96,768]{2,1,0:T(8,128)(2,1)}, bf16[4,96,768]{2,1,0:T(8,128)(2,1)S(1)}, u32[]{:S(2)}, u32[]{:S(2)}) collective-permute-start(bf16[4,96,768]{2,1,0:T(8,128)(2,1)} %shard_map.88.refs_9_.refs_4_), channel_id=1, source_target_pairs={{0,24},{8,16},{16,8},{24,0},{1,25},{9,17},{17,9},{25,1},{2,26},{10... | collective-permute-start | bytes 1769480 | tf_op jit(solution)/shard_map/ppermute | solution.py:384
  72.5 21.2 %copy-start.34 = (bf16[3,96,512]{2,1,0:T(8,128)(2,1)S(1)}, bf16[3,96,512]{2,1,0:T(8,128)(2,1)}, u32[]{:S(2)}) copy-start(bf16[3,96,512]{2,1,0:T(8,128)(2,1)} %get-tuple-element.125) | copy-start | bytes 884740
  82.1 13.9 %copy-start.10 = (bf16[3,96,512]{2,1,0:T(8,128)(2,1)}, bf16[3,96,512]{2,1,0:T(8,128)(2,1)S(1)}, u32[]{:S(2)}) copy-start(bf16[3,96,512]{2,1,0:T(8,128)(2,1)S(1)} %collective-permute-done.13.refs_7_) | copy-start | bytes 884740
  82.1 13.9 %copy-start.11 = (bf16[3,96,512]{2,1,0:T(8,128)(2,1)}, bf16[3,96,512]{2,1,0:T(8,128)(2,1)S(1)}, u32[]{:S(2)}) copy-start(bf16[3,96,512]{2,1,0:T(8,128)(2,1)S(1)} %collective-permute-done.14.refs_8_) | copy-start | bytes 884740
  82.1 13.9 %copy-start.3 = (bf16[4,96,768]{2,1,0:T(8,128)(2,1)}, bf16[4,96,768]{2,1,0:T(8,128)(2,1)S(1)}, u32[]{:S(2)}) copy-start(bf16[4,96,768]{2,1,0:T(8,128)(2,1)S(1)} %collective-permute-done.15.refs_10_.refs_5_) | copy-start | bytes 1769476
  93.7 14.3 %collective-permute-start.19 = (bf16[3,96,512]{2,1,0:T(8,128)(2,1)S(1)}, bf16[3,96,512]{2,1,0:T(8,128)(2,1)S(1)}, u32[]{:S(2)}, u32[]{:S(2)}) collective-permute-start(bf16[3,96,512]{2,1,0:T(8,128)(2,1)S(1)} %copy-done.34), channel_id=1, source_target_pairs={{0,2},{1,3},{2,0},{3,1},{4,6},{5,7},{6,4},{7,5},{8,10},{9,11},{10,... | collective-permute-start | bytes 884744 | tf_op jit(solution)/shard_map/ppermute | solution.py:387
  101.9 17.5 %collective-permute-start.21 = (bf16[8,64,512]{2,1,0:T(8,128)(2,1)}, bf16[8,64,512]{2,1,0:T(8,128)(2,1)S(1)}, u32[]{:S(2)}, u32[]{:S(2)}) collective-permute-start(bf16[8,64,512]{2,1,0:T(8,128)(2,1)} %get-tuple-element.128), channel_id=1, source_target_pairs={{0,0},{4,16},{8,8},{12,24},{16,4},{20,20},{24,12},{28,28},{1,1},{5... | collective-permute-start | bytes 1572872 | tf_op jit(solution)/shard_map/ppermute | solution.py:505
  103.6 16.3 %collective-permute-start.22 = (bf16[8,64,512]{2,1,0:T(8,128)(2,1)}, bf16[8,64,512]{2,1,0:T(8,128)(2,1)S(1)}, u32[]{:S(2)}, u32[]{:S(2)}) collective-permute-start(bf16[8,64,512]{2,1,0:T(8,128)(2,1)} %get-tuple-element.129), channel_id=1, source_target_pairs={{0,8},{4,24},{8,0},{12,16},{16,12},{20,28},{24,4},{28,20},{1,9},{5... | collective-permute-start | bytes 1572872 | tf_op jit(solution)/shard_map/ppermute | solution.py:505
  108.0 7.0 %copy-start.6 = (bf16[3,96,512]{2,1,0:T(8,128)(2,1)}, bf16[3,96,512]{2,1,0:T(8,128)(2,1)S(1)}, u32[]{:S(2)}) copy-start(bf16[3,96,512]{2,1,0:T(8,128)(2,1)S(1)} %collective-permute-done.19.refs_7_) | copy-start | bytes 884740
  108.0 7.0 %copy-start.31 = (bf16[8,64,512]{2,1,0:T(8,128)(2,1)S(1)}, bf16[8,64,512]{2,1,0:T(8,128)(2,1)}, u32[]{:S(2)}) copy-start(bf16[8,64,512]{2,1,0:T(8,128)(2,1)} %get-tuple-element.136) | copy-start | bytes 1572868
  108.0 8.3 %copy-start.33 = (bf16[3,96,512]{2,1,0:T(8,128)(2,1)S(1)}, bf16[3,96,512]{2,1,0:T(8,128)(2,1)}, u32[]{:S(2)}) copy-start(bf16[3,96,512]{2,1,0:T(8,128)(2,1)} %get-tuple-element.123) | copy-start | bytes 884740
  108.0 22.9 %copy-start.32 = (bf16[3,96,512]{2,1,0:T(8,128)(2,1)S(1)}, bf16[3,96,512]{2,1,0:T(8,128)(2,1)}, u32[]{:S(2)}) copy-start(bf16[3,96,512]{2,1,0:T(8,128)(2,1)} %get-tuple-element.127) | copy-start | bytes 884740
  115.0 15.1 %collective-permute-start.23 = (bf16[8,64,512]{2,1,0:T(8,128)(2,1)S(1)}, bf16[8,64,512]{2,1,0:T(8,128)(2,1)S(1)}, u32[]{:S(2)}, u32[]{:S(2)}) collective-permute-start(bf16[8,64,512]{2,1,0:T(8,128)(2,1)S(1)} %copy-done.31), channel_id=1, source_target_pairs={{0,16},{4,0},{8,24},{12,8},{16,20},{20,4},{24,28},{28,12},{1,17},{... | collective-permute-start | bytes 1572872 | tf_op jit(solution)/shard_map/ppermute | solution.py:505
  116.3 10.0 %collective-permute-start.18 = (bf16[3,96,512]{2,1,0:T(8,128)(2,1)S(1)}, bf16[3,96,512]{2,1,0:T(8,128)(2,1)S(1)}, u32[]{:S(2)}, u32[]{:S(2)}) collective-permute-start(bf16[3,96,512]{2,1,0:T(8,128)(2,1)S(1)} %copy-done.33), channel_id=1, source_target_pairs={{0,1},{1,2},{2,3},{3,0},{4,5},{5,6},{6,7},{7,4},{8,9},{9,10},{10,1... | collective-permute-start | bytes 884744 | tf_op jit(solution)/shard_map/ppermute | solution.py:387
  118.4 19.5 %collective-permute-start.24 = (bf16[8,64,512]{2,1,0:T(8,128)(2,1)}, bf16[8,64,512]{2,1,0:T(8,128)(2,1)}, u32[]{:S(2)}, u32[]{:S(2)}) collective-permute-start(bf16[8,64,512]{2,1,0:T(8,128)(2,1)} %get-tuple-element.137), channel_id=1, source_target_pairs={{0,24},{4,8},{8,16},{12,0},{16,28},{20,12},{24,20},{28,4},{1,25},{... | collective-permute-start | bytes 1572872 | tf_op jit(solution)/shard_map/ppermute | solution.py:505
  119.4 18.5 %copy-start.18 = (bf16[8,64,512]{2,1,0:T(8,128)(2,1)}, bf16[8,64,512]{2,1,0:T(8,128)(2,1)S(1)}, u32[]{:S(2)}) copy-start(bf16[8,64,512]{2,1,0:T(8,128)(2,1)S(1)} %collective-permute-done.21.refs_0_) | copy-start | bytes 1572868
  119.4 24.7 %collective-permute-start.9 = (f32[256,512]{1,0:T(8,128)}, f32[256,512]{1,0:T(8,128)S(1)}, u32[]{:S(2)}, u32[]{:S(2)}) collective-permute-start(f32[256,512]{1,0:T(8,128)} %get-tuple-element.112), channel_id=1, source_target_pairs={{0,8},{8,0},{16,24},{24,16},{1,9},{9,1},{17,25},{25,17},{2,10},{10... | collective-permute-start | bytes 1572872 | tf_op jit(solution)/shard_map/ppermute | solution.py:384
  120.0 8.0 %copy-start.19 = (bf16[8,64,512]{2,1,0:T(8,128)(2,1)}, bf16[8,64,512]{2,1,0:T(8,128)(2,1)S(1)}, u32[]{:S(2)}) copy-start(bf16[8,64,512]{2,1,0:T(8,128)(2,1)S(1)} %collective-permute-done.22.refs_1_) | copy-start | bytes 1572868
  120.0 24.2 %collective-permute-start.10 = (f32[256,512]{1,0:T(8,128)}, f32[256,512]{1,0:T(8,128)S(1)}, u32[]{:S(2)}, u32[]{:S(2)}) collective-permute-start(f32[256,512]{1,0:T(8,128)} %get-tuple-element.113), channel_id=1, source_target_pairs={{0,16},{8,24},{16,0},{24,8},{1,17},{9,25},{17,1},{25,9},{2,18},{10... | collective-permute-start | bytes 1572872 | tf_op jit(solution)/shard_map/ppermute | solution.py:384
  126.3 16.3 %copy-start.7 = (bf16[3,96,512]{2,1,0:T(8,128)(2,1)}, bf16[3,96,512]{2,1,0:T(8,128)(2,1)S(1)}, u32[]{:S(2)}) copy-start(bf16[3,96,512]{2,1,0:T(8,128)(2,1)S(1)} %collective-permute-done.18.refs_6_) | copy-start | bytes 884740
  126.3 28.2 %collective-permute-start.11 = (f32[256,512]{1,0:T(8,128)}, f32[256,512]{1,0:T(8,128)S(1)}, u32[]{:S(2)}, u32[]{:S(2)}) collective-permute-start(f32[256,512]{1,0:T(8,128)} %get-tuple-element.114), channel_id=1, source_target_pairs={{0,24},{8,16},{16,8},{24,0},{1,25},{9,17},{17,9},{25,1},{2,26},{10... | collective-permute-start | bytes 1572872 | tf_op jit(solution)/shard_map/ppermute | solution.py:384
  131.0 12.3 %collective-permute-start.20 = (bf16[3,96,512]{2,1,0:T(8,128)(2,1)S(1)}, bf16[3,96,512]{2,1,0:T(8,128)(2,1)S(1)}, u32[]{:S(2)}, u32[]{:S(2)}) collective-permute-start(bf16[3,96,512]{2,1,0:T(8,128)(2,1)S(1)} %copy-done.32), channel_id=1, source_target_pairs={{0,3},{1,0},{2,1},{3,2},{4,7},{5,4},{6,5},{7,6},{8,11},{9,8},{10,9... | collective-permute-start | bytes 884744 | tf_op jit(solution)/shard_map/ppermute | solution.py:387
  143.3 11.1 %copy-start.8 = (bf16[3,96,512]{2,1,0:T(8,128)(2,1)}, bf16[3,96,512]{2,1,0:T(8,128)(2,1)S(1)}, u32[]{:S(2)}) copy-start(bf16[3,96,512]{2,1,0:T(8,128)(2,1)S(1)} %collective-permute-done.20.refs_8_) | copy-start | bytes 884740
  144.2 17.7 %copy-start.15 = (f32[256,512]{1,0:T(8,128)}, f32[256,512]{1,0:T(8,128)S(1)}, u32[]{:S(2)}) copy-start(f32[256,512]{1,0:T(8,128)S(1)} %collective-permute-done.9.refs_1_) | copy-start | bytes 1572868
  144.2 17.7 %copy-start.16 = (f32[256,512]{1,0:T(8,128)}, f32[256,512]{1,0:T(8,128)S(1)}, u32[]{:S(2)}) copy-start(f32[256,512]{1,0:T(8,128)S(1)} %collective-permute-done.10.refs_2_) | copy-start | bytes 1572868
  154.4 7.4 %copy-start.17 = (f32[256,512]{1,0:T(8,128)}, f32[256,512]{1,0:T(8,128)S(1)}, u32[]{:S(2)}) copy-start(f32[256,512]{1,0:T(8,128)S(1)} %collective-permute-done.11.refs_3_) | copy-start | bytes 1572868
  161.9 2.6 %collective-permute-start.25 = (f32[4,4,96,128]{3,2,1,0:T(8,128)}, f32[4,4,96,128]{3,2,1,0:T(8,128)S(1)}, u32[]{:S(2)}, u32[]{:S(2)}) collective-permute-start(f32[4,4,96,128]{3,2,1,0:T(8,128)} %get-tuple-element.147), channel_id=1, source_target_pairs={{0,4},{4,0},{1,5},{5,1},{2,6},{6,2},{3,7},{7,3},{8,12},{12,8},{9,1... | collective-permute-start | bytes 2359304 | tf_op jit(solution)/shard_map/ppermute | solution.py:390
  165.7 12.9 %collective-permute-start.28 = (f32[4,96,128]{2,1,0:T(8,128)S(1)}, f32[4,96,128]{2,1,0:T(8,128)S(1)}, u32[]{:S(2)}, u32[]{:S(2)}) collective-permute-start(f32[4,96,128]{2,1,0:T(8,128)S(1)} %get-tuple-element.174), channel_id=1, source_target_pairs={{0,24},{8,16},{16,8},{24,0},{1,25},{9,17},{17,9},{25,1},{2,26},{10... | collective-permute-start | bytes 589832 | tf_op jit(solution)/shard_map/ppermute | solution.py:384
  169.0 9.6 %collective-permute-start.27 = (f32[4,96,128]{2,1,0:T(8,128)S(1)}, f32[4,96,128]{2,1,0:T(8,128)S(1)}, u32[]{:S(2)}, u32[]{:S(2)}) collective-permute-start(f32[4,96,128]{2,1,0:T(8,128)S(1)} %get-tuple-element.175), channel_id=1, source_target_pairs={{0,16},{8,24},{16,0},{24,8},{1,17},{9,25},{17,1},{25,9},{2,18},{10... | collective-permute-start | bytes 589832 | tf_op jit(solution)/shard_map/ppermute | solution.py:384
  169.0 9.7 %collective-permute-start.26 = (f32[4,96,128]{2,1,0:T(8,128)S(1)}, f32[4,96,128]{2,1,0:T(8,128)S(1)}, u32[]{:S(2)}, u32[]{:S(2)}) collective-permute-start(f32[4,96,128]{2,1,0:T(8,128)S(1)} %get-tuple-element.173), channel_id=1, source_target_pairs={{0,8},{8,0},{16,24},{24,16},{1,9},{9,1},{17,25},{25,17},{2,10},{10... | collective-permute-start | bytes 589832 | tf_op jit(solution)/shard_map/ppermute | solution.py:384
  175.5 27.7 %collective-permute-start.33 = (bf16[8,64,512]{2,1,0:T(8,128)(2,1)}, bf16[8,64,512]{2,1,0:T(8,128)(2,1)S(1)}, u32[]{:S(2)}, u32[]{:S(2)}) collective-permute-start(bf16[8,64,512]{2,1,0:T(8,128)(2,1)} %get-tuple-element.157), channel_id=1, source_target_pairs={{0,0},{4,16},{8,8},{12,24},{16,4},{20,20},{24,12},{28,28},{1,1},{5... | collective-permute-start | bytes 1572872 | tf_op jit(solution)/shard_map/ppermute | solution.py:505
  177.2 26.0 %collective-permute-start.34 = (bf16[8,64,512]{2,1,0:T(8,128)(2,1)}, bf16[8,64,512]{2,1,0:T(8,128)(2,1)S(1)}, u32[]{:S(2)}, u32[]{:S(2)}) collective-permute-start(bf16[8,64,512]{2,1,0:T(8,128)(2,1)} %get-tuple-element.158), channel_id=1, source_target_pairs={{0,8},{4,24},{8,0},{12,16},{16,12},{20,28},{24,4},{28,20},{1,9},{5... | collective-permute-start | bytes 1572872 | tf_op jit(solution)/shard_map/ppermute | solution.py:505
  178.8 2.8 %collective-permute-start.29 = (bf16[4,96,128]{2,1,0:T(8,128)(2,1)S(1)}, bf16[4,96,128]{2,1,0:T(8,128)(2,1)S(1)}, u32[]{:S(2)}, u32[]{:S(2)}) collective-permute-start(bf16[4,96,128]{2,1,0:T(8,128)(2,1)S(1)} %fusion.6.refs_1_), channel_id=1, source_target_pairs={{0,4},{4,0},{1,5},{5,1},{2,6},{6,2},{3,7},{7,3},{8,12},{12,8},{9,1... | collective-permute-start | bytes 294920 | tf_op jit(solution)/shard_map/ppermute | solution.py:390
  186.4 5.3 %collective-permute-start.30 = (bf16[96,512]{1,0:T(8,128)(2,1)}, bf16[96,512]{1,0:T(8,128)(2,1)S(1)}, u32[]{:S(2)}, u32[]{:S(2)}) collective-permute-start(bf16[96,512]{1,0:T(8,128)(2,1)} %get-tuple-element.150), channel_id=1, source_target_pairs={{0,3},{1,0},{2,1},{3,2},{4,7},{5,4},{6,5},{7,6},{8,11},{9,8},{10,9... | collective-permute-start | bytes 294920 | tf_op jit(solution)/shard_map/ppermute | solution.py:387
  188.1 10.0 %collective-permute-start.31 = (bf16[96,512]{1,0:T(8,128)(2,1)}, bf16[96,512]{1,0:T(8,128)(2,1)S(1)}, u32[]{:S(2)}, u32[]{:S(2)}) collective-permute-start(bf16[96,512]{1,0:T(8,128)(2,1)} %get-tuple-element.151), channel_id=1, source_target_pairs={{0,2},{1,3},{2,0},{3,1},{4,6},{5,7},{6,4},{7,5},{8,10},{9,11},{10,... | collective-permute-start | bytes 294920 | tf_op jit(solution)/shard_map/ppermute | solution.py:387
  188.1 11.7 %collective-permute-start.32 = (bf16[96,512]{1,0:T(8,128)(2,1)}, bf16[96,512]{1,0:T(8,128)(2,1)S(1)}, u32[]{:S(2)}, u32[]{:S(2)}) collective-permute-start(bf16[96,512]{1,0:T(8,128)(2,1)} %get-tuple-element.152), channel_id=1, source_target_pairs={{0,1},{1,2},{2,3},{3,0},{4,5},{5,6},{6,7},{7,4},{8,9},{9,10},{10,1... | collective-permute-start | bytes 294920 | tf_op jit(solution)/shard_map/ppermute | solution.py:387
  191.7 8.1 %copy-start.23 = (bf16[96,512]{1,0:T(8,128)(2,1)}, bf16[96,512]{1,0:T(8,128)(2,1)S(1)}, u32[]{:S(2)}) copy-start(bf16[96,512]{1,0:T(8,128)(2,1)S(1)} %collective-permute-done.30.refs_6_) | copy-start | bytes 294916
  191.7 17.3 %collective-permute-start.35 = (bf16[8,64,512]{2,1,0:T(8,128)(2,1)}, bf16[8,64,512]{2,1,0:T(8,128)(2,1)S(1)}, u32[]{:S(2)}, u32[]{:S(2)}) collective-permute-start(bf16[8,64,512]{2,1,0:T(8,128)(2,1)} %get-tuple-element.159), channel_id=1, source_target_pairs={{0,16},{4,0},{8,24},{12,8},{16,20},{20,4},{24,28},{28,12},{1,17},{... | collective-permute-start | bytes 1572872 | tf_op jit(solution)/shard_map/ppermute | solution.py:505
  198.1 14.4 %collective-permute-start.36 = (bf16[8,64,512]{2,1,0:T(8,128)(2,1)}, bf16[8,64,512]{2,1,0:T(8,128)(2,1)S(1)}, u32[]{:S(2)}, u32[]{:S(2)}) collective-permute-start(bf16[8,64,512]{2,1,0:T(8,128)(2,1)} %get-tuple-element.160), channel_id=1, source_target_pairs={{0,24},{4,8},{8,16},{12,0},{16,28},{20,12},{24,20},{28,4},{1,25},{... | collective-permute-start | bytes 1572872 | tf_op jit(solution)/shard_map/ppermute | solution.py:505
  203.3 12.5 %collective-permute-start.37 = (bf16[4,96,64]{2,1,0:T(8,128)(2,1)}, bf16[4,96,64]{2,1,0:T(8,128)(2,1)S(1)}, u32[]{:S(2)}, u32[]{:S(2)}) collective-permute-start(bf16[4,96,64]{2,1,0:T(8,128)(2,1)} %get-tuple-element.164), channel_id=1, source_target_pairs={{0,8},{8,0},{16,24},{24,16},{1,9},{9,1},{17,25},{25,17},{2,10},{10... | collective-permute-start | bytes 147464 | tf_op jit(solution)/shard_map/ppermute | solution.py:384
  204.8 10.9 %collective-permute-start.38 = (bf16[4,96,64]{2,1,0:T(8,128)(2,1)}, bf16[4,96,64]{2,1,0:T(8,128)(2,1)S(1)}, u32[]{:S(2)}, u32[]{:S(2)}) collective-permute-start(bf16[4,96,64]{2,1,0:T(8,128)(2,1)} %get-tuple-element.166), channel_id=1, source_target_pairs={{0,16},{8,24},{16,0},{24,8},{1,17},{9,25},{17,1},{25,9},{2,18},{10... | collective-permute-start | bytes 147464 | tf_op jit(solution)/shard_map/ppermute | solution.py:384
  204.8 12.2 %collective-permute-start.39 = (bf16[4,96,64]{2,1,0:T(8,128)(2,1)}, bf16[4,96,64]{2,1,0:T(8,128)(2,1)S(1)}, u32[]{:S(2)}, u32[]{:S(2)}) collective-permute-start(bf16[4,96,64]{2,1,0:T(8,128)(2,1)} %get-tuple-element.168), channel_id=1, source_target_pairs={{0,24},{8,16},{16,8},{24,0},{1,25},{9,17},{17,9},{25,1},{2,26},{10... | collective-permute-start | bytes 147464 | tf_op jit(solution)/shard_map/ppermute | solution.py:384
  (13 other events, 17.0 us)

commit v6 on v5

--- a/solution.py
+++ b/solution.py
@@ -219,10 +219,9 @@
 
 
 def others_kernel(fsdp, ad, slots, dom_total, at, *refs):
-    x_refs, outs, plain = refs[: fsdp - 1], refs[fsdp - 1 : -1], refs[-1]
+    x_refs, outs = refs[: fsdp - 1], refs[fsdp - 1 :]
     for kf in range(fsdp - 1):
         rows = x_refs[kf].shape[0] - 16
-        plain[kf] = x_refs[kf][:rows, :]
         dom = x_refs[kf][rows:, :rows].astype(F32).astype(jnp.int32)[:1]
         hot = one_hot(dom, at[0], slots, ad, dom_total)
         moved = dot(hot, x_refs[kf][:rows, :], ((1,), (0,))).astype(BF16)
@@ -349,14 +348,16 @@
     out[...] = (total + dot(hot[...], delta, ((0,), (0,)))).astype(BF16)
 
 
-def base_kernel(fsdp, at, own, mine, got, weight, *outs):
-    kt = mine.shape[2]
+def base_kernel(fsdp, at, own, *refs):
+    mine, got = refs[: fsdp - 1], refs[fsdp - 1 : 2 * fsdp - 2]
+    weight, outs = refs[2 * fsdp - 2], refs[2 * fsdp - 1 :]
+    rows, kt = own.shape[0], mine[0].shape[1]
     outs[0][...] = dot(own[...], weight[...], ((1,), (0,)))
     w_mine = weight[pl.ds(pl.multiple_of(at[0] * kt, kt), kt), :]
     w_got = weight[pl.ds(pl.multiple_of((1 - at[0]) * kt, kt), kt), :]
     for k in range(1, fsdp):
-        total = dot(mine[k - 1], w_mine, ((1,), (0,)))
-        outs[k][...] = total + dot(got[k - 1], w_got, ((1,), (0,)))
+        total = dot(mine[k - 1][:rows, :], w_mine, ((1,), (0,)))
+        outs[k][...] = total + dot(got[k - 1][:rows, :], w_got, ((1,), (0,)))
 
 
 def column_body(
@@ -412,53 +413,53 @@
         [(v, None) for v in (domain.T, x_in[0], layer_output_gradient)],
         at=numbers(a),
     )
-    held = after(adapter_down_weight, *sends)
+    held = after((adapter_down_weight, input_rows), *sends)
     sends[-1] = after(sends[-1], x_in[1])
     own = [over_a(v, ka) for ka, v in enumerate(sends)]
 
-    down_other = lax.dynamic_slice_in_dim(held, (fx * 2 + 1 - t) * kt, kt, 2)
+    down_other = lax.dynamic_slice_in_dim(held[0], (fx * 2 + 1 - t) * kt, kt, 2)
     pairs = [(i * 2 + i // 2, i * 2 + 1 - i // 2) for i in range(fsdp)]
 
-    ready, own, down_other = lax.optimization_barrier((x_in[1:], own, down_other))
-    *sends, x_plain = call(
+    x_other = [swap(v) for v in x_in[1:]]
+    x_chip = lax.dynamic_slice_in_dim(held[1], f * kf_width, kf_width, 1)
+    x_in, x_other, own, down_other, x_chip = lax.optimization_barrier(
+        (x_in, x_other, own, down_other, x_chip)
+    )
+    base = call(
+        functools.partial(base_kernel, fsdp),
+        [((rows, vloc), F32)] * fsdp,
+        [(v, None) for v in (x_chip, *x_in[1:], *x_other, value_weight_frozen)],
+        at=numbers(t),
+    )
+    ready = after(x_in[1:], base[0])
+    base = [over_f(v, k) for k, v in enumerate(base)]
+
+    sends = call(
         functools.partial(others_kernel, fsdp, ad, slots, ad * dloc),
-        [((fsdp - 1, slots, cw), BF16)] * (CHUNKS * ad) + [((fsdp - 1, rows, kt), BF16)],
+        [((fsdp - 1, slots, cw), BF16)] * (CHUNKS * ad),
         [(v, None) for v in ready],
         at=numbers(a),
     )
     x_routed = [[over_a(v, ka) for ka, v in enumerate(sends[:ad])]]
 
-    dy = [(v, (kt, vloc)) for v in after(own, x_plain)]
+    dy = [(v, (kt, vloc)) for v in after(own, *sends)]
     (back,) = call(
         functools.partial(back_kernel, ad, gslots),
         [((ad, slots, rank), F32)],
         [*dy, (adapter_up_weight, None)],
     )
+    back, back_got = after((back, swap(back)), base[1], base[2], x_routed[0][2])
     (both,) = call(
         functools.partial(both_kernel, ad),
         [((ad, slots, vloc + rank), BF16)],
-        [(back, None), (swap(back), None), *dy],
-    )
-
+        [(back, None), (back_got, None), *dy],
+    )
     down_got = lax.ppermute(after(down_other, both), ("fsdp", "tp"), pairs)
-
-    x_chip = lax.dynamic_slice_in_dim(input_rows, f * kf_width, kf_width, 1)
-    x_other = after(swap(x_plain), both, down_got)
-    base = call(
-        functools.partial(base_kernel, fsdp),
-        [((rows, vloc), F32)] * fsdp,
-        [(v, None) for v in (x_chip, x_plain, x_other, value_weight_frozen)],
-        at=numbers(t),
-        flops=20 * fsdp * rows * kt * vloc,
-    )
-    base_plain = base[0]
-
-    both = [both] * fsdp
-    both[1], both[2] = over_f(both[1], 1), over_f(both[2], 2)
-    both[3] = over_f(both[3], 3)
-    base = [over_f(v, k) for k, v in enumerate(base)]
+    both = [over_f(both, k) for k in range(fsdp)]
     for c in range(1, CHUNKS):
-        chunk = [after(v, *x_routed[c - 1], *both, base_plain) for v in sends[c * ad : (c + 1) * ad]]
+        chunk = [
+            after(v, *x_routed[c - 1], *both, base[3]) for v in sends[c * ad : (c + 1) * ad]
+        ]
         x_routed.append([over_a(v, ka) for ka, v in enumerate(chunk)])
 
     def chunk_of(c, routed):
@@ -480,20 +481,23 @@
         last = c == CHUNKS - 1
         if last:
             hid = hidden(c, hid, x_routed[c])
+            hid, both = lax.optimization_barrier((hid, both))
             hid = hid[0] + swap(hid[1])
-            hid, both = lax.optimization_barrier((hid, both))
-            hid = [over_f(hid[k], k) for k in range(fsdp)]
         sums = call(
             functools.partial(down_grad_kernel, fsdp, ad, gslots),
             [((dloc, rloc, cw), BF16)] * fsdp,
             [*chunk_of(c, x_routed[c]), *[(v, (vloc, rank)) for v in both]],
             at=numbers(*[(t ^ (r // 2)) * 2 + (fx ^ (r % 2)) for r in range(fsdp)]),
             scratch=[pltpu.VMEM((GROUP * rank, cw), F32)],
+            flops=20 * dloc * rank * cw * 192,
         )
         got = []
-        if not last:
+        if last:
+            hid, sums = lax.optimization_barrier((hid, sums))
+            hid = [over_f(hid[k], k) for k in range(fsdp)]
+        else:
             hid = hidden(c, hid, after(x_routed[c], x_routed[c + 1][2], *sums))
-            sums = [*sums[:2], *after(sums[2:], hid)]
+            sums = [*sums[:3], after(sums[3], hid)]
         for r in range(fsdp):
             p, q = r % 2, r // 2
             perm = [
@@ -519,7 +523,7 @@
                 ),
                 cost_estimate=pl.CostEstimate(flops=1, bytes_accessed=1, transcendentals=0),
             )(numbers(*at), *after(got, x_routed[1][1]))
-            x_routed[c + 1] = after(x_routed[c + 1], grad_a, *base)
+            x_routed[c + 1] = after(x_routed[c + 1], grad_a)
         else:
             for v, column in zip(got, at):
                 grad_a = lax.dynamic_update_slice_in_dim(
@@ -533,8 +537,8 @@
         [(v, None) for v in (hid_own, swap(hid_own), adapter_up_weight)],
         at=numbers(t, *[f ^ k for k in range(fsdp)]),
     )
-    returned = [over_a(v, (ad - ka) % ad) for ka, v in enumerate(outs[:ad])]
-    hid_cols = [over_f(after(v, got[0], got[1]), k) for k, v in enumerate(outs[ad:])]
+    returned = [over_a(after(v, got[0]), (ad - ka) % ad) for ka, v in enumerate(outs[:ad])]
+    hid_cols = [over_f(v, k) for k, v in enumerate(outs[ad:])]
 
     (y_out,) = call(
         functools.partial(output_kernel, fsdp, ad),

time: 222 us -> 251 us (1.13)
  waiting for transfers between devices: 67.2 us -> 113 us
  starting transfers between devices: 68.6 us -> 51.1 us
    ppermute x15, waiting for transfers between devices: 30.8 us -> 56.6 us  [over_f(): lax.ppermute(v, 'fsdp', [(i, i ^ k) for i in range(fsdp)])]
    ppermute x12, waiting for transfers between devices: 27.2 us -> 41.3 us  [over_a(): lax.ppermute(v, 'ad', [(i, (i + k) % ad) for i in range(ad)])]
    ppermute x12, starting transfers between devices: 30.1 us -> 19.8 us  [over_a(): lax.ppermute(v, 'ad', [(i, (i + k) % ad) for i in range(ad)])]
    ppermute x8, waiting for transfers between devices: 4.58 us -> 14.2 us  [column_body(): got.append(lax.ppermute(sums[r], ('fsdp', 'tp'), perm))]
    ppermute x4 -> x6, waiting for transfers between devices: 4.68 us -> 0.62 us  [swap(): return lax.ppermute(v, 'tp', [(0, 1), (1, 0)])]
    ppermute x15, starting transfers between devices: 20.6 us -> 16.7 us  [over_f(): lax.ppermute(v, 'fsdp', [(i, i ^ k) for i in range(fsdp)])]
  transfers between devices with their start and end apart: 40 -> 42, of which waited for: 21 -> 19; matrix products, arithmetic and copies ran while one was open for 7% -> 6% of each run, Pallas kernels for 18% -> 17%
where the time goes in v6:
time: 251 us
  waiting for transfers between devices  113 us (45%)
  Pallas kernels  60.5 us (24%)
  starting transfers between devices  51.1 us (20%)
  local copies, waits for them, and re-layouts  16.1 us (6%)
  other arithmetic  8.73 us (3%)
    ppermute x15, waiting for transfers between devices, over_f(): lax.ppermute(v, 'fsdp', [(i, i ^ k) for i in range(fsdp)])  56.6 us
    pallas_call x12, Pallas kernels, call(): pl.pallas_call(body, out_shape=[jax.ShapeDtypeStruct(shape, dtype) for sh...  55.9 us
    ppermute x12, waiting for transfers between devices, over_a(): lax.ppermute(v, 'ad', [(i, (i + k) % ad) for i in range(ad)])  41.3 us
    ppermute x12, starting transfers between devices, over_a(): lax.ppermute(v, 'ad', [(i, (i + k) % ad) for i in range(ad)])  19.8 us
    ppermute x15, starting transfers between devices, over_f(): lax.ppermute(v, 'fsdp', [(i, i ^ k) for i in range(fsdp)])  16.7 us
    ppermute x8, waiting for transfers between devices, column_body(): got.append(lax.ppermute(sums[r], ('fsdp', 'tp'), perm))  14.2 us
    ppermute x8, starting transfers between devices, column_body(): got.append(lax.ppermute(sums[r], ('fsdp', 'tp'), perm))  10.1 us
    unnamed x74, local copies, waits for them, and re-layouts  5.9 us
  transfers between devices with their start and end apart: 42, of which 19 were waited for; matrix products, arithmetic and copies ran while one was open for 6% of the time, Pallas kernels for 17%

profile of v6, /device:TPU:0, one launch (start us, length us, event | category | flops | bytes accessed | tf_op | source)
XLA Modules:
  0.0 250.5 jit_solution(7286873530053550061)
XLA Ops:
  1.3 2.5 %constant_dynamic-slice_fusion.2 = (bf16[256,1024]{1,0:T(8,128)(2,1)S(1)}, bf16[256,1024]{1,0:T(8,128)(2,1)S(1)}, bf16[256,1024]{1,0:T(8,128)(2,1)S(1)}, bf16[256,1024]{1,0:T(8,128)(2,1)}) fusion(bf16[256,8192]{1,0:T(8,128)(2,1)} %param.6, s32[]{:T(128)S(6)} %select_n.68, s32[]{:T(128)S(6)} %select_n.67, s32[]{:T(128)S(6)} %select_n.66, s32[]{:T(128)S(6)} %select_n.65), kind=kLoop, calls=%fused_computation.18 | loop fusion | bytes 4194320 | tf_op jit(solution)/shard_map/dynamic_slice | solution.py:401
  3.9 1.1 fusion.3
  5.0 2.9 %collective-permute-start = (bf16[272,1024]{1,0:T(8,128)(2,1)S(1)}, bf16[272,1024]{1,0:T(8,128)(2,1)S(1)}, u32[]{:S(2)}, u32[]{:S(2)}) collective-permute-start(bf16[272,1024]{1,0:T(8,128)(2,1)S(1)} %get-tuple-element.100), channel_id=1, source_target_pairs={{0,8},{8,0},{16,24},{24,16},{1,9},{9,1},{17,25},{25,17},{2,10},{10... | collective-permute-start | bytes 1671176 | tf_op jit(solution)/shard_map/ppermute | solution.py:385
  7.9 1.5 collective-permute-start.1
  9.5 2.7 %shard_map.85 = (bf16[384,256]{1,0:T(8,128)(2,1)}, bf16[96,1536]{1,0:T(8,128)(2,1)}, bf16[96,1536]{1,0:T(8,128)(2,1)}, bf16[96,1536]{1,0:T(8,128)(2,1)}, bf16[96,1536]{1,0:T(8,128)(2,1)}) custom-call(s32[1]{0:T(128)} %bitcast.2.refs_0_, s32[1,256]{1,0:T(1,128)} %bitcast.33, bf16[256,1024]{1,0:T(8,128)(2,1)} %get-tuple-element.99.refs_2_, ...), custom_call_target="tpu_custom_call" | custom-call | flops 1 | bytes 1 | tf_op jit(solution)/shard_map/pallas_call | solution.py:154
  12.2 2.1 collective-permute-start.6
  14.3 7.1 %collective-permute-done.refs_2_.refs_1_ = bf16[272,1024]{1,0:T(8,128)(2,1)S(1)} collective-permute-done((bf16[272,1024]{1,0:T(8,128)(2,1)S(1)}, bf16[272,1024]{1,0:T(8,128)(2,1)S(1)}, u32[]{:S(2)}, u32[]{:S(2)}) %collective-permute-start) | collective-permute-done | bytes 557088 | tf_op jit(solution)/shard_map/ppermute | solution.py:385
  21.4 12.8 %collective-permute-done.1.refs_3_.refs_2_ = bf16[272,1024]{1,0:T(8,128)(2,1)S(1)} collective-permute-done((bf16[272,1024]{1,0:T(8,128)(2,1)}, bf16[272,1024]{1,0:T(8,128)(2,1)S(1)}, u32[]{:S(2)}, u32[]{:S(2)}) %collective-permute-start.1) | collective-permute-done | bytes 557088 | tf_op jit(solution)/shard_map/ppermute | solution.py:385
  34.7 2.6 %collective-permute-start.7 = (bf16[96,1536]{1,0:T(8,128)(2,1)}, bf16[96,1536]{1,0:T(8,128)(2,1)S(1)}, u32[]{:S(2)}, u32[]{:S(2)}) collective-permute-start(bf16[96,1536]{1,0:T(8,128)(2,1)} %get-tuple-element.105), channel_id=1, source_target_pairs={{0,2},{1,3},{2,0},{3,1},{4,6},{5,7},{6,4},{7,5},{8,10},{9,11},{10,... | collective-permute-start | bytes 884744 | tf_op jit(solution)/shard_map/ppermute | solution.py:388
  37.3 1.3 collective-permute-start.8
  38.6 4.6 %constant_dynamic-slice_fusion.1 = bf16[8,256,1024]{2,1,0:T(8,128)(2,1)} fusion(bf16[8,256,4096]{2,1,0:T(8,128)(2,1)} %refs_10_.1, s32[]{:T(128)S(6)} %select_n.70), kind=kLoop, calls=%fused_computation.17 | loop fusion | bytes 8388612 | tf_op jit(solution)/shard_map/dynamic_slice | solution.py:420
  43.3 2.3 constant_dynamic-slice_fusion.refs_1_
  45.6 6.4 %collective-permute-done.7.refs_2_.refs_4_.refs_3_ = bf16[96,1536]{1,0:T(8,128)(2,1)S(1)} collective-permute-done((bf16[96,1536]{1,0:T(8,128)(2,1)}, bf16[96,1536]{1,0:T(8,128)(2,1)S(1)}, u32[]{:S(2)}, u32[]{:S(2)}) %collective-permute-start.7) | collective-permute-done | bytes 294944 | tf_op jit(solution)/shard_map/ppermute | solution.py:388
  52.1 0.9 copy-done.10
  53.0 6.1 %shard_map.86 = (f32[256,512]{1,0:T(8,128)}, f32[256,512]{1,0:T(8,128)}, f32[256,512]{1,0:T(8,128)}, f32[256,512]{1,0:T(8,128)}) custom-call(s32[1]{0:T(128)} %bitcast.refs_0_, bf16[256,2048]{1,0:T(8,128)(2,1)} %constant_dynamic-slice_fusion.refs_1_, bf16[272,1024]{1,0:T(8,128)(2,1)} %copy-done.3, bf16[272,1024]{1,0:T(8,128)(2,1)} %copy-done.4, ...), custom_call_target="tpu_custom_call" | custom-call | flops 1 | bytes 1 | tf_op jit(solution)/shard_map/pallas_call | solution.py:154
  59.6 1.6 collective-permute-start.10
  61.2 4.0 %shard_map.87 = (bf16[3,96,512]{2,1,0:T(8,128)(2,1)}, bf16[3,96,512]{2,1,0:T(8,128)(2,1)}, bf16[3,96,512]{2,1,0:T(8,128)(2,1)}, bf16[3,96,512]{2,1,0:T(8,128)(2,...) custom-call(s32[1]{0:T(128)} %bitcast.2.refs_0_, ...), custom_call_target="tpu_custom_call" | custom-call | flops 1 | bytes 1 | tf_op jit(solution)/shard_map/pallas_call | solution.py:154
  65.3 3.5 %shard_map.88.refs_0_ = f32[4,96,256]{2,1,0:T(8,128)} custom-call(bf16[96,1536]{1,0:T(8,128)(2,1)} %get-tuple-element.137.refs_0_.refs_2_.refs_1_, bf16[96,1536]{1,0:T(8,128)(2,1)} %copy-done, bf16[96,1536]{1,0:T(8,128)(2,1)} %copy-done.1, bf16[96,1536]{1,0:T(8,128)(2,1)} %copy-done.2, bf16[8,256,512]{2,1,0:T(8,128)(2,1)} %refs_3_.3), custom_call_target="tpu_custom_call" | custom-call | flops 1 | bytes 1 | tf_op jit(solution)/shard_map/pallas_call | solution.py:154
  68.9 5.1 %collective-permute-start.13 = (bf16[3,96,512]{2,1,0:T(8,128)(2,1)}, bf16[3,96,512]{2,1,0:T(8,128)(2,1)S(1)}, u32[]{:S(2)}, u32[]{:S(2)}) collective-permute-start(bf16[3,96,512]{2,1,0:T(8,128)(2,1)} %get-tuple-element.132), channel_id=1, source_target_pairs={{0,2},{1,3},{2,0},{3,1},{4,6},{5,7},{6,4},{7,5},{8,10},{9,11},{10,... | collective-permute-start | bytes 884744 | tf_op jit(solution)/shard_map/ppermute | solution.py:388
  74.0 14.1 %collective-permute-done.13.refs_7_ = bf16[3,96,512]{2,1,0:T(8,128)(2,1)S(1)} collective-permute-done((bf16[3,96,512]{2,1,0:T(8,128)(2,1)}, bf16[3,96,512]{2,1,0:T(8,128)(2,1)S(1)}, u32[]{:S(2)}, u32[]{:S(2)}) %collective-permute-start.13) | collective-permute-done | bytes 294944 | tf_op jit(solution)/shard_map/ppermute | solution.py:388
  88.2 0.8 copy-done.19
  88.9 2.3 shard_map.89.refs_9_.refs_4_
  91.3 3.8 %collective-permute-start.25 = (bf16[8,256,1024]{2,1,0:T(8,128)(2,1)}, bf16[8,256,1024]{2,1,0:T(8,128)(2,1)}, u32[]{:S(2)}, u32[]{:S(2)}) collective-permute-start(bf16[8,256,1024]{2,1,0:T(8,128)(2,1)} %constant_dynamic-slice_fusion.1), channel_id=1, source_target_pairs={{0,4},{8,12},{20,16},{28,24},{1,5},{9,13},{21,17},{29,25},{2,6},{1... | collective-permute-start | bytes 12582920 | tf_op jit(solution)/shard_map/ppermute | solution.py:457
  95.1 1.1 collective-permute-start.12
  96.2 2.8 %collective-permute-start.14 = (bf16[3,96,512]{2,1,0:T(8,128)(2,1)S(1)}, bf16[3,96,512]{2,1,0:T(8,128)(2,1)S(1)}, u32[]{:S(2)}, u32[]{:S(2)}) collective-permute-start(bf16[3,96,512]{2,1,0:T(8,128)(2,1)S(1)} %copy-done.34), channel_id=1, source_target_pairs={{0,3},{1,0},{2,1},{3,2},{4,7},{5,4},{6,5},{7,6},{8,11},{9,8},{10,9... | collective-permute-start | bytes 884744 | tf_op jit(solution)/shard_map/ppermute | solution.py:388
  98.9 1.5 collective-permute-start.16
  100.4 6.3 %collective-permute-done.12.refs_6_ = bf16[3,96,512]{2,1,0:T(8,128)(2,1)} collective-permute-done((bf16[3,96,512]{2,1,0:T(8,128)(2,1)S(1)}, bf16[3,96,512]{2,1,0:T(8,128)(2,1)}, u32[]{:S(2)}, u32[]{:S(2)}) %collective-permute-start.12) | collective-permute-done | bytes 294944 | tf_op jit(solution)/shard_map/ppermute | solution.py:388
  106.8 1.7 collective-permute-done.14.refs_8_
  109.2 1.5 collective-permute-start.11
  112.0 23.5 %collective-permute-done.11.refs_3_ = f32[256,512]{1,0:T(8,128)S(1)} collective-permute-done((f32[256,512]{1,0:T(8,128)}, f32[256,512]{1,0:T(8,128)S(1)}, u32[]{:S(2)}, u32[]{:S(2)}) %collective-permute-start.11) | collective-permute-done | bytes 524320 | tf_op jit(solution)/shard_map/ppermute | solution.py:385
  135.5 2.9 %collective-permute-done.17.refs_11_.refs_6_ = bf16[4,96,768]{2,1,0:T(8,128)(2,1)S(1)} collective-permute-done((bf16[4,96,768]{2,1,0:T(8,128)(2,1)}, bf16[4,96,768]{2,1,0:T(8,128)(2,1)S(1)}, u32[]{:S(2)}, u32[]{:S(2)}) %collective-permute-start.17) | collective-permute-done | bytes 589856 | tf_op jit(solution)/shard_map/ppermute | solution.py:385
  138.5 2.2 collective-permute-start.20
  140.7 5.9 %shard_map.90 = (bf16[8,64,512]{2,1,0:T(8,128)(2,1)}, bf16[8,64,512]{2,1,0:T(8,128)(2,1)}, bf16[8,64,512]{2,1,0:T(8,128)(2,1)}, bf16[8,64,512]{2,1,0:T(8,128)(2,1)}) custom-call(s32[4]{0:T(128)} %pad_add_fusion.1.refs_0_, bf16[96,1536]{1,0:T(8,128)(2,1)} %get-tuple-element.137.refs_0_.refs_2_.refs_1_, bf16[96,1536]{1,0:T(8,128)(2,1)} %copy-done, ...), custom_call_target="tpu_custom_call" | custom-call | flops 4026531840 | bytes 1 | tf_op jit(solution)/shard_map/pallas_call | solution.py:154
  146.7 1.7 collective-permute-start.22
  148.4 0.9 collective-permute-start.23
  149.3 10.7 %collective-permute-done.20.refs_7_ = bf16[3,96,512]{2,1,0:T(8,128)(2,1)S(1)} collective-permute-done((bf16[3,96,512]{2,1,0:T(8,128)(2,1)}, bf16[3,96,512]{2,1,0:T(8,128)(2,1)S(1)}, u32[]{:S(2)}, u32[]{:S(2)}) %collective-permute-start.20) | collective-permute-done | bytes 294944 | tf_op jit(solution)/shard_map/ppermute | solution.py:388
  160.1 2.4 collective-permute-start.24
  162.5 7.0 %shard_map.91.refs_9_ = f32[4,4,96,256]{3,2,1,0:T(8,128)} custom-call(s32[3]{0:T(128)} %add_add_fusion.1.refs_0_, bf16[96,1536]{1,0:T(8,128)(2,1)} %get-tuple-element.137.refs_0_.refs_2_.refs_1_, bf16[96,1536]{1,0:T(8,128)(2,1)} %copy-done, bf16[96,1536]{1,0:T(8,128)(2,1)} %copy-done.1, bf16[96,1536]{1,0:T(8,128)(2,1)} %copy-done.2, ...), custom_call_target="tpu_custom_call" | custom-call | flops 1 | bytes 1 | tf_op jit(solution)/shard_map/pallas_call | solution.py:154
  169.5 0.8 collective-permute-start.26
  171.9 12.0 %collective-permute-done.26.refs_3_ = bf16[8,64,512]{2,1,0:T(8,128)(2,1)S(1)} collective-permute-done((bf16[8,64,512]{2,1,0:T(8,128)(2,1)}, bf16[8,64,512]{2,1,0:T(8,128)(2,1)S(1)}, u32[]{:S(2)}, u32[]{:S(2)}) %collective-permute-start.26) | collective-permute-done | bytes 524320 | tf_op jit(solution)/shard_map/ppermute | solution.py:509
  184.0 0.8 copy-done.17
  184.7 4.6 %shard_map.92 = f32[8,64,4096]{2,1,0:T(8,128)} custom-call(s32[4]{0:T(128)} %pad_add_fusion.at, bf16[8,64,512]{2,1,0:T(8,128)(2,1)} %copy-done.14, bf16[8,64,512]{2,1,0:T(8,128)(2,1)} %copy-done.15, bf16[8,64,512]{2,1,0:T(8,128)(2,1)} %copy-done.16, bf16[8,64,512]{2,1,0:T(8,128)(2,1)} %copy-done.17), custom_call_target="tpu_custom_call" | custom-call | flops 1 | bytes 1 | tf_op jit(solution)/shard_map/pallas_call | solution.py:515
  190.1 7.4 %shard_map.93 = (f32[4,4,96,128]{3,2,1,0:T(8,128)}, f32[4,4,96,128]{3,2,1,0:T(8,128)}) custom-call(s32[3]{0:T(128)} %add_add_fusion.refs_0_, bf16[96,1536]{1,0:T(8,128)(2,1)} %get-tuple-element.137.refs_0_.refs_2_.refs_1_, bf16[96,1536]{1,0:T(8,128)(2,1)} %copy-done, bf16[96,1536]{1,0:T(8,128)(2,1)} %copy-done.1, bf16[96,1536]{1,0:T(8,128)(2,1)} %copy-done.2, ...), custom_call_target="tpu_custom_call" | custom-call | flops 1 | bytes 1 | tf_op jit(solution)/shard_map/pallas_call | solution.py:154
  197.6 6.1 %shard_map.94 = (bf16[8,64,512]{2,1,0:T(8,128)(2,1)}, bf16[8,64,512]{2,1,0:T(8,128)(2,1)}, bf16[8,64,512]{2,1,0:T(8,128)(2,1)}, bf16[8,64,512]{2,1,0:T(8,128)(2,1)}) custom-call(s32[4]{0:T(128)} %pad_add_fusion.1.refs_0_, bf16[96,1536]{1,0:T(8,128)(2,1)} %get-tuple-element.137.refs_0_.refs_2_.refs_1_, bf16[96,1536]{1,0:T(8,128)(2,1)} %copy-done, ...), custom_call_target="tpu_custom_call" | custom-call | flops 4026531840 | bytes 1 | tf_op jit(solution)/shard_map/pallas_call | solution.py:154
  203.9 2.3 collective-permute-start.30
  206.8 0.7 collective-permute-start.28
  207.5 1.7 collective-permute-start.32
  209.2 1.3 collective-permute-start.36
  210.5 2.2 collective-permute-done.30
  212.7 3.6 %collective-permute-done.29 = f32[4,96,128]{2,1,0:T(8,128)S(1)} collective-permute-done((f32[4,96,128]{2,1,0:T(8,128)S(1)}, f32[4,96,128]{2,1,0:T(8,128)S(1)}, u32[]{:S(2)}, u32[]{:S(2)}) %collective-permute-start.29) | collective-permute-done | bytes 196640 | tf_op jit(solution)/shard_map/ppermute | solution.py:385
  219.0 4.1 %shard_map.95 = (bf16[96,512]{1,0:T(8,128)(2,1)}, bf16[96,512]{1,0:T(8,128)(2,1)}, bf16[96,512]{1,0:T(8,128)(2,1)}, bf16[96,512]{1,0:T(8,128)(2,1)}, bf16[4,96,6...) custom-call(s32[5]{0:T(128)} %stack.85.refs_0_, ...), custom_call_target="tpu_custom_call" | custom-call | flops 1 | bytes 1 | tf_op jit(solution)/shard_map/pallas_call | solution.py:154
  223.1 1.4 collective-permute-start.39
  224.5 1.5 collective-permute-start.40
  226.7 3.6 %collective-permute-done.39.refs_1_ = bf16[4,96,64]{2,1,0:T(8,128)(2,1)S(1)} collective-permute-done((bf16[4,96,64]{2,1,0:T(8,128)(2,1)}, bf16[4,96,64]{2,1,0:T(8,128)(2,1)S(1)}, u32[]{:S(2)}, u32[]{:S(2)}) %collective-permute-start.39) | collective-permute-done | bytes 49184 | tf_op jit(solution)/shard_map/ppermute | solution.py:385
  230.6 0.9 collective-permute-start.38
  232.4 3.9 %shard_map.97 = f32[8,64,512]{2,1,0:T(8,128)} custom-call(bf16[4,96,64]{2,1,0:T(8,128)(2,1)} %get-tuple-element.191.refs_0_, bf16[4,96,64]{2,1,0:T(8,128)(2,1)} %copy-done.28, bf16[4,96,64]{2,1,0:T(8,128)(2,1)} %copy-done.29, bf16[4,96,64]{2,1,0:T(8,128)(2,1)} %copy-done.30, bf16[4,96,768]{2,1,0:T(8,128)(2,1)} %shard_map.89.refs_9_.refs_4_, ...), custom_call_target="tpu_custom_call" | custom-call | flops 1 | bytes 1 | tf_op jit(solution)/shard_map/pallas_call | solution.py:154
  236.8 1.1 convert_dynamic-update-slice_fusion.3
  237.9 1.6 collective-permute-start.35
  239.5 1.1 convert_dynamic-update-slice_fusion.2
  240.8 1.1 convert_dynamic-update-slice_fusion.1
  241.9 2.0 collective-permute-done.38
  243.9 1.1 convert_dynamic-update-slice_fusion
  245.0 1.9 collective-permute-done.34.refs_7_
  247.6 2.8 %shard_map.96 = bf16[256,512]{1,0:T(8,128)(2,1)} custom-call(f32[256,512]{1,0:T(8,128)} %get-tuple-element.117.refs_0_, f32[256,512]{1,0:T(8,128)} %copy-done.11, f32[256,512]{1,0:T(8,128)} %copy-done.12, f32[256,512]{1,0:T(8,128)} %copy-done.13, bf16[384,256]{1,0:T(8,128)(2,1)} %get-tuple-element.121.refs_4_, bf16[96,512]{1,0:T(8,128)(2,1)} %get-tuple-element.181.refs_5_, ...), custom_call_target="tpu_custom_call" | custom-call | flops 1 | bytes 1 | tf_op jit(solution)/shard_map/pallas_call | solution.py:154
  (124 shorter events, 13.0 us)
Async XLA Ops:
  5.0 16.4 %collective-permute-start = (bf16[272,1024]{1,0:T(8,128)(2,1)S(1)}, bf16[272,1024]{1,0:T(8,128)(2,1)S(1)}, u32[]{:S(2)}, u32[]{:S(2)}) collective-permute-start(bf16[272,1024]{1,0:T(8,128)(2,1)S(1)} %get-tuple-element.100), channel_id=1, source_target_pairs={{0,8},{8,0},{16,24},{24,16},{1,9},{9,1},{17,25},{25,17},{2,10},{10... | collective-permute-start | bytes 1671176 | tf_op jit(solution)/shard_map/ppermute | solution.py:385
  7.9 26.2 %collective-permute-start.1 = (bf16[272,1024]{1,0:T(8,128)(2,1)}, bf16[272,1024]{1,0:T(8,128)(2,1)S(1)}, u32[]{:S(2)}, u32[]{:S(2)}) collective-permute-start(bf16[272,1024]{1,0:T(8,128)(2,1)} %get-tuple-element.101), channel_id=1, source_target_pairs={{0,16},{8,24},{16,0},{24,8},{1,17},{9,25},{17,1},{25,9},{2,18},{10... | collective-permute-start | bytes 1671176 | tf_op jit(solution)/shard_map/ppermute | solution.py:385
  9.5 24.7 %collective-permute-start.2 = (bf16[272,1024]{1,0:T(8,128)(2,1)}, bf16[272,1024]{1,0:T(8,128)(2,1)S(1)}, u32[]{:S(2)}, u32[]{:S(2)}) collective-permute-start(bf16[272,1024]{1,0:T(8,128)(2,1)} %get-tuple-element.102), channel_id=1, source_target_pairs={{0,24},{8,16},{16,8},{24,0},{1,25},{9,17},{17,9},{25,1},{2,26},{10... | collective-permute-start | bytes 1671176 | tf_op jit(solution)/shard_map/ppermute | solution.py:385
  12.2 25.1 %collective-permute-start.6 = (bf16[96,1536]{1,0:T(8,128)(2,1)}, bf16[96,1536]{1,0:T(8,128)(2,1)S(1)}, u32[]{:S(2)}, u32[]{:S(2)}) collective-permute-start(bf16[96,1536]{1,0:T(8,128)(2,1)} %get-tuple-element.104), channel_id=1, source_target_pairs={{0,1},{1,2},{2,3},{3,0},{4,5},{5,6},{6,7},{7,4},{8,9},{9,10},{10,1... | collective-permute-start | bytes 884744 | tf_op jit(solution)/shard_map/ppermute | solution.py:388
  21.4 21.9 %copy-start.3 = (bf16[272,1024]{1,0:T(8,128)(2,1)}, bf16[272,1024]{1,0:T(8,128)(2,1)S(1)}, u32[]{:S(2)}) copy-start(bf16[272,1024]{1,0:T(8,128)(2,1)S(1)} %collective-permute-done.refs_2_.refs_1_) | copy-start | bytes 1671172
  21.4 30.6 %collective-permute-start.3 = (bf16[272,1024]{1,0:T(8,128)(2,1)S(1)}, bf16[272,1024]{1,0:T(8,128)(2,1)S(1)}, u32[]{:S(2)}, u32[]{:S(2)}) collective-permute-start(bf16[272,1024]{1,0:T(8,128)(2,1)S(1)} %collective-permute-done.refs_2_.refs_1_), channel_id=1, source_target_pairs={{0,4},{4,0},{1,5},{5,1},{2,6},{6,2},{3,7},{7,3},{8,12},{12,8},{9,1... | collective-permute-start | bytes 1671176 | tf_op jit(solution)/shard_map/ppermute | solution.py:391
  34.2 9.1 %copy-start.4 = (bf16[272,1024]{1,0:T(8,128)(2,1)}, bf16[272,1024]{1,0:T(8,128)(2,1)S(1)}, u32[]{:S(2)}) copy-start(bf16[272,1024]{1,0:T(8,128)(2,1)S(1)} %collective-permute-done.1.refs_3_.refs_2_) | copy-start | bytes 1671172
  34.2 17.9 %collective-permute-start.4 = (bf16[272,1024]{1,0:T(8,128)(2,1)S(1)}, bf16[272,1024]{1,0:T(8,128)(2,1)}, u32[]{:S(2)}, u32[]{:S(2)}) collective-permute-start(bf16[272,1024]{1,0:T(8,128)(2,1)S(1)} %collective-permute-done.1.refs_3_.refs_2_), channel_id=1, source_target_pairs={{0,4},{4,0},{1,5},{5,1},{2,6},{6,2},{3,7},{7,3},{8,12},{12,8},{9,1... | collective-permute-start | bytes 1671176 | tf_op jit(solution)/shard_map/ppermute | solution.py:391
  34.2 9.1 %copy-start.5 = (bf16[272,1024]{1,0:T(8,128)(2,1)}, bf16[272,1024]{1,0:T(8,128)(2,1)S(1)}, u32[]{:S(2)}) copy-start(bf16[272,1024]{1,0:T(8,128)(2,1)S(1)} %collective-permute-done.2.refs_4_.refs_3_) | copy-start | bytes 1671172
  34.2 17.9 %collective-permute-start.5 = (bf16[272,1024]{1,0:T(8,128)(2,1)S(1)}, bf16[272,1024]{1,0:T(8,128)(2,1)}, u32[]{:S(2)}, u32[]{:S(2)}) collective-permute-start(bf16[272,1024]{1,0:T(8,128)(2,1)S(1)} %collective-permute-done.2.refs_4_.refs_3_), channel_id=1, source_target_pairs={{0,4},{4,0},{1,5},{5,1},{2,6},{6,2},{3,7},{7,3},{8,12},{12,8},{9,1... | collective-permute-start | bytes 1671176 | tf_op jit(solution)/shard_map/ppermute | solution.py:391
  34.7 17.3 %collective-permute-start.7 = (bf16[96,1536]{1,0:T(8,128)(2,1)}, bf16[96,1536]{1,0:T(8,128)(2,1)S(1)}, u32[]{:S(2)}, u32[]{:S(2)}) collective-permute-start(bf16[96,1536]{1,0:T(8,128)(2,1)} %get-tuple-element.105), channel_id=1, source_target_pairs={{0,2},{1,3},{2,0},{3,1},{4,6},{5,7},{6,4},{7,5},{8,10},{9,11},{10,... | collective-permute-start | bytes 884744 | tf_op jit(solution)/shard_map/ppermute | solution.py:388
  37.3 6.0 %copy-start = (bf16[96,1536]{1,0:T(8,128)(2,1)}, bf16[96,1536]{1,0:T(8,128)(2,1)S(1)}, u32[]{:S(2)}) copy-start(bf16[96,1536]{1,0:T(8,128)(2,1)S(1)} %collective-permute-done.6.refs_1_.refs_3_.refs_2_) | copy-start | bytes 884740
  37.3 14.7 %collective-permute-start.8 = (bf16[96,1536]{1,0:T(8,128)(2,1)}, bf16[96,1536]{1,0:T(8,128)(2,1)S(1)}, u32[]{:S(2)}, u32[]{:S(2)}) collective-permute-start(bf16[96,1536]{1,0:T(8,128)(2,1)} %get-tuple-element.107), channel_id=1, source_target_pairs={{0,3},{1,0},{2,1},{3,2},{4,7},{5,4},{6,5},{7,6},{8,11},{9,8},{10,9... | collective-permute-start | bytes 884744 | tf_op jit(solution)/shard_map/ppermute | solution.py:388
  52.0 13.2 %copy-start.1 = (bf16[96,1536]{1,0:T(8,128)(2,1)}, bf16[96,1536]{1,0:T(8,128)(2,1)S(1)}, u32[]{:S(2)}) copy-start(bf16[96,1536]{1,0:T(8,128)(2,1)S(1)} %collective-permute-done.7.refs_2_.refs_4_.refs_3_) | copy-start | bytes 884740
  52.0 13.2 %copy-start.2 = (bf16[96,1536]{1,0:T(8,128)(2,1)}, bf16[96,1536]{1,0:T(8,128)(2,1)S(1)}, u32[]{:S(2)}) copy-start(bf16[96,1536]{1,0:T(8,128)(2,1)S(1)} %collective-permute-done.8.refs_3_.refs_5_.refs_4_) | copy-start | bytes 884740
  59.1 29.1 %collective-permute-start.9 = (f32[256,512]{1,0:T(8,128)}, f32[256,512]{1,0:T(8,128)S(1)}, u32[]{:S(2)}, u32[]{:S(2)}) collective-permute-start(f32[256,512]{1,0:T(8,128)} %get-tuple-element.118), channel_id=1, source_target_pairs={{0,8},{8,0},{16,24},{24,16},{1,9},{9,1},{17,25},{25,17},{2,10},{10... | collective-permute-start | bytes 1572872 | tf_op jit(solution)/shard_map/ppermute | solution.py:385
  59.6 28.5 %collective-permute-start.10 = (f32[256,512]{1,0:T(8,128)}, f32[256,512]{1,0:T(8,128)S(1)}, u32[]{:S(2)}, u32[]{:S(2)}) collective-permute-start(f32[256,512]{1,0:T(8,128)} %get-tuple-element.119), channel_id=1, source_target_pairs={{0,16},{8,24},{16,0},{24,8},{1,17},{9,25},{17,1},{25,9},{2,18},{10... | collective-permute-start | bytes 1572872 | tf_op jit(solution)/shard_map/ppermute | solution.py:385
  65.2 29.9 %copy-start.35 = (bf16[3,96,512]{2,1,0:T(8,128)(2,1)S(1)}, bf16[3,96,512]{2,1,0:T(8,128)(2,1)}, u32[]{:S(2)}) copy-start(bf16[3,96,512]{2,1,0:T(8,128)(2,1)} %get-tuple-element.131) | copy-start | bytes 884740
  65.3 30.9 %copy-start.34 = (bf16[3,96,512]{2,1,0:T(8,128)(2,1)S(1)}, bf16[3,96,512]{2,1,0:T(8,128)(2,1)}, u32[]{:S(2)}) copy-start(bf16[3,96,512]{2,1,0:T(8,128)(2,1)} %get-tuple-element.133) | copy-start | bytes 884740
  68.8 19.4 %collective-permute-start.15 = (f32[4,96,256]{2,1,0:T(8,128)}, f32[4,96,256]{2,1,0:T(8,128)S(1)}, u32[]{:S(2)}, u32[]{:S(2)}) collective-permute-start(f32[4,96,256]{2,1,0:T(8,128)} %shard_map.88.refs_0_), channel_id=1, source_target_pairs={{0,4},{4,0},{1,5},{5,1},{2,6},{6,2},{3,7},{7,3},{8,12},{12,8},{9,1... | collective-permute-start | bytes 1179656 | tf_op jit(solution)/shard_map/ppermute | solution.py:391
  68.9 19.3 %collective-permute-start.13 = (bf16[3,96,512]{2,1,0:T(8,128)(2,1)}, bf16[3,96,512]{2,1,0:T(8,128)(2,1)S(1)}, u32[]{:S(2)}, u32[]{:S(2)}) collective-permute-start(bf16[3,96,512]{2,1,0:T(8,128)(2,1)} %get-tuple-element.132), channel_id=1, source_target_pairs={{0,2},{1,3},{2,0},{3,1},{4,6},{5,7},{6,4},{7,5},{8,10},{9,11},{10,... | collective-permute-start | bytes 884744 | tf_op jit(solution)/shard_map/ppermute | solution.py:388
  88.1 20.4 %copy-start.22 = (bf16[3,96,512]{2,1,0:T(8,128)(2,1)}, bf16[3,96,512]{2,1,0:T(8,128)(2,1)S(1)}, u32[]{:S(2)}) copy-start(bf16[3,96,512]{2,1,0:T(8,128)(2,1)S(1)} %collective-permute-done.13.refs_7_) | copy-start | bytes 884740
  88.1 58.5 %copy-start.11 = (f32[256,512]{1,0:T(8,128)}, f32[256,512]{1,0:T(8,128)S(1)}, u32[]{:S(2)}) copy-start(f32[256,512]{1,0:T(8,128)S(1)} %collective-permute-done.9.refs_1_) | copy-start | bytes 1572868
  88.9 57.7 %copy-start.12 = (f32[256,512]{1,0:T(8,128)}, f32[256,512]{1,0:T(8,128)S(1)}, u32[]{:S(2)}) copy-start(f32[256,512]{1,0:T(8,128)S(1)} %collective-permute-done.10.refs_2_) | copy-start | bytes 1572868
  91.3 71.2 %collective-permute-start.25 = (bf16[8,256,1024]{2,1,0:T(8,128)(2,1)}, bf16[8,256,1024]{2,1,0:T(8,128)(2,1)}, u32[]{:S(2)}, u32[]{:S(2)}) collective-permute-start(bf16[8,256,1024]{2,1,0:T(8,128)(2,1)} %constant_dynamic-slice_fusion.1), channel_id=1, source_target_pairs={{0,4},{8,12},{20,16},{28,24},{1,5},{9,13},{21,17},{29,25},{2,6},{1... | collective-permute-start | bytes 12582920 | tf_op jit(solution)/shard_map/ppermute | solution.py:457
  95.1 11.7 %collective-permute-start.12 = (bf16[3,96,512]{2,1,0:T(8,128)(2,1)S(1)}, bf16[3,96,512]{2,1,0:T(8,128)(2,1)}, u32[]{:S(2)}, u32[]{:S(2)}) collective-permute-start(bf16[3,96,512]{2,1,0:T(8,128)(2,1)S(1)} %copy-done.35), channel_id=1, source_target_pairs={{0,1},{1,2},{2,3},{3,0},{4,5},{5,6},{6,7},{7,4},{8,9},{9,10},{10,1... | collective-permute-start | bytes 884744 | tf_op jit(solution)/shard_map/ppermute | solution.py:388
  96.2 12.3 %collective-permute-start.14 = (bf16[3,96,512]{2,1,0:T(8,128)(2,1)S(1)}, bf16[3,96,512]{2,1,0:T(8,128)(2,1)S(1)}, u32[]{:S(2)}, u32[]{:S(2)}) collective-permute-start(bf16[3,96,512]{2,1,0:T(8,128)(2,1)S(1)} %copy-done.34), channel_id=1, source_target_pairs={{0,3},{1,0},{2,1},{3,2},{4,7},{5,4},{6,5},{7,6},{8,11},{9,8},{10,9... | collective-permute-start | bytes 884744 | tf_op jit(solution)/shard_map/ppermute | solution.py:388
  98.9 36.6 %collective-permute-start.16 = (bf16[4,96,768]{2,1,0:T(8,128)(2,1)}, bf16[4,96,768]{2,1,0:T(8,128)(2,1)S(1)}, u32[]{:S(2)}, u32[]{:S(2)}) collective-permute-start(bf16[4,96,768]{2,1,0:T(8,128)(2,1)} %shard_map.89.refs_9_.refs_4_), channel_id=1, source_target_pairs={{0,8},{8,0},{16,24},{24,16},{1,9},{9,1},{17,25},{25,17},{2,10},{10... | collective-permute-start | bytes 1769480 | tf_op jit(solution)/shard_map/ppermute | solution.py:385
  100.4 38.0 %collective-permute-start.17 = (bf16[4,96,768]{2,1,0:T(8,128)(2,1)}, bf16[4,96,768]{2,1,0:T(8,128)(2,1)S(1)}, u32[]{:S(2)}, u32[]{:S(2)}) collective-permute-start(bf16[4,96,768]{2,1,0:T(8,128)(2,1)} %shard_map.89.refs_9_.refs_4_), channel_id=1, source_target_pairs={{0,16},{8,24},{16,0},{24,8},{1,17},{9,25},{17,1},{25,9},{2,18},{10... | collective-permute-start | bytes 1769480 | tf_op jit(solution)/shard_map/ppermute | solution.py:385
  106.8 31.7 %collective-permute-start.18 = (bf16[4,96,768]{2,1,0:T(8,128)(2,1)}, bf16[4,96,768]{2,1,0:T(8,128)(2,1)S(1)}, u32[]{:S(2)}, u32[]{:S(2)}) collective-permute-start(bf16[4,96,768]{2,1,0:T(8,128)(2,1)} %shard_map.89.refs_9_.refs_4_), channel_id=1, source_target_pairs={{0,24},{8,16},{16,8},{24,0},{1,25},{9,17},{17,9},{25,1},{2,26},{10... | collective-permute-start | bytes 1769480 | tf_op jit(solution)/shard_map/ppermute | solution.py:385
  109.2 26.2 %collective-permute-start.11 = (f32[256,512]{1,0:T(8,128)}, f32[256,512]{1,0:T(8,128)S(1)}, u32[]{:S(2)}, u32[]{:S(2)}) collective-permute-start(f32[256,512]{1,0:T(8,128)} %get-tuple-element.120), channel_id=1, source_target_pairs={{0,24},{8,16},{16,8},{24,0},{1,25},{9,17},{17,9},{25,1},{2,26},{10... | collective-permute-start | bytes 1572872 | tf_op jit(solution)/shard_map/ppermute | solution.py:385
  135.5 34.0 %copy-start.13 = (f32[256,512]{1,0:T(8,128)}, f32[256,512]{1,0:T(8,128)S(1)}, u32[]{:S(2)}) copy-start(f32[256,512]{1,0:T(8,128)S(1)} %collective-permute-done.11.refs_3_) | copy-start | bytes 1572868
  135.5 5.2 %copy-start.7 = (bf16[4,96,768]{2,1,0:T(8,128)(2,1)}, bf16[4,96,768]{2,1,0:T(8,128)(2,1)S(1)}, u32[]{:S(2)}) copy-start(bf16[4,96,768]{2,1,0:T(8,128)(2,1)S(1)} %collective-permute-done.16.refs_10_.refs_5_) | copy-start | bytes 1769476
  138.4 31.9 %collective-permute-start.19 = (bf16[3,96,512]{2,1,0:T(8,128)(2,1)}, bf16[3,96,512]{2,1,0:T(8,128)(2,1)}, u32[]{:S(2)}, u32[]{:S(2)}) collective-permute-start(bf16[3,96,512]{2,1,0:T(8,128)(2,1)} %get-tuple-element.144), channel_id=1, source_target_pairs={{0,1},{1,2},{2,3},{3,0},{4,5},{5,6},{6,7},{7,4},{8,9},{9,10},{10,1... | collective-permute-start | bytes 884744 | tf_op jit(solution)/shard_map/ppermute | solution.py:388
  138.5 21.6 %collective-permute-start.20 = (bf16[3,96,512]{2,1,0:T(8,128)(2,1)}, bf16[3,96,512]{2,1,0:T(8,128)(2,1)S(1)}, u32[]{:S(2)}, u32[]{:S(2)}) collective-permute-start(bf16[3,96,512]{2,1,0:T(8,128)(2,1)} %get-tuple-element.145), channel_id=1, source_target_pairs={{0,2},{1,3},{2,0},{3,1},{4,6},{5,7},{6,4},{7,5},{8,10},{9,11},{10,... | collective-permute-start | bytes 884744 | tf_op jit(solution)/shard_map/ppermute | solution.py:388
  146.7 25.2 %collective-permute-start.22 = (bf16[8,64,512]{2,1,0:T(8,128)(2,1)}, bf16[8,64,512]{2,1,0:T(8,128)(2,1)S(1)}, u32[]{:S(2)}, u32[]{:S(2)}) collective-permute-start(bf16[8,64,512]{2,1,0:T(8,128)(2,1)} %get-tuple-element.147), channel_id=1, source_target_pairs={{0,0},{4,16},{8,8},{12,24},{16,4},{20,20},{24,12},{28,28},{1,1},{5... | collective-permute-start | bytes 1572872 | tf_op jit(solution)/shard_map/ppermute | solution.py:509
  148.4 23.5 %collective-permute-start.23 = (bf16[8,64,512]{2,1,0:T(8,128)(2,1)}, bf16[8,64,512]{2,1,0:T(8,128)(2,1)S(1)}, u32[]{:S(2)}, u32[]{:S(2)}) collective-permute-start(bf16[8,64,512]{2,1,0:T(8,128)(2,1)} %get-tuple-element.148), channel_id=1, source_target_pairs={{0,8},{4,24},{8,0},{12,16},{16,12},{20,28},{24,4},{28,20},{1,9},{5... | collective-permute-start | bytes 1572872 | tf_op jit(solution)/shard_map/ppermute | solution.py:509
  160.1 9.4 %copy-start.20 = (bf16[3,96,512]{2,1,0:T(8,128)(2,1)}, bf16[3,96,512]{2,1,0:T(8,128)(2,1)S(1)}, u32[]{:S(2)}) copy-start(bf16[3,96,512]{2,1,0:T(8,128)(2,1)S(1)} %collective-permute-done.20.refs_7_) | copy-start | bytes 884740
  160.1 11.9 %collective-permute-start.24 = (bf16[8,64,512]{2,1,0:T(8,128)(2,1)}, bf16[8,64,512]{2,1,0:T(8,128)(2,1)S(1)}, u32[]{:S(2)}, u32[]{:S(2)}) collective-permute-start(bf16[8,64,512]{2,1,0:T(8,128)(2,1)} %get-tuple-element.149), channel_id=1, source_target_pairs={{0,16},{4,0},{8,24},{12,8},{16,20},{20,4},{24,28},{28,12},{1,17},{... | collective-permute-start | bytes 1572872 | tf_op jit(solution)/shard_map/ppermute | solution.py:509
  162.5 7.8 %copy-start.33 = (bf16[3,96,512]{2,1,0:T(8,128)(2,1)S(1)}, bf16[3,96,512]{2,1,0:T(8,128)(2,1)}, u32[]{:S(2)}) copy-start(bf16[3,96,512]{2,1,0:T(8,128)(2,1)} %get-tuple-element.146) | copy-start | bytes 884740
  169.5 14.5 %collective-permute-start.26 = (bf16[8,64,512]{2,1,0:T(8,128)(2,1)}, bf16[8,64,512]{2,1,0:T(8,128)(2,1)S(1)}, u32[]{:S(2)}, u32[]{:S(2)}) collective-permute-start(bf16[8,64,512]{2,1,0:T(8,128)(2,1)} %get-tuple-element.157), channel_id=1, source_target_pairs={{0,24},{4,8},{8,16},{12,0},{16,28},{20,12},{24,20},{28,4},{1,25},{... | collective-permute-start | bytes 1572872 | tf_op jit(solution)/shard_map/ppermute | solution.py:509
  170.3 19.1 %collective-permute-start.21 = (bf16[3,96,512]{2,1,0:T(8,128)(2,1)S(1)}, bf16[3,96,512]{2,1,0:T(8,128)(2,1)S(1)}, u32[]{:S(2)}, u32[]{:S(2)}) collective-permute-start(bf16[3,96,512]{2,1,0:T(8,128)(2,1)S(1)} %copy-done.33), channel_id=1, source_target_pairs={{0,3},{1,0},{2,1},{3,2},{4,7},{5,4},{6,5},{7,6},{8,11},{9,8},{10,9... | collective-permute-start | bytes 884744 | tf_op jit(solution)/shard_map/ppermute | solution.py:388
  171.9 12.0 %copy-start.14 = (bf16[8,64,512]{2,1,0:T(8,128)(2,1)}, bf16[8,64,512]{2,1,0:T(8,128)(2,1)S(1)}, u32[]{:S(2)}) copy-start(bf16[8,64,512]{2,1,0:T(8,128)(2,1)S(1)} %collective-permute-done.22.refs_0_) | copy-start | bytes 1572868
  171.9 12.0 %copy-start.15 = (bf16[8,64,512]{2,1,0:T(8,128)(2,1)}, bf16[8,64,512]{2,1,0:T(8,128)(2,1)S(1)}, u32[]{:S(2)}) copy-start(bf16[8,64,512]{2,1,0:T(8,128)(2,1)S(1)} %collective-permute-done.23.refs_1_) | copy-start | bytes 1572868
  171.9 12.0 %copy-start.16 = (bf16[8,64,512]{2,1,0:T(8,128)(2,1)}, bf16[8,64,512]{2,1,0:T(8,128)(2,1)S(1)}, u32[]{:S(2)}) copy-start(bf16[8,64,512]{2,1,0:T(8,128)(2,1)S(1)} %collective-permute-done.24.refs_2_) | copy-start | bytes 1572868
  197.5 6.3 %copy-start.6 = (f32[4,4,96,128]{3,2,1,0:T(8,128)S(1)}, f32[4,4,96,128]{3,2,1,0:T(8,128)}, u32[]{:S(2)}) copy-start(f32[4,4,96,128]{3,2,1,0:T(8,128)} %get-tuple-element.168) | copy-start | bytes 2359300
  197.5 6.2 %collective-permute-start.27 = (f32[4,4,96,128]{3,2,1,0:T(8,128)}, f32[4,4,96,128]{3,2,1,0:T(8,128)S(1)}, u32[]{:S(2)}, u32[]{:S(2)}) collective-permute-start(f32[4,4,96,128]{3,2,1,0:T(8,128)} %get-tuple-element.169), channel_id=1, source_target_pairs={{0,4},{4,0},{1,5},{5,1},{2,6},{6,2},{3,7},{7,3},{8,12},{12,8},{9,1... | collective-permute-start | bytes 2359304 | tf_op jit(solution)/shard_map/ppermute | solution.py:391
  203.8 26.5 %copy-start.32 = (bf16[8,64,512]{2,1,0:T(8,128)(2,1)S(1)}, bf16[8,64,512]{2,1,0:T(8,128)(2,1)}, u32[]{:S(2)}) copy-start(bf16[8,64,512]{2,1,0:T(8,128)(2,1)} %get-tuple-element.189) | copy-start | bytes 1572868
  203.8 26.8 %copy-start.31 = (bf16[8,64,512]{2,1,0:T(8,128)(2,1)S(1)}, bf16[8,64,512]{2,1,0:T(8,128)(2,1)}, u32[]{:S(2)}) copy-start(bf16[8,64,512]{2,1,0:T(8,128)(2,1)} %get-tuple-element.190) | copy-start | bytes 1572868
  203.9 8.7 %collective-permute-start.30 = (f32[4,96,128]{2,1,0:T(8,128)S(1)}, f32[4,96,128]{2,1,0:T(8,128)S(1)}, u32[]{:S(2)}, u32[]{:S(2)}) collective-permute-start(f32[4,96,128]{2,1,0:T(8,128)S(1)} %get-tuple-element.200), channel_id=1, source_target_pairs={{0,24},{8,16},{16,8},{24,0},{1,25},{9,17},{17,9},{25,1},{2,26},{10... | collective-permute-start | bytes 589832 | tf_op jit(solution)/shard_map/ppermute | solution.py:385
  206.2 10.1 %collective-permute-start.29 = (f32[4,96,128]{2,1,0:T(8,128)S(1)}, f32[4,96,128]{2,1,0:T(8,128)S(1)}, u32[]{:S(2)}, u32[]{:S(2)}) collective-permute-start(f32[4,96,128]{2,1,0:T(8,128)S(1)} %get-tuple-element.201), channel_id=1, source_target_pairs={{0,16},{8,24},{16,0},{24,8},{1,17},{9,25},{17,1},{25,9},{2,18},{10... | collective-permute-start | bytes 589832 | tf_op jit(solution)/shard_map/ppermute | solution.py:385
  206.8 10.1 %collective-permute-start.28 = (f32[4,96,128]{2,1,0:T(8,128)S(1)}, f32[4,96,128]{2,1,0:T(8,128)S(1)}, u32[]{:S(2)}, u32[]{:S(2)}) collective-permute-start(f32[4,96,128]{2,1,0:T(8,128)S(1)} %get-tuple-element.199), channel_id=1, source_target_pairs={{0,8},{8,0},{16,24},{24,16},{1,9},{9,1},{17,25},{25,17},{2,10},{10... | collective-permute-start | bytes 589832 | tf_op jit(solution)/shard_map/ppermute | solution.py:385
  207.5 28.8 %collective-permute-start.32 = (bf16[8,64,512]{2,1,0:T(8,128)(2,1)}, bf16[8,64,512]{2,1,0:T(8,128)(2,1)S(1)}, u32[]{:S(2)}, u32[]{:S(2)}) collective-permute-start(bf16[8,64,512]{2,1,0:T(8,128)(2,1)} %get-tuple-element.180), channel_id=1, source_target_pairs={{0,0},{4,16},{8,8},{12,24},{16,4},{20,20},{24,12},{28,28},{1,1},{5... | collective-permute-start | bytes 1572872 | tf_op jit(solution)/shard_map/ppermute | solution.py:509
  209.2 28.7 %collective-permute-start.36 = (bf16[8,64,512]{2,1,0:T(8,128)(2,1)}, bf16[8,64,512]{2,1,0:T(8,128)(2,1)S(1)}, u32[]{:S(2)}, u32[]{:S(2)}) collective-permute-start(bf16[8,64,512]{2,1,0:T(8,128)(2,1)} %get-tuple-element.188), channel_id=1, source_target_pairs={{0,8},{4,24},{8,0},{12,16},{16,12},{20,28},{24,4},{28,20},{1,9},{5... | collective-permute-start | bytes 1572872 | tf_op jit(solution)/shard_map/ppermute | solution.py:509
  217.0 1.4 collective-permute-start.31
  223.1 14.8 %copy-start.36 = (bf16[96,512]{1,0:T(8,128)(2,1)S(1)}, bf16[96,512]{1,0:T(8,128)(2,1)}, u32[]{:S(2)}) copy-start(bf16[96,512]{1,0:T(8,128)(2,1)} %get-tuple-element.187) | copy-start | bytes 294916
  223.1 7.1 %collective-permute-start.39 = (bf16[4,96,64]{2,1,0:T(8,128)(2,1)}, bf16[4,96,64]{2,1,0:T(8,128)(2,1)S(1)}, u32[]{:S(2)}, u32[]{:S(2)}) collective-permute-start(bf16[4,96,64]{2,1,0:T(8,128)(2,1)} %get-tuple-element.192), channel_id=1, source_target_pairs={{0,8},{8,0},{16,24},{24,16},{1,9},{9,1},{17,25},{25,17},{2,10},{10... | collective-permute-start | bytes 147464 | tf_op jit(solution)/shard_map/ppermute | solution.py:385
  224.5 6.1 %collective-permute-start.40 = (bf16[4,96,64]{2,1,0:T(8,128)(2,1)}, bf16[4,96,64]{2,1,0:T(8,128)(2,1)S(1)}, u32[]{:S(2)}, u32[]{:S(2)}) collective-permute-start(bf16[4,96,64]{2,1,0:T(8,128)(2,1)} %get-tuple-element.193), channel_id=1, source_target_pairs={{0,16},{8,24},{16,0},{24,8},{1,17},{9,25},{17,1},{25,9},{2,18},{10... | collective-permute-start | bytes 147464 | tf_op jit(solution)/shard_map/ppermute | solution.py:385
  226.0 5.8 %collective-permute-start.41 = (bf16[4,96,64]{2,1,0:T(8,128)(2,1)}, bf16[4,96,64]{2,1,0:T(8,128)(2,1)S(1)}, u32[]{:S(2)}, u32[]{:S(2)}) collective-permute-start(bf16[4,96,64]{2,1,0:T(8,128)(2,1)} %get-tuple-element.194), channel_id=1, source_target_pairs={{0,24},{8,16},{16,8},{24,0},{1,25},{9,17},{17,9},{25,1},{2,26},{10... | collective-permute-start | bytes 147464 | tf_op jit(solution)/shard_map/ppermute | solution.py:385
  230.3 10.6 %collective-permute-start.37 = (bf16[8,64,512]{2,1,0:T(8,128)(2,1)S(1)}, bf16[8,64,512]{2,1,0:T(8,128)(2,1)S(1)}, u32[]{:S(2)}, u32[]{:S(2)}) collective-permute-start(bf16[8,64,512]{2,1,0:T(8,128)(2,1)S(1)} %copy-done.32), channel_id=1, source_target_pairs={{0,16},{4,0},{8,24},{12,8},{16,20},{20,4},{24,28},{28,12},{1,17},{... | collective-permute-start | bytes 1572872 | tf_op jit(solution)/shard_map/ppermute | solution.py:509
  230.6 13.3 %collective-permute-start.38 = (bf16[8,64,512]{2,1,0:T(8,128)(2,1)S(1)}, bf16[8,64,512]{2,1,0:T(8,128)(2,1)S(1)}, u32[]{:S(2)}, u32[]{:S(2)}) collective-permute-start(bf16[8,64,512]{2,1,0:T(8,128)(2,1)S(1)} %copy-done.31), channel_id=1, source_target_pairs={{0,24},{4,8},{8,16},{12,0},{16,28},{20,12},{24,20},{28,4},{1,25},{... | collective-permute-start | bytes 1572872 | tf_op jit(solution)/shard_map/ppermute | solution.py:509
  236.3 8.7 %collective-permute-start.33 = (bf16[96,512]{1,0:T(8,128)(2,1)}, bf16[96,512]{1,0:T(8,128)(2,1)S(1)}, u32[]{:S(2)}, u32[]{:S(2)}) collective-permute-start(bf16[96,512]{1,0:T(8,128)(2,1)} %get-tuple-element.183), channel_id=1, source_target_pairs={{0,3},{1,0},{2,1},{3,2},{4,7},{5,4},{6,5},{7,6},{8,11},{9,8},{10,9... | collective-permute-start | bytes 294920 | tf_op jit(solution)/shard_map/ppermute | solution.py:388
  236.8 10.1 %collective-permute-start.34 = (bf16[96,512]{1,0:T(8,128)(2,1)}, bf16[96,512]{1,0:T(8,128)(2,1)S(1)}, u32[]{:S(2)}, u32[]{:S(2)}) collective-permute-start(bf16[96,512]{1,0:T(8,128)(2,1)} %get-tuple-element.185), channel_id=1, source_target_pairs={{0,2},{1,3},{2,0},{3,1},{4,6},{5,7},{6,4},{7,5},{8,10},{9,11},{10,... | collective-permute-start | bytes 294920 | tf_op jit(solution)/shard_map/ppermute | solution.py:388
  237.9 9.0 %collective-permute-start.35 = (bf16[96,512]{1,0:T(8,128)(2,1)S(1)}, bf16[96,512]{1,0:T(8,128)(2,1)S(1)}, u32[]{:S(2)}, u32[]{:S(2)}) collective-permute-start(bf16[96,512]{1,0:T(8,128)(2,1)S(1)} %copy-done.36), channel_id=1, source_target_pairs={{0,1},{1,2},{2,3},{3,0},{4,5},{5,6},{6,7},{7,4},{8,9},{9,10},{10,1... | collective-permute-start | bytes 294920 | tf_op jit(solution)/shard_map/ppermute | solution.py:388
  (15 other events, 17.2 us)

commit v7 on v5

--- a/solution.py
+++ b/solution.py
@@ -9,7 +9,7 @@
 
 CAPD = 12
 GROUP = 4
-CHUNKS = 2
+CHUNKS = 1
 
 adapter_scale = 0.5
 
@@ -294,14 +294,6 @@
                 outs[r][g * GROUP + e] = total[pl.ds(first, rloc), :].astype(BF16)
 
 
-def place_kernel(fsdp, at, *refs):
-    for r in range(fsdp):
-
-        @pl.when(pl.program_id(0) == r)
-        def _():
-            refs[-1][...] = refs[r][...].astype(F32)
-
-
 def delta_kernel(fsdp, ad, gslots, at, own, got, up, *outs):
     for g in range(up.shape[0] // GROUP):
         rows = pl.ds(g * gslots, gslots)
@@ -434,32 +426,26 @@
         [((ad, slots, rank), F32)],
         [*dy, (adapter_up_weight, None)],
     )
+    x_other = swap(x_plain)
+    back, back_got = after((back, swap(back)), x_other)
     (both,) = call(
         functools.partial(both_kernel, ad),
         [((ad, slots, vloc + rank), BF16)],
-        [(back, None), (swap(back), None), *dy],
-    )
-
+        [(back, None), (back_got, None), *dy],
+    )
     down_got = lax.ppermute(after(down_other, both), ("fsdp", "tp"), pairs)
+    both = [over_f(both, k) for k in range(fsdp)]
 
     x_chip = lax.dynamic_slice_in_dim(input_rows, f * kf_width, kf_width, 1)
-    x_other = after(swap(x_plain), both, down_got)
+    x_chip = after(x_chip, x_routed[0][2], *both, down_got)
     base = call(
         functools.partial(base_kernel, fsdp),
         [((rows, vloc), F32)] * fsdp,
         [(v, None) for v in (x_chip, x_plain, x_other, value_weight_frozen)],
         at=numbers(t),
-        flops=20 * fsdp * rows * kt * vloc,
-    )
-    base_plain = base[0]
-
-    both = [both] * fsdp
-    both[1], both[2] = over_f(both[1], 1), over_f(both[2], 2)
-    both[3] = over_f(both[3], 3)
+    )
     base = [over_f(v, k) for k, v in enumerate(base)]
-    for c in range(1, CHUNKS):
-        chunk = [after(v, *x_routed[c - 1], *both, base_plain) for v in sends[c * ad : (c + 1) * ad]]
-        x_routed.append([over_a(v, ka) for ka, v in enumerate(chunk)])
+    x_routed[0] = after(x_routed[0], *base)
 
     def chunk_of(c, routed):
         return [(v, (c * cw, cw)) for v in own] + [(v, None) for v in routed]
@@ -474,57 +460,32 @@
             either=(adapter_down_weight, down_got, (c * cw, cw)),
         )
 
-    grad_a = None
-    hid = []
-    for c in range(CHUNKS):
-        last = c == CHUNKS - 1
-        if last:
-            hid = hidden(c, hid, x_routed[c])
-            hid = hid[0] + swap(hid[1])
-            hid, both = lax.optimization_barrier((hid, both))
-            hid = [over_f(hid[k], k) for k in range(fsdp)]
-        sums = call(
-            functools.partial(down_grad_kernel, fsdp, ad, gslots),
-            [((dloc, rloc, cw), BF16)] * fsdp,
-            [*chunk_of(c, x_routed[c]), *[(v, (vloc, rank)) for v in both]],
-            at=numbers(*[(t ^ (r // 2)) * 2 + (fx ^ (r % 2)) for r in range(fsdp)]),
-            scratch=[pltpu.VMEM((GROUP * rank, cw), F32)],
-        )
-        got = []
-        if not last:
-            hid = hidden(c, hid, after(x_routed[c], x_routed[c + 1][2], *sums))
-            sums = [*sums[:2], *after(sums[2:], hid)]
-        for r in range(fsdp):
-            p, q = r % 2, r // 2
-            perm = [
-                ((y * 2 + x) * 2 + s, ((s ^ q) * 2 + (x ^ p)) * 2 + y)
-                for y in range(2)
-                for x in range(2)
-                for s in range(2)
-            ]
-            got.append(lax.ppermute(sums[r], ("fsdp", "tp"), perm))
-        at = [
-            ((fx ^ (r % 2)) * kf_width + (fy ^ (r // 2)) * kt + c * cw) // cw
-            for r in range(fsdp)
+    hid = hidden(0, [], x_routed[0])
+    hid, both = lax.optimization_barrier((hid, both))
+    hid = hid[0] + swap(hid[1])
+
+    sums = call(
+        functools.partial(down_grad_kernel, fsdp, ad, gslots),
+        [((dloc, rloc, kt), BF16)] * fsdp,
+        [*chunk_of(0, x_routed[0]), *[(v, (vloc, rank)) for v in both]],
+        at=numbers(*[(t ^ (r // 2)) * 2 + (fx ^ (r % 2)) for r in range(fsdp)]),
+        scratch=[pltpu.VMEM((GROUP * rank, kt), F32)],
+        flops=20 * dloc * rank * kt * 192,
+    )
+    hid, sums = lax.optimization_barrier((hid, sums))
+    hid = [over_f(hid[k], k) for k in range(fsdp)]
+    grad_a = jnp.zeros((dloc, rloc, half), F32)
+    for r in range(fsdp):
+        p, q = r % 2, r // 2
+        perm = [
+            ((y * 2 + x) * 2 + s, ((s ^ q) * 2 + (x ^ p)) * 2 + y)
+            for y in range(2)
+            for x in range(2)
+            for s in range(2)
         ]
-        if c == 0:
-            grad_a = pl.pallas_call(
-                functools.partial(place_kernel, fsdp),
-                out_shape=jax.ShapeDtypeStruct((dloc, rloc, half), F32),
-                grid_spec=pltpu.PrefetchScalarGridSpec(
-                    num_scalar_prefetch=1,
-                    grid=(fsdp,),
-                    in_specs=[VMEM] * fsdp,
-                    out_specs=pl.BlockSpec((dloc, rloc, cw), lambda i, at: (0, 0, at[i])),
-                ),
-                cost_estimate=pl.CostEstimate(flops=1, bytes_accessed=1, transcendentals=0),
-            )(numbers(*at), *after(got, x_routed[1][1]))
-            x_routed[c + 1] = after(x_routed[c + 1], grad_a, *base)
-        else:
-            for v, column in zip(got, at):
-                grad_a = lax.dynamic_update_slice_in_dim(
-                    grad_a, v.astype(F32), column * cw, 2
-                )
+        got = lax.ppermute(sums[r], ("fsdp", "tp"), perm)
+        at = (fx ^ p) * kf_width + (fy ^ q) * kt
+        grad_a = lax.dynamic_update_slice_in_dim(grad_a, got.astype(F32), at, 2)
 
     hid_own = (hid[0] + hid[1] + hid[2] + hid[3]).astype(BF16)
     outs = call(
@@ -534,7 +495,7 @@
         at=numbers(t, *[f ^ k for k in range(fsdp)]),
     )
     returned = [over_a(v, (ad - ka) % ad) for ka, v in enumerate(outs[:ad])]
-    hid_cols = [over_f(after(v, got[0], got[1]), k) for k, v in enumerate(outs[ad:])]
+    hid_cols = [over_f(v, k) for k, v in enumerate(outs[ad:])]
 
     (y_out,) = call(
         functools.partial(output_kernel, fsdp, ad),

time: 222 us -> 238 us (1.072)
  waiting for transfers between devices: 67.2 us -> 109 us
  starting transfers between devices: 68.6 us -> 52.9 us
  Pallas kernels: 60.7 us -> 50.2 us
  other arithmetic: 9.91 us -> 5.38 us
  local copies, waits for them, and re-layouts: 14.1 us -> 18.1 us
    ppermute x15, waiting for transfers between devices: 30.8 us -> 57.1 us  [over_f(): lax.ppermute(v, 'fsdp', [(i, i ^ k) for i in range(fsdp)])]
    ppermute x12 -> x9, waiting for transfers between devices: 27.2 us -> 42.3 us  [over_a(): lax.ppermute(v, 'ad', [(i, (i + k) % ad) for i in range(ad)])]
    ppermute x12 -> x9, starting transfers between devices: 30.1 us -> 21.3 us  [over_a(): lax.ppermute(v, 'ad', [(i, (i + k) % ad) for i in range(ad)])]
    pallas_call x12 -> x10, Pallas kernels: 56 us -> 50.2 us  [call(): pl.pallas_call(body, out_shape=[jax.ShapeDtypeStruct(shape, dtype) for sh...]
    pallas_call x1 -> x0, Pallas kernels: 4.65 us -> none  [column_body(): pl.pallas_call(functools.partial(place_kernel, fsdp), out_shape=jax.Shape...]
    ppermute x8 -> x4, starting transfers between devices: 11.8 us -> 8.18 us  [column_body(): got = lax.ppermute(sums[r], ('fsdp', 'tp'), perm)]
    ppermute x8 -> x4, waiting for transfers between devices: 4.58 us -> 7.8 us  [column_body(): got = lax.ppermute(sums[r], ('fsdp', 'tp'), perm)]
    unnamed x74 -> x48, local copies, waits for them, and re-layouts: 3.88 us -> 6.99 us
  transfers between devices with their start and end apart: 40 -> 33, of which waited for: 21 -> 20; matrix products, arithmetic and copies ran while one was open for 7% -> 4% of each run, Pallas kernels for 18% -> 14%
where the time goes in v7:
time: 238 us; the launch traced here: 237 us
  waiting for transfers between devices  109 us (46%)
  starting transfers between devices  52.9 us (22%)
  Pallas kernels  50.2 us (21%)
  local copies, waits for them, and re-layouts  18.1 us (8%)
  other arithmetic  5.38 us (2%)
    ppermute x15, waiting for transfers between devices, over_f(): lax.ppermute(v, 'fsdp', [(i, i ^ k) for i in range(fsdp)])  57.1 us
    pallas_call x10, Pallas kernels, call(): pl.pallas_call(body, out_shape=[jax.ShapeDtypeStruct(shape, dtype) for sh...  50.2 us
    ppermute x9, waiting for transfers between devices, over_a(): lax.ppermute(v, 'ad', [(i, (i + k) % ad) for i in range(ad)])  42.3 us
    ppermute x9, starting transfers between devices, over_a(): lax.ppermute(v, 'ad', [(i, (i + k) % ad) for i in range(ad)])  21.3 us
    ppermute x15, starting transfers between devices, over_f(): lax.ppermute(v, 'fsdp', [(i, i ^ k) for i in range(fsdp)])  18.4 us
    ppermute x4, starting transfers between devices, column_body(): got = lax.ppermute(sums[r], ('fsdp', 'tp'), perm)  8.18 us
    ppermute x4, waiting for transfers between devices, column_body(): got = lax.ppermute(sums[r], ('fsdp', 'tp'), perm)  7.8 us
    unnamed x48, local copies, waits for them, and re-layouts  6.99 us
  transfers between devices with their start and end apart: 33, of which 20 were waited for; matrix products, arithmetic and copies ran while one was open for 4% of the time, Pallas kernels for 14%

profile of v7, /device:TPU:0, one launch (start us, length us, event | category | flops | bytes accessed | tf_op | source)
XLA Modules:
  0.0 237.0 jit_solution(18136951275644396698)
XLA Ops:
  0.7 0.7 bitcast_convert_fusion
  1.3 2.5 %constant_dynamic-slice_fusion.1 = (bf16[256,1024]{1,0:T(8,128)(2,1)S(1)}, bf16[256,1024]{1,0:T(8,128)(2,1)S(1)}, bf16[256,1024]{1,0:T(8,128)(2,1)}, bf16[256,1024]{1,0:T(8,128)(2,1)S(1)}) fusion(bf16[256,8192]{1,0:T(8,128)(2,1)} %param.6, s32[]{:T(128)S(6)} %select_n.45, s32[]{:T(128)S(6)} %select_n.43, s32[]{:T(128)S(6)} %select_n.42, s32[]{:T(128)S(6)} %select_n.44), kind=kLoop, calls=%fused_computation.17 | loop fusion | bytes 4194320 | tf_op jit(solution)/shard_map/dynamic_slice | solution.py:392
  3.9 1.1 fusion.3
  5.0 2.9 %collective-permute-start = (bf16[272,1024]{1,0:T(8,128)(2,1)}, bf16[272,1024]{1,0:T(8,128)(2,1)S(1)}, u32[]{:S(2)}, u32[]{:S(2)}) collective-permute-start(bf16[272,1024]{1,0:T(8,128)(2,1)} %get-tuple-element.68), channel_id=1, source_target_pairs={{0,8},{8,0},{16,24},{24,16},{1,9},{9,1},{17,25},{25,17},{2,10},{10... | collective-permute-start | bytes 1671176 | tf_op jit(solution)/shard_map/ppermute | solution.py:376
  7.9 1.5 collective-permute-start.1
  9.5 2.7 %shard_map.85 = (bf16[384,256]{1,0:T(8,128)(2,1)}, bf16[96,1536]{1,0:T(8,128)(2,1)}, bf16[96,1536]{1,0:T(8,128)(2,1)}, bf16[96,1536]{1,0:T(8,128)(2,1)}, bf16[96,1536]{1,0:T(8,128)(2,1)}) custom-call(s32[1]{0:T(128)} %bitcast.1.refs_0_, s32[1,256]{1,0:T(1,128)} %bitcast.28, bf16[256,1024]{1,0:T(8,128)(2,1)} %get-tuple-element.71.refs_2_, ...), custom_call_target="tpu_custom_call" | custom-call | flops 1 | bytes 1 | tf_op jit(solution)/shard_map/pallas_call | solution.py:154
  12.2 2.1 collective-permute-start.3
  14.3 2.6 %collective-permute-start.4 = (bf16[96,1536]{1,0:T(8,128)(2,1)}, bf16[96,1536]{1,0:T(8,128)(2,1)S(1)}, u32[]{:S(2)}, u32[]{:S(2)}) collective-permute-start(bf16[96,1536]{1,0:T(8,128)(2,1)} %get-tuple-element.74), channel_id=1, source_target_pairs={{0,2},{1,3},{2,0},{3,1},{4,6},{5,7},{6,4},{7,5},{8,10},{9,11},{10,... | collective-permute-start | bytes 884744 | tf_op jit(solution)/shard_map/ppermute | solution.py:379
  16.9 4.7 %collective-permute-done.refs_1_ = bf16[272,1024]{1,0:T(8,128)(2,1)S(1)} collective-permute-done((bf16[272,1024]{1,0:T(8,128)(2,1)}, bf16[272,1024]{1,0:T(8,128)(2,1)S(1)}, u32[]{:S(2)}, u32[]{:S(2)}) %collective-permute-start) | collective-permute-done | bytes 557088 | tf_op jit(solution)/shard_map/ppermute | solution.py:376
  21.6 4.2 %collective-permute-start.5 = (bf16[96,1536]{1,0:T(8,128)(2,1)}, bf16[96,1536]{1,0:T(8,128)(2,1)S(1)}, u32[]{:S(2)}, u32[]{:S(2)}) collective-permute-start(bf16[96,1536]{1,0:T(8,128)(2,1)} %get-tuple-element.76), channel_id=1, source_target_pairs={{0,3},{1,0},{2,1},{3,2},{4,7},{5,4},{6,5},{7,6},{8,11},{9,8},{10,9... | collective-permute-start | bytes 884744 | tf_op jit(solution)/shard_map/ppermute | solution.py:379
  25.8 4.6 %constant_dynamic-slice_fusion = bf16[8,256,1024]{2,1,0:T(8,128)(2,1)} fusion(bf16[8,256,4096]{2,1,0:T(8,128)(2,1)} %refs_9_.1, s32[]{:T(128)S(6)} %select_n.47), kind=kLoop, calls=%fused_computation.16 | loop fusion | bytes 8388612 | tf_op jit(solution)/shard_map/dynamic_slice | solution.py:411
  30.4 5.1 %collective-permute-done.4.refs_2_.refs_4_.refs_3_ = bf16[96,1536]{1,0:T(8,128)(2,1)S(1)} collective-permute-done((bf16[96,1536]{1,0:T(8,128)(2,1)}, bf16[96,1536]{1,0:T(8,128)(2,1)S(1)}, u32[]{:S(2)}, u32[]{:S(2)}) %collective-permute-start.4) | collective-permute-done | bytes 294944 | tf_op jit(solution)/shard_map/ppermute | solution.py:379
  35.5 0.7 collective-permute-done.5.refs_3_.refs_5_.refs_4_
  36.5 4.7 %shard_map.86 = (bf16[3,96,1024]{2,1,0:T(8,128)(2,1)}, bf16[3,96,1024]{2,1,0:T(8,128)(2,1)}, bf16[3,96,1024]{2,1,0:T(8,128)(2,1)}, bf16[3,96,1024]{2,1,0:T(8,128)(2,1)}, bf16[3,256,1024]{2,1,0:T(8,128)(2,1)}) custom-call(s32[1]{0:T(128)} %bitcast.1.refs_0_, bf16[272,1024]{1,0:T(8,128)(2,1)} %copy-done.8, bf16[272,1024]{1,0:T(8,128)(2,1)} %copy-done.9, ...), custom_call_target="tpu_custom_call" | custom-call | flops 1 | bytes 1 | tf_op jit(solution)/shard_map/pallas_call | solution.py:154
  41.4 3.5 %shard_map.87.refs_0_ = f32[4,96,256]{2,1,0:T(8,128)} custom-call(bf16[96,1536]{1,0:T(8,128)(2,1)} %get-tuple-element.87.refs_0_.refs_2_.refs_1_, bf16[96,1536]{1,0:T(8,128)(2,1)} %copy-done.1, bf16[96,1536]{1,0:T(8,128)(2,1)} %copy-done.2, bf16[96,1536]{1,0:T(8,128)(2,1)} %copy-done.3, bf16[8,256,512]{2,1,0:T(8,128)(2,1)} %refs_3_.3), custom_call_target="tpu_custom_call" | custom-call | flops 1 | bytes 1 | tf_op jit(solution)/shard_map/pallas_call | solution.py:154
  45.4 1.6 collective-permute-done.7.refs_1_
  46.9 0.7 copy-done.15
  47.7 2.8 %shard_map.88.refs_9_.refs_4_ = bf16[4,96,768]{2,1,0:T(8,128)(2,1)} custom-call(f32[4,96,256]{2,1,0:T(8,128)} %shard_map.87.refs_0_, f32[4,96,256]{2,1,0:T(8,128)} %copy-done.15, bf16[96,1536]{1,0:T(8,128)(2,1)} %get-tuple-element.87.refs_0_.refs_2_.refs_1_, bf16[96,1536]{1,0:T(8,128)(2,1)} %copy-done.1, bf16[96,1536]{1,0:T(8,128)(2,1)} %copy-done.2, ...), custom_call_target="tpu_custom_call" | custom-call | flops 1 | bytes 1 | tf_op jit(solution)/shard_map/pallas_call | solution.py:154
  50.4 4.3 %collective-permute-start.12 = (bf16[8,256,1024]{2,1,0:T(8,128)(2,1)}, bf16[8,256,1024]{2,1,0:T(8,128)(2,1)}, u32[]{:S(2)}, u32[]{:S(2)}) collective-permute-start(bf16[8,256,1024]{2,1,0:T(8,128)(2,1)} %constant_dynamic-slice_fusion), channel_id=1, source_target_pairs={{0,4},{8,12},{20,16},{28,24},{1,5},{9,13},{21,17},{29,25},{2,6},{1... | collective-permute-start | bytes 12582920 | tf_op jit(solution)/shard_map/ppermute | solution.py:436
  54.7 4.9 %collective-permute-start.6 = (bf16[3,96,1024]{2,1,0:T(8,128)(2,1)S(1)}, bf16[3,96,1024]{2,1,0:T(8,128)(2,1)S(1)}, u32[]{:S(2)}, u32[]{:S(2)}) collective-permute-start(bf16[3,96,1024]{2,1,0:T(8,128)(2,1)S(1)} %copy-done.23), channel_id=1, source_target_pairs={{0,2},{1,3},{2,0},{3,1},{4,6},{5,7},{6,4},{7,5},{8,10},{9,11},{10,... | collective-permute-start | bytes 1769480 | tf_op jit(solution)/shard_map/ppermute | solution.py:379
  59.6 3.0 %collective-permute-start.10 = (bf16[4,96,768]{2,1,0:T(8,128)(2,1)}, bf16[4,96,768]{2,1,0:T(8,128)(2,1)}, u32[]{:S(2)}, u32[]{:S(2)}) collective-permute-start(bf16[4,96,768]{2,1,0:T(8,128)(2,1)} %shard_map.88.refs_9_.refs_4_), channel_id=1, source_target_pairs={{0,16},{8,24},{16,0},{24,8},{1,17},{9,25},{17,1},{25,9},{2,18},{10... | collective-permute-start | bytes 1769480 | tf_op jit(solution)/shard_map/ppermute | solution.py:376
  63.1 20.1 %collective-permute-done.6.refs_7_ = bf16[3,96,1024]{2,1,0:T(8,128)(2,1)S(1)} collective-permute-done((bf16[3,96,1024]{2,1,0:T(8,128)(2,1)S(1)}, bf16[3,96,1024]{2,1,0:T(8,128)(2,1)S(1)}, u32[]{:S(2)}, u32[]{:S(2)}) %collective-permute-start.6) | collective-permute-done | bytes 589856 | tf_op jit(solution)/shard_map/ppermute | solution.py:379
  83.2 0.7 collective-permute-start.16
  83.9 3.1 %collective-permute-start.17 = (bf16[3,96,1024]{2,1,0:T(8,128)(2,1)}, bf16[3,96,1024]{2,1,0:T(8,128)(2,1)}, u32[]{:S(2)}, u32[]{:S(2)}) collective-permute-start(bf16[3,96,1024]{2,1,0:T(8,128)(2,1)} %get-tuple-element.103), channel_id=1, source_target_pairs={{0,3},{1,0},{2,1},{3,2},{4,7},{5,4},{6,5},{7,6},{8,11},{9,8},{10,9... | collective-permute-start | bytes 1769480 | tf_op jit(solution)/shard_map/ppermute | solution.py:379
  87.0 2.3 constant_dynamic-slice_fusion.5.refs_1_
  89.3 6.0 %shard_map.89 = (f32[256,512]{1,0:T(8,128)}, f32[256,512]{1,0:T(8,128)}, f32[256,512]{1,0:T(8,128)}, f32[256,512]{1,0:T(8,128)}) custom-call(s32[1]{0:T(128)} %bitcast.refs_0_, bf16[256,2048]{1,0:T(8,128)(2,1)} %constant_dynamic-slice_fusion.5.refs_1_, bf16[3,256,1024]{2,1,0:T(8,128)(2,1)} %get-tuple-element.86.refs_2_, bf16[3,256,1024]{2,1,0:T(8,128)(2,1)} %copy-done.4, ...), custom_call_target="tpu_custom_call" | custom-call | flops 1 | bytes 1 | tf_op jit(solution)/shard_map/pallas_call | solution.py:154
  95.4 1.6 collective-permute-start.13
  96.9 2.0 collective-permute-start.14
  98.9 0.6 pad_add_fusion.refs_0_
  99.5 1.9 collective-permute-done.16.refs_6_
  101.4 10.4 %collective-permute-done.17.refs_8_ = bf16[3,96,1024]{2,1,0:T(8,128)(2,1)} collective-permute-done((bf16[3,96,1024]{2,1,0:T(8,128)(2,1)}, bf16[3,96,1024]{2,1,0:T(8,128)(2,1)}, u32[]{:S(2)}, u32[]{:S(2)}) %collective-permute-start.17) | collective-permute-done | bytes 589856 | tf_op jit(solution)/shard_map/ppermute | solution.py:379
  111.8 9.5 %collective-permute-done.14.refs_2_ = f32[256,512]{1,0:T(8,128)S(1)} collective-permute-done((f32[256,512]{1,0:T(8,128)}, f32[256,512]{1,0:T(8,128)S(1)}, u32[]{:S(2)}, u32[]{:S(2)}) %collective-permute-start.14) | collective-permute-done | bytes 524320 | tf_op jit(solution)/shard_map/ppermute | solution.py:376
  121.4 0.6 collective-permute-done.15.refs_3_
  122.0 10.7 %shard_map.90 = (f32[4,4,96,128]{3,2,1,0:T(8,128)}, f32[4,4,96,128]{3,2,1,0:T(8,128)}) custom-call(s32[3]{0:T(128)} %pad_add_fusion.refs_0_, bf16[96,1536]{1,0:T(8,128)(2,1)} %get-tuple-element.87.refs_0_.refs_2_.refs_1_, bf16[96,1536]{1,0:T(8,128)(2,1)} %copy-done.1, bf16[96,1536]{1,0:T(8,128)(2,1)} %copy-done.2, bf16[96,1536]{1,0:T(8,128)(2,1)} %copy-done.3, ...), custom_call_target="tpu_custom_call" | custom-call | flops 1 | bytes 1 | tf_op jit(solution)/shard_map/pallas_call | solution.py:154
  133.4 9.0 %shard_map.91 = (bf16[8,64,1024]{2,1,0:T(8,128)(2,1)}, bf16[8,64,1024]{2,1,0:T(8,128)(2,1)}, bf16[8,64,1024]{2,1,0:T(8,128)(2,1)}, bf16[8,64,1024]{2,1,0:T(8,128)(2,1)}) custom-call(s32[4]{0:T(128)} %pad_add_fusion.1.refs_0_, bf16[96,1536]{1,0:T(8,128)(2,1)} %get-tuple-element.87.refs_0_.refs_2_.refs_1_, bf16[96,1536]{1,0:T(8,128)(2,1)} %copy-done.1, ...), custom_call_target="tpu_custom_call" | custom-call | flops 8053063680 | bytes 1 | tf_op jit(solution)/shard_map/pallas_call | solution.py:154
  142.5 1.9 collective-permute-start.26
  144.4 1.5 collective-permute-start.19
  145.9 2.2 collective-permute-start.21
  148.1 1.5 collective-permute-start.27
  149.6 1.7 collective-permute-done.19
  151.3 3.1 %collective-permute-start.28 = (bf16[8,64,1024]{2,1,0:T(8,128)(2,1)}, bf16[8,64,1024]{2,1,0:T(8,128)(2,1)S(1)}, u32[]{:S(2)}, u32[]{:S(2)}) collective-permute-start(bf16[8,64,1024]{2,1,0:T(8,128)(2,1)} %get-tuple-element.127), channel_id=1, source_target_pairs={{0,16},{4,0},{8,24},{12,8},{16,20},{20,4},{24,28},{28,12},{1,17},{... | collective-permute-start | bytes 3145736 | tf_op jit(solution)/shard_map/ppermute | solution.py:486
  154.4 3.7 %collective-permute-done.21 = f32[4,96,128]{2,1,0:T(8,128)S(1)} collective-permute-done((f32[4,96,128]{2,1,0:T(8,128)S(1)}, f32[4,96,128]{2,1,0:T(8,128)S(1)}, u32[]{:S(2)}, u32[]{:S(2)}) %collective-permute-start.21) | collective-permute-done | bytes 196640 | tf_op jit(solution)/shard_map/ppermute | solution.py:376
  158.1 30.2 %collective-permute-done.20 = f32[4,96,128]{2,1,0:T(8,128)S(1)} collective-permute-done((f32[4,96,128]{2,1,0:T(8,128)S(1)}, f32[4,96,128]{2,1,0:T(8,128)S(1)}, u32[]{:S(2)}, u32[]{:S(2)}) %collective-permute-start.20) | collective-permute-done | bytes 196640 | tf_op jit(solution)/shard_map/ppermute | solution.py:376
  189.0 0.7 collective-permute-done.22.refs_2_
  189.8 0.6 copy-done.19
  190.4 4.1 %shard_map.92 = (bf16[96,512]{1,0:T(8,128)(2,1)}, bf16[96,512]{1,0:T(8,128)(2,1)}, bf16[96,512]{1,0:T(8,128)(2,1)}, bf16[96,512]{1,0:T(8,128)(2,1)}, bf16[4,96,6...) custom-call(s32[5]{0:T(128)} %stack.57.refs_0_, ...), custom_call_target="tpu_custom_call" | custom-call | flops 1 | bytes 1 | tf_op jit(solution)/shard_map/pallas_call | solution.py:154
  194.5 2.5 %collective-permute-start.30 = (bf16[4,96,64]{2,1,0:T(8,128)(2,1)}, bf16[4,96,64]{2,1,0:T(8,128)(2,1)S(1)}, u32[]{:S(2)}, u32[]{:S(2)}) collective-permute-start(bf16[4,96,64]{2,1,0:T(8,128)(2,1)} %get-tuple-element.130), channel_id=1, source_target_pairs={{0,8},{8,0},{16,24},{24,16},{1,9},{9,1},{17,25},{25,17},{2,10},{10... | collective-permute-start | bytes 147464 | tf_op jit(solution)/shard_map/ppermute | solution.py:376
  197.1 3.3 %collective-permute-done.30.refs_1_ = bf16[4,96,64]{2,1,0:T(8,128)(2,1)S(1)} collective-permute-done((bf16[4,96,64]{2,1,0:T(8,128)(2,1)}, bf16[4,96,64]{2,1,0:T(8,128)(2,1)S(1)}, u32[]{:S(2)}, u32[]{:S(2)}) %collective-permute-start.30) | collective-permute-done | bytes 49184 | tf_op jit(solution)/shard_map/ppermute | solution.py:376
  200.4 0.7 collective-permute-start.32
  201.1 0.8 collective-permute-done.31.refs_2_
  201.9 0.6 copy-done.21
  202.5 1.1 collective-permute-start.23
  203.7 2.4 %collective-permute-done.32.refs_3_ = bf16[4,96,64]{2,1,0:T(8,128)(2,1)S(1)} collective-permute-done((bf16[4,96,64]{2,1,0:T(8,128)(2,1)}, bf16[4,96,64]{2,1,0:T(8,128)(2,1)S(1)}, u32[]{:S(2)}, u32[]{:S(2)}) %collective-permute-start.32) | collective-permute-done | bytes 49184 | tf_op jit(solution)/shard_map/ppermute | solution.py:376
  206.1 0.6 copy-done.22
  207.3 1.7 collective-permute-start.29
  209.1 3.4 %collective-permute-done.24.refs_7_ = bf16[96,512]{1,0:T(8,128)(2,1)S(1)} collective-permute-done((bf16[96,512]{1,0:T(8,128)(2,1)}, bf16[96,512]{1,0:T(8,128)(2,1)S(1)}, u32[]{:S(2)}, u32[]{:S(2)}) %collective-permute-start.24) | collective-permute-done | bytes 98336 | tf_op jit(solution)/shard_map/ppermute | solution.py:379
  212.5 2.3 collective-permute-start.25
  214.8 3.9 %shard_map.94 = f32[8,64,512]{2,1,0:T(8,128)} custom-call(bf16[4,96,64]{2,1,0:T(8,128)(2,1)} %get-tuple-element.129.refs_0_, bf16[4,96,64]{2,1,0:T(8,128)(2,1)} %copy-done.20, bf16[4,96,64]{2,1,0:T(8,128)(2,1)} %copy-done.21, bf16[4,96,64]{2,1,0:T(8,128)(2,1)} %copy-done.22, bf16[4,96,768]{2,1,0:T(8,128)(2,1)} %shard_map.88.refs_9_.refs_4_, ...), custom_call_target="tpu_custom_call" | custom-call | flops 1 | bytes 1 | tf_op jit(solution)/shard_map/pallas_call | solution.py:154
  219.1 0.6 copy-done.18
  219.8 2.8 %shard_map.93 = bf16[256,512]{1,0:T(8,128)(2,1)} custom-call(f32[256,512]{1,0:T(8,128)} %get-tuple-element.96.refs_0_, f32[256,512]{1,0:T(8,128)} %copy-done.11, f32[256,512]{1,0:T(8,128)} %copy-done.12, f32[256,512]{1,0:T(8,128)} %copy-done.13, bf16[384,256]{1,0:T(8,128)(2,1)} %get-tuple-element.100.refs_4_, bf16[96,512]{1,0:T(8,128)(2,1)} %get-tuple-element.121.refs_5_, ...), custom_call_target="tpu_custom_call" | custom-call | flops 1 | bytes 1 | tf_op jit(solution)/shard_map/pallas_call | solution.py:154
  222.6 1.0 broadcast_in_dim.3
  224.3 7.8 %collective-permute-done.29 = bf16[8,64,1024]{2,1,0:T(8,128)(2,1)} collective-permute-done((bf16[8,64,1024]{2,1,0:T(8,128)(2,1)}, bf16[8,64,1024]{2,1,0:T(8,128)(2,1)}, u32[]{:S(2)}, u32[]{:S(2)}) %collective-permute-start.29) | collective-permute-done | bytes 1048608 | tf_op jit(solution)/shard_map/ppermute | solution.py:486
  232.1 1.5 convert_dynamic-update-slice_fusion
  233.6 3.4 %copy-done = f32[8,64,4096]{2,1,0:T(8,128)} copy-done((f32[8,64,4096]{2,1,0:T(8,128)}, f32[8,64,4096]{2,1,0:T(8,128)S(1)}, u32[]{:S(2)}) %copy-start) | copy-done | bytes 8388632
  (76 shorter events, 4.8 us)
Async XLA Ops:
  5.0 16.6 %collective-permute-start = (bf16[272,1024]{1,0:T(8,128)(2,1)}, bf16[272,1024]{1,0:T(8,128)(2,1)S(1)}, u32[]{:S(2)}, u32[]{:S(2)}) collective-permute-start(bf16[272,1024]{1,0:T(8,128)(2,1)} %get-tuple-element.68), channel_id=1, source_target_pairs={{0,8},{8,0},{16,24},{24,16},{1,9},{9,1},{17,25},{25,17},{2,10},{10... | collective-permute-start | bytes 1671176 | tf_op jit(solution)/shard_map/ppermute | solution.py:376
  7.9 27.6 %collective-permute-start.1 = (bf16[272,1024]{1,0:T(8,128)(2,1)}, bf16[272,1024]{1,0:T(8,128)(2,1)S(1)}, u32[]{:S(2)}, u32[]{:S(2)}) collective-permute-start(bf16[272,1024]{1,0:T(8,128)(2,1)} %get-tuple-element.69), channel_id=1, source_target_pairs={{0,16},{8,24},{16,0},{24,8},{1,17},{9,25},{17,1},{25,9},{2,18},{10... | collective-permute-start | bytes 1671176 | tf_op jit(solution)/shard_map/ppermute | solution.py:376
  9.5 26.1 %collective-permute-start.2 = (bf16[272,1024]{1,0:T(8,128)(2,1)S(1)}, bf16[272,1024]{1,0:T(8,128)(2,1)S(1)}, u32[]{:S(2)}, u32[]{:S(2)}) collective-permute-start(bf16[272,1024]{1,0:T(8,128)(2,1)S(1)} %get-tuple-element.70), channel_id=1, source_target_pairs={{0,24},{8,16},{16,8},{24,0},{1,25},{9,17},{17,9},{25,1},{2,26},{10... | collective-permute-start | bytes 1671176 | tf_op jit(solution)/shard_map/ppermute | solution.py:376
  12.2 18.2 %collective-permute-start.3 = (bf16[96,1536]{1,0:T(8,128)(2,1)}, bf16[96,1536]{1,0:T(8,128)(2,1)S(1)}, u32[]{:S(2)}, u32[]{:S(2)}) collective-permute-start(bf16[96,1536]{1,0:T(8,128)(2,1)} %get-tuple-element.73), channel_id=1, source_target_pairs={{0,1},{1,2},{2,3},{3,0},{4,5},{5,6},{6,7},{7,4},{8,9},{9,10},{10,1... | collective-permute-start | bytes 884744 | tf_op jit(solution)/shard_map/ppermute | solution.py:379
  14.3 21.2 %collective-permute-start.4 = (bf16[96,1536]{1,0:T(8,128)(2,1)}, bf16[96,1536]{1,0:T(8,128)(2,1)S(1)}, u32[]{:S(2)}, u32[]{:S(2)}) collective-permute-start(bf16[96,1536]{1,0:T(8,128)(2,1)} %get-tuple-element.74), channel_id=1, source_target_pairs={{0,2},{1,3},{2,0},{3,1},{4,6},{5,7},{6,4},{7,5},{8,10},{9,11},{10,... | collective-permute-start | bytes 884744 | tf_op jit(solution)/shard_map/ppermute | solution.py:379
  21.6 8.8 %copy-start.8 = (bf16[272,1024]{1,0:T(8,128)(2,1)}, bf16[272,1024]{1,0:T(8,128)(2,1)S(1)}, u32[]{:S(2)}) copy-start(bf16[272,1024]{1,0:T(8,128)(2,1)S(1)} %collective-permute-done.refs_1_) | copy-start | bytes 1671172
  21.6 14.7 %collective-permute-start.5 = (bf16[96,1536]{1,0:T(8,128)(2,1)}, bf16[96,1536]{1,0:T(8,128)(2,1)S(1)}, u32[]{:S(2)}, u32[]{:S(2)}) collective-permute-start(bf16[96,1536]{1,0:T(8,128)(2,1)} %get-tuple-element.76), channel_id=1, source_target_pairs={{0,3},{1,0},{2,1},{3,2},{4,7},{5,4},{6,5},{7,6},{8,11},{9,8},{10,9... | collective-permute-start | bytes 884744 | tf_op jit(solution)/shard_map/ppermute | solution.py:379
  30.4 10.9 %copy-start.1 = (bf16[96,1536]{1,0:T(8,128)(2,1)}, bf16[96,1536]{1,0:T(8,128)(2,1)S(1)}, u32[]{:S(2)}) copy-start(bf16[96,1536]{1,0:T(8,128)(2,1)S(1)} %collective-permute-done.3.refs_1_.refs_3_.refs_2_) | copy-start | bytes 884740
  35.5 5.8 %copy-start.2 = (bf16[96,1536]{1,0:T(8,128)(2,1)}, bf16[96,1536]{1,0:T(8,128)(2,1)S(1)}, u32[]{:S(2)}) copy-start(bf16[96,1536]{1,0:T(8,128)(2,1)S(1)} %collective-permute-done.4.refs_2_.refs_4_.refs_3_) | copy-start | bytes 884740
  35.5 0.8 copy-start.9
  35.5 1.0 copy-start.10
  36.5 4.8 %copy-start.3 = (bf16[96,1536]{1,0:T(8,128)(2,1)}, bf16[96,1536]{1,0:T(8,128)(2,1)S(1)}, u32[]{:S(2)}) copy-start(bf16[96,1536]{1,0:T(8,128)(2,1)S(1)} %collective-permute-done.5.refs_3_.refs_5_.refs_4_) | copy-start | bytes 884740
  41.2 13.5 %copy-start.23 = (bf16[3,96,1024]{2,1,0:T(8,128)(2,1)S(1)}, bf16[3,96,1024]{2,1,0:T(8,128)(2,1)}, u32[]{:S(2)}) copy-start(bf16[3,96,1024]{2,1,0:T(8,128)(2,1)} %get-tuple-element.81) | copy-start | bytes 1769476
  41.3 5.7 %collective-permute-start.8 = (bf16[3,256,1024]{2,1,0:T(8,128)(2,1)}, bf16[3,256,1024]{2,1,0:T(8,128)(2,1)S(1)}, u32[]{:S(2)}, u32[]{:S(2)}) collective-permute-start(bf16[3,256,1024]{2,1,0:T(8,128)(2,1)} %get-tuple-element.86.refs_2_), channel_id=1, source_target_pairs={{0,4},{4,0},{1,5},{5,1},{2,6},{6,2},{3,7},{7,3},{8,12},{12,8},{9,1... | collective-permute-start | bytes 4718600 | tf_op jit(solution)/shard_map/ppermute | solution.py:382
  44.9 2.1 collective-permute-start.7
  46.9 0.7 copy-start.15
  47.6 41.7 %copy-start.4 = (bf16[3,256,1024]{2,1,0:T(8,128)(2,1)}, bf16[3,256,1024]{2,1,0:T(8,128)(2,1)S(1)}, u32[]{:S(2)}) copy-start(bf16[3,256,1024]{2,1,0:T(8,128)(2,1)S(1)} %collective-permute-done.8.refs_3_) | copy-start | bytes 4718596
  50.4 38.9 %collective-permute-start.12 = (bf16[8,256,1024]{2,1,0:T(8,128)(2,1)}, bf16[8,256,1024]{2,1,0:T(8,128)(2,1)}, u32[]{:S(2)}, u32[]{:S(2)}) collective-permute-start(bf16[8,256,1024]{2,1,0:T(8,128)(2,1)} %constant_dynamic-slice_fusion), channel_id=1, source_target_pairs={{0,4},{8,12},{20,16},{28,24},{1,5},{9,13},{21,17},{29,25},{2,6},{1... | collective-permute-start | bytes 12582920 | tf_op jit(solution)/shard_map/ppermute | solution.py:436
  54.7 28.5 %collective-permute-start.6 = (bf16[3,96,1024]{2,1,0:T(8,128)(2,1)S(1)}, bf16[3,96,1024]{2,1,0:T(8,128)(2,1)S(1)}, u32[]{:S(2)}, u32[]{:S(2)}) collective-permute-start(bf16[3,96,1024]{2,1,0:T(8,128)(2,1)S(1)} %copy-done.23), channel_id=1, source_target_pairs={{0,2},{1,3},{2,0},{3,1},{4,6},{5,7},{6,4},{7,5},{8,10},{9,11},{10,... | collective-permute-start | bytes 1769480 | tf_op jit(solution)/shard_map/ppermute | solution.py:379
  59.6 24.3 %collective-permute-start.11 = (bf16[4,96,768]{2,1,0:T(8,128)(2,1)}, bf16[4,96,768]{2,1,0:T(8,128)(2,1)}, u32[]{:S(2)}, u32[]{:S(2)}) collective-permute-start(bf16[4,96,768]{2,1,0:T(8,128)(2,1)} %shard_map.88.refs_9_.refs_4_), channel_id=1, source_target_pairs={{0,24},{8,16},{16,8},{24,0},{1,25},{9,17},{17,9},{25,1},{2,26},{10... | collective-permute-start | bytes 1769480 | tf_op jit(solution)/shard_map/ppermute | solution.py:376
  59.6 29.7 %collective-permute-start.10 = (bf16[4,96,768]{2,1,0:T(8,128)(2,1)}, bf16[4,96,768]{2,1,0:T(8,128)(2,1)}, u32[]{:S(2)}, u32[]{:S(2)}) collective-permute-start(bf16[4,96,768]{2,1,0:T(8,128)(2,1)} %shard_map.88.refs_9_.refs_4_), channel_id=1, source_target_pairs={{0,16},{8,24},{16,0},{24,8},{1,17},{9,25},{17,1},{25,9},{2,18},{10... | collective-permute-start | bytes 1769480 | tf_op jit(solution)/shard_map/ppermute | solution.py:376
  62.5 26.8 %collective-permute-start.9 = (bf16[4,96,768]{2,1,0:T(8,128)(2,1)}, bf16[4,96,768]{2,1,0:T(8,128)(2,1)}, u32[]{:S(2)}, u32[]{:S(2)}) collective-permute-start(bf16[4,96,768]{2,1,0:T(8,128)(2,1)} %shard_map.88.refs_9_.refs_4_), channel_id=1, source_target_pairs={{0,8},{8,0},{16,24},{24,16},{1,9},{9,1},{17,25},{25,17},{2,10},{10... | collective-permute-start | bytes 1769480 | tf_op jit(solution)/shard_map/ppermute | solution.py:376
  83.2 12.2 %copy-start.6 = (bf16[3,96,1024]{2,1,0:T(8,128)(2,1)}, bf16[3,96,1024]{2,1,0:T(8,128)(2,1)S(1)}, u32[]{:S(2)}) copy-start(bf16[3,96,1024]{2,1,0:T(8,128)(2,1)S(1)} %collective-permute-done.6.refs_7_) | copy-start | bytes 1769476
  83.2 18.2 %collective-permute-start.16 = (bf16[3,96,1024]{2,1,0:T(8,128)(2,1)}, bf16[3,96,1024]{2,1,0:T(8,128)(2,1)S(1)}, u32[]{:S(2)}, u32[]{:S(2)}) collective-permute-start(bf16[3,96,1024]{2,1,0:T(8,128)(2,1)} %get-tuple-element.102), channel_id=1, source_target_pairs={{0,1},{1,2},{2,3},{3,0},{4,5},{5,6},{6,7},{7,4},{8,9},{9,10},{10,1... | collective-permute-start | bytes 1769480 | tf_op jit(solution)/shard_map/ppermute | solution.py:379
  83.9 27.9 %collective-permute-start.17 = (bf16[3,96,1024]{2,1,0:T(8,128)(2,1)}, bf16[3,96,1024]{2,1,0:T(8,128)(2,1)}, u32[]{:S(2)}, u32[]{:S(2)}) collective-permute-start(bf16[3,96,1024]{2,1,0:T(8,128)(2,1)} %get-tuple-element.103), channel_id=1, source_target_pairs={{0,3},{1,0},{2,1},{3,2},{4,7},{5,4},{6,5},{7,6},{8,11},{9,8},{10,9... | collective-permute-start | bytes 1769480 | tf_op jit(solution)/shard_map/ppermute | solution.py:379
  95.4 16.5 %collective-permute-start.13 = (f32[256,512]{1,0:T(8,128)}, f32[256,512]{1,0:T(8,128)S(1)}, u32[]{:S(2)}, u32[]{:S(2)}) collective-permute-start(f32[256,512]{1,0:T(8,128)} %get-tuple-element.97), channel_id=1, source_target_pairs={{0,8},{8,0},{16,24},{24,16},{1,9},{9,1},{17,25},{25,17},{2,10},{10... | collective-permute-start | bytes 1572872 | tf_op jit(solution)/shard_map/ppermute | solution.py:376
  96.9 24.4 %collective-permute-start.14 = (f32[256,512]{1,0:T(8,128)}, f32[256,512]{1,0:T(8,128)S(1)}, u32[]{:S(2)}, u32[]{:S(2)}) collective-permute-start(f32[256,512]{1,0:T(8,128)} %get-tuple-element.98), channel_id=1, source_target_pairs={{0,16},{8,24},{16,0},{24,8},{1,17},{9,25},{17,1},{25,9},{2,18},{10... | collective-permute-start | bytes 1572872 | tf_op jit(solution)/shard_map/ppermute | solution.py:376
  98.9 23.1 %collective-permute-start.15 = (f32[256,512]{1,0:T(8,128)}, f32[256,512]{1,0:T(8,128)S(1)}, u32[]{:S(2)}, u32[]{:S(2)}) collective-permute-start(f32[256,512]{1,0:T(8,128)} %get-tuple-element.99), channel_id=1, source_target_pairs={{0,24},{8,16},{16,8},{24,0},{1,25},{9,17},{17,9},{25,1},{2,26},{10... | collective-permute-start | bytes 1572872 | tf_op jit(solution)/shard_map/ppermute | solution.py:376
  101.4 20.6 %copy-start.7 = (bf16[3,96,1024]{2,1,0:T(8,128)(2,1)}, bf16[3,96,1024]{2,1,0:T(8,128)(2,1)S(1)}, u32[]{:S(2)}) copy-start(bf16[3,96,1024]{2,1,0:T(8,128)(2,1)S(1)} %collective-permute-done.16.refs_6_) | copy-start | bytes 1769476
  111.8 20.8 %copy-start.11 = (f32[256,512]{1,0:T(8,128)}, f32[256,512]{1,0:T(8,128)S(1)}, u32[]{:S(2)}) copy-start(f32[256,512]{1,0:T(8,128)S(1)} %collective-permute-done.13.refs_1_) | copy-start | bytes 1572868
  121.4 11.3 %copy-start.12 = (f32[256,512]{1,0:T(8,128)}, f32[256,512]{1,0:T(8,128)S(1)}, u32[]{:S(2)}) copy-start(f32[256,512]{1,0:T(8,128)S(1)} %collective-permute-done.14.refs_2_) | copy-start | bytes 1572868
  122.0 10.7 %copy-start.13 = (f32[256,512]{1,0:T(8,128)}, f32[256,512]{1,0:T(8,128)S(1)}, u32[]{:S(2)}) copy-start(f32[256,512]{1,0:T(8,128)S(1)} %collective-permute-done.15.refs_3_) | copy-start | bytes 1572868
  132.7 9.7 %collective-permute-start.18 = (f32[4,4,96,128]{3,2,1,0:T(8,128)}, f32[4,4,96,128]{3,2,1,0:T(8,128)S(1)}, u32[]{:S(2)}, u32[]{:S(2)}) collective-permute-start(f32[4,4,96,128]{3,2,1,0:T(8,128)} %get-tuple-element.111), channel_id=1, source_target_pairs={{0,4},{4,0},{1,5},{5,1},{2,6},{6,2},{3,7},{7,3},{8,12},{12,8},{9,1... | collective-permute-start | bytes 2359304 | tf_op jit(solution)/shard_map/ppermute | solution.py:382
  133.4 9.0 %copy-start.5 = (f32[4,4,96,128]{3,2,1,0:T(8,128)S(1)}, f32[4,4,96,128]{3,2,1,0:T(8,128)}, u32[]{:S(2)}) copy-start(f32[4,4,96,128]{3,2,1,0:T(8,128)} %get-tuple-element.110) | copy-start | bytes 2359300
  142.5 80.1 %collective-permute-start.26 = (bf16[8,64,1024]{2,1,0:T(8,128)(2,1)}, bf16[8,64,1024]{2,1,0:T(8,128)(2,1)S(1)}, u32[]{:S(2)}, u32[]{:S(2)}) collective-permute-start(bf16[8,64,1024]{2,1,0:T(8,128)(2,1)} %get-tuple-element.125), channel_id=1, source_target_pairs={{0,0},{4,16},{8,8},{12,24},{16,4},{20,20},{24,12},{28,28},{1,1},{5... | collective-permute-start | bytes 3145736 | tf_op jit(solution)/shard_map/ppermute | solution.py:486
  144.4 6.9 %collective-permute-start.19 = (f32[4,96,128]{2,1,0:T(8,128)S(1)}, f32[4,96,128]{2,1,0:T(8,128)S(1)}, u32[]{:S(2)}, u32[]{:S(2)}) collective-permute-start(f32[4,96,128]{2,1,0:T(8,128)S(1)} %get-tuple-element.137), channel_id=1, source_target_pairs={{0,8},{8,0},{16,24},{24,16},{1,9},{9,1},{17,25},{25,17},{2,10},{10... | collective-permute-start | bytes 589832 | tf_op jit(solution)/shard_map/ppermute | solution.py:376
  145.9 12.1 %collective-permute-start.21 = (f32[4,96,128]{2,1,0:T(8,128)S(1)}, f32[4,96,128]{2,1,0:T(8,128)S(1)}, u32[]{:S(2)}, u32[]{:S(2)}) collective-permute-start(f32[4,96,128]{2,1,0:T(8,128)S(1)} %get-tuple-element.138), channel_id=1, source_target_pairs={{0,24},{8,16},{16,8},{24,0},{1,25},{9,17},{17,9},{25,1},{2,26},{10... | collective-permute-start | bytes 589832 | tf_op jit(solution)/shard_map/ppermute | solution.py:376
  148.1 40.2 %collective-permute-start.20 = (f32[4,96,128]{2,1,0:T(8,128)S(1)}, f32[4,96,128]{2,1,0:T(8,128)S(1)}, u32[]{:S(2)}, u32[]{:S(2)}) collective-permute-start(f32[4,96,128]{2,1,0:T(8,128)S(1)} %get-tuple-element.139), channel_id=1, source_target_pairs={{0,16},{8,24},{16,0},{24,8},{1,17},{9,25},{17,1},{25,9},{2,18},{10... | collective-permute-start | bytes 589832 | tf_op jit(solution)/shard_map/ppermute | solution.py:376
  148.1 75.7 %collective-permute-start.27 = (bf16[8,64,1024]{2,1,0:T(8,128)(2,1)}, bf16[8,64,1024]{2,1,0:T(8,128)(2,1)S(1)}, u32[]{:S(2)}, u32[]{:S(2)}) collective-permute-start(bf16[8,64,1024]{2,1,0:T(8,128)(2,1)} %get-tuple-element.126), channel_id=1, source_target_pairs={{0,8},{4,24},{8,0},{12,16},{16,12},{20,28},{24,4},{28,20},{1,9},{5... | collective-permute-start | bytes 3145736 | tf_op jit(solution)/shard_map/ppermute | solution.py:486
  151.3 72.8 %collective-permute-start.28 = (bf16[8,64,1024]{2,1,0:T(8,128)(2,1)}, bf16[8,64,1024]{2,1,0:T(8,128)(2,1)S(1)}, u32[]{:S(2)}, u32[]{:S(2)}) collective-permute-start(bf16[8,64,1024]{2,1,0:T(8,128)(2,1)} %get-tuple-element.127), channel_id=1, source_target_pairs={{0,16},{4,0},{8,24},{12,8},{16,20},{20,4},{24,28},{28,12},{1,17},{... | collective-permute-start | bytes 3145736 | tf_op jit(solution)/shard_map/ppermute | solution.py:486
  188.4 1.4 copy-start.14
  188.4 1.4 collective-permute-start.22
  189.8 0.6 copy-start.19
  194.5 5.8 %collective-permute-start.30 = (bf16[4,96,64]{2,1,0:T(8,128)(2,1)}, bf16[4,96,64]{2,1,0:T(8,128)(2,1)S(1)}, u32[]{:S(2)}, u32[]{:S(2)}) collective-permute-start(bf16[4,96,64]{2,1,0:T(8,128)(2,1)} %get-tuple-element.130), channel_id=1, source_target_pairs={{0,8},{8,0},{16,24},{24,16},{1,9},{9,1},{17,25},{25,17},{2,10},{10... | collective-permute-start | bytes 147464 | tf_op jit(solution)/shard_map/ppermute | solution.py:376
  197.1 4.8 %collective-permute-start.31 = (bf16[4,96,64]{2,1,0:T(8,128)(2,1)}, bf16[4,96,64]{2,1,0:T(8,128)(2,1)S(1)}, u32[]{:S(2)}, u32[]{:S(2)}) collective-permute-start(bf16[4,96,64]{2,1,0:T(8,128)(2,1)} %get-tuple-element.131), channel_id=1, source_target_pairs={{0,16},{8,24},{16,0},{24,8},{1,17},{9,25},{17,1},{25,9},{2,18},{10... | collective-permute-start | bytes 147464 | tf_op jit(solution)/shard_map/ppermute | solution.py:376
  200.4 14.4 %copy-start.20 = (bf16[4,96,64]{2,1,0:T(8,128)(2,1)}, bf16[4,96,64]{2,1,0:T(8,128)(2,1)S(1)}, u32[]{:S(2)}) copy-start(bf16[4,96,64]{2,1,0:T(8,128)(2,1)S(1)} %collective-permute-done.30.refs_1_) | copy-start | bytes 147460
  200.4 5.7 %collective-permute-start.32 = (bf16[4,96,64]{2,1,0:T(8,128)(2,1)}, bf16[4,96,64]{2,1,0:T(8,128)(2,1)S(1)}, u32[]{:S(2)}, u32[]{:S(2)}) collective-permute-start(bf16[4,96,64]{2,1,0:T(8,128)(2,1)} %get-tuple-element.132), channel_id=1, source_target_pairs={{0,24},{8,16},{16,8},{24,0},{1,25},{9,17},{17,9},{25,1},{2,26},{10... | collective-permute-start | bytes 147464 | tf_op jit(solution)/shard_map/ppermute | solution.py:376
  201.9 0.6 copy-start.21
  202.5 4.8 %collective-permute-start.23 = (bf16[96,512]{1,0:T(8,128)(2,1)}, bf16[96,512]{1,0:T(8,128)(2,1)S(1)}, u32[]{:S(2)}, u32[]{:S(2)}) collective-permute-start(bf16[96,512]{1,0:T(8,128)(2,1)} %get-tuple-element.122), channel_id=1, source_target_pairs={{0,3},{1,0},{2,1},{3,2},{4,7},{5,4},{6,5},{7,6},{8,11},{9,8},{10,9... | collective-permute-start | bytes 294920 | tf_op jit(solution)/shard_map/ppermute | solution.py:379
  206.1 0.6 copy-start.22
  206.7 5.8 %collective-permute-start.24 = (bf16[96,512]{1,0:T(8,128)(2,1)}, bf16[96,512]{1,0:T(8,128)(2,1)S(1)}, u32[]{:S(2)}, u32[]{:S(2)}) collective-permute-start(bf16[96,512]{1,0:T(8,128)(2,1)} %get-tuple-element.123), channel_id=1, source_target_pairs={{0,2},{1,3},{2,0},{3,1},{4,6},{5,7},{6,4},{7,5},{8,10},{9,11},{10,... | collective-permute-start | bytes 294920 | tf_op jit(solution)/shard_map/ppermute | solution.py:379
  207.3 11.8 %copy-start.16 = (bf16[96,512]{1,0:T(8,128)(2,1)}, bf16[96,512]{1,0:T(8,128)(2,1)S(1)}, u32[]{:S(2)}) copy-start(bf16[96,512]{1,0:T(8,128)(2,1)S(1)} %collective-permute-done.23.refs_6_) | copy-start | bytes 294916
  207.3 24.8 %collective-permute-start.29 = (bf16[8,64,1024]{2,1,0:T(8,128)(2,1)}, bf16[8,64,1024]{2,1,0:T(8,128)(2,1)}, u32[]{:S(2)}, u32[]{:S(2)}) collective-permute-start(bf16[8,64,1024]{2,1,0:T(8,128)(2,1)} %get-tuple-element.128), channel_id=1, source_target_pairs={{0,24},{4,8},{8,16},{12,0},{16,28},{20,12},{24,20},{28,4},{1,25},{... | collective-permute-start | bytes 3145736 | tf_op jit(solution)/shard_map/ppermute | solution.py:486
  212.5 6.6 %copy-start.17 = (bf16[96,512]{1,0:T(8,128)(2,1)}, bf16[96,512]{1,0:T(8,128)(2,1)S(1)}, u32[]{:S(2)}) copy-start(bf16[96,512]{1,0:T(8,128)(2,1)S(1)} %collective-permute-done.24.refs_7_) | copy-start | bytes 294916
  212.5 6.6 %collective-permute-start.25 = (bf16[96,512]{1,0:T(8,128)(2,1)}, bf16[96,512]{1,0:T(8,128)(2,1)S(1)}, u32[]{:S(2)}, u32[]{:S(2)}) collective-permute-start(bf16[96,512]{1,0:T(8,128)(2,1)} %get-tuple-element.124), channel_id=1, source_target_pairs={{0,1},{1,2},{2,3},{3,0},{4,5},{5,6},{6,7},{7,4},{8,9},{9,10},{10,1... | collective-permute-start | bytes 294920 | tf_op jit(solution)/shard_map/ppermute | solution.py:379
  219.1 0.6 copy-start.18
  233.6 3.4 %copy-start = (f32[8,64,4096]{2,1,0:T(8,128)}, f32[8,64,4096]{2,1,0:T(8,128)S(1)}, u32[]{:S(2)}) copy-start(f32[8,64,4096]{2,1,0:T(8,128)S(1)} %convert_dynamic-update-slice_fusion) | copy-start | bytes 25165828

commit v8 on v7

--- a/solution.py
+++ b/solution.py
@@ -219,10 +219,9 @@
 
 
 def others_kernel(fsdp, ad, slots, dom_total, at, *refs):
-    x_refs, outs, plain = refs[: fsdp - 1], refs[fsdp - 1 : -1], refs[-1]
+    x_refs, outs = refs[: fsdp - 1], refs[fsdp - 1 :]
     for kf in range(fsdp - 1):
         rows = x_refs[kf].shape[0] - 16
-        plain[kf] = x_refs[kf][:rows, :]
         dom = x_refs[kf][rows:, :rows].astype(F32).astype(jnp.int32)[:1]
         hot = one_hot(dom, at[0], slots, ad, dom_total)
         moved = dot(hot, x_refs[kf][:rows, :], ((1,), (0,))).astype(BF16)
@@ -252,29 +251,23 @@
         out[ka, :, width:] = (adapter_scale * (mine[ka] + got[ka])).astype(BF16)
 
 
-def hidden_kernel(fsdp, ad, gslots, first, last, at, *refs):
-    own_refs, x_refs, outs, held = refs[:ad], refs[ad : 2 * ad], refs[2 * ad : -1], refs[-1]
-    earlier = None
-    if not first:
-        earlier, outs = outs[0], outs[1:]
+def hidden_kernel(fsdp, gslots, at, *refs):
+    count = (len(refs) - 3) // 2
+    own_refs, x_refs, outs, held = refs[:count], refs[count:-3], refs[-3:-1], refs[-1]
     cw = held.shape[2]
+    second = at[2] == 1
     for g in range(held.shape[0] // GROUP):
         weights = held[g * GROUP : (g + 1) * GROUP].reshape(-1, cw)
         rows = pl.ds(g * gslots, gslots)
-        for ka in range(ad):
-            x = group_rows((own_refs[ka], x_refs[ka]), g, gslots)
+        for i in range(count):
+            x = group_rows((own_refs[i], x_refs[i]), g, gslots)
             part = narrow(dot(x, weights, ((1,), (1,))), gslots)
+            n = part.shape[1] // 2
+            halves = jnp.where(second, part[:, n:], part[:, :n])
+            others = jnp.where(second, part[:, :n], part[:, n:])
             for kf in range(fsdp):
-                new = part[kf * gslots : (kf + 1) * gslots]
-                if earlier is not None:
-                    new = new + earlier[kf, ka, rows, :]
-                if not last:
-                    outs[0][kf, ka, rows, :] = new
-                else:
-                    n = new.shape[1] // 2
-                    second = at[2] == 1
-                    outs[0][kf, ka, rows, :] = jnp.where(second, new[:, n:], new[:, :n])
-                    outs[1][kf, ka, rows, :] = jnp.where(second, new[:, :n], new[:, n:])
+                outs[0][kf, i, rows, :] = halves[kf * gslots : (kf + 1) * gslots]
+                outs[1][kf, i, rows, :] = others[kf * gslots : (kf + 1) * gslots]
 
 
 def down_grad_kernel(fsdp, ad, gslots, at, *refs):
@@ -341,14 +334,16 @@
     out[...] = (total + dot(hot[...], delta, ((0,), (0,)))).astype(BF16)
 
 
-def base_kernel(fsdp, at, own, mine, got, weight, *outs):
-    kt = mine.shape[2]
+def base_kernel(fsdp, at, own, *refs):
+    mine, got = refs[: fsdp - 1], refs[fsdp - 1 : 2 * fsdp - 2]
+    weight, outs = refs[2 * fsdp - 2], refs[2 * fsdp - 1 :]
+    rows, kt = own.shape[0], mine[0].shape[1]
     outs[0][...] = dot(own[...], weight[...], ((1,), (0,)))
     w_mine = weight[pl.ds(pl.multiple_of(at[0] * kt, kt), kt), :]
     w_got = weight[pl.ds(pl.multiple_of((1 - at[0]) * kt, kt), kt), :]
     for k in range(1, fsdp):
-        total = dot(mine[k - 1], w_mine, ((1,), (0,)))
-        outs[k][...] = total + dot(got[k - 1], w_got, ((1,), (0,)))
+        total = dot(mine[k - 1][:rows, :], w_mine, ((1,), (0,)))
+        outs[k][...] = total + dot(got[k - 1][:rows, :], w_got, ((1,), (0,)))
 
 
 def column_body(
@@ -404,77 +399,81 @@
         [(v, None) for v in (domain.T, x_in[0], layer_output_gradient)],
         at=numbers(a),
     )
-    held = after(adapter_down_weight, *sends)
+    held = after((adapter_down_weight, input_rows), *sends)
     sends[-1] = after(sends[-1], x_in[1])
     own = [over_a(v, ka) for ka, v in enumerate(sends)]
 
-    down_other = lax.dynamic_slice_in_dim(held, (fx * 2 + 1 - t) * kt, kt, 2)
+    down_other = lax.dynamic_slice_in_dim(held[0], (fx * 2 + 1 - t) * kt, kt, 2)
     pairs = [(i * 2 + i // 2, i * 2 + 1 - i // 2) for i in range(fsdp)]
 
-    ready, own, down_other = lax.optimization_barrier((x_in[1:], own, down_other))
-    *sends, x_plain = call(
+    x_chip = lax.dynamic_slice_in_dim(held[1], f * kf_width, kf_width, 1)
+    x_in, own, down_other, x_chip = lax.optimization_barrier((x_in, own, down_other, x_chip))
+    x_other = [swap(v) for v in x_in[1:]]
+    down_got = lax.ppermute(down_other, ("fsdp", "tp"), pairs)
+    sends = call(
         functools.partial(others_kernel, fsdp, ad, slots, ad * dloc),
-        [((fsdp - 1, slots, cw), BF16)] * (CHUNKS * ad) + [((fsdp - 1, rows, kt), BF16)],
-        [(v, None) for v in ready],
+        [((fsdp - 1, slots, cw), BF16)] * (CHUNKS * ad),
+        [(v, None) for v in x_in[1:]],
         at=numbers(a),
     )
     x_routed = [[over_a(v, ka) for ka, v in enumerate(sends[:ad])]]
 
-    dy = [(v, (kt, vloc)) for v in after(own, x_plain)]
+    base = call(
+        functools.partial(base_kernel, fsdp),
+        [((rows, vloc), F32)] * fsdp,
+        [(v, None) for v in (x_chip, *x_in[1:], *after(x_other, *sends), value_weight_frozen)],
+        at=numbers(t),
+    )
+    dy = [(v, (kt, vloc)) for v in after(own, base[0], down_got)]
+    base = [over_f(v, k) for k, v in enumerate(base)]
+
     (back,) = call(
         functools.partial(back_kernel, ad, gslots),
         [((ad, slots, rank), F32)],
         [*dy, (adapter_up_weight, None)],
-    )
-    x_other = swap(x_plain)
-    back, back_got = after((back, swap(back)), x_other)
+        flops=10**10,
+    )
     (both,) = call(
         functools.partial(both_kernel, ad),
         [((ad, slots, vloc + rank), BF16)],
-        [(back, None), (back_got, None), *dy],
-    )
-    down_got = lax.ppermute(after(down_other, both), ("fsdp", "tp"), pairs)
+        [(back, None), (swap(back), None), *dy],
+    )
+    both = after(both, *base, x_routed[0][2])
     both = [over_f(both, k) for k in range(fsdp)]
 
-    x_chip = lax.dynamic_slice_in_dim(input_rows, f * kf_width, kf_width, 1)
-    x_chip = after(x_chip, x_routed[0][2], *both, down_got)
-    base = call(
-        functools.partial(base_kernel, fsdp),
-        [((rows, vloc), F32)] * fsdp,
-        [(v, None) for v in (x_chip, x_plain, x_other, value_weight_frozen)],
-        at=numbers(t),
-    )
-    base = [over_f(v, k) for k, v in enumerate(base)]
-    x_routed[0] = after(x_routed[0], *base)
-
-    def chunk_of(c, routed):
-        return [(v, (c * cw, cw)) for v in own] + [(v, None) for v in routed]
-
-    def hidden(c, earlier, routed):
-        last = c == CHUNKS - 1
+    def hidden(shifts, routed):
         return call(
-            functools.partial(hidden_kernel, fsdp, ad, gslots, c == 0, last),
-            [((fsdp, ad, slots, rank // 2 if last else rank), F32)] * (2 if last else 1),
-            [*chunk_of(c, routed), *[(v, None) for v in earlier]],
-            at=numbers(t == fy, fx * kf_width + t * kt + c * cw, t),
-            either=(adapter_down_weight, down_got, (c * cw, cw)),
+            functools.partial(hidden_kernel, fsdp, gslots),
+            [((fsdp, len(shifts), slots, rank // 2), F32)] * 2,
+            [(own[ka], (0, kt)) for ka in shifts] + [(v, None) for v in routed],
+            at=numbers(t == fy, fx * kf_width + t * kt, t),
+            either=(adapter_down_weight, down_got, (0, kt)),
+            flops=10**10,
         )
 
-    hid = hidden(0, [], x_routed[0])
-    hid, both = lax.optimization_barrier((hid, both))
-    hid = hid[0] + swap(hid[1])
+    early, late = [ka for ka in range(ad) if ka % 2 == 0], [ka for ka in range(ad) if ka % 2]
+    hid_early = hidden(early, after([x_routed[0][ka] for ka in early], both[0]))
+    x_last = after(x_routed[0], *base, *hid_early)
+    hid_late = hidden(late, [x_last[ka] for ka in late])
+    x_last, both = after((x_last, both), *hid_late)
+    hid = jnp.concatenate(
+        [hid_early[0] + swap(hid_early[1]), hid_late[0] + swap(hid_late[1])], axis=1
+    )
 
     sums = call(
         functools.partial(down_grad_kernel, fsdp, ad, gslots),
         [((dloc, rloc, kt), BF16)] * fsdp,
-        [*chunk_of(0, x_routed[0]), *[(v, (vloc, rank)) for v in both]],
+        [(v, (0, kt)) for v in own]
+        + [(v, None) for v in x_last]
+        + [(v, (vloc, rank)) for v in both],
         at=numbers(*[(t ^ (r // 2)) * 2 + (fx ^ (r % 2)) for r in range(fsdp)]),
         scratch=[pltpu.VMEM((GROUP * rank, kt), F32)],
-        flops=20 * dloc * rank * kt * 192,
-    )
-    hid, sums = lax.optimization_barrier((hid, sums))
+        flops=10**10,
+    )
     hid = [over_f(hid[k], k) for k in range(fsdp)]
+    sums = [sums[0], sums[1], *after(sums[2:], *hid[1:])]
     grad_a = jnp.zeros((dloc, rloc, half), F32)
+    got = []
     for r in range(fsdp):
         p, q = r % 2, r // 2
         perm = [
@@ -483,11 +482,13 @@
             for x in range(2)
             for s in range(2)
         ]
-        got = lax.ppermute(sums[r], ("fsdp", "tp"), perm)
+        got.append(lax.ppermute(sums[r], ("fsdp", "tp"), perm))
         at = (fx ^ p) * kf_width + (fy ^ q) * kt
-        grad_a = lax.dynamic_update_slice_in_dim(grad_a, got.astype(F32), at, 2)
+        grad_a = lax.dynamic_update_slice_in_dim(grad_a, got[r].astype(F32), at, 2)
 
     hid_own = (hid[0] + hid[1] + hid[2] + hid[3]).astype(BF16)
+    shift_order = [(early + late).index(ka) for ka in range(ad)]
+    hid_own = jnp.concatenate([hid_own[i : i + 1] for i in shift_order], axis=0)
     outs = call(
         functools.partial(delta_kernel, fsdp, ad, gslots),
         [((slots, vloc), BF16)] * ad + [((ad, slots, rloc), BF16)] * fsdp,
@@ -495,7 +496,7 @@
         at=numbers(t, *[f ^ k for k in range(fsdp)]),
     )
     returned = [over_a(v, (ad - ka) % ad) for ka, v in enumerate(outs[:ad])]
-    hid_cols = [over_f(v, k) for k, v in enumerate(outs[ad:])]
+    hid_cols = [over_f(after(v, got[2], *returned[1:]), k) for k, v in enumerate(outs[ad:])]
 
     (y_out,) = call(
         functools.partial(output_kernel, fsdp, ad),
@@ -519,7 +520,7 @@
         P(("fsdp", "ad"), "tp"),
         P(("fsdp", "ad"), None),
     )
-    square = mesh.shape["fsdp"] == 4 and mesh.shape["tp"] == 2
+    square = mesh.shape["fsdp"] == 4 and mesh.shape["tp"] == 2 and mesh.shape["ad"] == 4
     return jax.shard_map(
         column_body if square else general_body,
         mesh=mesh,

time: 238 us -> 197 us (0.83)
  waiting for transfers between devices: 109 us -> 55.7 us
  other arithmetic: 5.38 us -> 10.7 us
  local copies, waits for them, and re-layouts: 18.1 us -> 22.4 us
  Pallas kernels: 50.2 us -> 52.6 us
    ppermute x15, waiting for transfers between devices: 57.1 us -> 6.68 us  [over_f(): lax.ppermute(v, 'fsdp', [(i, i ^ k) for i in range(fsdp)])]
    dynamic_update_slice x4, other arithmetic: 2.19 us -> 7.49 us  [column_body(): grad_a = lax.dynamic_update_slice_in_dim(grad_a, got[r].astype(F32), at, 2)]
    ppermute x5, starting transfers between devices: 12.5 us -> 7.39 us  [the longest x4 4.12 us: column_body(): got.append(lax.ppermute(sums[r], ('fsdp', 'tp'), perm))]
    ppermute x9, waiting for transfers between devices: 42.3 us -> 37.5 us  [over_a(): lax.ppermute(v, 'ad', [(i, (i + k) % ad) for i in range(ad)])]
    ppermute x15, starting transfers between devices: 18.4 us -> 22.6 us  [over_f(): lax.ppermute(v, 'fsdp', [(i, i ^ k) for i in range(fsdp)])]
    broadcast_in_dim x1, local copies, waits for them, and re-layouts: 1 us -> 4.43 us  [column_body(): grad_a = jnp.zeros((dloc, rloc, half), F32)]
    pallas_call x10 -> x11, Pallas kernels: 50.2 us -> 52.6 us  [call(): pl.pallas_call(body, out_shape=[jax.ShapeDtypeStruct(shape, dtype) for sh...]
    unnamed x48 -> x52, local copies, waits for them, and re-layouts: 6.99 us -> 7.88 us
  transfers between devices with their start and end apart: 33 -> 36, of which waited for: 20 -> 14; matrix products, arithmetic and copies ran while one was open for 4% -> 11% of each run, Pallas kernels for 14% -> 25%
where the time goes in v8:
time: 197 us; the launch traced here: 196 us
  waiting for transfers between devices  55.7 us (28%)
  starting transfers between devices  53.5 us (27%)
  Pallas kernels  52.6 us (27%)
  local copies, waits for them, and re-layouts  22.4 us (11%)
  other arithmetic  10.7 us (5%)
    pallas_call x11, Pallas kernels, call(): pl.pallas_call(body, out_shape=[jax.ShapeDtypeStruct(shape, dtype) for sh...  52.6 us
    ppermute x9, waiting for transfers between devices, over_a(): lax.ppermute(v, 'ad', [(i, (i + k) % ad) for i in range(ad)])  37.5 us
    ppermute x15, starting transfers between devices, over_f(): lax.ppermute(v, 'fsdp', [(i, i ^ k) for i in range(fsdp)])  22.6 us
    ppermute x9, starting transfers between devices, over_a(): lax.ppermute(v, 'ad', [(i, (i + k) % ad) for i in range(ad)])  21.5 us
    ppermute x4, waiting for transfers between devices, column_body(): got.append(lax.ppermute(sums[r], ('fsdp', 'tp'), perm))  8.7 us
    unnamed x52, local copies, waits for them, and re-layouts  7.88 us
    dynamic_update_slice x4, other arithmetic, column_body(): grad_a = lax.dynamic_update_slice_in_dim(grad_a, got[r].astype(F32), at, 2)  7.49 us
    ppermute x15, waiting for transfers between devices, over_f(): lax.ppermute(v, 'fsdp', [(i, i ^ k) for i in range(fsdp)])  6.68 us
  transfers between devices with their start and end apart: 36, of which 14 were waited for; matrix products, arithmetic and copies ran while one was open for 11% of the time, Pallas kernels for 25%

profile of v8, /device:TPU:0, one launch (start us, length us, event | category | flops | bytes accessed | tf_op | source)
XLA Modules:
  0.0 196.2 jit_solution(15488394380450548872)
XLA Ops:
  0.7 0.7 bitcast_convert_fusion
  1.3 2.5 %constant_dynamic-slice_fusion.2 = (bf16[256,1024]{1,0:T(8,128)(2,1)S(1)}, bf16[256,1024]{1,0:T(8,128)(2,1)S(1)}, bf16[256,1024]{1,0:T(8,128)(2,1)S(1)}, bf16[256,1024]{1,0:T(8,128)(2,1)}) fusion(bf16[256,8192]{1,0:T(8,128)(2,1)} %param.6, s32[]{:T(128)S(6)} %select_n.44, s32[]{:T(128)S(6)} %select_n.43, s32[]{:T(128)S(6)} %select_n.42, s32[]{:T(128)S(6)} %select_n.41), kind=kLoop, calls=%fused_computation.30 | loop fusion | bytes 4194320 | tf_op jit(solution)/shard_map/dynamic_slice | solution.py:387
  4.0 3.0 %collective-permute-start = (bf16[272,1024]{1,0:T(8,128)(2,1)S(1)}, bf16[272,1024]{1,0:T(8,128)(2,1)S(1)}, u32[]{:S(2)}, u32[]{:S(2)}) collective-permute-start(bf16[272,1024]{1,0:T(8,128)(2,1)S(1)} %get-tuple-element.77), channel_id=1, source_target_pairs={{0,8},{8,0},{16,24},{24,16},{1,9},{9,1},{17,25},{25,17},{2,10},{10... | collective-permute-start | bytes 1671176 | tf_op jit(solution)/shard_map/ppermute | solution.py:371
  7.0 1.5 collective-permute-start.1
  8.6 2.7 %shard_map.85 = (bf16[384,256]{1,0:T(8,128)(2,1)}, bf16[96,1536]{1,0:T(8,128)(2,1)}, bf16[96,1536]{1,0:T(8,128)(2,1)}, bf16[96,1536]{1,0:T(8,128)(2,1)}, bf16[96,1536]{1,0:T(8,128)(2,1)}) custom-call(s32[1]{0:T(128)} %bitcast.2.refs_0_, s32[1,256]{1,0:T(1,128)} %bitcast.30, bf16[256,1024]{1,0:T(8,128)(2,1)} %get-tuple-element.76.refs_2_, ...), custom_call_target="tpu_custom_call" | custom-call | flops 1 | bytes 1 | tf_op jit(solution)/shard_map/pallas_call | solution.py:154
  11.3 2.1 %collective-permute-start.3 = (bf16[96,1536]{1,0:T(8,128)(2,1)}, bf16[96,1536]{1,0:T(8,128)(2,1)}, u32[]{:S(2)}, u32[]{:S(2)}) collective-permute-start(bf16[96,1536]{1,0:T(8,128)(2,1)} %get-tuple-element.81), channel_id=1, source_target_pairs={{0,1},{1,2},{2,3},{3,0},{4,5},{5,6},{6,7},{7,4},{8,9},{9,10},{10,1... | collective-permute-start | bytes 884744 | tf_op jit(solution)/shard_map/ppermute | solution.py:374
  13.4 2.6 %collective-permute-start.4 = (bf16[96,1536]{1,0:T(8,128)(2,1)}, bf16[96,1536]{1,0:T(8,128)(2,1)}, u32[]{:S(2)}, u32[]{:S(2)}) collective-permute-start(bf16[96,1536]{1,0:T(8,128)(2,1)} %get-tuple-element.82), channel_id=1, source_target_pairs={{0,2},{1,3},{2,0},{3,1},{4,6},{5,7},{6,4},{7,5},{8,10},{9,11},{10,... | collective-permute-start | bytes 884744 | tf_op jit(solution)/shard_map/ppermute | solution.py:374
  16.0 4.5 %collective-permute-done.refs_1_.refs_2_ = bf16[272,1024]{1,0:T(8,128)(2,1)S(1)} collective-permute-done((bf16[272,1024]{1,0:T(8,128)(2,1)S(1)}, bf16[272,1024]{1,0:T(8,128)(2,1)S(1)}, u32[]{:S(2)}, u32[]{:S(2)}) %collective-permute-start) | collective-permute-done | bytes 557088 | tf_op jit(solution)/shard_map/ppermute | solution.py:371
  20.5 4.2 %collective-permute-start.5 = (bf16[96,1536]{1,0:T(8,128)(2,1)}, bf16[96,1536]{1,0:T(8,128)(2,1)S(1)}, u32[]{:S(2)}, u32[]{:S(2)}) collective-permute-start(bf16[96,1536]{1,0:T(8,128)(2,1)} %get-tuple-element.84), channel_id=1, source_target_pairs={{0,3},{1,0},{2,1},{3,2},{4,7},{5,4},{6,5},{7,6},{8,11},{9,8},{10,9... | collective-permute-start | bytes 884744 | tf_op jit(solution)/shard_map/ppermute | solution.py:374
  24.6 4.6 %constant_dynamic-slice_fusion.1 = bf16[8,256,1024]{2,1,0:T(8,128)(2,1)} fusion(bf16[8,256,4096]{2,1,0:T(8,128)(2,1)} %refs_5_.3, s32[]{:T(128)S(6)} %select_n.46), kind=kLoop, calls=%fused_computation.29 | loop fusion | bytes 8388612 | tf_op jit(solution)/shard_map/dynamic_slice | solution.py:406
  29.3 2.3 %constant_dynamic-slice_fusion.refs_1_ = bf16[256,2048]{1,0:T(8,128)(2,1)} fusion(bf16[256,8192]{1,0:T(8,128)(2,1)} %param.6, s32[]{:T(128)S(6)} %select_n.47), kind=kLoop, calls=%fused_computation.28 | loop fusion | bytes 2097156 | tf_op jit(solution)/shard_map/dynamic_slice | solution.py:409
  31.6 3.1 %collective-permute-done.4.refs_2_.refs_4_.refs_3_ = bf16[96,1536]{1,0:T(8,128)(2,1)} collective-permute-done((bf16[96,1536]{1,0:T(8,128)(2,1)}, bf16[96,1536]{1,0:T(8,128)(2,1)}, u32[]{:S(2)}, u32[]{:S(2)}) %collective-permute-start.4) | collective-permute-done | bytes 294944 | tf_op jit(solution)/shard_map/ppermute | solution.py:374
  35.3 3.3 %collective-permute-start.13 = (bf16[8,256,1024]{2,1,0:T(8,128)(2,1)}, bf16[8,256,1024]{2,1,0:T(8,128)(2,1)}, u32[]{:S(2)}, u32[]{:S(2)}) collective-permute-start(bf16[8,256,1024]{2,1,0:T(8,128)(2,1)} %constant_dynamic-slice_fusion.1), channel_id=1, source_target_pairs={{0,4},{8,12},{20,16},{28,24},{1,5},{9,13},{21,17},{29,25},{2,6},{1... | collective-permute-start | bytes 12582920 | tf_op jit(solution)/shard_map/ppermute | solution.py:412
  39.1 4.0 %shard_map.86 = (bf16[3,96,1024]{2,1,0:T(8,128)(2,1)}, bf16[3,96,1024]{2,1,0:T(8,128)(2,1)}, bf16[3,96,1024]{2,1,0:T(8,128)(2,1)}, bf16[3,96,1024]{2,1,0:T(8,128)(2,1)}) custom-call(s32[1]{0:T(128)} %bitcast.2.refs_0_, bf16[272,1024]{1,0:T(8,128)(2,1)} %copy-done, bf16[272,1024]{1,0:T(8,128)(2,1)} %copy-done.1, bf16[272,1024]{1,0:T(8,128)(2,1)} %copy-done.2), custom_call_target="tpu_custom_call" | custom-call | flops 1 | bytes 1 | tf_op jit(solution)/shard_map/pallas_call | solution.py:154
  43.1 5.9 %collective-permute-start.12 = (bf16[3,96,1024]{2,1,0:T(8,128)(2,1)}, bf16[3,96,1024]{2,1,0:T(8,128)(2,1)S(1)}, u32[]{:S(2)}, u32[]{:S(2)}) collective-permute-start(bf16[3,96,1024]{2,1,0:T(8,128)(2,1)} %get-tuple-element.93), channel_id=1, source_target_pairs={{0,2},{1,3},{2,0},{3,1},{4,6},{5,7},{6,4},{7,5},{8,10},{9,11},{10,... | collective-permute-start | bytes 1769480 | tf_op jit(solution)/shard_map/ppermute | solution.py:374
  49.0 0.8 copy-done.6
  50.1 6.1 %shard_map.87 = (f32[256,512]{1,0:T(8,128)}, f32[256,512]{1,0:T(8,128)}, f32[256,512]{1,0:T(8,128)}, f32[256,512]{1,0:T(8,128)}) custom-call(s32[1]{0:T(128)} %bitcast.refs_0_, bf16[256,2048]{1,0:T(8,128)(2,1)} %constant_dynamic-slice_fusion.refs_1_, bf16[272,1024]{1,0:T(8,128)(2,1)} %copy-done, bf16[272,1024]{1,0:T(8,128)(2,1)} %copy-done.1, ...), custom_call_target="tpu_custom_call" | custom-call | flops 1 | bytes 1 | tf_op jit(solution)/shard_map/pallas_call | solution.py:154
  56.2 1.6 collective-permute-start.9
  57.8 2.0 %collective-permute-start.10 = (f32[256,512]{1,0:T(8,128)}, f32[256,512]{1,0:T(8,128)S(1)}, u32[]{:S(2)}, u32[]{:S(2)}) collective-permute-start(f32[256,512]{1,0:T(8,128)} %get-tuple-element.100), channel_id=1, source_target_pairs={{0,16},{8,24},{16,0},{24,8},{1,17},{9,25},{17,1},{25,9},{2,18},{10... | collective-permute-start | bytes 1572872 | tf_op jit(solution)/shard_map/ppermute | solution.py:371
  59.8 3.4 %shard_map.88.refs_0_ = f32[4,96,256]{2,1,0:T(8,128)} custom-call(bf16[96,1536]{1,0:T(8,128)(2,1)} %get-tuple-element.108.refs_0_.refs_2_.refs_1_, bf16[96,1536]{1,0:T(8,128)(2,1)} %collective-permute-done.3.refs_1_.refs_3_.refs_2_, bf16[96,1536]{1,0:T(8,128)(2,1)} %collective-permute-done.4.refs_2_.refs_4_.refs_3_, bf16[96,1536]{1,0:T(8,128)(2,1)} %copy-done.15, ...), custom_call_target="tpu_custom_call" | custom-call | flops 10000000000 | bytes 1 | tf_op jit(solution)/shard_map/pallas_call | solution.py:154
  64.0 1.3 collective-permute-done.14.refs_1_
  65.2 3.2 %collective-permute-start.16 = (bf16[3,96,1024]{2,1,0:T(8,128)(2,1)}, bf16[3,96,1024]{2,1,0:T(8,128)(2,1)S(1)}, u32[]{:S(2)}, u32[]{:S(2)}) collective-permute-start(bf16[3,96,1024]{2,1,0:T(8,128)(2,1)} %get-tuple-element.92), channel_id=1, source_target_pairs={{0,1},{1,2},{2,3},{3,0},{4,5},{5,6},{6,7},{7,4},{8,9},{9,10},{10,1... | collective-permute-start | bytes 1769480 | tf_op jit(solution)/shard_map/ppermute | solution.py:374
  68.4 2.2 %shard_map.89.refs_9_.refs_4_ = bf16[4,96,768]{2,1,0:T(8,128)(2,1)} custom-call(f32[4,96,256]{2,1,0:T(8,128)} %shard_map.88.refs_0_, f32[4,96,256]{2,1,0:T(8,128)} %copy-done.13, bf16[96,1536]{1,0:T(8,128)(2,1)} %get-tuple-element.108.refs_0_.refs_2_.refs_1_, bf16[96,1536]{1,0:T(8,128)(2,1)} %collective-permute-done.3.refs_1_.refs_3_.refs_2_, ...), custom_call_target="tpu_custom_call" | custom-call | flops 1 | bytes 1 | tf_op jit(solution)/shard_map/pallas_call | solution.py:154
  70.6 17.8 %collective-permute-done.12.refs_4_.refs_7_ = bf16[3,96,1024]{2,1,0:T(8,128)(2,1)S(1)} collective-permute-done((bf16[3,96,1024]{2,1,0:T(8,128)(2,1)}, bf16[3,96,1024]{2,1,0:T(8,128)(2,1)S(1)}, u32[]{:S(2)}, u32[]{:S(2)}) %collective-permute-start.12) | collective-permute-done | bytes 589856 | tf_op jit(solution)/shard_map/ppermute | solution.py:374
  88.4 0.8 copy-done.9
  89.2 0.8 copy-done.10
  90.0 0.8 copy-done.11
  90.8 2.4 %collective-permute-start.28 = (bf16[4,96,768]{2,1,0:T(8,128)(2,1)}, bf16[4,96,768]{2,1,0:T(8,128)(2,1)S(1)}, u32[]{:S(2)}, u32[]{:S(2)}) collective-permute-start(bf16[4,96,768]{2,1,0:T(8,128)(2,1)} %shard_map.89.refs_9_.refs_4_), channel_id=1, source_target_pairs={{0,24},{8,16},{16,8},{24,0},{1,25},{9,17},{17,9},{25,1},{2,26},{10... | collective-permute-start | bytes 1769480 | tf_op jit(solution)/shard_map/ppermute | solution.py:371
  94.3 7.2 %shard_map.90 = (f32[4,2,96,128]{3,2,1,0:T(8,128)}, f32[4,2,96,128]{3,2,1,0:T(8,128)}) custom-call(s32[3]{0:T(128)} %pad_add_fusion.refs_0_, bf16[96,1536]{1,0:T(8,128)(2,1)} %get-tuple-element.108.refs_0_.refs_2_.refs_1_, bf16[96,1536]{1,0:T(8,128)(2,1)} %collective-permute-done.4.refs_2_.refs_4_.refs_3_, ...), custom_call_target="tpu_custom_call" | custom-call | flops 10000000000 | bytes 1 | tf_op jit(solution)/shard_map/pallas_call | solution.py:154
  101.6 2.2 %collective-permute-done.17.refs_4_.refs_8_ = bf16[3,96,1024]{2,1,0:T(8,128)(2,1)S(1)} collective-permute-done((bf16[3,96,1024]{2,1,0:T(8,128)(2,1)}, bf16[3,96,1024]{2,1,0:T(8,128)(2,1)S(1)}, u32[]{:S(2)}, u32[]{:S(2)}) %collective-permute-start.17) | collective-permute-done | bytes 589856 | tf_op jit(solution)/shard_map/ppermute | solution.py:374
  103.8 0.9 copy-done.25
  104.6 7.3 %shard_map.91 = (f32[4,2,96,128]{3,2,1,0:T(8,128)}, f32[4,2,96,128]{3,2,1,0:T(8,128)}) custom-call(s32[3]{0:T(128)} %pad_add_fusion.refs_0_, bf16[96,1536]{1,0:T(8,128)(2,1)} %collective-permute-done.3.refs_1_.refs_3_.refs_2_, bf16[96,1536]{1,0:T(8,128)(2,1)} %copy-done.15, bf16[3,96,1024]{2,1,0:T(8,128)(2,1)} %copy-done.24, ...), custom_call_target="tpu_custom_call" | custom-call | flops 10000000000 | bytes 1 | tf_op jit(solution)/shard_map/pallas_call | solution.py:154
  112.7 1.2 collective-permute-done.18
  114.0 1.0 add.109
  115.1 1.6 collective-permute-start.19
  116.6 1.1 collective-permute-start.21
  117.7 0.9 collective-permute-start.20
  118.6 1.1 collective-permute-done.27.refs_11_.refs_6_
  119.7 1.1 collective-permute-done.26.refs_10_.refs_5_
  120.8 0.8 copy-done.5
  121.6 8.9 %shard_map.94 = (bf16[8,64,1024]{2,1,0:T(8,128)(2,1)}, bf16[8,64,1024]{2,1,0:T(8,128)(2,1)}, bf16[8,64,1024]{2,1,0:T(8,128)(2,1)}, bf16[8,64,1024]{2,1,0:T(8,128)(2,1)}) custom-call(s32[4]{0:T(128)} %pad_add_fusion.1.refs_0_, bf16[96,1536]{1,0:T(8,128)(2,1)} %get-tuple-element.108.refs_0_.refs_2_.refs_1_, ...), custom_call_target="tpu_custom_call" | custom-call | flops 10000000000 | bytes 1 | tf_op jit(solution)/shard_map/pallas_call | solution.py:154
  130.5 0.8 collective-permute-start.31
  131.4 1.9 collective-permute-start.29
  133.2 1.2 collective-permute-start.30
  134.6 1.3 collective-permute-start.22
  137.5 4.1 %shard_map.92 = (bf16[96,512]{1,0:T(8,128)(2,1)}, bf16[96,512]{1,0:T(8,128)(2,1)}, bf16[96,512]{1,0:T(8,128)(2,1)}, bf16[96,512]{1,0:T(8,128)(2,1)}, bf16[4,96,6...) custom-call(s32[5]{0:T(128)} %stack.61.refs_0_, ...), custom_call_target="tpu_custom_call" | custom-call | flops 1 | bytes 1 | tf_op jit(solution)/shard_map/pallas_call | solution.py:154
  141.6 0.8 collective-permute-start.23
  142.4 2.8 %collective-permute-start.24 = (bf16[96,512]{1,0:T(8,128)(2,1)}, bf16[96,512]{1,0:T(8,128)(2,1)S(1)}, u32[]{:S(2)}, u32[]{:S(2)}) collective-permute-start(bf16[96,512]{1,0:T(8,128)(2,1)} %get-tuple-element.123), channel_id=1, source_target_pairs={{0,2},{1,3},{2,0},{3,1},{4,6},{5,7},{6,4},{7,5},{8,10},{9,11},{10,... | collective-permute-start | bytes 294920 | tf_op jit(solution)/shard_map/ppermute | solution.py:374
  145.2 2.0 %collective-permute-done.23.refs_6_ = bf16[96,512]{1,0:T(8,128)(2,1)S(1)} collective-permute-done((bf16[96,512]{1,0:T(8,128)(2,1)}, bf16[96,512]{1,0:T(8,128)(2,1)S(1)}, u32[]{:S(2)}, u32[]{:S(2)}) %collective-permute-start.23) | collective-permute-done | bytes 98336 | tf_op jit(solution)/shard_map/ppermute | solution.py:374
  147.4 5.2 %collective-permute-done.24.refs_7_ = bf16[96,512]{1,0:T(8,128)(2,1)S(1)} collective-permute-done((bf16[96,512]{1,0:T(8,128)(2,1)}, bf16[96,512]{1,0:T(8,128)(2,1)S(1)}, u32[]{:S(2)}, u32[]{:S(2)}) %collective-permute-start.24) | collective-permute-done | bytes 98336 | tf_op jit(solution)/shard_map/ppermute | solution.py:374
  152.6 6.6 %collective-permute-done.25.refs_8_ = bf16[96,512]{1,0:T(8,128)(2,1)S(1)} collective-permute-done((bf16[96,512]{1,0:T(8,128)(2,1)}, bf16[96,512]{1,0:T(8,128)(2,1)S(1)}, u32[]{:S(2)}, u32[]{:S(2)}) %collective-permute-start.25) | collective-permute-done | bytes 98336 | tf_op jit(solution)/shard_map/ppermute | solution.py:374
  159.3 0.6 copy-done.18
  159.9 2.8 %shard_map.93 = bf16[256,512]{1,0:T(8,128)(2,1)} custom-call(f32[256,512]{1,0:T(8,128)} %get-tuple-element.98.refs_0_, f32[256,512]{1,0:T(8,128)} %copy-done.9, f32[256,512]{1,0:T(8,128)} %copy-done.10, f32[256,512]{1,0:T(8,128)} %copy-done.11, bf16[384,256]{1,0:T(8,128)(2,1)} %get-tuple-element.102.refs_4_, bf16[96,512]{1,0:T(8,128)(2,1)} %get-tuple-element.121.refs_5_, ...), custom_call_target="tpu_custom_call" | custom-call | flops 1 | bytes 1 | tf_op jit(solution)/shard_map/pallas_call | solution.py:154
  162.7 8.7 %collective-permute-done.31 = bf16[8,64,1024]{2,1,0:T(8,128)(2,1)S(1)} collective-permute-done((bf16[8,64,1024]{2,1,0:T(8,128)(2,1)}, bf16[8,64,1024]{2,1,0:T(8,128)(2,1)S(1)}, u32[]{:S(2)}, u32[]{:S(2)}) %collective-permute-start.31) | collective-permute-done | bytes 1048608 | tf_op jit(solution)/shard_map/ppermute | solution.py:485
  171.4 1.5 collective-permute-start.33
  172.8 2.9 %collective-permute-start.34 = (bf16[4,96,64]{2,1,0:T(8,128)(2,1)}, bf16[4,96,64]{2,1,0:T(8,128)(2,1)S(1)}, u32[]{:S(2)}, u32[]{:S(2)}) collective-permute-start(bf16[4,96,64]{2,1,0:T(8,128)(2,1)} %get-tuple-element.146), channel_id=1, source_target_pairs={{0,16},{8,24},{16,0},{24,8},{1,17},{9,25},{17,1},{25,9},{2,18},{10... | collective-permute-start | bytes 147464 | tf_op jit(solution)/shard_map/ppermute | solution.py:371
  175.7 3.1 %collective-permute-start.35 = (bf16[4,96,64]{2,1,0:T(8,128)(2,1)}, bf16[4,96,64]{2,1,0:T(8,128)(2,1)S(1)}, u32[]{:S(2)}, u32[]{:S(2)}) collective-permute-start(bf16[4,96,64]{2,1,0:T(8,128)(2,1)} %get-tuple-element.148), channel_id=1, source_target_pairs={{0,24},{8,16},{16,8},{24,0},{1,25},{9,17},{17,9},{25,1},{2,26},{10... | collective-permute-start | bytes 147464 | tf_op jit(solution)/shard_map/ppermute | solution.py:371
  178.9 4.4 %broadcast_in_dim.3 = f32[8,64,4096]{2,1,0:T(8,128)} broadcast(f32[]{:T(128)} %constant.51.clone.1), dimensions={} | broadcast | bytes 8388612 | tf_op jit(solution)/shard_map/broadcast_in_dim | solution.py:475
  183.3 1.6 convert_dynamic-update-slice_fusion.3
  184.9 1.6 convert_dynamic-update-slice_fusion.2
  186.4 1.6 convert_dynamic-update-slice_fusion.1
  188.0 2.8 %convert_dynamic-update-slice_fusion = f32[8,64,4096]{2,1,0:T(8,128)} fusion(f32[8,64,4096]{2,1,0:T(8,128)} %convert_dynamic-update-slice_fusion.1, s32[]{:T(128)S(6)} %select_n.52, bf16[8,64,1024]{2,1,0:T(8,128)(2,1)} %collective-permute-done.32), kind=kLoop, calls=%fused_computation | loop fusion | flops 524288 | bytes 3145732 | tf_op jit(solution)/shard_map/dynamic_update_slice | solution.py:487
  190.8 0.6 copy-done.20
  192.1 3.9 %shard_map.95 = f32[8,64,512]{2,1,0:T(8,128)} custom-call(bf16[4,96,64]{2,1,0:T(8,128)(2,1)} %get-tuple-element.142.refs_0_, bf16[4,96,64]{2,1,0:T(8,128)(2,1)} %copy-done.20, bf16[4,96,64]{2,1,0:T(8,128)(2,1)} %copy-done.21, bf16[4,96,64]{2,1,0:T(8,128)(2,1)} %copy-done.22, bf16[4,96,768]{2,1,0:T(8,128)(2,1)} %shard_map.89.refs_9_.refs_4_, ...), custom_call_target="tpu_custom_call" | custom-call | flops 1 | bytes 1 | tf_op jit(solution)/shard_map/pallas_call | solution.py:154
  (90 shorter events, 6.8 us)
Async XLA Ops:
  4.0 16.5 %collective-permute-start = (bf16[272,1024]{1,0:T(8,128)(2,1)S(1)}, bf16[272,1024]{1,0:T(8,128)(2,1)S(1)}, u32[]{:S(2)}, u32[]{:S(2)}) collective-permute-start(bf16[272,1024]{1,0:T(8,128)(2,1)S(1)} %get-tuple-element.77), channel_id=1, source_target_pairs={{0,8},{8,0},{16,24},{24,16},{1,9},{9,1},{17,25},{25,17},{2,10},{10... | collective-permute-start | bytes 1671176 | tf_op jit(solution)/shard_map/ppermute | solution.py:371
  7.0 27.7 %collective-permute-start.1 = (bf16[272,1024]{1,0:T(8,128)(2,1)S(1)}, bf16[272,1024]{1,0:T(8,128)(2,1)S(1)}, u32[]{:S(2)}, u32[]{:S(2)}) collective-permute-start(bf16[272,1024]{1,0:T(8,128)(2,1)S(1)} %get-tuple-element.78), channel_id=1, source_target_pairs={{0,16},{8,24},{16,0},{24,8},{1,17},{9,25},{17,1},{25,9},{2,18},{10... | collective-permute-start | bytes 1671176 | tf_op jit(solution)/shard_map/ppermute | solution.py:371
  8.5 26.1 %collective-permute-start.2 = (bf16[272,1024]{1,0:T(8,128)(2,1)S(1)}, bf16[272,1024]{1,0:T(8,128)(2,1)S(1)}, u32[]{:S(2)}, u32[]{:S(2)}) collective-permute-start(bf16[272,1024]{1,0:T(8,128)(2,1)S(1)} %get-tuple-element.79), channel_id=1, source_target_pairs={{0,24},{8,16},{16,8},{24,0},{1,25},{9,17},{17,9},{25,1},{2,26},{10... | collective-permute-start | bytes 1671176 | tf_op jit(solution)/shard_map/ppermute | solution.py:371
  11.3 20.3 %collective-permute-start.3 = (bf16[96,1536]{1,0:T(8,128)(2,1)}, bf16[96,1536]{1,0:T(8,128)(2,1)}, u32[]{:S(2)}, u32[]{:S(2)}) collective-permute-start(bf16[96,1536]{1,0:T(8,128)(2,1)} %get-tuple-element.81), channel_id=1, source_target_pairs={{0,1},{1,2},{2,3},{3,0},{4,5},{5,6},{6,7},{7,4},{8,9},{9,10},{10,1... | collective-permute-start | bytes 884744 | tf_op jit(solution)/shard_map/ppermute | solution.py:374
  13.4 21.3 %collective-permute-start.4 = (bf16[96,1536]{1,0:T(8,128)(2,1)}, bf16[96,1536]{1,0:T(8,128)(2,1)}, u32[]{:S(2)}, u32[]{:S(2)}) collective-permute-start(bf16[96,1536]{1,0:T(8,128)(2,1)} %get-tuple-element.82), channel_id=1, source_target_pairs={{0,2},{1,3},{2,0},{3,1},{4,6},{5,7},{6,4},{7,5},{8,10},{9,11},{10,... | collective-permute-start | bytes 884744 | tf_op jit(solution)/shard_map/ppermute | solution.py:374
  20.5 18.1 %copy-start = (bf16[272,1024]{1,0:T(8,128)(2,1)}, bf16[272,1024]{1,0:T(8,128)(2,1)S(1)}, u32[]{:S(2)}) copy-start(bf16[272,1024]{1,0:T(8,128)(2,1)S(1)} %collective-permute-done.refs_1_.refs_2_) | copy-start | bytes 1671172
  20.5 14.8 %collective-permute-start.5 = (bf16[96,1536]{1,0:T(8,128)(2,1)}, bf16[96,1536]{1,0:T(8,128)(2,1)S(1)}, u32[]{:S(2)}, u32[]{:S(2)}) collective-permute-start(bf16[96,1536]{1,0:T(8,128)(2,1)} %get-tuple-element.84), channel_id=1, source_target_pairs={{0,3},{1,0},{2,1},{3,2},{4,7},{5,4},{6,5},{7,6},{8,11},{9,8},{10,9... | collective-permute-start | bytes 884744 | tf_op jit(solution)/shard_map/ppermute | solution.py:374
  34.7 4.4 %copy-start.1 = (bf16[272,1024]{1,0:T(8,128)(2,1)}, bf16[272,1024]{1,0:T(8,128)(2,1)S(1)}, u32[]{:S(2)}) copy-start(bf16[272,1024]{1,0:T(8,128)(2,1)S(1)} %collective-permute-done.1.refs_2_.refs_3_) | copy-start | bytes 1671172
  34.7 4.4 %copy-start.2 = (bf16[272,1024]{1,0:T(8,128)(2,1)}, bf16[272,1024]{1,0:T(8,128)(2,1)S(1)}, u32[]{:S(2)}) copy-start(bf16[272,1024]{1,0:T(8,128)(2,1)S(1)} %collective-permute-done.2.refs_3_.refs_4_) | copy-start | bytes 1671172
  35.3 24.5 %copy-start.15 = (bf16[96,1536]{1,0:T(8,128)(2,1)}, bf16[96,1536]{1,0:T(8,128)(2,1)S(1)}, u32[]{:S(2)}) copy-start(bf16[96,1536]{1,0:T(8,128)(2,1)S(1)} %collective-permute-done.5.refs_3_.refs_5_.refs_2_.refs_4_) | copy-start | bytes 884740
  35.3 24.5 %collective-permute-start.13 = (bf16[8,256,1024]{2,1,0:T(8,128)(2,1)}, bf16[8,256,1024]{2,1,0:T(8,128)(2,1)}, u32[]{:S(2)}, u32[]{:S(2)}) collective-permute-start(bf16[8,256,1024]{2,1,0:T(8,128)(2,1)} %constant_dynamic-slice_fusion.1), channel_id=1, source_target_pairs={{0,4},{8,12},{20,16},{28,24},{1,5},{9,13},{21,17},{29,25},{2,6},{1... | collective-permute-start | bytes 12582920 | tf_op jit(solution)/shard_map/ppermute | solution.py:412
  38.6 10.4 %collective-permute-start.6 = (bf16[272,1024]{1,0:T(8,128)(2,1)S(1)}, bf16[272,1024]{1,0:T(8,128)(2,1)S(1)}, u32[]{:S(2)}, u32[]{:S(2)}) collective-permute-start(bf16[272,1024]{1,0:T(8,128)(2,1)S(1)} %collective-permute-done.refs_1_.refs_2_), channel_id=1, source_target_pairs={{0,4},{4,0},{1,5},{5,1},{2,6},{6,2},{3,7},{7,3},{8,12},{12,8},{9,1... | collective-permute-start | bytes 1671176 | tf_op jit(solution)/shard_map/ppermute | solution.py:377
  38.6 10.4 %collective-permute-start.7 = (bf16[272,1024]{1,0:T(8,128)(2,1)S(1)}, bf16[272,1024]{1,0:T(8,128)(2,1)S(1)}, u32[]{:S(2)}, u32[]{:S(2)}) collective-permute-start(bf16[272,1024]{1,0:T(8,128)(2,1)S(1)} %collective-permute-done.1.refs_2_.refs_3_), channel_id=1, source_target_pairs={{0,4},{4,0},{1,5},{5,1},{2,6},{6,2},{3,7},{7,3},{8,12},{12,8},{9,1... | collective-permute-start | bytes 1671176 | tf_op jit(solution)/shard_map/ppermute | solution.py:377
  39.1 9.9 %collective-permute-start.8 = (bf16[272,1024]{1,0:T(8,128)(2,1)S(1)}, bf16[272,1024]{1,0:T(8,128)(2,1)S(1)}, u32[]{:S(2)}, u32[]{:S(2)}) collective-permute-start(bf16[272,1024]{1,0:T(8,128)(2,1)S(1)} %collective-permute-done.2.refs_3_.refs_4_), channel_id=1, source_target_pairs={{0,4},{4,0},{1,5},{5,1},{2,6},{6,2},{3,7},{7,3},{8,12},{12,8},{9,1... | collective-permute-start | bytes 1671176 | tf_op jit(solution)/shard_map/ppermute | solution.py:377
  43.1 45.3 %collective-permute-start.12 = (bf16[3,96,1024]{2,1,0:T(8,128)(2,1)}, bf16[3,96,1024]{2,1,0:T(8,128)(2,1)S(1)}, u32[]{:S(2)}, u32[]{:S(2)}) collective-permute-start(bf16[3,96,1024]{2,1,0:T(8,128)(2,1)} %get-tuple-element.93), channel_id=1, source_target_pairs={{0,2},{1,3},{2,0},{3,1},{4,6},{5,7},{6,4},{7,5},{8,10},{9,11},{10,... | collective-permute-start | bytes 1769480 | tf_op jit(solution)/shard_map/ppermute | solution.py:374
  48.9 0.8 copy-start.6
  48.9 1.0 copy-start.7
  48.9 1.2 copy-start.8
  56.2 32.2 %collective-permute-start.9 = (f32[256,512]{1,0:T(8,128)}, f32[256,512]{1,0:T(8,128)S(1)}, u32[]{:S(2)}, u32[]{:S(2)}) collective-permute-start(f32[256,512]{1,0:T(8,128)} %get-tuple-element.99), channel_id=1, source_target_pairs={{0,8},{8,0},{16,24},{24,16},{1,9},{9,1},{17,25},{25,17},{2,10},{10... | collective-permute-start | bytes 1572872 | tf_op jit(solution)/shard_map/ppermute | solution.py:371
  57.8 30.6 %collective-permute-start.10 = (f32[256,512]{1,0:T(8,128)}, f32[256,512]{1,0:T(8,128)S(1)}, u32[]{:S(2)}, u32[]{:S(2)}) collective-permute-start(f32[256,512]{1,0:T(8,128)} %get-tuple-element.100), channel_id=1, source_target_pairs={{0,16},{8,24},{16,0},{24,8},{1,17},{9,25},{17,1},{25,9},{2,18},{10... | collective-permute-start | bytes 1572872 | tf_op jit(solution)/shard_map/ppermute | solution.py:371
  59.8 30.2 %collective-permute-start.11 = (f32[256,512]{1,0:T(8,128)}, f32[256,512]{1,0:T(8,128)S(1)}, u32[]{:S(2)}, u32[]{:S(2)}) collective-permute-start(f32[256,512]{1,0:T(8,128)} %get-tuple-element.101), channel_id=1, source_target_pairs={{0,24},{8,16},{16,8},{24,0},{1,25},{9,17},{17,9},{25,1},{2,26},{10... | collective-permute-start | bytes 1572872 | tf_op jit(solution)/shard_map/ppermute | solution.py:371
  63.2 2.0 %collective-permute-start.14 = (f32[4,96,256]{2,1,0:T(8,128)}, f32[4,96,256]{2,1,0:T(8,128)S(1)}, u32[]{:S(2)}, u32[]{:S(2)}) collective-permute-start(f32[4,96,256]{2,1,0:T(8,128)} %shard_map.88.refs_0_), channel_id=1, source_target_pairs={{0,4},{4,0},{1,5},{5,1},{2,6},{6,2},{3,7},{7,3},{8,12},{12,8},{9,1... | collective-permute-start | bytes 1179656 | tf_op jit(solution)/shard_map/ppermute | solution.py:377
  65.2 3.2 %copy-start.13 = (f32[4,96,256]{2,1,0:T(8,128)}, f32[4,96,256]{2,1,0:T(8,128)S(1)}, u32[]{:S(2)}) copy-start(f32[4,96,256]{2,1,0:T(8,128)S(1)} %collective-permute-done.14.refs_1_) | copy-start | bytes 1179652
  65.2 36.3 %collective-permute-start.16 = (bf16[3,96,1024]{2,1,0:T(8,128)(2,1)}, bf16[3,96,1024]{2,1,0:T(8,128)(2,1)S(1)}, u32[]{:S(2)}, u32[]{:S(2)}) collective-permute-start(bf16[3,96,1024]{2,1,0:T(8,128)(2,1)} %get-tuple-element.92), channel_id=1, source_target_pairs={{0,1},{1,2},{2,3},{3,0},{4,5},{5,6},{6,7},{7,4},{8,9},{9,10},{10,1... | collective-permute-start | bytes 1769480 | tf_op jit(solution)/shard_map/ppermute | solution.py:374
  88.4 5.9 %copy-start.23 = (bf16[3,96,1024]{2,1,0:T(8,128)(2,1)}, bf16[3,96,1024]{2,1,0:T(8,128)(2,1)S(1)}, u32[]{:S(2)}) copy-start(bf16[3,96,1024]{2,1,0:T(8,128)(2,1)S(1)} %collective-permute-done.12.refs_4_.refs_7_) | copy-start | bytes 1769476
  88.4 15.4 %collective-permute-start.17 = (bf16[3,96,1024]{2,1,0:T(8,128)(2,1)}, bf16[3,96,1024]{2,1,0:T(8,128)(2,1)S(1)}, u32[]{:S(2)}, u32[]{:S(2)}) collective-permute-start(bf16[3,96,1024]{2,1,0:T(8,128)(2,1)} %get-tuple-element.94), channel_id=1, source_target_pairs={{0,3},{1,0},{2,1},{3,2},{4,7},{5,4},{6,5},{7,6},{8,11},{9,8},{10,9... | collective-permute-start | bytes 1769480 | tf_op jit(solution)/shard_map/ppermute | solution.py:374
  88.4 0.8 copy-start.9
  89.2 0.8 copy-start.10
  90.0 0.8 copy-start.11
  90.8 26.9 %collective-permute-start.28 = (bf16[4,96,768]{2,1,0:T(8,128)(2,1)}, bf16[4,96,768]{2,1,0:T(8,128)(2,1)S(1)}, u32[]{:S(2)}, u32[]{:S(2)}) collective-permute-start(bf16[4,96,768]{2,1,0:T(8,128)(2,1)} %shard_map.89.refs_9_.refs_4_), channel_id=1, source_target_pairs={{0,24},{8,16},{16,8},{24,0},{1,25},{9,17},{17,9},{25,1},{2,26},{10... | collective-permute-start | bytes 1769480 | tf_op jit(solution)/shard_map/ppermute | solution.py:371
  93.3 26.5 %collective-permute-start.27 = (bf16[4,96,768]{2,1,0:T(8,128)(2,1)}, bf16[4,96,768]{2,1,0:T(8,128)(2,1)S(1)}, u32[]{:S(2)}, u32[]{:S(2)}) collective-permute-start(bf16[4,96,768]{2,1,0:T(8,128)(2,1)} %shard_map.89.refs_9_.refs_4_), channel_id=1, source_target_pairs={{0,16},{8,24},{16,0},{24,8},{1,17},{9,25},{17,1},{25,9},{2,18},{10... | collective-permute-start | bytes 1769480 | tf_op jit(solution)/shard_map/ppermute | solution.py:371
  93.8 27.0 %collective-permute-start.26 = (bf16[4,96,768]{2,1,0:T(8,128)(2,1)}, bf16[4,96,768]{2,1,0:T(8,128)(2,1)S(1)}, u32[]{:S(2)}, u32[]{:S(2)}) collective-permute-start(bf16[4,96,768]{2,1,0:T(8,128)(2,1)} %shard_map.89.refs_9_.refs_4_), channel_id=1, source_target_pairs={{0,8},{8,0},{16,24},{24,16},{1,9},{9,1},{17,25},{25,17},{2,10},{10... | collective-permute-start | bytes 1769480 | tf_op jit(solution)/shard_map/ppermute | solution.py:371
  101.5 2.3 %copy-start.24 = (bf16[3,96,1024]{2,1,0:T(8,128)(2,1)}, bf16[3,96,1024]{2,1,0:T(8,128)(2,1)S(1)}, u32[]{:S(2)}) copy-start(bf16[3,96,1024]{2,1,0:T(8,128)(2,1)S(1)} %collective-permute-done.16.refs_3_.refs_6_) | copy-start | bytes 1769476
  101.5 11.2 %collective-permute-start.15 = (f32[4,2,96,128]{3,2,1,0:T(8,128)}, f32[4,2,96,128]{3,2,1,0:T(8,128)S(1)}, u32[]{:S(2)}, u32[]{:S(2)}) collective-permute-start(f32[4,2,96,128]{3,2,1,0:T(8,128)} %get-tuple-element.116), channel_id=1, source_target_pairs={{0,4},{4,0},{1,5},{5,1},{2,6},{6,2},{3,7},{7,3},{8,12},{12,8},{9,1... | collective-permute-start | bytes 1179656 | tf_op jit(solution)/shard_map/ppermute | solution.py:377
  103.8 0.9 copy-start.25
  104.6 8.1 %copy-start.14 = (f32[4,2,96,128]{3,2,1,0:T(8,128)S(1)}, f32[4,2,96,128]{3,2,1,0:T(8,128)}, u32[]{:S(2)}) copy-start(f32[4,2,96,128]{3,2,1,0:T(8,128)} %get-tuple-element.115) | copy-start | bytes 1179652
  112.0 2.0 %collective-permute-start.18 = (f32[4,2,96,128]{3,2,1,0:T(8,128)}, f32[4,2,96,128]{3,2,1,0:T(8,128)S(1)}, u32[]{:S(2)}, u32[]{:S(2)}) collective-permute-start(f32[4,2,96,128]{3,2,1,0:T(8,128)} %get-tuple-element.120), channel_id=1, source_target_pairs={{0,4},{4,0},{1,5},{5,1},{2,6},{6,2},{3,7},{7,3},{8,12},{12,8},{9,1... | collective-permute-start | bytes 1179656 | tf_op jit(solution)/shard_map/ppermute | solution.py:377
  115.1 15.4 %collective-permute-start.19 = (f32[4,96,128]{2,1,0:T(8,128)S(1)}, f32[4,96,128]{2,1,0:T(8,128)S(1)}, u32[]{:S(2)}, u32[]{:S(2)}) collective-permute-start(f32[4,96,128]{2,1,0:T(8,128)S(1)} %get-tuple-element.153), channel_id=1, source_target_pairs={{0,8},{8,0},{16,24},{24,16},{1,9},{9,1},{17,25},{25,17},{2,10},{10... | collective-permute-start | bytes 589832 | tf_op jit(solution)/shard_map/ppermute | solution.py:371
  116.6 13.9 %collective-permute-start.21 = (f32[4,96,128]{2,1,0:T(8,128)S(1)}, f32[4,96,128]{2,1,0:T(8,128)S(1)}, u32[]{:S(2)}, u32[]{:S(2)}) collective-permute-start(f32[4,96,128]{2,1,0:T(8,128)S(1)} %get-tuple-element.154), channel_id=1, source_target_pairs={{0,24},{8,16},{16,8},{24,0},{1,25},{9,17},{17,9},{25,1},{2,26},{10... | collective-permute-start | bytes 589832 | tf_op jit(solution)/shard_map/ppermute | solution.py:371
  117.7 3.1 %copy-start.3 = (bf16[4,96,768]{2,1,0:T(8,128)(2,1)}, bf16[4,96,768]{2,1,0:T(8,128)(2,1)S(1)}, u32[]{:S(2)}) copy-start(bf16[4,96,768]{2,1,0:T(8,128)(2,1)S(1)} %collective-permute-done.28.refs_12_.refs_7_) | copy-start | bytes 1769476
  117.7 12.8 %collective-permute-start.20 = (f32[4,96,128]{2,1,0:T(8,128)S(1)}, f32[4,96,128]{2,1,0:T(8,128)S(1)}, u32[]{:S(2)}, u32[]{:S(2)}) collective-permute-start(f32[4,96,128]{2,1,0:T(8,128)S(1)} %get-tuple-element.155), channel_id=1, source_target_pairs={{0,16},{8,24},{16,0},{24,8},{1,17},{9,25},{17,1},{25,9},{2,18},{10... | collective-permute-start | bytes 589832 | tf_op jit(solution)/shard_map/ppermute | solution.py:371
  119.7 1.1 copy-start.4
  120.8 0.8 copy-start.5
  130.5 40.9 %collective-permute-start.31 = (bf16[8,64,1024]{2,1,0:T(8,128)(2,1)}, bf16[8,64,1024]{2,1,0:T(8,128)(2,1)S(1)}, u32[]{:S(2)}, u32[]{:S(2)}) collective-permute-start(bf16[8,64,1024]{2,1,0:T(8,128)(2,1)} %get-tuple-element.139), channel_id=1, source_target_pairs={{0,16},{4,0},{8,24},{12,8},{16,20},{20,4},{24,28},{28,12},{1,17},{... | collective-permute-start | bytes 3145736 | tf_op jit(solution)/shard_map/ppermute | solution.py:485
  131.4 44.3 %collective-permute-start.29 = (bf16[8,64,1024]{2,1,0:T(8,128)(2,1)}, bf16[8,64,1024]{2,1,0:T(8,128)(2,1)S(1)}, u32[]{:S(2)}, u32[]{:S(2)}) collective-permute-start(bf16[8,64,1024]{2,1,0:T(8,128)(2,1)} %get-tuple-element.135), channel_id=1, source_target_pairs={{0,0},{4,16},{8,8},{12,24},{16,4},{20,20},{24,12},{28,28},{1,1},{5... | collective-permute-start | bytes 3145736 | tf_op jit(solution)/shard_map/ppermute | solution.py:485
  133.2 51.6 %collective-permute-start.30 = (bf16[8,64,1024]{2,1,0:T(8,128)(2,1)}, bf16[8,64,1024]{2,1,0:T(8,128)(2,1)S(1)}, u32[]{:S(2)}, u32[]{:S(2)}) collective-permute-start(bf16[8,64,1024]{2,1,0:T(8,128)(2,1)} %get-tuple-element.136), channel_id=1, source_target_pairs={{0,8},{4,24},{8,0},{12,16},{16,12},{20,28},{24,4},{28,20},{1,9},{5... | collective-permute-start | bytes 3145736 | tf_op jit(solution)/shard_map/ppermute | solution.py:485
  134.5 2.3 %copy-start.12 = (bf16[4,96,128]{2,1,0:T(8,128)(2,1)}, bf16[4,96,128]{2,1,0:T(8,128)(2,1)S(1)}, u32[]{:S(2)}) copy-start(bf16[4,96,128]{2,1,0:T(8,128)(2,1)S(1)} %pad_maximum_fusion.1.refs_1_) | copy-start | bytes 294916
  134.6 2.3 %collective-permute-start.22 = (bf16[4,96,128]{2,1,0:T(8,128)(2,1)S(1)}, bf16[4,96,128]{2,1,0:T(8,128)(2,1)S(1)}, u32[]{:S(2)}, u32[]{:S(2)}) collective-permute-start(bf16[4,96,128]{2,1,0:T(8,128)(2,1)S(1)} %pad_maximum_fusion.1.refs_1_), channel_id=1, source_target_pairs={{0,4},{4,0},{1,5},{5,1},{2,6},{6,2},{3,7},{7,3},{8,12},{12,8},{9,1... | collective-permute-start | bytes 294920 | tf_op jit(solution)/shard_map/ppermute | solution.py:377
  136.8 0.6 copy-start.19
  141.6 5.6 %collective-permute-start.23 = (bf16[96,512]{1,0:T(8,128)(2,1)}, bf16[96,512]{1,0:T(8,128)(2,1)S(1)}, u32[]{:S(2)}, u32[]{:S(2)}) collective-permute-start(bf16[96,512]{1,0:T(8,128)(2,1)} %get-tuple-element.122), channel_id=1, source_target_pairs={{0,3},{1,0},{2,1},{3,2},{4,7},{5,4},{6,5},{7,6},{8,11},{9,8},{10,9... | collective-permute-start | bytes 294920 | tf_op jit(solution)/shard_map/ppermute | solution.py:374
  142.4 10.2 %collective-permute-start.24 = (bf16[96,512]{1,0:T(8,128)(2,1)}, bf16[96,512]{1,0:T(8,128)(2,1)S(1)}, u32[]{:S(2)}, u32[]{:S(2)}) collective-permute-start(bf16[96,512]{1,0:T(8,128)(2,1)} %get-tuple-element.123), channel_id=1, source_target_pairs={{0,2},{1,3},{2,0},{3,1},{4,6},{5,7},{6,4},{7,5},{8,10},{9,11},{10,... | collective-permute-start | bytes 294920 | tf_op jit(solution)/shard_map/ppermute | solution.py:374
  147.2 12.0 %copy-start.16 = (bf16[96,512]{1,0:T(8,128)(2,1)}, bf16[96,512]{1,0:T(8,128)(2,1)S(1)}, u32[]{:S(2)}) copy-start(bf16[96,512]{1,0:T(8,128)(2,1)S(1)} %collective-permute-done.23.refs_6_) | copy-start | bytes 294916
  147.2 40.8 %collective-permute-start.32 = (bf16[8,64,1024]{2,1,0:T(8,128)(2,1)}, bf16[8,64,1024]{2,1,0:T(8,128)(2,1)}, u32[]{:S(2)}, u32[]{:S(2)}) collective-permute-start(bf16[8,64,1024]{2,1,0:T(8,128)(2,1)} %get-tuple-element.140), channel_id=1, source_target_pairs={{0,24},{4,8},{8,16},{12,0},{16,28},{20,12},{24,20},{28,4},{1,25},{... | collective-permute-start | bytes 3145736 | tf_op jit(solution)/shard_map/ppermute | solution.py:485
  152.6 6.6 %copy-start.17 = (bf16[96,512]{1,0:T(8,128)(2,1)}, bf16[96,512]{1,0:T(8,128)(2,1)S(1)}, u32[]{:S(2)}) copy-start(bf16[96,512]{1,0:T(8,128)(2,1)S(1)} %collective-permute-done.24.refs_7_) | copy-start | bytes 294916
  152.6 6.6 %collective-permute-start.25 = (bf16[96,512]{1,0:T(8,128)(2,1)}, bf16[96,512]{1,0:T(8,128)(2,1)S(1)}, u32[]{:S(2)}, u32[]{:S(2)}) collective-permute-start(bf16[96,512]{1,0:T(8,128)(2,1)} %get-tuple-element.124), channel_id=1, source_target_pairs={{0,1},{1,2},{2,3},{3,0},{4,5},{5,6},{6,7},{7,4},{8,9},{9,10},{10,1... | collective-permute-start | bytes 294920 | tf_op jit(solution)/shard_map/ppermute | solution.py:374
  159.3 0.6 copy-start.18
  171.4 19.4 %collective-permute-start.33 = (bf16[4,96,64]{2,1,0:T(8,128)(2,1)}, bf16[4,96,64]{2,1,0:T(8,128)(2,1)S(1)}, u32[]{:S(2)}, u32[]{:S(2)}) collective-permute-start(bf16[4,96,64]{2,1,0:T(8,128)(2,1)} %get-tuple-element.144), channel_id=1, source_target_pairs={{0,8},{8,0},{16,24},{24,16},{1,9},{9,1},{17,25},{25,17},{2,10},{10... | collective-permute-start | bytes 147464 | tf_op jit(solution)/shard_map/ppermute | solution.py:371
  172.8 18.0 %collective-permute-start.34 = (bf16[4,96,64]{2,1,0:T(8,128)(2,1)}, bf16[4,96,64]{2,1,0:T(8,128)(2,1)S(1)}, u32[]{:S(2)}, u32[]{:S(2)}) collective-permute-start(bf16[4,96,64]{2,1,0:T(8,128)(2,1)} %get-tuple-element.146), channel_id=1, source_target_pairs={{0,16},{8,24},{16,0},{24,8},{1,17},{9,25},{17,1},{25,9},{2,18},{10... | collective-permute-start | bytes 147464 | tf_op jit(solution)/shard_map/ppermute | solution.py:371
  175.7 15.1 %collective-permute-start.35 = (bf16[4,96,64]{2,1,0:T(8,128)(2,1)}, bf16[4,96,64]{2,1,0:T(8,128)(2,1)S(1)}, u32[]{:S(2)}, u32[]{:S(2)}) collective-permute-start(bf16[4,96,64]{2,1,0:T(8,128)(2,1)} %get-tuple-element.148), channel_id=1, source_target_pairs={{0,24},{8,16},{16,8},{24,0},{1,25},{9,17},{17,9},{25,1},{2,26},{10... | collective-permute-start | bytes 147464 | tf_op jit(solution)/shard_map/ppermute | solution.py:371
  190.8 0.7 copy-start.20
  190.8 0.7 copy-start.21
  191.5 0.6 copy-start.22

commit v9 on v8

--- a/solution.py
+++ b/solution.py
@@ -232,23 +232,19 @@
                 outs[c * ad + ka][kf] = part
 
 
-def back_kernel(ad, gslots, *refs):
-    dy_refs, up, out = refs[:ad], refs[ad], refs[ad + 1]
+def back_kernel(gslots, dy_ref, up, out):
+    ad = dy_ref.shape[0]
     for g in range(up.shape[0] // GROUP):
         rows = pl.ds(g * gslots, gslots)
-        dy = jnp.concatenate([r[rows, :] for r in dy_refs], axis=0)
+        dy = jnp.concatenate([dy_ref[ka, rows, :] for ka in range(ad)], axis=0)
         weights = up[g * GROUP : (g + 1) * GROUP].reshape(-1, up.shape[2])
         part = narrow(dot(dy, weights, ((1,), (1,))), gslots)
         for ka in range(ad):
             out[ka, rows, :] = part[ka * gslots : (ka + 1) * gslots]
 
 
-def both_kernel(ad, mine, got, *refs):
-    dy_refs, out = refs[:ad], refs[ad]
-    width = dy_refs[0].shape[1]
-    for ka in range(ad):
-        out[ka, :, :width] = dy_refs[ka][...]
-        out[ka, :, width:] = (adapter_scale * (mine[ka] + got[ka])).astype(BF16)
+def sum_kernel(mine, got, out):
+    out[...] = (adapter_scale * (mine[...] + got[...])).astype(BF16)
 
 
 def hidden_kernel(fsdp, gslots, at, *refs):
@@ -409,7 +405,9 @@
     x_chip = lax.dynamic_slice_in_dim(held[1], f * kf_width, kf_width, 1)
     x_in, own, down_other, x_chip = lax.optimization_barrier((x_in, own, down_other, x_chip))
     x_other = [swap(v) for v in x_in[1:]]
-    down_got = lax.ppermute(down_other, ("fsdp", "tp"), pairs)
+    down_got = lax.ppermute(after(down_other, x_other), ("fsdp", "tp"), pairs)
+    dy = jnp.stack([v[:, kt:] for v in own])
+    dy_all = [over_f(dy, k) for k in range(fsdp)]
     sends = call(
         functools.partial(others_kernel, fsdp, ad, slots, ad * dloc),
         [((fsdp - 1, slots, cw), BF16)] * (CHUNKS * ad),
@@ -421,25 +419,23 @@
     base = call(
         functools.partial(base_kernel, fsdp),
         [((rows, vloc), F32)] * fsdp,
-        [(v, None) for v in (x_chip, *x_in[1:], *after(x_other, *sends), value_weight_frozen)],
+        [(v, None) for v in (x_chip, *x_in[1:], *after(x_other, *sends, *dy_all), value_weight_frozen)],
         at=numbers(t),
     )
-    dy = [(v, (kt, vloc)) for v in after(own, base[0], down_got)]
+    dy = after(dy, base[0], down_got)
     base = [over_f(v, k) for k, v in enumerate(base)]
 
     (back,) = call(
-        functools.partial(back_kernel, ad, gslots),
+        functools.partial(back_kernel, gslots),
         [((ad, slots, rank), F32)],
-        [*dy, (adapter_up_weight, None)],
+        [(dy, None), (adapter_up_weight, None)],
         flops=10**10,
     )
-    (both,) = call(
-        functools.partial(both_kernel, ad),
-        [((ad, slots, vloc + rank), BF16)],
-        [(back, None), (swap(back), None), *dy],
-    )
-    both = after(both, *base, x_routed[0][2])
-    both = [over_f(both, k) for k in range(fsdp)]
+    (back,) = call(
+        sum_kernel, [((ad, slots, rank), BF16)], [(back, None), (swap(back), None)]
+    )
+    back = after(back, *base, x_routed[0][2])
+    back = [over_f(back, k) for k in range(fsdp)]
 
     def hidden(shifts, routed):
         return call(
@@ -452,10 +448,10 @@
         )
 
     early, late = [ka for ka in range(ad) if ka % 2 == 0], [ka for ka in range(ad) if ka % 2]
-    hid_early = hidden(early, after([x_routed[0][ka] for ka in early], both[0]))
-    x_last = after(x_routed[0], *base, *hid_early)
+    hid_early = hidden(early, after([x_routed[0][ka] for ka in early], back[0]))
+    x_last = after(x_routed[0], *base, *hid_early, *back)
     hid_late = hidden(late, [x_last[ka] for ka in late])
-    x_last, both = after((x_last, both), *hid_late)
+    x_last, back = after((x_last, back), *hid_late)
     hid = jnp.concatenate(
         [hid_early[0] + swap(hid_early[1]), hid_late[0] + swap(hid_late[1])], axis=1
     )
@@ -465,14 +461,25 @@
         [((dloc, rloc, kt), BF16)] * fsdp,
         [(v, (0, kt)) for v in own]
         + [(v, None) for v in x_last]
-        + [(v, (vloc, rank)) for v in both],
+        + [(v, None) for v in back],
         at=numbers(*[(t ^ (r // 2)) * 2 + (fx ^ (r % 2)) for r in range(fsdp)]),
         scratch=[pltpu.VMEM((GROUP * rank, kt), F32)],
         flops=10**10,
     )
     hid = [over_f(hid[k], k) for k in range(fsdp)]
-    sums = [sums[0], sums[1], *after(sums[2:], *hid[1:])]
+    hid_own = (hid[0] + hid[1] + hid[2] + hid[3]).astype(BF16)
+    shift_order = [(early + late).index(ka) for ka in range(ad)]
+    hid_own = jnp.concatenate([hid_own[i : i + 1] for i in shift_order], axis=0)
+    outs = call(
+        functools.partial(delta_kernel, fsdp, ad, gslots),
+        [((slots, vloc), BF16)] * ad + [((ad, slots, rloc), BF16)] * fsdp,
+        [(v, None) for v in (hid_own, swap(hid_own), adapter_up_weight)],
+        at=numbers(t, *[f ^ k for k in range(fsdp)]),
+    )
+    returned = [over_a(v, (ad - ka) % ad) for ka, v in enumerate(outs[:ad])]
     grad_a = jnp.zeros((dloc, rloc, half), F32)
+    hid_cols, grad_a = after((outs[ad:], grad_a), *returned[1:])
+    hid_cols = [over_f(v, k) for k, v in enumerate(hid_cols)]
     got = []
     for r in range(fsdp):
         p, q = r % 2, r // 2
@@ -482,21 +489,10 @@
             for x in range(2)
             for s in range(2)
         ]
-        got.append(lax.ppermute(sums[r], ("fsdp", "tp"), perm))
+        block = after(sums[r], *(hid[1:] if r < 2 else [*got[:2], *hid_cols[1:]]))
+        got.append(lax.ppermute(block, ("fsdp", "tp"), perm))
         at = (fx ^ p) * kf_width + (fy ^ q) * kt
         grad_a = lax.dynamic_update_slice_in_dim(grad_a, got[r].astype(F32), at, 2)
-
-    hid_own = (hid[0] + hid[1] + hid[2] + hid[3]).astype(BF16)
-    shift_order = [(early + late).index(ka) for ka in range(ad)]
-    hid_own = jnp.concatenate([hid_own[i : i + 1] for i in shift_order], axis=0)
-    outs = call(
-        functools.partial(delta_kernel, fsdp, ad, gslots),
-        [((slots, vloc), BF16)] * ad + [((ad, slots, rloc), BF16)] * fsdp,
-        [(v, None) for v in (hid_own, swap(hid_own), adapter_up_weight)],
-        at=numbers(t, *[f ^ k for k in range(fsdp)]),
-    )
-    returned = [over_a(v, (ad - ka) % ad) for ka, v in enumerate(outs[:ad])]
-    hid_cols = [over_f(after(v, got[2], *returned[1:]), k) for k, v in enumerate(outs[ad:])]
 
     (y_out,) = call(
         functools.partial(output_kernel, fsdp, ad),
@@ -506,7 +502,7 @@
     (grad_b,) = call(
         functools.partial(up_grad_kernel, fsdp, ad, gslots),
         [((dloc, rloc, vloc), F32)],
-        [(v, None) for v in hid_cols] + [(v, (0, vloc)) for v in both],
+        [(v, None) for v in [*hid_cols, *dy_all]],
     )
     return y_out, grad_a, grad_b
 

time: 197 us -> 202 us (1.025)
  waiting for transfers between devices: 55.7 us -> 65.5 us
  other arithmetic: 10.7 us -> 5.53 us
  starting transfers between devices: 53.5 us -> 58.6 us
  local copies, waits for them, and re-layouts: 22.4 us -> 17.9 us
    ppermute x15 -> x18, waiting for transfers between devices: 6.68 us -> 25.9 us  [over_f(): lax.ppermute(v, 'fsdp', [(i, i ^ k) for i in range(fsdp)])]
    ppermute x9, waiting for transfers between devices: 37.5 us -> 19 us  [over_a(): lax.ppermute(v, 'ad', [(i, (i + k) % ad) for i in range(ad)])]
    ppermute x5, waiting for transfers between devices: 8.71 us -> 14.9 us  [the longest x4 14.9 us: column_body(): got.append(lax.ppermute(block, ('fsdp', 'tp'), perm))]
    dynamic_update_slice x4, other arithmetic: 7.49 us -> 2.19 us  [column_body(): grad_a = lax.dynamic_update_slice_in_dim(grad_a, got[r].astype(F32), at, 2)]
    ppermute x9, starting transfers between devices: 21.5 us -> 25.4 us  [over_a(): lax.ppermute(v, 'ad', [(i, (i + k) % ad) for i in range(ad)])]
    broadcast_in_dim x1, local copies, waits for them, and re-layouts: 4.43 us -> 1 us  [column_body(): grad_a = jnp.zeros((dloc, rloc, half), F32)]
    unnamed x52 -> x64, local copies, waits for them, and re-layouts: 7.88 us -> 4.89 us
    ppermute x7, waiting for transfers between devices: 2.86 us -> 5.7 us  [swap(): return lax.ppermute(v, 'tp', [(0, 1), (1, 0)])]
  transfers between devices with their start and end apart: 36 -> 39, of which waited for: 14 -> 20; matrix products, arithmetic and copies ran while one was open for 11% -> 7% of each run, Pallas kernels for 25% -> 26%
where the time goes in v9:
time: 202 us; the launch traced here: 201 us
  waiting for transfers between devices  65.5 us (32%)
  starting transfers between devices  58.6 us (29%)
  Pallas kernels  52.5 us (26%)
  local copies, waits for them, and re-layouts  17.9 us (9%)
  other arithmetic  5.53 us (3%)
    pallas_call x11, Pallas kernels, call(): pl.pallas_call(body, out_shape=[jax.ShapeDtypeStruct(shape, dtype) for sh...  52.5 us
    ppermute x18, waiting for transfers between devices, over_f(): lax.ppermute(v, 'fsdp', [(i, i ^ k) for i in range(fsdp)])  25.9 us
    ppermute x9, starting transfers between devices, over_a(): lax.ppermute(v, 'ad', [(i, (i + k) % ad) for i in range(ad)])  25.4 us
    ppermute x18, starting transfers between devices, over_f(): lax.ppermute(v, 'fsdp', [(i, i ^ k) for i in range(fsdp)])  22.2 us
    ppermute x9, waiting for transfers between devices, over_a(): lax.ppermute(v, 'ad', [(i, (i + k) % ad) for i in range(ad)])  19 us
    ppermute x4, waiting for transfers between devices, column_body(): got.append(lax.ppermute(block, ('fsdp', 'tp'), perm))  14.9 us
    ppermute x7, waiting for transfers between devices, swap(): return lax.ppermute(v, 'tp', [(0, 1), (1, 0)])  5.7 us
    ppermute x4, starting transfers between devices, column_body(): got.append(lax.ppermute(block, ('fsdp', 'tp'), perm))  5.14 us
  transfers between devices with their start and end apart: 39, of which 20 were waited for; matrix products, arithmetic and copies ran while one was open for 7% of the time, Pallas kernels for 26%

profile of v9, /device:TPU:0, one launch (start us, length us, event | category | flops | bytes accessed | tf_op | source)
XLA Modules:
  0.0 201.3 jit_solution(8667558391773117052)
XLA Ops:
  0.7 0.7 bitcast_convert_fusion
  1.3 2.5 %constant_dynamic-slice_fusion.2 = (bf16[256,1024]{1,0:T(8,128)(2,1)S(1)}, bf16[256,1024]{1,0:T(8,128)(2,1)S(1)}, bf16[256,1024]{1,0:T(8,128)(2,1)S(1)}, bf16[256,1024]{1,0:T(8,128)(2,1)}) fusion(bf16[256,8192]{1,0:T(8,128)(2,1)} %param.6, s32[]{:T(128)S(6)} %select_n.44, s32[]{:T(128)S(6)} %select_n.43, s32[]{:T(128)S(6)} %select_n.42, s32[]{:T(128)S(6)} %select_n.41), kind=kLoop, calls=%fused_computation.35 | loop fusion | bytes 4194320 | tf_op jit(solution)/shard_map/dynamic_slice | solution.py:383
  4.0 3.0 %collective-permute-start = (bf16[272,1024]{1,0:T(8,128)(2,1)S(1)}, bf16[272,1024]{1,0:T(8,128)(2,1)S(1)}, u32[]{:S(2)}, u32[]{:S(2)}) collective-permute-start(bf16[272,1024]{1,0:T(8,128)(2,1)S(1)} %get-tuple-element.78), channel_id=1, source_target_pairs={{0,8},{8,0},{16,24},{24,16},{1,9},{9,1},{17,25},{25,17},{2,10},{10... | collective-permute-start | bytes 1671176 | tf_op jit(solution)/shard_map/ppermute | solution.py:367
  7.0 1.5 collective-permute-start.1
  8.6 2.8 %shard_map.85 = (bf16[384,256]{1,0:T(8,128)(2,1)}, bf16[96,1536]{1,0:T(8,128)(2,1)}, bf16[96,1536]{1,0:T(8,128)(2,1)}, bf16[96,1536]{1,0:T(8,128)(2,1)}, bf16[96,1536]{1,0:T(8,128)(2,1)}) custom-call(s32[1]{0:T(128)} %bitcast.2.refs_0_, s32[1,256]{1,0:T(1,128)} %bitcast.38, bf16[256,1024]{1,0:T(8,128)(2,1)} %get-tuple-element.77.refs_2_, ...), custom_call_target="tpu_custom_call" | custom-call | flops 1 | bytes 1 | tf_op jit(solution)/shard_map/pallas_call | solution.py:154
  11.3 2.1 %collective-permute-start.3 = (bf16[96,1536]{1,0:T(8,128)(2,1)}, bf16[96,1536]{1,0:T(8,128)(2,1)}, u32[]{:S(2)}, u32[]{:S(2)}) collective-permute-start(bf16[96,1536]{1,0:T(8,128)(2,1)} %get-tuple-element.82), channel_id=1, source_target_pairs={{0,1},{1,2},{2,3},{3,0},{4,5},{5,6},{6,7},{7,4},{8,9},{9,10},{10,1... | collective-permute-start | bytes 884744 | tf_op jit(solution)/shard_map/ppermute | solution.py:370
  13.4 2.6 %collective-permute-start.4 = (bf16[96,1536]{1,0:T(8,128)(2,1)}, bf16[96,1536]{1,0:T(8,128)(2,1)}, u32[]{:S(2)}, u32[]{:S(2)}) collective-permute-start(bf16[96,1536]{1,0:T(8,128)(2,1)} %get-tuple-element.83), channel_id=1, source_target_pairs={{0,2},{1,3},{2,0},{3,1},{4,6},{5,7},{6,4},{7,5},{8,10},{9,11},{10,... | collective-permute-start | bytes 884744 | tf_op jit(solution)/shard_map/ppermute | solution.py:370
  16.0 4.5 %collective-permute-done.refs_1_.refs_2_ = bf16[272,1024]{1,0:T(8,128)(2,1)S(1)} collective-permute-done((bf16[272,1024]{1,0:T(8,128)(2,1)S(1)}, bf16[272,1024]{1,0:T(8,128)(2,1)S(1)}, u32[]{:S(2)}, u32[]{:S(2)}) %collective-permute-start) | collective-permute-done | bytes 557088 | tf_op jit(solution)/shard_map/ppermute | solution.py:367
  20.5 4.2 %collective-permute-start.5 = (bf16[96,1536]{1,0:T(8,128)(2,1)}, bf16[96,1536]{1,0:T(8,128)(2,1)S(1)}, u32[]{:S(2)}, u32[]{:S(2)}) collective-permute-start(bf16[96,1536]{1,0:T(8,128)(2,1)} %get-tuple-element.85), channel_id=1, source_target_pairs={{0,3},{1,0},{2,1},{3,2},{4,7},{5,4},{6,5},{7,6},{8,11},{9,8},{10,9... | collective-permute-start | bytes 884744 | tf_op jit(solution)/shard_map/ppermute | solution.py:370
  24.6 4.6 %constant_dynamic-slice_fusion.1 = bf16[8,256,1024]{2,1,0:T(8,128)(2,1)} fusion(bf16[8,256,4096]{2,1,0:T(8,128)(2,1)} %refs_5_.3, s32[]{:T(128)S(6)} %select_n.46), kind=kLoop, calls=%fused_computation.34 | loop fusion | bytes 8388612 | tf_op jit(solution)/shard_map/dynamic_slice | solution.py:402
  29.3 2.3 %constant_dynamic-slice_fusion.refs_1_ = bf16[256,2048]{1,0:T(8,128)(2,1)} fusion(bf16[256,8192]{1,0:T(8,128)(2,1)} %param.6, s32[]{:T(128)S(6)} %select_n.47), kind=kLoop, calls=%fused_computation.33 | loop fusion | bytes 2097156 | tf_op jit(solution)/shard_map/dynamic_slice | solution.py:405
  31.6 3.1 %collective-permute-done.4.refs_2_.refs_3_ = bf16[96,1536]{1,0:T(8,128)(2,1)} collective-permute-done((bf16[96,1536]{1,0:T(8,128)(2,1)}, bf16[96,1536]{1,0:T(8,128)(2,1)}, u32[]{:S(2)}, u32[]{:S(2)}) %collective-permute-start.4) | collective-permute-done | bytes 294944 | tf_op jit(solution)/shard_map/ppermute | solution.py:370
  35.9 1.4 collective-permute-done.6.refs_5_
  37.3 0.8 collective-permute-done.7.refs_6_
  38.1 0.8 collective-permute-done.8.refs_7_
  38.9 4.0 %collective-permute-start.16 = (bf16[8,256,1024]{2,1,0:T(8,128)(2,1)}, bf16[8,256,1024]{2,1,0:T(8,128)(2,1)}, u32[]{:S(2)}, u32[]{:S(2)}) collective-permute-start(bf16[8,256,1024]{2,1,0:T(8,128)(2,1)} %constant_dynamic-slice_fusion.1), channel_id=1, source_target_pairs={{0,4},{8,12},{20,16},{28,24},{1,5},{9,13},{21,17},{29,25},{2,6},{1... | collective-permute-start | bytes 12582920 | tf_op jit(solution)/shard_map/ppermute | solution.py:408
  42.9 1.0 slice_bitcast_fusion.2
  43.8 0.9 slice_bitcast_fusion
  44.9 3.0 %collective-permute-start.10 = (bf16[4,96,512]{2,1,0:T(8,128)(2,1)S(1)}, bf16[4,96,512]{2,1,0:T(8,128)(2,1)S(1)}, u32[]{:S(2)}, u32[]{:S(2)}) collective-permute-start(bf16[4,96,512]{2,1,0:T(8,128)(2,1)S(1)} %pad_maximum_fusion.refs_0_.refs_4_), channel_id=1, source_target_pairs={{0,16},{8,24},{16,0},{24,8},{1,17},{9,25},{17,1},{25,9},{2,18},{10... | collective-permute-start | bytes 1179656 | tf_op jit(solution)/shard_map/ppermute | solution.py:367
  48.4 4.0 %shard_map.86 = (bf16[3,96,1024]{2,1,0:T(8,128)(2,1)}, bf16[3,96,1024]{2,1,0:T(8,128)(2,1)}, bf16[3,96,1024]{2,1,0:T(8,128)(2,1)}, bf16[3,96,1024]{2,1,0:T(8,128)(2,1)}) custom-call(s32[1]{0:T(128)} %bitcast.2.refs_0_, bf16[272,1024]{1,0:T(8,128)(2,1)} %copy-done.1, bf16[272,1024]{1,0:T(8,128)(2,1)} %copy-done.2, bf16[272,1024]{1,0:T(8,128)(2,1)} %copy-done.3), custom_call_target="tpu_custom_call" | custom-call | flops 1 | bytes 1 | tf_op jit(solution)/shard_map/pallas_call | solution.py:154
  52.4 5.2 %collective-permute-start.15 = (bf16[3,96,1024]{2,1,0:T(8,128)(2,1)}, bf16[3,96,1024]{2,1,0:T(8,128)(2,1)S(1)}, u32[]{:S(2)}, u32[]{:S(2)}) collective-permute-start(bf16[3,96,1024]{2,1,0:T(8,128)(2,1)} %get-tuple-element.94), channel_id=1, source_target_pairs={{0,2},{1,3},{2,0},{3,1},{4,6},{5,7},{6,4},{7,5},{8,10},{9,11},{10,... | collective-permute-start | bytes 1769480 | tf_op jit(solution)/shard_map/ppermute | solution.py:370
  57.8 7.6 %collective-permute-done.10.refs_6_ = bf16[4,96,512]{2,1,0:T(8,128)(2,1)S(1)} collective-permute-done((bf16[4,96,512]{2,1,0:T(8,128)(2,1)S(1)}, bf16[4,96,512]{2,1,0:T(8,128)(2,1)S(1)}, u32[]{:S(2)}, u32[]{:S(2)}) %collective-permute-start.10) | collective-permute-done | bytes 393248 | tf_op jit(solution)/shard_map/ppermute | solution.py:367
  65.5 6.4 %shard_map.87 = (f32[256,512]{1,0:T(8,128)}, f32[256,512]{1,0:T(8,128)}, f32[256,512]{1,0:T(8,128)}, f32[256,512]{1,0:T(8,128)}) custom-call(s32[1]{0:T(128)} %bitcast.refs_0_, bf16[256,2048]{1,0:T(8,128)(2,1)} %constant_dynamic-slice_fusion.refs_1_, bf16[272,1024]{1,0:T(8,128)(2,1)} %copy-done.1, bf16[272,1024]{1,0:T(8,128)(2,1)} %copy-done.2, ...), custom_call_target="tpu_custom_call" | custom-call | flops 1 | bytes 1 | tf_op jit(solution)/shard_map/pallas_call | solution.py:154
  72.5 0.8 collective-permute-start.13
  73.3 2.1 %collective-permute-start.14 = (f32[256,512]{1,0:T(8,128)}, f32[256,512]{1,0:T(8,128)S(1)}, u32[]{:S(2)}, u32[]{:S(2)}) collective-permute-start(f32[256,512]{1,0:T(8,128)} %get-tuple-element.106), channel_id=1, source_target_pairs={{0,24},{8,16},{16,8},{24,0},{1,25},{9,17},{17,9},{25,1},{2,26},{10... | collective-permute-start | bytes 1572872 | tf_op jit(solution)/shard_map/ppermute | solution.py:367
  75.4 3.4 %shard_map.88.refs_0_ = f32[4,96,256]{2,1,0:T(8,128)} custom-call(bf16[4,96,512]{2,1,0:T(8,128)(2,1)} %copy-done.4, bf16[8,256,512]{2,1,0:T(8,128)(2,1)} %refs_3_.3), custom_call_target="tpu_custom_call" | custom-call | flops 10000000000 | bytes 1 | tf_op jit(solution)/shard_map/pallas_call | solution.py:154
  78.9 0.6 pad_add_fusion.refs_0_
  79.6 1.2 collective-permute-done.17.refs_1_
  80.8 6.0 %collective-permute-start.19 = (bf16[3,96,1024]{2,1,0:T(8,128)(2,1)}, bf16[3,96,1024]{2,1,0:T(8,128)(2,1)S(1)}, u32[]{:S(2)}, u32[]{:S(2)}) collective-permute-start(bf16[3,96,1024]{2,1,0:T(8,128)(2,1)} %get-tuple-element.93), channel_id=1, source_target_pairs={{0,1},{1,2},{2,3},{3,0},{4,5},{5,6},{6,7},{7,4},{8,9},{9,10},{10,1... | collective-permute-start | bytes 1769480 | tf_op jit(solution)/shard_map/ppermute | solution.py:370
  86.9 1.8 shard_map.89.refs_9_
  88.8 2.2 %collective-permute-start.20 = (bf16[3,96,1024]{2,1,0:T(8,128)(2,1)S(1)}, bf16[3,96,1024]{2,1,0:T(8,128)(2,1)S(1)}, u32[]{:S(2)}, u32[]{:S(2)}) collective-permute-start(bf16[3,96,1024]{2,1,0:T(8,128)(2,1)S(1)} %copy-done.26), channel_id=1, source_target_pairs={{0,3},{1,0},{2,1},{3,2},{4,7},{5,4},{6,5},{7,6},{8,11},{9,8},{10,9... | collective-permute-start | bytes 1769480 | tf_op jit(solution)/shard_map/ppermute | solution.py:370
  91.0 6.7 %collective-permute-done.14.refs_3_ = f32[256,512]{1,0:T(8,128)S(1)} collective-permute-done((f32[256,512]{1,0:T(8,128)}, f32[256,512]{1,0:T(8,128)S(1)}, u32[]{:S(2)}, u32[]{:S(2)}) %collective-permute-start.14) | collective-permute-done | bytes 524320 | tf_op jit(solution)/shard_map/ppermute | solution.py:367
  97.6 1.7 collective-permute-start.23
  99.4 1.3 collective-permute-start.22
  101.1 7.2 %shard_map.90 = (f32[4,2,96,128]{3,2,1,0:T(8,128)}, f32[4,2,96,128]{3,2,1,0:T(8,128)}) custom-call(s32[3]{0:T(128)} %pad_add_fusion.refs_0_, bf16[96,1536]{1,0:T(8,128)(2,1)} %get-tuple-element.96.refs_1_, bf16[96,1536]{1,0:T(8,128)(2,1)} %collective-permute-done.4.refs_2_.refs_3_, bf16[3,96,1024]{2,1,0:T(8,128)(2,1)} %get-tuple-element.131.refs_3_.refs_5_, ...), custom_call_target="tpu_custom_call" | custom-call | flops 10000000000 | bytes 1 | tf_op jit(solution)/shard_map/pallas_call | solution.py:154
  108.4 6.1 %collective-permute-done.20.refs_4_.refs_8_ = bf16[3,96,1024]{2,1,0:T(8,128)(2,1)S(1)} collective-permute-done((bf16[3,96,1024]{2,1,0:T(8,128)(2,1)S(1)}, bf16[3,96,1024]{2,1,0:T(8,128)(2,1)S(1)}, u32[]{:S(2)}, u32[]{:S(2)}) %collective-permute-start.20) | collective-permute-done | bytes 589856 | tf_op jit(solution)/shard_map/ppermute | solution.py:370
  114.6 0.7 copy-done.28
  115.4 7.3 %shard_map.91 = (f32[4,2,96,128]{3,2,1,0:T(8,128)}, f32[4,2,96,128]{3,2,1,0:T(8,128)}) custom-call(s32[3]{0:T(128)} %pad_add_fusion.refs_0_, bf16[96,1536]{1,0:T(8,128)(2,1)} %collective-permute-done.3.refs_1_.refs_2_, bf16[96,1536]{1,0:T(8,128)(2,1)} %copy-done.24, bf16[3,96,1024]{2,1,0:T(8,128)(2,1)} %copy-done.27, bf16[3,96,1024]{2,1,0:T(8,128)(2,1)} %copy-done.28, ...), custom_call_target="tpu_custom_call" | custom-call | flops 10000000000 | bytes 1 | tf_op jit(solution)/shard_map/pallas_call | solution.py:154
  122.8 0.7 pad_add_fusion.1.refs_0_
  123.6 1.2 collective-permute-done.24
  124.7 1.0 add.109
  126.4 1.8 collective-permute-start.27
  128.2 1.2 collective-permute-start.26
  129.4 8.9 %shard_map.94 = (bf16[8,64,1024]{2,1,0:T(8,128)(2,1)}, bf16[8,64,1024]{2,1,0:T(8,128)(2,1)}, bf16[8,64,1024]{2,1,0:T(8,128)(2,1)}, bf16[8,64,1024]{2,1,0:T(8,128)(2,1)}) custom-call(s32[4]{0:T(128)} %pad_add_fusion.1.refs_0_, bf16[96,1536]{1,0:T(8,128)(2,1)} %get-tuple-element.96.refs_1_, bf16[96,1536]{1,0:T(8,128)(2,1)} %collective-permute-done.3.refs_1_.refs_2_, ...), custom_call_target="tpu_custom_call" | custom-call | flops 10000000000 | bytes 1 | tf_op jit(solution)/shard_map/pallas_call | solution.py:154
  138.8 1.9 collective-permute-start.32
  141.3 0.9 collective-permute-start.28
  142.3 0.7 stack.81.refs_0_
  143.2 0.6 copy-done.23
  143.8 4.1 %shard_map.92 = (bf16[96,512]{1,0:T(8,128)(2,1)}, bf16[96,512]{1,0:T(8,128)(2,1)}, bf16[96,512]{1,0:T(8,128)(2,1)}, bf16[96,512]{1,0:T(8,128)(2,1)}, bf16[4,96,6...) custom-call(s32[5]{0:T(128)} %stack.81.refs_0_, ...), custom_call_target="tpu_custom_call" | custom-call | flops 1 | bytes 1 | tf_op jit(solution)/shard_map/pallas_call | solution.py:154
  148.0 2.5 %collective-permute-start.29 = (bf16[96,512]{1,0:T(8,128)(2,1)}, bf16[96,512]{1,0:T(8,128)(2,1)S(1)}, u32[]{:S(2)}, u32[]{:S(2)}) collective-permute-start(bf16[96,512]{1,0:T(8,128)(2,1)} %get-tuple-element.121), channel_id=1, source_target_pairs={{0,3},{1,0},{2,1},{3,2},{4,7},{5,4},{6,5},{7,6},{8,11},{9,8},{10,9... | collective-permute-start | bytes 294920 | tf_op jit(solution)/shard_map/ppermute | solution.py:370
  151.1 2.9 %collective-permute-done.29.refs_6_ = bf16[96,512]{1,0:T(8,128)(2,1)S(1)} collective-permute-done((bf16[96,512]{1,0:T(8,128)(2,1)}, bf16[96,512]{1,0:T(8,128)(2,1)S(1)}, u32[]{:S(2)}, u32[]{:S(2)}) %collective-permute-start.29) | collective-permute-done | bytes 98336 | tf_op jit(solution)/shard_map/ppermute | solution.py:370
  153.9 6.3 %collective-permute-done.30.refs_7_ = bf16[96,512]{1,0:T(8,128)(2,1)S(1)} collective-permute-done((bf16[96,512]{1,0:T(8,128)(2,1)}, bf16[96,512]{1,0:T(8,128)(2,1)S(1)}, u32[]{:S(2)}, u32[]{:S(2)}) %collective-permute-start.30) | collective-permute-done | bytes 98336 | tf_op jit(solution)/shard_map/ppermute | solution.py:370
  160.3 1.4 collective-permute-start.34
  161.7 1.7 collective-permute-start.35
  163.8 5.1 %collective-permute-done.34.refs_1_ = bf16[4,96,64]{2,1,0:T(8,128)(2,1)S(1)} collective-permute-done((bf16[4,96,64]{2,1,0:T(8,128)(2,1)}, bf16[4,96,64]{2,1,0:T(8,128)(2,1)S(1)}, u32[]{:S(2)}, u32[]{:S(2)}) %collective-permute-start.34) | collective-permute-done | bytes 49184 | tf_op jit(solution)/shard_map/ppermute | solution.py:367
  168.9 1.4 collective-permute-done.35.refs_2_
  170.3 2.2 %collective-permute-start.37 = (bf16[8,64,1024]{2,1,0:T(8,128)(2,1)}, bf16[8,64,1024]{2,1,0:T(8,128)(2,1)}, u32[]{:S(2)}, u32[]{:S(2)}) collective-permute-start(bf16[8,64,1024]{2,1,0:T(8,128)(2,1)} %get-tuple-element.147), channel_id=1, source_target_pairs={{0,16},{4,0},{8,24},{12,8},{16,20},{20,4},{24,28},{28,12},{1,17},{... | collective-permute-start | bytes 3145736 | tf_op jit(solution)/shard_map/ppermute | solution.py:493
  173.1 2.8 %shard_map.93 = bf16[256,512]{1,0:T(8,128)(2,1)} custom-call(f32[256,512]{1,0:T(8,128)} %get-tuple-element.103.refs_0_, f32[256,512]{1,0:T(8,128)} %copy-done.8, f32[256,512]{1,0:T(8,128)} %copy-done.9, f32[256,512]{1,0:T(8,128)} %copy-done.10, bf16[384,256]{1,0:T(8,128)(2,1)} %get-tuple-element.107.refs_4_, bf16[96,512]{1,0:T(8,128)(2,1)} %get-tuple-element.120.refs_5_, ...), custom_call_target="tpu_custom_call" | custom-call | flops 1 | bytes 1 | tf_op jit(solution)/shard_map/pallas_call | solution.py:154
  175.9 3.9 %shard_map.95 = f32[8,64,512]{2,1,0:T(8,128)} custom-call(bf16[4,96,64]{2,1,0:T(8,128)(2,1)} %get-tuple-element.150.refs_0_, bf16[4,96,64]{2,1,0:T(8,128)(2,1)} %copy-done.20, bf16[4,96,64]{2,1,0:T(8,128)(2,1)} %copy-done.21, bf16[4,96,64]{2,1,0:T(8,128)(2,1)} %copy-done.22, bf16[4,96,512]{2,1,0:T(8,128)(2,1)} %copy-done.4, bf16[4,96,512]{2,1,0:T(8,128)(2,1)} %copy-done.16, ...), custom_call_target="tpu_custom_call" | custom-call | flops 1 | bytes 1 | tf_op jit(solution)/shard_map/pallas_call | solution.py:154
  179.8 1.0 broadcast_in_dim.3
  181.3 13.5 %collective-permute-done.37 = bf16[8,64,1024]{2,1,0:T(8,128)(2,1)} collective-permute-done((bf16[8,64,1024]{2,1,0:T(8,128)(2,1)}, bf16[8,64,1024]{2,1,0:T(8,128)(2,1)}, u32[]{:S(2)}, u32[]{:S(2)}) %collective-permute-start.37) | collective-permute-done | bytes 1048608 | tf_op jit(solution)/shard_map/ppermute | solution.py:493
  194.8 1.5 convert_dynamic-update-slice_fusion.1
  196.2 1.4 collective-permute-done.38
  197.9 3.4 %copy-done = f32[8,64,4096]{2,1,0:T(8,128)} copy-done((f32[8,64,4096]{2,1,0:T(8,128)}, f32[8,64,4096]{2,1,0:T(8,128)S(1)}, u32[]{:S(2)}) %copy-start) | copy-done | bytes 8388632
  (111 shorter events, 8.0 us)
Async XLA Ops:
  4.0 16.5 %collective-permute-start = (bf16[272,1024]{1,0:T(8,128)(2,1)S(1)}, bf16[272,1024]{1,0:T(8,128)(2,1)S(1)}, u32[]{:S(2)}, u32[]{:S(2)}) collective-permute-start(bf16[272,1024]{1,0:T(8,128)(2,1)S(1)} %get-tuple-element.78), channel_id=1, source_target_pairs={{0,8},{8,0},{16,24},{24,16},{1,9},{9,1},{17,25},{25,17},{2,10},{10... | collective-permute-start | bytes 1671176 | tf_op jit(solution)/shard_map/ppermute | solution.py:367
  7.0 27.7 %collective-permute-start.1 = (bf16[272,1024]{1,0:T(8,128)(2,1)S(1)}, bf16[272,1024]{1,0:T(8,128)(2,1)S(1)}, u32[]{:S(2)}, u32[]{:S(2)}) collective-permute-start(bf16[272,1024]{1,0:T(8,128)(2,1)S(1)} %get-tuple-element.79), channel_id=1, source_target_pairs={{0,16},{8,24},{16,0},{24,8},{1,17},{9,25},{17,1},{25,9},{2,18},{10... | collective-permute-start | bytes 1671176 | tf_op jit(solution)/shard_map/ppermute | solution.py:367
  8.5 26.2 %collective-permute-start.2 = (bf16[272,1024]{1,0:T(8,128)(2,1)S(1)}, bf16[272,1024]{1,0:T(8,128)(2,1)S(1)}, u32[]{:S(2)}, u32[]{:S(2)}) collective-permute-start(bf16[272,1024]{1,0:T(8,128)(2,1)S(1)} %get-tuple-element.80), channel_id=1, source_target_pairs={{0,24},{8,16},{16,8},{24,0},{1,25},{9,17},{17,9},{25,1},{2,26},{10... | collective-permute-start | bytes 1671176 | tf_op jit(solution)/shard_map/ppermute | solution.py:367
  11.3 20.2 %collective-permute-start.3 = (bf16[96,1536]{1,0:T(8,128)(2,1)}, bf16[96,1536]{1,0:T(8,128)(2,1)}, u32[]{:S(2)}, u32[]{:S(2)}) collective-permute-start(bf16[96,1536]{1,0:T(8,128)(2,1)} %get-tuple-element.82), channel_id=1, source_target_pairs={{0,1},{1,2},{2,3},{3,0},{4,5},{5,6},{6,7},{7,4},{8,9},{9,10},{10,1... | collective-permute-start | bytes 884744 | tf_op jit(solution)/shard_map/ppermute | solution.py:370
  13.4 21.3 %collective-permute-start.4 = (bf16[96,1536]{1,0:T(8,128)(2,1)}, bf16[96,1536]{1,0:T(8,128)(2,1)}, u32[]{:S(2)}, u32[]{:S(2)}) collective-permute-start(bf16[96,1536]{1,0:T(8,128)(2,1)} %get-tuple-element.83), channel_id=1, source_target_pairs={{0,2},{1,3},{2,0},{3,1},{4,6},{5,7},{6,4},{7,5},{8,10},{9,11},{10,... | collective-permute-start | bytes 884744 | tf_op jit(solution)/shard_map/ppermute | solution.py:370
  20.5 14.8 %copy-start.1 = (bf16[272,1024]{1,0:T(8,128)(2,1)}, bf16[272,1024]{1,0:T(8,128)(2,1)S(1)}, u32[]{:S(2)}) copy-start(bf16[272,1024]{1,0:T(8,128)(2,1)S(1)} %collective-permute-done.refs_1_.refs_2_) | copy-start | bytes 1671172
  20.5 14.8 %collective-permute-start.5 = (bf16[96,1536]{1,0:T(8,128)(2,1)}, bf16[96,1536]{1,0:T(8,128)(2,1)S(1)}, u32[]{:S(2)}, u32[]{:S(2)}) collective-permute-start(bf16[96,1536]{1,0:T(8,128)(2,1)} %get-tuple-element.85), channel_id=1, source_target_pairs={{0,3},{1,0},{2,1},{3,2},{4,7},{5,4},{6,5},{7,6},{8,11},{9,8},{10,9... | collective-permute-start | bytes 884744 | tf_op jit(solution)/shard_map/ppermute | solution.py:370
  34.7 13.7 %copy-start.2 = (bf16[272,1024]{1,0:T(8,128)(2,1)}, bf16[272,1024]{1,0:T(8,128)(2,1)S(1)}, u32[]{:S(2)}) copy-start(bf16[272,1024]{1,0:T(8,128)(2,1)S(1)} %collective-permute-done.1.refs_2_.refs_3_) | copy-start | bytes 1671172
  34.7 13.7 %copy-start.3 = (bf16[272,1024]{1,0:T(8,128)(2,1)}, bf16[272,1024]{1,0:T(8,128)(2,1)S(1)}, u32[]{:S(2)}) copy-start(bf16[272,1024]{1,0:T(8,128)(2,1)S(1)} %collective-permute-done.2.refs_3_.refs_4_) | copy-start | bytes 1671172
  35.3 36.6 %copy-start.24 = (bf16[96,1536]{1,0:T(8,128)(2,1)}, bf16[96,1536]{1,0:T(8,128)(2,1)S(1)}, u32[]{:S(2)}) copy-start(bf16[96,1536]{1,0:T(8,128)(2,1)S(1)} %collective-permute-done.5.refs_2_.refs_4_) | copy-start | bytes 884740
  35.3 2.0 collective-permute-start.6
  35.3 2.7 %collective-permute-start.7 = (bf16[272,1024]{1,0:T(8,128)(2,1)S(1)}, bf16[272,1024]{1,0:T(8,128)(2,1)S(1)}, u32[]{:S(2)}, u32[]{:S(2)}) collective-permute-start(bf16[272,1024]{1,0:T(8,128)(2,1)S(1)} %collective-permute-done.1.refs_2_.refs_3_), channel_id=1, source_target_pairs={{0,4},{4,0},{1,5},{5,1},{2,6},{6,2},{3,7},{7,3},{8,12},{12,8},{9,1... | collective-permute-start | bytes 1671176 | tf_op jit(solution)/shard_map/ppermute | solution.py:373
  35.8 3.0 %collective-permute-start.8 = (bf16[272,1024]{1,0:T(8,128)(2,1)S(1)}, bf16[272,1024]{1,0:T(8,128)(2,1)S(1)}, u32[]{:S(2)}, u32[]{:S(2)}) collective-permute-start(bf16[272,1024]{1,0:T(8,128)(2,1)S(1)} %collective-permute-done.2.refs_3_.refs_4_), channel_id=1, source_target_pairs={{0,4},{4,0},{1,5},{5,1},{2,6},{6,2},{3,7},{7,3},{8,12},{12,8},{9,1... | collective-permute-start | bytes 1671176 | tf_op jit(solution)/shard_map/ppermute | solution.py:373
  37.3 28.2 %copy-start.5 = (bf16[272,1024]{1,0:T(8,128)(2,1)}, bf16[272,1024]{1,0:T(8,128)(2,1)S(1)}, u32[]{:S(2)}) copy-start(bf16[272,1024]{1,0:T(8,128)(2,1)S(1)} %collective-permute-done.6.refs_5_) | copy-start | bytes 1671172
  38.1 27.4 %copy-start.6 = (bf16[272,1024]{1,0:T(8,128)(2,1)}, bf16[272,1024]{1,0:T(8,128)(2,1)S(1)}, u32[]{:S(2)}) copy-start(bf16[272,1024]{1,0:T(8,128)(2,1)S(1)} %collective-permute-done.7.refs_6_) | copy-start | bytes 1671172
  38.9 26.6 %copy-start.7 = (bf16[272,1024]{1,0:T(8,128)(2,1)}, bf16[272,1024]{1,0:T(8,128)(2,1)S(1)}, u32[]{:S(2)}) copy-start(bf16[272,1024]{1,0:T(8,128)(2,1)S(1)} %collective-permute-done.8.refs_7_) | copy-start | bytes 1671172
  38.9 36.6 %collective-permute-start.16 = (bf16[8,256,1024]{2,1,0:T(8,128)(2,1)}, bf16[8,256,1024]{2,1,0:T(8,128)(2,1)}, u32[]{:S(2)}, u32[]{:S(2)}) collective-permute-start(bf16[8,256,1024]{2,1,0:T(8,128)(2,1)} %constant_dynamic-slice_fusion.1), channel_id=1, source_target_pairs={{0,4},{8,12},{20,16},{28,24},{1,5},{9,13},{21,17},{29,25},{2,6},{1... | collective-permute-start | bytes 12582920 | tf_op jit(solution)/shard_map/ppermute | solution.py:408
  44.8 30.6 %copy-start.4 = (bf16[4,96,512]{2,1,0:T(8,128)(2,1)}, bf16[4,96,512]{2,1,0:T(8,128)(2,1)S(1)}, u32[]{:S(2)}) copy-start(bf16[4,96,512]{2,1,0:T(8,128)(2,1)S(1)} %pad_maximum_fusion.refs_0_.refs_4_) | copy-start | bytes 1179652
  44.8 13.0 %collective-permute-start.11 = (bf16[4,96,512]{2,1,0:T(8,128)(2,1)S(1)}, bf16[4,96,512]{2,1,0:T(8,128)(2,1)S(1)}, u32[]{:S(2)}, u32[]{:S(2)}) collective-permute-start(bf16[4,96,512]{2,1,0:T(8,128)(2,1)S(1)} %pad_maximum_fusion.refs_0_.refs_4_), channel_id=1, source_target_pairs={{0,24},{8,16},{16,8},{24,0},{1,25},{9,17},{17,9},{25,1},{2,26},{10... | collective-permute-start | bytes 1179656 | tf_op jit(solution)/shard_map/ppermute | solution.py:367
  44.9 20.5 %collective-permute-start.10 = (bf16[4,96,512]{2,1,0:T(8,128)(2,1)S(1)}, bf16[4,96,512]{2,1,0:T(8,128)(2,1)S(1)}, u32[]{:S(2)}, u32[]{:S(2)}) collective-permute-start(bf16[4,96,512]{2,1,0:T(8,128)(2,1)S(1)} %pad_maximum_fusion.refs_0_.refs_4_), channel_id=1, source_target_pairs={{0,16},{8,24},{16,0},{24,8},{1,17},{9,25},{17,1},{25,9},{2,18},{10... | collective-permute-start | bytes 1179656 | tf_op jit(solution)/shard_map/ppermute | solution.py:367
  47.9 17.5 %collective-permute-start.9 = (bf16[4,96,512]{2,1,0:T(8,128)(2,1)S(1)}, bf16[4,96,512]{2,1,0:T(8,128)(2,1)S(1)}, u32[]{:S(2)}, u32[]{:S(2)}) collective-permute-start(bf16[4,96,512]{2,1,0:T(8,128)(2,1)S(1)} %pad_maximum_fusion.refs_0_.refs_4_), channel_id=1, source_target_pairs={{0,8},{8,0},{16,24},{24,16},{1,9},{9,1},{17,25},{25,17},{2,10},{10... | collective-permute-start | bytes 1179656 | tf_op jit(solution)/shard_map/ppermute | solution.py:367
  52.4 36.3 %collective-permute-start.15 = (bf16[3,96,1024]{2,1,0:T(8,128)(2,1)}, bf16[3,96,1024]{2,1,0:T(8,128)(2,1)S(1)}, u32[]{:S(2)}, u32[]{:S(2)}) collective-permute-start(bf16[3,96,1024]{2,1,0:T(8,128)(2,1)} %get-tuple-element.94), channel_id=1, source_target_pairs={{0,2},{1,3},{2,0},{3,1},{4,6},{5,7},{6,4},{7,5},{8,10},{9,11},{10,... | collective-permute-start | bytes 1769480 | tf_op jit(solution)/shard_map/ppermute | solution.py:370
  57.8 21.0 %copy-start.14 = (bf16[4,96,512]{2,1,0:T(8,128)(2,1)}, bf16[4,96,512]{2,1,0:T(8,128)(2,1)S(1)}, u32[]{:S(2)}) copy-start(bf16[4,96,512]{2,1,0:T(8,128)(2,1)S(1)} %collective-permute-done.11.refs_7_) | copy-start | bytes 1179652
  65.4 13.4 %copy-start.15 = (bf16[4,96,512]{2,1,0:T(8,128)(2,1)}, bf16[4,96,512]{2,1,0:T(8,128)(2,1)S(1)}, u32[]{:S(2)}) copy-start(bf16[4,96,512]{2,1,0:T(8,128)(2,1)S(1)} %collective-permute-done.10.refs_6_) | copy-start | bytes 1179652
  65.4 7.8 %copy-start.16 = (bf16[4,96,512]{2,1,0:T(8,128)(2,1)}, bf16[4,96,512]{2,1,0:T(8,128)(2,1)S(1)}, u32[]{:S(2)}) copy-start(bf16[4,96,512]{2,1,0:T(8,128)(2,1)S(1)} %collective-permute-done.9.refs_5_) | copy-start | bytes 1179652
  71.9 19.1 %collective-permute-start.12 = (f32[256,512]{1,0:T(8,128)}, f32[256,512]{1,0:T(8,128)S(1)}, u32[]{:S(2)}, u32[]{:S(2)}) collective-permute-start(f32[256,512]{1,0:T(8,128)} %get-tuple-element.104), channel_id=1, source_target_pairs={{0,8},{8,0},{16,24},{24,16},{1,9},{9,1},{17,25},{25,17},{2,10},{10... | collective-permute-start | bytes 1572872 | tf_op jit(solution)/shard_map/ppermute | solution.py:367
  72.5 18.5 %collective-permute-start.13 = (f32[256,512]{1,0:T(8,128)}, f32[256,512]{1,0:T(8,128)S(1)}, u32[]{:S(2)}, u32[]{:S(2)}) collective-permute-start(f32[256,512]{1,0:T(8,128)} %get-tuple-element.105), channel_id=1, source_target_pairs={{0,16},{8,24},{16,0},{24,8},{1,17},{9,25},{17,1},{25,9},{2,18},{10... | collective-permute-start | bytes 1572872 | tf_op jit(solution)/shard_map/ppermute | solution.py:367
  73.3 24.4 %collective-permute-start.14 = (f32[256,512]{1,0:T(8,128)}, f32[256,512]{1,0:T(8,128)S(1)}, u32[]{:S(2)}, u32[]{:S(2)}) collective-permute-start(f32[256,512]{1,0:T(8,128)} %get-tuple-element.106), channel_id=1, source_target_pairs={{0,24},{8,16},{16,8},{24,0},{1,25},{9,17},{17,9},{25,1},{2,26},{10... | collective-permute-start | bytes 1572872 | tf_op jit(solution)/shard_map/ppermute | solution.py:367
  75.4 13.3 %copy-start.26 = (bf16[3,96,1024]{2,1,0:T(8,128)(2,1)S(1)}, bf16[3,96,1024]{2,1,0:T(8,128)(2,1)}, u32[]{:S(2)}) copy-start(bf16[3,96,1024]{2,1,0:T(8,128)(2,1)} %get-tuple-element.95) | copy-start | bytes 1769476
  78.8 2.0 collective-permute-start.17
  80.8 27.5 %collective-permute-start.19 = (bf16[3,96,1024]{2,1,0:T(8,128)(2,1)}, bf16[3,96,1024]{2,1,0:T(8,128)(2,1)S(1)}, u32[]{:S(2)}, u32[]{:S(2)}) collective-permute-start(bf16[3,96,1024]{2,1,0:T(8,128)(2,1)} %get-tuple-element.93), channel_id=1, source_target_pairs={{0,1},{1,2},{2,3},{3,0},{4,5},{5,6},{6,7},{7,4},{8,9},{9,10},{10,1... | collective-permute-start | bytes 1769480 | tf_op jit(solution)/shard_map/ppermute | solution.py:370
  88.7 12.4 %copy-start.25 = (bf16[3,96,1024]{2,1,0:T(8,128)(2,1)}, bf16[3,96,1024]{2,1,0:T(8,128)(2,1)S(1)}, u32[]{:S(2)}) copy-start(bf16[3,96,1024]{2,1,0:T(8,128)(2,1)S(1)} %collective-permute-done.15.refs_4_.refs_7_) | copy-start | bytes 1769476
  88.8 25.8 %collective-permute-start.20 = (bf16[3,96,1024]{2,1,0:T(8,128)(2,1)S(1)}, bf16[3,96,1024]{2,1,0:T(8,128)(2,1)S(1)}, u32[]{:S(2)}, u32[]{:S(2)}) collective-permute-start(bf16[3,96,1024]{2,1,0:T(8,128)(2,1)S(1)} %copy-done.26), channel_id=1, source_target_pairs={{0,3},{1,0},{2,1},{3,2},{4,7},{5,4},{6,5},{7,6},{8,11},{9,8},{10,9... | collective-permute-start | bytes 1769480 | tf_op jit(solution)/shard_map/ppermute | solution.py:370
  91.0 17.4 %copy-start.8 = (f32[256,512]{1,0:T(8,128)}, f32[256,512]{1,0:T(8,128)S(1)}, u32[]{:S(2)}) copy-start(f32[256,512]{1,0:T(8,128)S(1)} %collective-permute-done.12.refs_1_) | copy-start | bytes 1572868
  91.0 17.4 %copy-start.9 = (f32[256,512]{1,0:T(8,128)}, f32[256,512]{1,0:T(8,128)S(1)}, u32[]{:S(2)}) copy-start(f32[256,512]{1,0:T(8,128)S(1)} %collective-permute-done.13.refs_2_) | copy-start | bytes 1572868
  97.6 10.7 %copy-start.10 = (f32[256,512]{1,0:T(8,128)}, f32[256,512]{1,0:T(8,128)S(1)}, u32[]{:S(2)}) copy-start(f32[256,512]{1,0:T(8,128)S(1)} %collective-permute-done.14.refs_3_) | copy-start | bytes 1572868
  97.6 16.9 %collective-permute-start.23 = (bf16[4,96,256]{2,1,0:T(8,128)(2,1)}, bf16[4,96,256]{2,1,0:T(8,128)(2,1)S(1)}, u32[]{:S(2)}, u32[]{:S(2)}) collective-permute-start(bf16[4,96,256]{2,1,0:T(8,128)(2,1)} %shard_map.89.refs_9_), channel_id=1, source_target_pairs={{0,24},{8,16},{16,8},{24,0},{1,25},{9,17},{17,9},{25,1},{2,26},{10... | collective-permute-start | bytes 589832 | tf_op jit(solution)/shard_map/ppermute | solution.py:367
  99.4 15.2 %collective-permute-start.22 = (bf16[4,96,256]{2,1,0:T(8,128)(2,1)}, bf16[4,96,256]{2,1,0:T(8,128)(2,1)S(1)}, u32[]{:S(2)}, u32[]{:S(2)}) collective-permute-start(bf16[4,96,256]{2,1,0:T(8,128)(2,1)} %shard_map.89.refs_9_), channel_id=1, source_target_pairs={{0,16},{8,24},{16,0},{24,8},{1,17},{9,25},{17,1},{25,9},{2,18},{10... | collective-permute-start | bytes 589832 | tf_op jit(solution)/shard_map/ppermute | solution.py:367
  100.7 13.9 %collective-permute-start.21 = (bf16[4,96,256]{2,1,0:T(8,128)(2,1)}, bf16[4,96,256]{2,1,0:T(8,128)(2,1)S(1)}, u32[]{:S(2)}, u32[]{:S(2)}) collective-permute-start(bf16[4,96,256]{2,1,0:T(8,128)(2,1)} %shard_map.89.refs_9_), channel_id=1, source_target_pairs={{0,8},{8,0},{16,24},{24,16},{1,9},{9,1},{17,25},{25,17},{2,10},{10... | collective-permute-start | bytes 589832 | tf_op jit(solution)/shard_map/ppermute | solution.py:367
  108.4 6.3 %copy-start.27 = (bf16[3,96,1024]{2,1,0:T(8,128)(2,1)}, bf16[3,96,1024]{2,1,0:T(8,128)(2,1)S(1)}, u32[]{:S(2)}) copy-start(bf16[3,96,1024]{2,1,0:T(8,128)(2,1)S(1)} %collective-permute-done.19.refs_3_.refs_6_) | copy-start | bytes 1769476
  108.4 15.1 %collective-permute-start.18 = (f32[4,2,96,128]{3,2,1,0:T(8,128)}, f32[4,2,96,128]{3,2,1,0:T(8,128)S(1)}, u32[]{:S(2)}, u32[]{:S(2)}) collective-permute-start(f32[4,2,96,128]{3,2,1,0:T(8,128)} %get-tuple-element.115), channel_id=1, source_target_pairs={{0,4},{4,0},{1,5},{5,1},{2,6},{6,2},{3,7},{7,3},{8,12},{12,8},{9,1... | collective-permute-start | bytes 1179656 | tf_op jit(solution)/shard_map/ppermute | solution.py:373
  114.6 8.1 %copy-start.29 = (bf16[4,96,256]{2,1,0:T(8,128)(2,1)}, bf16[4,96,256]{2,1,0:T(8,128)(2,1)S(1)}, u32[]{:S(2)}) copy-start(bf16[4,96,256]{2,1,0:T(8,128)(2,1)S(1)} %collective-permute-done.23.refs_12_) | copy-start | bytes 589828
  114.6 8.1 %copy-start.30 = (bf16[4,96,256]{2,1,0:T(8,128)(2,1)}, bf16[4,96,256]{2,1,0:T(8,128)(2,1)S(1)}, u32[]{:S(2)}) copy-start(bf16[4,96,256]{2,1,0:T(8,128)(2,1)S(1)} %collective-permute-done.22.refs_11_) | copy-start | bytes 589828
  114.6 8.1 %copy-start.31 = (bf16[4,96,256]{2,1,0:T(8,128)(2,1)}, bf16[4,96,256]{2,1,0:T(8,128)(2,1)S(1)}, u32[]{:S(2)}) copy-start(bf16[4,96,256]{2,1,0:T(8,128)(2,1)S(1)} %collective-permute-done.21.refs_10_) | copy-start | bytes 589828
  115.4 8.1 %copy-start.12 = (f32[4,2,96,128]{3,2,1,0:T(8,128)S(1)}, f32[4,2,96,128]{3,2,1,0:T(8,128)}, u32[]{:S(2)}) copy-start(f32[4,2,96,128]{3,2,1,0:T(8,128)} %get-tuple-element.114) | copy-start | bytes 1179652
  122.7 2.0 collective-permute-start.24
  125.8 12.4 %collective-permute-start.25 = (f32[4,96,128]{2,1,0:T(8,128)S(1)}, f32[4,96,128]{2,1,0:T(8,128)S(1)}, u32[]{:S(2)}, u32[]{:S(2)}) collective-permute-start(f32[4,96,128]{2,1,0:T(8,128)S(1)} %get-tuple-element.155), channel_id=1, source_target_pairs={{0,8},{8,0},{16,24},{24,16},{1,9},{9,1},{17,25},{25,17},{2,10},{10... | collective-permute-start | bytes 589832 | tf_op jit(solution)/shard_map/ppermute | solution.py:367
  126.4 11.8 %collective-permute-start.27 = (f32[4,96,128]{2,1,0:T(8,128)S(1)}, f32[4,96,128]{2,1,0:T(8,128)S(1)}, u32[]{:S(2)}, u32[]{:S(2)}) collective-permute-start(f32[4,96,128]{2,1,0:T(8,128)S(1)} %get-tuple-element.156), channel_id=1, source_target_pairs={{0,24},{8,16},{16,8},{24,0},{1,25},{9,17},{17,9},{25,1},{2,26},{10... | collective-permute-start | bytes 589832 | tf_op jit(solution)/shard_map/ppermute | solution.py:367
  128.2 10.6 %collective-permute-start.26 = (f32[4,96,128]{2,1,0:T(8,128)S(1)}, f32[4,96,128]{2,1,0:T(8,128)S(1)}, u32[]{:S(2)}, u32[]{:S(2)}) collective-permute-start(f32[4,96,128]{2,1,0:T(8,128)S(1)} %get-tuple-element.157), channel_id=1, source_target_pairs={{0,16},{8,24},{16,0},{24,8},{1,17},{9,25},{17,1},{25,9},{2,18},{10... | collective-permute-start | bytes 589832 | tf_op jit(solution)/shard_map/ppermute | solution.py:367
  138.8 31.5 %collective-permute-start.32 = (bf16[8,64,1024]{2,1,0:T(8,128)(2,1)}, bf16[8,64,1024]{2,1,0:T(8,128)(2,1)S(1)}, u32[]{:S(2)}, u32[]{:S(2)}) collective-permute-start(bf16[8,64,1024]{2,1,0:T(8,128)(2,1)} %get-tuple-element.140), channel_id=1, source_target_pairs={{0,0},{4,16},{8,8},{12,24},{16,4},{20,20},{24,12},{28,28},{1,1},{5... | collective-permute-start | bytes 3145736 | tf_op jit(solution)/shard_map/ppermute | solution.py:493
  140.7 29.6 %collective-permute-start.33 = (bf16[8,64,1024]{2,1,0:T(8,128)(2,1)}, bf16[8,64,1024]{2,1,0:T(8,128)(2,1)S(1)}, u32[]{:S(2)}, u32[]{:S(2)}) collective-permute-start(bf16[8,64,1024]{2,1,0:T(8,128)(2,1)} %get-tuple-element.142), channel_id=1, source_target_pairs={{0,8},{4,24},{8,0},{12,16},{16,12},{20,28},{24,4},{28,20},{1,9},{5... | collective-permute-start | bytes 3145736 | tf_op jit(solution)/shard_map/ppermute | solution.py:493
  141.3 1.9 collective-permute-start.28
  148.0 6.0 %collective-permute-start.29 = (bf16[96,512]{1,0:T(8,128)(2,1)}, bf16[96,512]{1,0:T(8,128)(2,1)S(1)}, u32[]{:S(2)}, u32[]{:S(2)}) collective-permute-start(bf16[96,512]{1,0:T(8,128)(2,1)} %get-tuple-element.121), channel_id=1, source_target_pairs={{0,3},{1,0},{2,1},{3,2},{4,7},{5,4},{6,5},{7,6},{8,11},{9,8},{10,9... | collective-permute-start | bytes 294920 | tf_op jit(solution)/shard_map/ppermute | solution.py:370
  150.4 9.8 %collective-permute-start.30 = (bf16[96,512]{1,0:T(8,128)(2,1)}, bf16[96,512]{1,0:T(8,128)(2,1)S(1)}, u32[]{:S(2)}, u32[]{:S(2)}) collective-permute-start(bf16[96,512]{1,0:T(8,128)(2,1)} %get-tuple-element.122), channel_id=1, source_target_pairs={{0,2},{1,3},{2,0},{3,1},{4,6},{5,7},{6,4},{7,5},{8,10},{9,11},{10,... | collective-permute-start | bytes 294920 | tf_op jit(solution)/shard_map/ppermute | solution.py:370
  150.7 9.6 %collective-permute-start.31 = (bf16[96,512]{1,0:T(8,128)(2,1)}, bf16[96,512]{1,0:T(8,128)(2,1)S(1)}, u32[]{:S(2)}, u32[]{:S(2)}) collective-permute-start(bf16[96,512]{1,0:T(8,128)(2,1)} %get-tuple-element.123), channel_id=1, source_target_pairs={{0,1},{1,2},{2,3},{3,0},{4,5},{5,6},{6,7},{7,4},{8,9},{9,10},{10,1... | collective-permute-start | bytes 294920 | tf_op jit(solution)/shard_map/ppermute | solution.py:370
  153.9 19.1 %copy-start.17 = (bf16[96,512]{1,0:T(8,128)(2,1)}, bf16[96,512]{1,0:T(8,128)(2,1)S(1)}, u32[]{:S(2)}) copy-start(bf16[96,512]{1,0:T(8,128)(2,1)S(1)} %collective-permute-done.29.refs_6_) | copy-start | bytes 294916
  160.3 12.8 %copy-start.18 = (bf16[96,512]{1,0:T(8,128)(2,1)}, bf16[96,512]{1,0:T(8,128)(2,1)S(1)}, u32[]{:S(2)}) copy-start(bf16[96,512]{1,0:T(8,128)(2,1)S(1)} %collective-permute-done.30.refs_7_) | copy-start | bytes 294916
  160.3 12.8 %copy-start.19 = (bf16[96,512]{1,0:T(8,128)(2,1)}, bf16[96,512]{1,0:T(8,128)(2,1)S(1)}, u32[]{:S(2)}) copy-start(bf16[96,512]{1,0:T(8,128)(2,1)S(1)} %collective-permute-done.31.refs_8_) | copy-start | bytes 294916
  160.3 8.6 %collective-permute-start.34 = (bf16[4,96,64]{2,1,0:T(8,128)(2,1)}, bf16[4,96,64]{2,1,0:T(8,128)(2,1)S(1)}, u32[]{:S(2)}, u32[]{:S(2)}) collective-permute-start(bf16[4,96,64]{2,1,0:T(8,128)(2,1)} %get-tuple-element.144), channel_id=1, source_target_pairs={{0,8},{8,0},{16,24},{24,16},{1,9},{9,1},{17,25},{25,17},{2,10},{10... | collective-permute-start | bytes 147464 | tf_op jit(solution)/shard_map/ppermute | solution.py:367
  161.7 8.6 %collective-permute-start.35 = (bf16[4,96,64]{2,1,0:T(8,128)(2,1)}, bf16[4,96,64]{2,1,0:T(8,128)(2,1)S(1)}, u32[]{:S(2)}, u32[]{:S(2)}) collective-permute-start(bf16[4,96,64]{2,1,0:T(8,128)(2,1)} %get-tuple-element.145), channel_id=1, source_target_pairs={{0,16},{8,24},{16,0},{24,8},{1,17},{9,25},{17,1},{25,9},{2,18},{10... | collective-permute-start | bytes 147464 | tf_op jit(solution)/shard_map/ppermute | solution.py:367
  163.4 6.9 %collective-permute-start.36 = (bf16[4,96,64]{2,1,0:T(8,128)(2,1)}, bf16[4,96,64]{2,1,0:T(8,128)(2,1)S(1)}, u32[]{:S(2)}, u32[]{:S(2)}) collective-permute-start(bf16[4,96,64]{2,1,0:T(8,128)(2,1)} %get-tuple-element.146), channel_id=1, source_target_pairs={{0,24},{8,16},{16,8},{24,0},{1,25},{9,17},{17,9},{25,1},{2,26},{10... | collective-permute-start | bytes 147464 | tf_op jit(solution)/shard_map/ppermute | solution.py:367
  168.9 7.0 %copy-start.20 = (bf16[4,96,64]{2,1,0:T(8,128)(2,1)}, bf16[4,96,64]{2,1,0:T(8,128)(2,1)S(1)}, u32[]{:S(2)}) copy-start(bf16[4,96,64]{2,1,0:T(8,128)(2,1)S(1)} %collective-permute-done.34.refs_1_) | copy-start | bytes 147460
  170.3 24.4 %collective-permute-start.37 = (bf16[8,64,1024]{2,1,0:T(8,128)(2,1)}, bf16[8,64,1024]{2,1,0:T(8,128)(2,1)}, u32[]{:S(2)}, u32[]{:S(2)}) collective-permute-start(bf16[8,64,1024]{2,1,0:T(8,128)(2,1)} %get-tuple-element.147), channel_id=1, source_target_pairs={{0,16},{4,0},{8,24},{12,8},{16,20},{20,4},{24,28},{28,12},{1,17},{... | collective-permute-start | bytes 3145736 | tf_op jit(solution)/shard_map/ppermute | solution.py:493
  172.5 25.1 %collective-permute-start.38 = (bf16[8,64,1024]{2,1,0:T(8,128)(2,1)}, bf16[8,64,1024]{2,1,0:T(8,128)(2,1)S(1)}, u32[]{:S(2)}, u32[]{:S(2)}) collective-permute-start(bf16[8,64,1024]{2,1,0:T(8,128)(2,1)} %get-tuple-element.149), channel_id=1, source_target_pairs={{0,24},{4,8},{8,16},{12,0},{16,28},{20,12},{24,20},{28,4},{1,25},{... | collective-permute-start | bytes 3145736 | tf_op jit(solution)/shard_map/ppermute | solution.py:493
  (7 other events, 17.1 us)

commit v10 on v8

--- a/solution.py
+++ b/solution.py
@@ -471,8 +471,19 @@
         flops=10**10,
     )
     hid = [over_f(hid[k], k) for k in range(fsdp)]
-    sums = [sums[0], sums[1], *after(sums[2:], *hid[1:])]
+    hid_own = (hid[0] + hid[1] + hid[2] + hid[3]).astype(BF16)
+    shift_order = [(early + late).index(ka) for ka in range(ad)]
+    hid_own = jnp.concatenate([hid_own[i : i + 1] for i in shift_order], axis=0)
+    outs = call(
+        functools.partial(delta_kernel, fsdp, ad, gslots),
+        [((slots, vloc), BF16)] * ad + [((ad, slots, rloc), BF16)] * fsdp,
+        [(v, None) for v in (hid_own, swap(hid_own), adapter_up_weight)],
+        at=numbers(t, *[f ^ k for k in range(fsdp)]),
+    )
+    returned = [over_a(v, (ad - ka) % ad) for ka, v in enumerate(outs[:ad])]
     grad_a = jnp.zeros((dloc, rloc, half), F32)
+    hid_cols, grad_a = after((outs[ad:], grad_a), *returned[1:])
+    hid_cols = [over_f(v, k) for k, v in enumerate(hid_cols)]
     got = []
     for r in range(fsdp):
         p, q = r % 2, r // 2
@@ -482,21 +493,10 @@
             for x in range(2)
             for s in range(2)
         ]
-        got.append(lax.ppermute(sums[r], ("fsdp", "tp"), perm))
+        block = after(sums[r], *(hid[1:] if r < 2 else [*got[:2], *returned[1:]]))
+        got.append(lax.ppermute(block, ("fsdp", "tp"), perm))
         at = (fx ^ p) * kf_width + (fy ^ q) * kt
         grad_a = lax.dynamic_update_slice_in_dim(grad_a, got[r].astype(F32), at, 2)
-
-    hid_own = (hid[0] + hid[1] + hid[2] + hid[3]).astype(BF16)
-    shift_order = [(early + late).index(ka) for ka in range(ad)]
-    hid_own = jnp.concatenate([hid_own[i : i + 1] for i in shift_order], axis=0)
-    outs = call(
-        functools.partial(delta_kernel, fsdp, ad, gslots),
-        [((slots, vloc), BF16)] * ad + [((ad, slots, rloc), BF16)] * fsdp,
-        [(v, None) for v in (hid_own, swap(hid_own), adapter_up_weight)],
-        at=numbers(t, *[f ^ k for k in range(fsdp)]),
-    )
-    returned = [over_a(v, (ad - ka) % ad) for ka, v in enumerate(outs[:ad])]
-    hid_cols = [over_f(after(v, got[2], *returned[1:]), k) for k, v in enumerate(outs[ad:])]
 
     (y_out,) = call(
         functools.partial(output_kernel, fsdp, ad),

time: 197 us -> 200 us (1.015)
  waiting for transfers between devices: 55.7 us -> 69.2 us
  other arithmetic: 10.7 us -> 5.4 us
  starting transfers between devices: 53.5 us -> 50.7 us
  local copies, waits for them, and re-layouts: 22.4 us -> 20.4 us
    ppermute x15, waiting for transfers between devices: 6.68 us -> 29.9 us  [over_f(): lax.ppermute(v, 'fsdp', [(i, i ^ k) for i in range(fsdp)])]
    ppermute x4, waiting for transfers between devices: 8.7 us -> 3.2 us  [column_body(): got.append(lax.ppermute(block, ('fsdp', 'tp'), perm))]
    dynamic_update_slice x4, other arithmetic: 7.49 us -> 2.2 us  [column_body(): grad_a = lax.dynamic_update_slice_in_dim(grad_a, got[r].astype(F32), at, 2)]
    ppermute x9, waiting for transfers between devices: 37.5 us -> 33.2 us  [over_a(): lax.ppermute(v, 'ad', [(i, (i + k) % ad) for i in range(ad)])]
    ppermute x15, starting transfers between devices: 22.6 us -> 18.6 us  [over_f(): lax.ppermute(v, 'fsdp', [(i, i ^ k) for i in range(fsdp)])]
    broadcast_in_dim x1, local copies, waits for them, and re-layouts: 4.43 us -> 1 us  [column_body(): grad_a = jnp.zeros((dloc, rloc, half), F32)]
    ppermute x4, starting transfers between devices: 4.12 us -> 6.18 us  [column_body(): got.append(lax.ppermute(block, ('fsdp', 'tp'), perm))]
    unnamed x52 -> x50, local copies, waits for them, and re-layouts: 7.88 us -> 9.33 us
  transfers between devices with their start and end apart: 36 -> 36, of which waited for: 14 -> 15; matrix products, arithmetic and copies ran while one was open for 11% -> 6% of each run, Pallas kernels for 25% -> 26%
where the time goes in v10:
time: 200 us; the launch traced here: 199 us
  waiting for transfers between devices  69.2 us (35%)
  Pallas kernels  52.6 us (26%)
  starting transfers between devices  50.7 us (25%)
  local copies, waits for them, and re-layouts  20.4 us (10%)
  other arithmetic  5.4 us (3%)
    pallas_call x11, Pallas kernels, call(): pl.pallas_call(body, out_shape=[jax.ShapeDtypeStruct(shape, dtype) for sh...  52.6 us
    ppermute x9, waiting for transfers between devices, over_a(): lax.ppermute(v, 'ad', [(i, (i + k) % ad) for i in range(ad)])  33.2 us
    ppermute x15, waiting for transfers between devices, over_f(): lax.ppermute(v, 'fsdp', [(i, i ^ k) for i in range(fsdp)])  29.9 us
    ppermute x9, starting transfers between devices, over_a(): lax.ppermute(v, 'ad', [(i, (i + k) % ad) for i in range(ad)])  21.1 us
    ppermute x15, starting transfers between devices, over_f(): lax.ppermute(v, 'fsdp', [(i, i ^ k) for i in range(fsdp)])  18.6 us
    unnamed x50, local copies, waits for them, and re-layouts  9.33 us
    ppermute x4, starting transfers between devices, column_body(): got.append(lax.ppermute(block, ('fsdp', 'tp'), perm))  6.18 us
    dynamic_slice x1, local copies, waits for them, and re-layouts, column_body(): down_other = lax.dynamic_slice_in_dim(held[0], (fx * 2 + 1 - t) * kt, kt, 2)  4.64 us
  transfers between devices with their start and end apart: 36, of which 15 were waited for; matrix products, arithmetic and copies ran while one was open for 6% of the time, Pallas kernels for 26%

profile of v10, /device:TPU:0, one launch (start us, length us, event | category | flops | bytes accessed | tf_op | source)
XLA Modules:
  0.0 199.4 jit_solution(1434227268961416317)
XLA Ops:
  0.7 0.7 bitcast_convert_fusion
  1.3 2.5 %constant_dynamic-slice_fusion.2 = (bf16[256,1024]{1,0:T(8,128)(2,1)S(1)}, bf16[256,1024]{1,0:T(8,128)(2,1)S(1)}, bf16[256,1024]{1,0:T(8,128)(2,1)S(1)}, bf16[256,1024]{1,0:T(8,128)(2,1)}) fusion(bf16[256,8192]{1,0:T(8,128)(2,1)} %param.6, s32[]{:T(128)S(6)} %select_n.44, s32[]{:T(128)S(6)} %select_n.43, s32[]{:T(128)S(6)} %select_n.42, s32[]{:T(128)S(6)} %select_n.41), kind=kLoop, calls=%fused_computation.30 | loop fusion | bytes 4194320 | tf_op jit(solution)/shard_map/dynamic_slice | solution.py:387
  4.0 3.0 %collective-permute-start = (bf16[272,1024]{1,0:T(8,128)(2,1)S(1)}, bf16[272,1024]{1,0:T(8,128)(2,1)S(1)}, u32[]{:S(2)}, u32[]{:S(2)}) collective-permute-start(bf16[272,1024]{1,0:T(8,128)(2,1)S(1)} %get-tuple-element.80), channel_id=1, source_target_pairs={{0,8},{8,0},{16,24},{24,16},{1,9},{9,1},{17,25},{25,17},{2,10},{10... | collective-permute-start | bytes 1671176 | tf_op jit(solution)/shard_map/ppermute | solution.py:371
  7.0 1.5 collective-permute-start.1
  8.6 2.7 %shard_map.85 = (bf16[384,256]{1,0:T(8,128)(2,1)}, bf16[96,1536]{1,0:T(8,128)(2,1)}, bf16[96,1536]{1,0:T(8,128)(2,1)}, bf16[96,1536]{1,0:T(8,128)(2,1)}, bf16[96,1536]{1,0:T(8,128)(2,1)}) custom-call(s32[1]{0:T(128)} %bitcast.2.refs_0_, s32[1,256]{1,0:T(1,128)} %bitcast.30, bf16[256,1024]{1,0:T(8,128)(2,1)} %get-tuple-element.79.refs_2_, ...), custom_call_target="tpu_custom_call" | custom-call | flops 1 | bytes 1 | tf_op jit(solution)/shard_map/pallas_call | solution.py:154
  11.3 2.1 %collective-permute-start.3 = (bf16[96,1536]{1,0:T(8,128)(2,1)}, bf16[96,1536]{1,0:T(8,128)(2,1)}, u32[]{:S(2)}, u32[]{:S(2)}) collective-permute-start(bf16[96,1536]{1,0:T(8,128)(2,1)} %get-tuple-element.84), channel_id=1, source_target_pairs={{0,1},{1,2},{2,3},{3,0},{4,5},{5,6},{6,7},{7,4},{8,9},{9,10},{10,1... | collective-permute-start | bytes 884744 | tf_op jit(solution)/shard_map/ppermute | solution.py:374
  13.4 2.6 %collective-permute-start.4 = (bf16[96,1536]{1,0:T(8,128)(2,1)}, bf16[96,1536]{1,0:T(8,128)(2,1)}, u32[]{:S(2)}, u32[]{:S(2)}) collective-permute-start(bf16[96,1536]{1,0:T(8,128)(2,1)} %get-tuple-element.85), channel_id=1, source_target_pairs={{0,2},{1,3},{2,0},{3,1},{4,6},{5,7},{6,4},{7,5},{8,10},{9,11},{10,... | collective-permute-start | bytes 884744 | tf_op jit(solution)/shard_map/ppermute | solution.py:374
  16.0 4.5 %collective-permute-done.refs_1_.refs_2_ = bf16[272,1024]{1,0:T(8,128)(2,1)S(1)} collective-permute-done((bf16[272,1024]{1,0:T(8,128)(2,1)S(1)}, bf16[272,1024]{1,0:T(8,128)(2,1)S(1)}, u32[]{:S(2)}, u32[]{:S(2)}) %collective-permute-start) | collective-permute-done | bytes 557088 | tf_op jit(solution)/shard_map/ppermute | solution.py:371
  20.5 4.2 %collective-permute-start.5 = (bf16[96,1536]{1,0:T(8,128)(2,1)}, bf16[96,1536]{1,0:T(8,128)(2,1)S(1)}, u32[]{:S(2)}, u32[]{:S(2)}) collective-permute-start(bf16[96,1536]{1,0:T(8,128)(2,1)} %get-tuple-element.87), channel_id=1, source_target_pairs={{0,3},{1,0},{2,1},{3,2},{4,7},{5,4},{6,5},{7,6},{8,11},{9,8},{10,9... | collective-permute-start | bytes 884744 | tf_op jit(solution)/shard_map/ppermute | solution.py:374
  24.6 4.6 %constant_dynamic-slice_fusion.1 = bf16[8,256,1024]{2,1,0:T(8,128)(2,1)} fusion(bf16[8,256,4096]{2,1,0:T(8,128)(2,1)} %refs_5_.3, s32[]{:T(128)S(6)} %select_n.46), kind=kLoop, calls=%fused_computation.29 | loop fusion | bytes 8388612 | tf_op jit(solution)/shard_map/dynamic_slice | solution.py:406
  29.3 2.3 %constant_dynamic-slice_fusion.refs_1_ = bf16[256,2048]{1,0:T(8,128)(2,1)} fusion(bf16[256,8192]{1,0:T(8,128)(2,1)} %param.6, s32[]{:T(128)S(6)} %select_n.47), kind=kLoop, calls=%fused_computation.28 | loop fusion | bytes 2097156 | tf_op jit(solution)/shard_map/dynamic_slice | solution.py:409
  31.6 3.1 %collective-permute-done.4.refs_2_.refs_4_.refs_3_ = bf16[96,1536]{1,0:T(8,128)(2,1)} collective-permute-done((bf16[96,1536]{1,0:T(8,128)(2,1)}, bf16[96,1536]{1,0:T(8,128)(2,1)}, u32[]{:S(2)}, u32[]{:S(2)}) %collective-permute-start.4) | collective-permute-done | bytes 294944 | tf_op jit(solution)/shard_map/ppermute | solution.py:374
  35.3 3.3 %collective-permute-start.13 = (bf16[8,256,1024]{2,1,0:T(8,128)(2,1)}, bf16[8,256,1024]{2,1,0:T(8,128)(2,1)}, u32[]{:S(2)}, u32[]{:S(2)}) collective-permute-start(bf16[8,256,1024]{2,1,0:T(8,128)(2,1)} %constant_dynamic-slice_fusion.1), channel_id=1, source_target_pairs={{0,4},{8,12},{20,16},{28,24},{1,5},{9,13},{21,17},{29,25},{2,6},{1... | collective-permute-start | bytes 12582920 | tf_op jit(solution)/shard_map/ppermute | solution.py:412
  39.1 4.0 %shard_map.86 = (bf16[3,96,1024]{2,1,0:T(8,128)(2,1)}, bf16[3,96,1024]{2,1,0:T(8,128)(2,1)}, bf16[3,96,1024]{2,1,0:T(8,128)(2,1)}, bf16[3,96,1024]{2,1,0:T(8,128)(2,1)}) custom-call(s32[1]{0:T(128)} %bitcast.2.refs_0_, bf16[272,1024]{1,0:T(8,128)(2,1)} %copy-done.1, bf16[272,1024]{1,0:T(8,128)(2,1)} %copy-done.2, bf16[272,1024]{1,0:T(8,128)(2,1)} %copy-done.3), custom_call_target="tpu_custom_call" | custom-call | flops 1 | bytes 1 | tf_op jit(solution)/shard_map/pallas_call | solution.py:154
  43.1 5.9 %collective-permute-start.12 = (bf16[3,96,1024]{2,1,0:T(8,128)(2,1)}, bf16[3,96,1024]{2,1,0:T(8,128)(2,1)S(1)}, u32[]{:S(2)}, u32[]{:S(2)}) collective-permute-start(bf16[3,96,1024]{2,1,0:T(8,128)(2,1)} %get-tuple-element.96), channel_id=1, source_target_pairs={{0,2},{1,3},{2,0},{3,1},{4,6},{5,7},{6,4},{7,5},{8,10},{9,11},{10,... | collective-permute-start | bytes 1769480 | tf_op jit(solution)/shard_map/ppermute | solution.py:374
  48.9 0.8 copy-done.7
  50.1 6.1 %shard_map.87 = (f32[256,512]{1,0:T(8,128)}, f32[256,512]{1,0:T(8,128)}, f32[256,512]{1,0:T(8,128)}, f32[256,512]{1,0:T(8,128)}) custom-call(s32[1]{0:T(128)} %bitcast.refs_0_, bf16[256,2048]{1,0:T(8,128)(2,1)} %constant_dynamic-slice_fusion.refs_1_, bf16[272,1024]{1,0:T(8,128)(2,1)} %copy-done.1, bf16[272,1024]{1,0:T(8,128)(2,1)} %copy-done.2, ...), custom_call_target="tpu_custom_call" | custom-call | flops 1 | bytes 1 | tf_op jit(solution)/shard_map/pallas_call | solution.py:154
  56.2 1.6 collective-permute-start.9
  57.8 2.0 %collective-permute-start.10 = (f32[256,512]{1,0:T(8,128)}, f32[256,512]{1,0:T(8,128)S(1)}, u32[]{:S(2)}, u32[]{:S(2)}) collective-permute-start(f32[256,512]{1,0:T(8,128)} %get-tuple-element.103), channel_id=1, source_target_pairs={{0,16},{8,24},{16,0},{24,8},{1,17},{9,25},{17,1},{25,9},{2,18},{10... | collective-permute-start | bytes 1572872 | tf_op jit(solution)/shard_map/ppermute | solution.py:371
  59.8 3.4 %shard_map.88.refs_0_ = f32[4,96,256]{2,1,0:T(8,128)} custom-call(bf16[96,1536]{1,0:T(8,128)(2,1)} %get-tuple-element.111.refs_0_.refs_2_.refs_1_, bf16[96,1536]{1,0:T(8,128)(2,1)} %collective-permute-done.3.refs_1_.refs_3_.refs_2_, bf16[96,1536]{1,0:T(8,128)(2,1)} %collective-permute-done.4.refs_2_.refs_4_.refs_3_, bf16[96,1536]{1,0:T(8,128)(2,1)} %copy-done.16, ...), custom_call_target="tpu_custom_call" | custom-call | flops 10000000000 | bytes 1 | tf_op jit(solution)/shard_map/pallas_call | solution.py:154
  63.9 1.3 collective-permute-done.14.refs_1_
  65.2 3.2 %collective-permute-start.16 = (bf16[3,96,1024]{2,1,0:T(8,128)(2,1)}, bf16[3,96,1024]{2,1,0:T(8,128)(2,1)S(1)}, u32[]{:S(2)}, u32[]{:S(2)}) collective-permute-start(bf16[3,96,1024]{2,1,0:T(8,128)(2,1)} %get-tuple-element.95), channel_id=1, source_target_pairs={{0,1},{1,2},{2,3},{3,0},{4,5},{5,6},{6,7},{7,4},{8,9},{9,10},{10,1... | collective-permute-start | bytes 1769480 | tf_op jit(solution)/shard_map/ppermute | solution.py:374
  68.4 2.2 %shard_map.89.refs_9_.refs_4_ = bf16[4,96,768]{2,1,0:T(8,128)(2,1)} custom-call(f32[4,96,256]{2,1,0:T(8,128)} %shard_map.88.refs_0_, f32[4,96,256]{2,1,0:T(8,128)} %copy-done.14, bf16[96,1536]{1,0:T(8,128)(2,1)} %get-tuple-element.111.refs_0_.refs_2_.refs_1_, bf16[96,1536]{1,0:T(8,128)(2,1)} %collective-permute-done.3.refs_1_.refs_3_.refs_2_, ...), custom_call_target="tpu_custom_call" | custom-call | flops 1 | bytes 1 | tf_op jit(solution)/shard_map/pallas_call | solution.py:154
  70.6 17.8 %collective-permute-done.12.refs_4_.refs_7_ = bf16[3,96,1024]{2,1,0:T(8,128)(2,1)S(1)} collective-permute-done((bf16[3,96,1024]{2,1,0:T(8,128)(2,1)}, bf16[3,96,1024]{2,1,0:T(8,128)(2,1)S(1)}, u32[]{:S(2)}, u32[]{:S(2)}) %collective-permute-start.12) | collective-permute-done | bytes 589856 | tf_op jit(solution)/shard_map/ppermute | solution.py:374
  88.4 0.8 copy-done.10
  89.2 0.8 copy-done.11
  90.0 0.8 copy-done.12
  90.8 2.4 %collective-permute-start.28 = (bf16[4,96,768]{2,1,0:T(8,128)(2,1)}, bf16[4,96,768]{2,1,0:T(8,128)(2,1)S(1)}, u32[]{:S(2)}, u32[]{:S(2)}) collective-permute-start(bf16[4,96,768]{2,1,0:T(8,128)(2,1)} %shard_map.89.refs_9_.refs_4_), channel_id=1, source_target_pairs={{0,24},{8,16},{16,8},{24,0},{1,25},{9,17},{17,9},{25,1},{2,26},{10... | collective-permute-start | bytes 1769480 | tf_op jit(solution)/shard_map/ppermute | solution.py:371
  94.3 7.2 %shard_map.90 = (f32[4,2,96,128]{3,2,1,0:T(8,128)}, f32[4,2,96,128]{3,2,1,0:T(8,128)}) custom-call(s32[3]{0:T(128)} %pad_add_fusion.refs_0_, bf16[96,1536]{1,0:T(8,128)(2,1)} %get-tuple-element.111.refs_0_.refs_2_.refs_1_, bf16[96,1536]{1,0:T(8,128)(2,1)} %collective-permute-done.4.refs_2_.refs_4_.refs_3_, ...), custom_call_target="tpu_custom_call" | custom-call | flops 10000000000 | bytes 1 | tf_op jit(solution)/shard_map/pallas_call | solution.py:154
  101.6 2.2 %collective-permute-done.17.refs_4_.refs_8_ = bf16[3,96,1024]{2,1,0:T(8,128)(2,1)S(1)} collective-permute-done((bf16[3,96,1024]{2,1,0:T(8,128)(2,1)}, bf16[3,96,1024]{2,1,0:T(8,128)(2,1)S(1)}, u32[]{:S(2)}, u32[]{:S(2)}) %collective-permute-start.17) | collective-permute-done | bytes 589856 | tf_op jit(solution)/shard_map/ppermute | solution.py:374
  103.8 0.9 copy-done.24
  104.6 7.3 %shard_map.91 = (f32[4,2,96,128]{3,2,1,0:T(8,128)}, f32[4,2,96,128]{3,2,1,0:T(8,128)}) custom-call(s32[3]{0:T(128)} %pad_add_fusion.refs_0_, bf16[96,1536]{1,0:T(8,128)(2,1)} %collective-permute-done.3.refs_1_.refs_3_.refs_2_, bf16[96,1536]{1,0:T(8,128)(2,1)} %copy-done.16, bf16[3,96,1024]{2,1,0:T(8,128)(2,1)} %copy-done.23, ...), custom_call_target="tpu_custom_call" | custom-call | flops 10000000000 | bytes 1 | tf_op jit(solution)/shard_map/pallas_call | solution.py:154
  112.1 0.6 pad_add_fusion.1.refs_0_
  112.7 1.2 collective-permute-done.18
  114.0 1.0 add.109
  115.1 1.6 collective-permute-start.19
  116.6 1.0 collective-permute-start.21
  117.7 1.0 collective-permute-start.20
  118.6 1.1 collective-permute-done.27.refs_11_.refs_6_
  119.7 1.1 collective-permute-done.26.refs_10_.refs_5_
  120.8 0.8 copy-done.6
  121.6 8.9 %shard_map.94 = (bf16[8,64,1024]{2,1,0:T(8,128)(2,1)}, bf16[8,64,1024]{2,1,0:T(8,128)(2,1)}, bf16[8,64,1024]{2,1,0:T(8,128)(2,1)}, bf16[8,64,1024]{2,1,0:T(8,128)(2,1)}) custom-call(s32[4]{0:T(128)} %pad_add_fusion.1.refs_0_, bf16[96,1536]{1,0:T(8,128)(2,1)} %get-tuple-element.111.refs_0_.refs_2_.refs_1_, ...), custom_call_target="tpu_custom_call" | custom-call | flops 10000000000 | bytes 1 | tf_op jit(solution)/shard_map/pallas_call | solution.py:154
  130.6 1.5 collective-permute-start.30
  132.1 1.9 collective-permute-start.29
  134.1 0.8 collective-permute-start.22
  134.9 0.6 stack.61.refs_0_
  135.8 0.6 copy-done.20
  136.4 4.1 %shard_map.92 = (bf16[96,512]{1,0:T(8,128)(2,1)}, bf16[96,512]{1,0:T(8,128)(2,1)}, bf16[96,512]{1,0:T(8,128)(2,1)}, bf16[96,512]{1,0:T(8,128)(2,1)}, bf16[4,96,6...) custom-call(s32[5]{0:T(128)} %stack.61.refs_0_, ...), custom_call_target="tpu_custom_call" | custom-call | flops 1 | bytes 1 | tf_op jit(solution)/shard_map/pallas_call | solution.py:154
  140.6 0.8 collective-permute-start.23
  141.4 2.4 %collective-permute-start.24 = (bf16[96,512]{1,0:T(8,128)(2,1)}, bf16[96,512]{1,0:T(8,128)(2,1)S(1)}, u32[]{:S(2)}, u32[]{:S(2)}) collective-permute-start(bf16[96,512]{1,0:T(8,128)(2,1)} %get-tuple-element.126), channel_id=1, source_target_pairs={{0,2},{1,3},{2,0},{3,1},{4,6},{5,7},{6,4},{7,5},{8,10},{9,11},{10,... | collective-permute-start | bytes 294920 | tf_op jit(solution)/shard_map/ppermute | solution.py:374
  143.8 2.1 %collective-permute-done.23.refs_6_ = bf16[96,512]{1,0:T(8,128)(2,1)S(1)} collective-permute-done((bf16[96,512]{1,0:T(8,128)(2,1)}, bf16[96,512]{1,0:T(8,128)(2,1)S(1)}, u32[]{:S(2)}, u32[]{:S(2)}) %collective-permute-start.23) | collective-permute-done | bytes 98336 | tf_op jit(solution)/shard_map/ppermute | solution.py:374
  145.9 7.5 %collective-permute-done.24.refs_7_ = bf16[96,512]{1,0:T(8,128)(2,1)S(1)} collective-permute-done((bf16[96,512]{1,0:T(8,128)(2,1)}, bf16[96,512]{1,0:T(8,128)(2,1)S(1)}, u32[]{:S(2)}, u32[]{:S(2)}) %collective-permute-start.24) | collective-permute-done | bytes 98336 | tf_op jit(solution)/shard_map/ppermute | solution.py:374
  153.4 3.2 %collective-permute-done.30 = bf16[8,64,1024]{2,1,0:T(8,128)(2,1)S(1)} collective-permute-done((bf16[8,64,1024]{2,1,0:T(8,128)(2,1)}, bf16[8,64,1024]{2,1,0:T(8,128)(2,1)S(1)}, u32[]{:S(2)}, u32[]{:S(2)}) %collective-permute-start.30) | collective-permute-done | bytes 1048608 | tf_op jit(solution)/shard_map/ppermute | solution.py:497
  156.6 2.4 %collective-permute-start.31 = (bf16[8,64,1024]{2,1,0:T(8,128)(2,1)}, bf16[8,64,1024]{2,1,0:T(8,128)(2,1)}, u32[]{:S(2)}, u32[]{:S(2)}) collective-permute-start(bf16[8,64,1024]{2,1,0:T(8,128)(2,1)} %get-tuple-element.148), channel_id=1, source_target_pairs={{0,16},{4,0},{8,24},{12,8},{16,20},{20,4},{24,28},{28,12},{1,17},{... | collective-permute-start | bytes 3145736 | tf_op jit(solution)/shard_map/ppermute | solution.py:497
  159.3 1.1 collective-permute-start.33
  160.4 1.3 collective-permute-start.34
  161.7 1.1 collective-permute-start.35
  162.8 2.8 %shard_map.93 = bf16[256,512]{1,0:T(8,128)(2,1)} custom-call(f32[256,512]{1,0:T(8,128)} %get-tuple-element.101.refs_0_, f32[256,512]{1,0:T(8,128)} %copy-done.10, f32[256,512]{1,0:T(8,128)} %copy-done.11, f32[256,512]{1,0:T(8,128)} %copy-done.12, bf16[384,256]{1,0:T(8,128)(2,1)} %get-tuple-element.105.refs_4_, bf16[96,512]{1,0:T(8,128)(2,1)} %get-tuple-element.124.refs_5_, ...), custom_call_target="tpu_custom_call" | custom-call | flops 1 | bytes 1 | tf_op jit(solution)/shard_map/pallas_call | solution.py:154
  165.6 21.1 %collective-permute-done.33.refs_1_ = bf16[4,96,64]{2,1,0:T(8,128)(2,1)S(1)} collective-permute-done((bf16[4,96,64]{2,1,0:T(8,128)(2,1)}, bf16[4,96,64]{2,1,0:T(8,128)(2,1)S(1)}, u32[]{:S(2)}, u32[]{:S(2)}) %collective-permute-start.33) | collective-permute-done | bytes 49184 | tf_op jit(solution)/shard_map/ppermute | solution.py:371
  186.7 2.1 %collective-permute-done.35.refs_3_ = bf16[4,96,64]{2,1,0:T(8,128)(2,1)} collective-permute-done((bf16[4,96,64]{2,1,0:T(8,128)(2,1)}, bf16[4,96,64]{2,1,0:T(8,128)(2,1)}, u32[]{:S(2)}, u32[]{:S(2)}) %collective-permute-start.35) | collective-permute-done | bytes 49184 | tf_op jit(solution)/shard_map/ppermute | solution.py:371
  188.9 3.9 %shard_map.95 = f32[8,64,512]{2,1,0:T(8,128)} custom-call(bf16[4,96,64]{2,1,0:T(8,128)(2,1)} %get-tuple-element.151.refs_0_, bf16[4,96,64]{2,1,0:T(8,128)(2,1)} %copy-done.21, bf16[4,96,64]{2,1,0:T(8,128)(2,1)} %collective-permute-done.34.refs_2_, bf16[4,96,64]{2,1,0:T(8,128)(2,1)} %collective-permute-done.35.refs_3_, ...), custom_call_target="tpu_custom_call" | custom-call | flops 1 | bytes 1 | tf_op jit(solution)/shard_map/pallas_call | solution.py:154
  192.7 1.0 broadcast_in_dim.3
  194.3 1.5 convert_dynamic-update-slice_fusion.1
  196.0 3.4 %copy-done = f32[8,64,4096]{2,1,0:T(8,128)} copy-done((f32[8,64,4096]{2,1,0:T(8,128)}, f32[8,64,4096]{2,1,0:T(8,128)S(1)}, u32[]{:S(2)}) %copy-start) | copy-done | bytes 8388632
  (88 shorter events, 5.2 us)
Async XLA Ops:
  4.0 16.5 %collective-permute-start = (bf16[272,1024]{1,0:T(8,128)(2,1)S(1)}, bf16[272,1024]{1,0:T(8,128)(2,1)S(1)}, u32[]{:S(2)}, u32[]{:S(2)}) collective-permute-start(bf16[272,1024]{1,0:T(8,128)(2,1)S(1)} %get-tuple-element.80), channel_id=1, source_target_pairs={{0,8},{8,0},{16,24},{24,16},{1,9},{9,1},{17,25},{25,17},{2,10},{10... | collective-permute-start | bytes 1671176 | tf_op jit(solution)/shard_map/ppermute | solution.py:371
  7.0 27.6 %collective-permute-start.1 = (bf16[272,1024]{1,0:T(8,128)(2,1)S(1)}, bf16[272,1024]{1,0:T(8,128)(2,1)S(1)}, u32[]{:S(2)}, u32[]{:S(2)}) collective-permute-start(bf16[272,1024]{1,0:T(8,128)(2,1)S(1)} %get-tuple-element.81), channel_id=1, source_target_pairs={{0,16},{8,24},{16,0},{24,8},{1,17},{9,25},{17,1},{25,9},{2,18},{10... | collective-permute-start | bytes 1671176 | tf_op jit(solution)/shard_map/ppermute | solution.py:371
  8.5 26.1 %collective-permute-start.2 = (bf16[272,1024]{1,0:T(8,128)(2,1)S(1)}, bf16[272,1024]{1,0:T(8,128)(2,1)S(1)}, u32[]{:S(2)}, u32[]{:S(2)}) collective-permute-start(bf16[272,1024]{1,0:T(8,128)(2,1)S(1)} %get-tuple-element.82), channel_id=1, source_target_pairs={{0,24},{8,16},{16,8},{24,0},{1,25},{9,17},{17,9},{25,1},{2,26},{10... | collective-permute-start | bytes 1671176 | tf_op jit(solution)/shard_map/ppermute | solution.py:371
  11.3 20.3 %collective-permute-start.3 = (bf16[96,1536]{1,0:T(8,128)(2,1)}, bf16[96,1536]{1,0:T(8,128)(2,1)}, u32[]{:S(2)}, u32[]{:S(2)}) collective-permute-start(bf16[96,1536]{1,0:T(8,128)(2,1)} %get-tuple-element.84), channel_id=1, source_target_pairs={{0,1},{1,2},{2,3},{3,0},{4,5},{5,6},{6,7},{7,4},{8,9},{9,10},{10,1... | collective-permute-start | bytes 884744 | tf_op jit(solution)/shard_map/ppermute | solution.py:374
  13.4 21.3 %collective-permute-start.4 = (bf16[96,1536]{1,0:T(8,128)(2,1)}, bf16[96,1536]{1,0:T(8,128)(2,1)}, u32[]{:S(2)}, u32[]{:S(2)}) collective-permute-start(bf16[96,1536]{1,0:T(8,128)(2,1)} %get-tuple-element.85), channel_id=1, source_target_pairs={{0,2},{1,3},{2,0},{3,1},{4,6},{5,7},{6,4},{7,5},{8,10},{9,11},{10,... | collective-permute-start | bytes 884744 | tf_op jit(solution)/shard_map/ppermute | solution.py:374
  20.5 18.1 %copy-start.1 = (bf16[272,1024]{1,0:T(8,128)(2,1)}, bf16[272,1024]{1,0:T(8,128)(2,1)S(1)}, u32[]{:S(2)}) copy-start(bf16[272,1024]{1,0:T(8,128)(2,1)S(1)} %collective-permute-done.refs_1_.refs_2_) | copy-start | bytes 1671172
  20.5 14.8 %collective-permute-start.5 = (bf16[96,1536]{1,0:T(8,128)(2,1)}, bf16[96,1536]{1,0:T(8,128)(2,1)S(1)}, u32[]{:S(2)}, u32[]{:S(2)}) collective-permute-start(bf16[96,1536]{1,0:T(8,128)(2,1)} %get-tuple-element.87), channel_id=1, source_target_pairs={{0,3},{1,0},{2,1},{3,2},{4,7},{5,4},{6,5},{7,6},{8,11},{9,8},{10,9... | collective-permute-start | bytes 884744 | tf_op jit(solution)/shard_map/ppermute | solution.py:374
  34.7 4.4 %copy-start.2 = (bf16[272,1024]{1,0:T(8,128)(2,1)}, bf16[272,1024]{1,0:T(8,128)(2,1)S(1)}, u32[]{:S(2)}) copy-start(bf16[272,1024]{1,0:T(8,128)(2,1)S(1)} %collective-permute-done.1.refs_2_.refs_3_) | copy-start | bytes 1671172
  34.7 4.4 %copy-start.3 = (bf16[272,1024]{1,0:T(8,128)(2,1)}, bf16[272,1024]{1,0:T(8,128)(2,1)S(1)}, u32[]{:S(2)}) copy-start(bf16[272,1024]{1,0:T(8,128)(2,1)S(1)} %collective-permute-done.2.refs_3_.refs_4_) | copy-start | bytes 1671172
  35.3 24.5 %copy-start.16 = (bf16[96,1536]{1,0:T(8,128)(2,1)}, bf16[96,1536]{1,0:T(8,128)(2,1)S(1)}, u32[]{:S(2)}) copy-start(bf16[96,1536]{1,0:T(8,128)(2,1)S(1)} %collective-permute-done.5.refs_3_.refs_5_.refs_2_.refs_4_) | copy-start | bytes 884740
  35.3 24.5 %collective-permute-start.13 = (bf16[8,256,1024]{2,1,0:T(8,128)(2,1)}, bf16[8,256,1024]{2,1,0:T(8,128)(2,1)}, u32[]{:S(2)}, u32[]{:S(2)}) collective-permute-start(bf16[8,256,1024]{2,1,0:T(8,128)(2,1)} %constant_dynamic-slice_fusion.1), channel_id=1, source_target_pairs={{0,4},{8,12},{20,16},{28,24},{1,5},{9,13},{21,17},{29,25},{2,6},{1... | collective-permute-start | bytes 12582920 | tf_op jit(solution)/shard_map/ppermute | solution.py:412
  38.6 10.4 %collective-permute-start.6 = (bf16[272,1024]{1,0:T(8,128)(2,1)S(1)}, bf16[272,1024]{1,0:T(8,128)(2,1)S(1)}, u32[]{:S(2)}, u32[]{:S(2)}) collective-permute-start(bf16[272,1024]{1,0:T(8,128)(2,1)S(1)} %collective-permute-done.refs_1_.refs_2_), channel_id=1, source_target_pairs={{0,4},{4,0},{1,5},{5,1},{2,6},{6,2},{3,7},{7,3},{8,12},{12,8},{9,1... | collective-permute-start | bytes 1671176 | tf_op jit(solution)/shard_map/ppermute | solution.py:377
  38.6 10.4 %collective-permute-start.7 = (bf16[272,1024]{1,0:T(8,128)(2,1)S(1)}, bf16[272,1024]{1,0:T(8,128)(2,1)S(1)}, u32[]{:S(2)}, u32[]{:S(2)}) collective-permute-start(bf16[272,1024]{1,0:T(8,128)(2,1)S(1)} %collective-permute-done.1.refs_2_.refs_3_), channel_id=1, source_target_pairs={{0,4},{4,0},{1,5},{5,1},{2,6},{6,2},{3,7},{7,3},{8,12},{12,8},{9,1... | collective-permute-start | bytes 1671176 | tf_op jit(solution)/shard_map/ppermute | solution.py:377
  39.1 9.9 %collective-permute-start.8 = (bf16[272,1024]{1,0:T(8,128)(2,1)S(1)}, bf16[272,1024]{1,0:T(8,128)(2,1)S(1)}, u32[]{:S(2)}, u32[]{:S(2)}) collective-permute-start(bf16[272,1024]{1,0:T(8,128)(2,1)S(1)} %collective-permute-done.2.refs_3_.refs_4_), channel_id=1, source_target_pairs={{0,4},{4,0},{1,5},{5,1},{2,6},{6,2},{3,7},{7,3},{8,12},{12,8},{9,1... | collective-permute-start | bytes 1671176 | tf_op jit(solution)/shard_map/ppermute | solution.py:377
  43.1 45.3 %collective-permute-start.12 = (bf16[3,96,1024]{2,1,0:T(8,128)(2,1)}, bf16[3,96,1024]{2,1,0:T(8,128)(2,1)S(1)}, u32[]{:S(2)}, u32[]{:S(2)}) collective-permute-start(bf16[3,96,1024]{2,1,0:T(8,128)(2,1)} %get-tuple-element.96), channel_id=1, source_target_pairs={{0,2},{1,3},{2,0},{3,1},{4,6},{5,7},{6,4},{7,5},{8,10},{9,11},{10,... | collective-permute-start | bytes 1769480 | tf_op jit(solution)/shard_map/ppermute | solution.py:374
  48.9 0.8 copy-start.7
  48.9 1.0 copy-start.8
  48.9 1.2 copy-start.9
  56.2 32.2 %collective-permute-start.9 = (f32[256,512]{1,0:T(8,128)}, f32[256,512]{1,0:T(8,128)S(1)}, u32[]{:S(2)}, u32[]{:S(2)}) collective-permute-start(f32[256,512]{1,0:T(8,128)} %get-tuple-element.102), channel_id=1, source_target_pairs={{0,8},{8,0},{16,24},{24,16},{1,9},{9,1},{17,25},{25,17},{2,10},{10... | collective-permute-start | bytes 1572872 | tf_op jit(solution)/shard_map/ppermute | solution.py:371
  57.8 30.6 %collective-permute-start.10 = (f32[256,512]{1,0:T(8,128)}, f32[256,512]{1,0:T(8,128)S(1)}, u32[]{:S(2)}, u32[]{:S(2)}) collective-permute-start(f32[256,512]{1,0:T(8,128)} %get-tuple-element.103), channel_id=1, source_target_pairs={{0,16},{8,24},{16,0},{24,8},{1,17},{9,25},{17,1},{25,9},{2,18},{10... | collective-permute-start | bytes 1572872 | tf_op jit(solution)/shard_map/ppermute | solution.py:371
  59.8 30.2 %collective-permute-start.11 = (f32[256,512]{1,0:T(8,128)}, f32[256,512]{1,0:T(8,128)S(1)}, u32[]{:S(2)}, u32[]{:S(2)}) collective-permute-start(f32[256,512]{1,0:T(8,128)} %get-tuple-element.104), channel_id=1, source_target_pairs={{0,24},{8,16},{16,8},{24,0},{1,25},{9,17},{17,9},{25,1},{2,26},{10... | collective-permute-start | bytes 1572872 | tf_op jit(solution)/shard_map/ppermute | solution.py:371
  63.2 2.0 %collective-permute-start.14 = (f32[4,96,256]{2,1,0:T(8,128)}, f32[4,96,256]{2,1,0:T(8,128)S(1)}, u32[]{:S(2)}, u32[]{:S(2)}) collective-permute-start(f32[4,96,256]{2,1,0:T(8,128)} %shard_map.88.refs_0_), channel_id=1, source_target_pairs={{0,4},{4,0},{1,5},{5,1},{2,6},{6,2},{3,7},{7,3},{8,12},{12,8},{9,1... | collective-permute-start | bytes 1179656 | tf_op jit(solution)/shard_map/ppermute | solution.py:377
  65.2 3.2 %copy-start.14 = (f32[4,96,256]{2,1,0:T(8,128)}, f32[4,96,256]{2,1,0:T(8,128)S(1)}, u32[]{:S(2)}) copy-start(f32[4,96,256]{2,1,0:T(8,128)S(1)} %collective-permute-done.14.refs_1_) | copy-start | bytes 1179652
  65.2 36.3 %collective-permute-start.16 = (bf16[3,96,1024]{2,1,0:T(8,128)(2,1)}, bf16[3,96,1024]{2,1,0:T(8,128)(2,1)S(1)}, u32[]{:S(2)}, u32[]{:S(2)}) collective-permute-start(bf16[3,96,1024]{2,1,0:T(8,128)(2,1)} %get-tuple-element.95), channel_id=1, source_target_pairs={{0,1},{1,2},{2,3},{3,0},{4,5},{5,6},{6,7},{7,4},{8,9},{9,10},{10,1... | collective-permute-start | bytes 1769480 | tf_op jit(solution)/shard_map/ppermute | solution.py:374
  88.4 5.9 %copy-start.22 = (bf16[3,96,1024]{2,1,0:T(8,128)(2,1)}, bf16[3,96,1024]{2,1,0:T(8,128)(2,1)S(1)}, u32[]{:S(2)}) copy-start(bf16[3,96,1024]{2,1,0:T(8,128)(2,1)S(1)} %collective-permute-done.12.refs_4_.refs_7_) | copy-start | bytes 1769476
  88.4 15.4 %collective-permute-start.17 = (bf16[3,96,1024]{2,1,0:T(8,128)(2,1)}, bf16[3,96,1024]{2,1,0:T(8,128)(2,1)S(1)}, u32[]{:S(2)}, u32[]{:S(2)}) collective-permute-start(bf16[3,96,1024]{2,1,0:T(8,128)(2,1)} %get-tuple-element.97), channel_id=1, source_target_pairs={{0,3},{1,0},{2,1},{3,2},{4,7},{5,4},{6,5},{7,6},{8,11},{9,8},{10,9... | collective-permute-start | bytes 1769480 | tf_op jit(solution)/shard_map/ppermute | solution.py:374
  88.4 0.8 copy-start.10
  89.2 0.8 copy-start.11
  90.0 0.8 copy-start.12
  90.8 26.9 %collective-permute-start.28 = (bf16[4,96,768]{2,1,0:T(8,128)(2,1)}, bf16[4,96,768]{2,1,0:T(8,128)(2,1)S(1)}, u32[]{:S(2)}, u32[]{:S(2)}) collective-permute-start(bf16[4,96,768]{2,1,0:T(8,128)(2,1)} %shard_map.89.refs_9_.refs_4_), channel_id=1, source_target_pairs={{0,24},{8,16},{16,8},{24,0},{1,25},{9,17},{17,9},{25,1},{2,26},{10... | collective-permute-start | bytes 1769480 | tf_op jit(solution)/shard_map/ppermute | solution.py:371
  93.2 26.5 %collective-permute-start.27 = (bf16[4,96,768]{2,1,0:T(8,128)(2,1)}, bf16[4,96,768]{2,1,0:T(8,128)(2,1)S(1)}, u32[]{:S(2)}, u32[]{:S(2)}) collective-permute-start(bf16[4,96,768]{2,1,0:T(8,128)(2,1)} %shard_map.89.refs_9_.refs_4_), channel_id=1, source_target_pairs={{0,16},{8,24},{16,0},{24,8},{1,17},{9,25},{17,1},{25,9},{2,18},{10... | collective-permute-start | bytes 1769480 | tf_op jit(solution)/shard_map/ppermute | solution.py:371
  93.8 27.0 %collective-permute-start.26 = (bf16[4,96,768]{2,1,0:T(8,128)(2,1)}, bf16[4,96,768]{2,1,0:T(8,128)(2,1)S(1)}, u32[]{:S(2)}, u32[]{:S(2)}) collective-permute-start(bf16[4,96,768]{2,1,0:T(8,128)(2,1)} %shard_map.89.refs_9_.refs_4_), channel_id=1, source_target_pairs={{0,8},{8,0},{16,24},{24,16},{1,9},{9,1},{17,25},{25,17},{2,10},{10... | collective-permute-start | bytes 1769480 | tf_op jit(solution)/shard_map/ppermute | solution.py:371
  101.5 2.3 %copy-start.23 = (bf16[3,96,1024]{2,1,0:T(8,128)(2,1)}, bf16[3,96,1024]{2,1,0:T(8,128)(2,1)S(1)}, u32[]{:S(2)}) copy-start(bf16[3,96,1024]{2,1,0:T(8,128)(2,1)S(1)} %collective-permute-done.16.refs_3_.refs_6_) | copy-start | bytes 1769476
  101.5 11.2 %collective-permute-start.15 = (f32[4,2,96,128]{3,2,1,0:T(8,128)}, f32[4,2,96,128]{3,2,1,0:T(8,128)S(1)}, u32[]{:S(2)}, u32[]{:S(2)}) collective-permute-start(f32[4,2,96,128]{3,2,1,0:T(8,128)} %get-tuple-element.119), channel_id=1, source_target_pairs={{0,4},{4,0},{1,5},{5,1},{2,6},{6,2},{3,7},{7,3},{8,12},{12,8},{9,1... | collective-permute-start | bytes 1179656 | tf_op jit(solution)/shard_map/ppermute | solution.py:377
  103.8 0.9 copy-start.24
  104.6 8.0 %copy-start.15 = (f32[4,2,96,128]{3,2,1,0:T(8,128)S(1)}, f32[4,2,96,128]{3,2,1,0:T(8,128)}, u32[]{:S(2)}) copy-start(f32[4,2,96,128]{3,2,1,0:T(8,128)} %get-tuple-element.118) | copy-start | bytes 1179652
  112.0 2.0 %collective-permute-start.18 = (f32[4,2,96,128]{3,2,1,0:T(8,128)}, f32[4,2,96,128]{3,2,1,0:T(8,128)S(1)}, u32[]{:S(2)}, u32[]{:S(2)}) collective-permute-start(f32[4,2,96,128]{3,2,1,0:T(8,128)} %get-tuple-element.123), channel_id=1, source_target_pairs={{0,4},{4,0},{1,5},{5,1},{2,6},{6,2},{3,7},{7,3},{8,12},{12,8},{9,1... | collective-permute-start | bytes 1179656 | tf_op jit(solution)/shard_map/ppermute | solution.py:377
  115.1 15.5 %collective-permute-start.19 = (f32[4,96,128]{2,1,0:T(8,128)S(1)}, f32[4,96,128]{2,1,0:T(8,128)S(1)}, u32[]{:S(2)}, u32[]{:S(2)}) collective-permute-start(f32[4,96,128]{2,1,0:T(8,128)S(1)} %get-tuple-element.159), channel_id=1, source_target_pairs={{0,8},{8,0},{16,24},{24,16},{1,9},{9,1},{17,25},{25,17},{2,10},{10... | collective-permute-start | bytes 589832 | tf_op jit(solution)/shard_map/ppermute | solution.py:371
  116.6 13.9 %collective-permute-start.21 = (f32[4,96,128]{2,1,0:T(8,128)S(1)}, f32[4,96,128]{2,1,0:T(8,128)S(1)}, u32[]{:S(2)}, u32[]{:S(2)}) collective-permute-start(f32[4,96,128]{2,1,0:T(8,128)S(1)} %get-tuple-element.160), channel_id=1, source_target_pairs={{0,24},{8,16},{16,8},{24,0},{1,25},{9,17},{17,9},{25,1},{2,26},{10... | collective-permute-start | bytes 589832 | tf_op jit(solution)/shard_map/ppermute | solution.py:371
  117.7 3.1 %copy-start.4 = (bf16[4,96,768]{2,1,0:T(8,128)(2,1)}, bf16[4,96,768]{2,1,0:T(8,128)(2,1)S(1)}, u32[]{:S(2)}) copy-start(bf16[4,96,768]{2,1,0:T(8,128)(2,1)S(1)} %collective-permute-done.28.refs_12_.refs_7_) | copy-start | bytes 1769476
  117.7 12.9 %collective-permute-start.20 = (f32[4,96,128]{2,1,0:T(8,128)S(1)}, f32[4,96,128]{2,1,0:T(8,128)S(1)}, u32[]{:S(2)}, u32[]{:S(2)}) collective-permute-start(f32[4,96,128]{2,1,0:T(8,128)S(1)} %get-tuple-element.161), channel_id=1, source_target_pairs={{0,16},{8,24},{16,0},{24,8},{1,17},{9,25},{17,1},{25,9},{2,18},{10... | collective-permute-start | bytes 589832 | tf_op jit(solution)/shard_map/ppermute | solution.py:371
  119.7 1.1 copy-start.5
  120.8 0.8 copy-start.6
  130.6 26.0 %collective-permute-start.30 = (bf16[8,64,1024]{2,1,0:T(8,128)(2,1)}, bf16[8,64,1024]{2,1,0:T(8,128)(2,1)S(1)}, u32[]{:S(2)}, u32[]{:S(2)}) collective-permute-start(bf16[8,64,1024]{2,1,0:T(8,128)(2,1)} %get-tuple-element.146), channel_id=1, source_target_pairs={{0,8},{4,24},{8,0},{12,16},{16,12},{20,28},{24,4},{28,20},{1,9},{5... | collective-permute-start | bytes 3145736 | tf_op jit(solution)/shard_map/ppermute | solution.py:497
  132.1 24.4 %collective-permute-start.29 = (bf16[8,64,1024]{2,1,0:T(8,128)(2,1)}, bf16[8,64,1024]{2,1,0:T(8,128)(2,1)S(1)}, u32[]{:S(2)}, u32[]{:S(2)}) collective-permute-start(bf16[8,64,1024]{2,1,0:T(8,128)(2,1)} %get-tuple-element.144), channel_id=1, source_target_pairs={{0,0},{4,16},{8,8},{12,24},{16,4},{20,20},{24,12},{28,28},{1,1},{5... | collective-permute-start | bytes 3145736 | tf_op jit(solution)/shard_map/ppermute | solution.py:497
  134.1 1.7 copy-start.13
  134.1 1.7 collective-permute-start.22
  135.8 0.6 copy-start.20
  140.6 5.3 %collective-permute-start.23 = (bf16[96,512]{1,0:T(8,128)(2,1)}, bf16[96,512]{1,0:T(8,128)(2,1)S(1)}, u32[]{:S(2)}, u32[]{:S(2)}) collective-permute-start(bf16[96,512]{1,0:T(8,128)(2,1)} %get-tuple-element.125), channel_id=1, source_target_pairs={{0,3},{1,0},{2,1},{3,2},{4,7},{5,4},{6,5},{7,6},{8,11},{9,8},{10,9... | collective-permute-start | bytes 294920 | tf_op jit(solution)/shard_map/ppermute | solution.py:374
  141.4 11.9 %collective-permute-start.24 = (bf16[96,512]{1,0:T(8,128)(2,1)}, bf16[96,512]{1,0:T(8,128)(2,1)S(1)}, u32[]{:S(2)}, u32[]{:S(2)}) collective-permute-start(bf16[96,512]{1,0:T(8,128)(2,1)} %get-tuple-element.126), channel_id=1, source_target_pairs={{0,2},{1,3},{2,0},{3,1},{4,6},{5,7},{6,4},{7,5},{8,10},{9,11},{10,... | collective-permute-start | bytes 294920 | tf_op jit(solution)/shard_map/ppermute | solution.py:374
  143.8 9.6 %collective-permute-start.25 = (bf16[96,512]{1,0:T(8,128)(2,1)}, bf16[96,512]{1,0:T(8,128)(2,1)S(1)}, u32[]{:S(2)}, u32[]{:S(2)}) collective-permute-start(bf16[96,512]{1,0:T(8,128)(2,1)} %get-tuple-element.127), channel_id=1, source_target_pairs={{0,1},{1,2},{2,3},{3,0},{4,5},{5,6},{6,7},{7,4},{8,9},{9,10},{10,1... | collective-permute-start | bytes 294920 | tf_op jit(solution)/shard_map/ppermute | solution.py:374
  145.9 16.9 %copy-start.17 = (bf16[96,512]{1,0:T(8,128)(2,1)}, bf16[96,512]{1,0:T(8,128)(2,1)S(1)}, u32[]{:S(2)}) copy-start(bf16[96,512]{1,0:T(8,128)(2,1)S(1)} %collective-permute-done.23.refs_6_) | copy-start | bytes 294916
  153.4 9.5 %copy-start.18 = (bf16[96,512]{1,0:T(8,128)(2,1)}, bf16[96,512]{1,0:T(8,128)(2,1)S(1)}, u32[]{:S(2)}) copy-start(bf16[96,512]{1,0:T(8,128)(2,1)S(1)} %collective-permute-done.24.refs_7_) | copy-start | bytes 294916
  153.4 9.5 %copy-start.19 = (bf16[96,512]{1,0:T(8,128)(2,1)}, bf16[96,512]{1,0:T(8,128)(2,1)S(1)}, u32[]{:S(2)}) copy-start(bf16[96,512]{1,0:T(8,128)(2,1)S(1)} %collective-permute-done.25.refs_8_) | copy-start | bytes 294916
  156.6 37.7 %collective-permute-start.31 = (bf16[8,64,1024]{2,1,0:T(8,128)(2,1)}, bf16[8,64,1024]{2,1,0:T(8,128)(2,1)}, u32[]{:S(2)}, u32[]{:S(2)}) collective-permute-start(bf16[8,64,1024]{2,1,0:T(8,128)(2,1)} %get-tuple-element.148), channel_id=1, source_target_pairs={{0,16},{4,0},{8,24},{12,8},{16,20},{20,4},{24,28},{28,12},{1,17},{... | collective-permute-start | bytes 3145736 | tf_op jit(solution)/shard_map/ppermute | solution.py:497
  159.0 36.8 %collective-permute-start.32 = (bf16[8,64,1024]{2,1,0:T(8,128)(2,1)}, bf16[8,64,1024]{2,1,0:T(8,128)(2,1)S(1)}, u32[]{:S(2)}, u32[]{:S(2)}) collective-permute-start(bf16[8,64,1024]{2,1,0:T(8,128)(2,1)} %get-tuple-element.150), channel_id=1, source_target_pairs={{0,24},{4,8},{8,16},{12,0},{16,28},{20,12},{24,20},{28,4},{1,25},{... | collective-permute-start | bytes 3145736 | tf_op jit(solution)/shard_map/ppermute | solution.py:497
  159.3 27.4 %collective-permute-start.33 = (bf16[4,96,64]{2,1,0:T(8,128)(2,1)}, bf16[4,96,64]{2,1,0:T(8,128)(2,1)S(1)}, u32[]{:S(2)}, u32[]{:S(2)}) collective-permute-start(bf16[4,96,64]{2,1,0:T(8,128)(2,1)} %get-tuple-element.152), channel_id=1, source_target_pairs={{0,8},{8,0},{16,24},{24,16},{1,9},{9,1},{17,25},{25,17},{2,10},{10... | collective-permute-start | bytes 147464 | tf_op jit(solution)/shard_map/ppermute | solution.py:371
  160.4 26.3 %collective-permute-start.34 = (bf16[4,96,64]{2,1,0:T(8,128)(2,1)}, bf16[4,96,64]{2,1,0:T(8,128)(2,1)}, u32[]{:S(2)}, u32[]{:S(2)}) collective-permute-start(bf16[4,96,64]{2,1,0:T(8,128)(2,1)} %get-tuple-element.153), channel_id=1, source_target_pairs={{0,16},{8,24},{16,0},{24,8},{1,17},{9,25},{17,1},{25,9},{2,18},{10... | collective-permute-start | bytes 147464 | tf_op jit(solution)/shard_map/ppermute | solution.py:371
  161.7 27.1 %collective-permute-start.35 = (bf16[4,96,64]{2,1,0:T(8,128)(2,1)}, bf16[4,96,64]{2,1,0:T(8,128)(2,1)}, u32[]{:S(2)}, u32[]{:S(2)}) collective-permute-start(bf16[4,96,64]{2,1,0:T(8,128)(2,1)} %get-tuple-element.154), channel_id=1, source_target_pairs={{0,24},{8,16},{16,8},{24,0},{1,25},{9,17},{17,9},{25,1},{2,26},{10... | collective-permute-start | bytes 147464 | tf_op jit(solution)/shard_map/ppermute | solution.py:371
  186.7 2.1 %copy-start.21 = (bf16[4,96,64]{2,1,0:T(8,128)(2,1)}, bf16[4,96,64]{2,1,0:T(8,128)(2,1)S(1)}, u32[]{:S(2)}) copy-start(bf16[4,96,64]{2,1,0:T(8,128)(2,1)S(1)} %collective-permute-done.33.refs_1_) | copy-start | bytes 147460
  196.0 3.4 %copy-start = (f32[8,64,4096]{2,1,0:T(8,128)}, f32[8,64,4096]{2,1,0:T(8,128)S(1)}, u32[]{:S(2)}) copy-start(f32[8,64,4096]{2,1,0:T(8,128)S(1)} %convert_dynamic-update-slice_fusion) | copy-start | bytes 25165828

commit v11 on v10

--- a/solution.py
+++ b/solution.py
@@ -480,10 +480,10 @@
         [(v, None) for v in (hid_own, swap(hid_own), adapter_up_weight)],
         at=numbers(t, *[f ^ k for k in range(fsdp)]),
     )
-    returned = [over_a(v, (ad - ka) % ad) for ka, v in enumerate(outs[:ad])]
+    hid_cols = [over_f(v, k) for k, v in enumerate(outs[ad:])]
+    returned = after(outs[:ad], *hid_cols[1:])
+    returned = [over_a(v, (ad - ka) % ad) for ka, v in enumerate(returned)]
     grad_a = jnp.zeros((dloc, rloc, half), F32)
-    hid_cols, grad_a = after((outs[ad:], grad_a), *returned[1:])
-    hid_cols = [over_f(v, k) for k, v in enumerate(hid_cols)]
     got = []
     for r in range(fsdp):
         p, q = r % 2, r // 2
@@ -493,7 +493,7 @@
             for x in range(2)
             for s in range(2)
         ]
-        block = after(sums[r], *(hid[1:] if r < 2 else [*got[:2], *returned[1:]]))
+        block = after(sums[r], *(hid[1:] if r < 2 else [*got[:2], *hid_cols[1:]]))
         got.append(lax.ppermute(block, ("fsdp", "tp"), perm))
         at = (fx ^ p) * kf_width + (fy ^ q) * kt
         grad_a = lax.dynamic_update_slice_in_dim(grad_a, got[r].astype(F32), at, 2)

time: 200 us -> 193 us (0.965)
  waiting for transfers between devices: 69.2 us -> 63.1 us
  starting transfers between devices: 50.7 us -> 48.5 us
    ppermute x15, waiting for transfers between devices: 29.9 us -> 25.3 us  [over_f(): lax.ppermute(v, 'fsdp', [(i, i ^ k) for i in range(fsdp)])]
    ppermute x9, waiting for transfers between devices: 33.2 us -> 29.5 us  [over_a(): lax.ppermute(v, 'ad', [(i, (i + k) % ad) for i in range(ad)])]
    ppermute x4, starting transfers between devices: 6.18 us -> 3.71 us  [column_body(): got.append(lax.ppermute(block, ('fsdp', 'tp'), perm))]
    ppermute x4, waiting for transfers between devices: 3.2 us -> 5.37 us  [column_body(): got.append(lax.ppermute(block, ('fsdp', 'tp'), perm))]
    unnamed x50 -> x54, local copies, waits for them, and re-layouts: 9.33 us -> 10.6 us
  transfers between devices with their start and end apart: 36 -> 36, of which waited for: 15 -> 15; matrix products, arithmetic and copies ran while one was open for 6% -> 7% of each run, Pallas kernels for 26% -> 27%
where the time goes in v11:
time: 193 us; the launch traced here: 192 us
  waiting for transfers between devices  63.1 us (33%)
  Pallas kernels  52.7 us (27%)
  starting transfers between devices  48.5 us (25%)
  local copies, waits for them, and re-layouts  21.7 us (11%)
  other arithmetic  5.36 us (3%)
    pallas_call x11, Pallas kernels, call(): pl.pallas_call(body, out_shape=[jax.ShapeDtypeStruct(shape, dtype) for sh...  52.7 us
    ppermute x9, waiting for transfers between devices, over_a(): lax.ppermute(v, 'ad', [(i, (i + k) % ad) for i in range(ad)])  29.5 us
    ppermute x15, waiting for transfers between devices, over_f(): lax.ppermute(v, 'fsdp', [(i, i ^ k) for i in range(fsdp)])  25.3 us
    ppermute x9, starting transfers between devices, over_a(): lax.ppermute(v, 'ad', [(i, (i + k) % ad) for i in range(ad)])  21.4 us
    ppermute x15, starting transfers between devices, over_f(): lax.ppermute(v, 'fsdp', [(i, i ^ k) for i in range(fsdp)])  18.7 us
    unnamed x54, local copies, waits for them, and re-layouts  10.6 us
    ppermute x4, waiting for transfers between devices, column_body(): got.append(lax.ppermute(block, ('fsdp', 'tp'), perm))  5.37 us
    dynamic_slice x1, local copies, waits for them, and re-layouts, column_body(): down_other = lax.dynamic_slice_in_dim(held[0], (fx * 2 + 1 - t) * kt, kt, 2)  4.64 us
  transfers between devices with their start and end apart: 36, of which 15 were waited for; matrix products, arithmetic and copies ran while one was open for 7% of the time, Pallas kernels for 27%

profile of v11, /device:TPU:0, one launch (start us, length us, event | category | flops | bytes accessed | tf_op | source)
XLA Modules:
  0.0 192.5 jit_solution(17931683989927761872)
XLA Ops:
  0.7 0.7 bitcast_convert_fusion
  1.3 2.5 %constant_dynamic-slice_fusion.2 = (bf16[256,1024]{1,0:T(8,128)(2,1)S(1)}, bf16[256,1024]{1,0:T(8,128)(2,1)S(1)}, bf16[256,1024]{1,0:T(8,128)(2,1)S(1)}, bf16[256,1024]{1,0:T(8,128)(2,1)}) fusion(bf16[256,8192]{1,0:T(8,128)(2,1)} %param.6, s32[]{:T(128)S(6)} %select_n.44, s32[]{:T(128)S(6)} %select_n.43, s32[]{:T(128)S(6)} %select_n.42, s32[]{:T(128)S(6)} %select_n.41), kind=kLoop, calls=%fused_computation.30 | loop fusion | bytes 4194320 | tf_op jit(solution)/shard_map/dynamic_slice | solution.py:387
  4.0 3.0 %collective-permute-start = (bf16[272,1024]{1,0:T(8,128)(2,1)S(1)}, bf16[272,1024]{1,0:T(8,128)(2,1)S(1)}, u32[]{:S(2)}, u32[]{:S(2)}) collective-permute-start(bf16[272,1024]{1,0:T(8,128)(2,1)S(1)} %get-tuple-element.79), channel_id=1, source_target_pairs={{0,8},{8,0},{16,24},{24,16},{1,9},{9,1},{17,25},{25,17},{2,10},{10... | collective-permute-start | bytes 1671176 | tf_op jit(solution)/shard_map/ppermute | solution.py:371
  7.0 1.5 collective-permute-start.1
  8.6 2.7 %shard_map.85 = (bf16[384,256]{1,0:T(8,128)(2,1)}, bf16[96,1536]{1,0:T(8,128)(2,1)}, bf16[96,1536]{1,0:T(8,128)(2,1)}, bf16[96,1536]{1,0:T(8,128)(2,1)}, bf16[96,1536]{1,0:T(8,128)(2,1)}) custom-call(s32[1]{0:T(128)} %bitcast.2.refs_0_, s32[1,256]{1,0:T(1,128)} %bitcast.30, bf16[256,1024]{1,0:T(8,128)(2,1)} %get-tuple-element.78.refs_2_, ...), custom_call_target="tpu_custom_call" | custom-call | flops 1 | bytes 1 | tf_op jit(solution)/shard_map/pallas_call | solution.py:154
  11.3 2.1 %collective-permute-start.3 = (bf16[96,1536]{1,0:T(8,128)(2,1)}, bf16[96,1536]{1,0:T(8,128)(2,1)}, u32[]{:S(2)}, u32[]{:S(2)}) collective-permute-start(bf16[96,1536]{1,0:T(8,128)(2,1)} %get-tuple-element.83), channel_id=1, source_target_pairs={{0,1},{1,2},{2,3},{3,0},{4,5},{5,6},{6,7},{7,4},{8,9},{9,10},{10,1... | collective-permute-start | bytes 884744 | tf_op jit(solution)/shard_map/ppermute | solution.py:374
  13.4 2.6 %collective-permute-start.4 = (bf16[96,1536]{1,0:T(8,128)(2,1)}, bf16[96,1536]{1,0:T(8,128)(2,1)}, u32[]{:S(2)}, u32[]{:S(2)}) collective-permute-start(bf16[96,1536]{1,0:T(8,128)(2,1)} %get-tuple-element.84), channel_id=1, source_target_pairs={{0,2},{1,3},{2,0},{3,1},{4,6},{5,7},{6,4},{7,5},{8,10},{9,11},{10,... | collective-permute-start | bytes 884744 | tf_op jit(solution)/shard_map/ppermute | solution.py:374
  16.0 4.5 %collective-permute-done.refs_1_.refs_2_ = bf16[272,1024]{1,0:T(8,128)(2,1)S(1)} collective-permute-done((bf16[272,1024]{1,0:T(8,128)(2,1)S(1)}, bf16[272,1024]{1,0:T(8,128)(2,1)S(1)}, u32[]{:S(2)}, u32[]{:S(2)}) %collective-permute-start) | collective-permute-done | bytes 557088 | tf_op jit(solution)/shard_map/ppermute | solution.py:371
  20.5 4.2 %collective-permute-start.5 = (bf16[96,1536]{1,0:T(8,128)(2,1)}, bf16[96,1536]{1,0:T(8,128)(2,1)S(1)}, u32[]{:S(2)}, u32[]{:S(2)}) collective-permute-start(bf16[96,1536]{1,0:T(8,128)(2,1)} %get-tuple-element.86), channel_id=1, source_target_pairs={{0,3},{1,0},{2,1},{3,2},{4,7},{5,4},{6,5},{7,6},{8,11},{9,8},{10,9... | collective-permute-start | bytes 884744 | tf_op jit(solution)/shard_map/ppermute | solution.py:374
  24.6 4.6 %constant_dynamic-slice_fusion.1 = bf16[8,256,1024]{2,1,0:T(8,128)(2,1)} fusion(bf16[8,256,4096]{2,1,0:T(8,128)(2,1)} %refs_5_.3, s32[]{:T(128)S(6)} %select_n.46), kind=kLoop, calls=%fused_computation.29 | loop fusion | bytes 8388612 | tf_op jit(solution)/shard_map/dynamic_slice | solution.py:406
  29.3 2.3 %constant_dynamic-slice_fusion.refs_1_ = bf16[256,2048]{1,0:T(8,128)(2,1)} fusion(bf16[256,8192]{1,0:T(8,128)(2,1)} %param.6, s32[]{:T(128)S(6)} %select_n.47), kind=kLoop, calls=%fused_computation.28 | loop fusion | bytes 2097156 | tf_op jit(solution)/shard_map/dynamic_slice | solution.py:409
  31.6 3.1 %collective-permute-done.4.refs_2_.refs_4_.refs_3_ = bf16[96,1536]{1,0:T(8,128)(2,1)} collective-permute-done((bf16[96,1536]{1,0:T(8,128)(2,1)}, bf16[96,1536]{1,0:T(8,128)(2,1)}, u32[]{:S(2)}, u32[]{:S(2)}) %collective-permute-start.4) | collective-permute-done | bytes 294944 | tf_op jit(solution)/shard_map/ppermute | solution.py:374
  35.3 3.3 %collective-permute-start.13 = (bf16[8,256,1024]{2,1,0:T(8,128)(2,1)}, bf16[8,256,1024]{2,1,0:T(8,128)(2,1)}, u32[]{:S(2)}, u32[]{:S(2)}) collective-permute-start(bf16[8,256,1024]{2,1,0:T(8,128)(2,1)} %constant_dynamic-slice_fusion.1), channel_id=1, source_target_pairs={{0,4},{8,12},{20,16},{28,24},{1,5},{9,13},{21,17},{29,25},{2,6},{1... | collective-permute-start | bytes 12582920 | tf_op jit(solution)/shard_map/ppermute | solution.py:412
  39.1 4.0 %shard_map.86 = (bf16[3,96,1024]{2,1,0:T(8,128)(2,1)}, bf16[3,96,1024]{2,1,0:T(8,128)(2,1)}, bf16[3,96,1024]{2,1,0:T(8,128)(2,1)}, bf16[3,96,1024]{2,1,0:T(8,128)(2,1)}) custom-call(s32[1]{0:T(128)} %bitcast.2.refs_0_, bf16[272,1024]{1,0:T(8,128)(2,1)} %copy-done.1, bf16[272,1024]{1,0:T(8,128)(2,1)} %copy-done.2, bf16[272,1024]{1,0:T(8,128)(2,1)} %copy-done.3), custom_call_target="tpu_custom_call" | custom-call | flops 1 | bytes 1 | tf_op jit(solution)/shard_map/pallas_call | solution.py:154
  43.1 5.9 %collective-permute-start.12 = (bf16[3,96,1024]{2,1,0:T(8,128)(2,1)}, bf16[3,96,1024]{2,1,0:T(8,128)(2,1)S(1)}, u32[]{:S(2)}, u32[]{:S(2)}) collective-permute-start(bf16[3,96,1024]{2,1,0:T(8,128)(2,1)} %get-tuple-element.95), channel_id=1, source_target_pairs={{0,2},{1,3},{2,0},{3,1},{4,6},{5,7},{6,4},{7,5},{8,10},{9,11},{10,... | collective-permute-start | bytes 1769480 | tf_op jit(solution)/shard_map/ppermute | solution.py:374
  49.0 0.8 copy-done.7
  50.1 6.1 %shard_map.87 = (f32[256,512]{1,0:T(8,128)}, f32[256,512]{1,0:T(8,128)}, f32[256,512]{1,0:T(8,128)}, f32[256,512]{1,0:T(8,128)}) custom-call(s32[1]{0:T(128)} %bitcast.refs_0_, bf16[256,2048]{1,0:T(8,128)(2,1)} %constant_dynamic-slice_fusion.refs_1_, bf16[272,1024]{1,0:T(8,128)(2,1)} %copy-done.1, bf16[272,1024]{1,0:T(8,128)(2,1)} %copy-done.2, ...), custom_call_target="tpu_custom_call" | custom-call | flops 1 | bytes 1 | tf_op jit(solution)/shard_map/pallas_call | solution.py:154
  56.3 1.6 collective-permute-start.9
  57.8 2.0 %collective-permute-start.10 = (f32[256,512]{1,0:T(8,128)}, f32[256,512]{1,0:T(8,128)S(1)}, u32[]{:S(2)}, u32[]{:S(2)}) collective-permute-start(f32[256,512]{1,0:T(8,128)} %get-tuple-element.102), channel_id=1, source_target_pairs={{0,16},{8,24},{16,0},{24,8},{1,17},{9,25},{17,1},{25,9},{2,18},{10... | collective-permute-start | bytes 1572872 | tf_op jit(solution)/shard_map/ppermute | solution.py:371
  59.8 3.4 %shard_map.88.refs_0_ = f32[4,96,256]{2,1,0:T(8,128)} custom-call(bf16[96,1536]{1,0:T(8,128)(2,1)} %get-tuple-element.110.refs_0_.refs_2_.refs_1_, bf16[96,1536]{1,0:T(8,128)(2,1)} %collective-permute-done.3.refs_1_.refs_3_.refs_2_, bf16[96,1536]{1,0:T(8,128)(2,1)} %collective-permute-done.4.refs_2_.refs_4_.refs_3_, bf16[96,1536]{1,0:T(8,128)(2,1)} %copy-done.16, ...), custom_call_target="tpu_custom_call" | custom-call | flops 10000000000 | bytes 1 | tf_op jit(solution)/shard_map/pallas_call | solution.py:154
  64.0 1.3 collective-permute-done.14.refs_1_
  65.3 3.1 %collective-permute-start.16 = (bf16[3,96,1024]{2,1,0:T(8,128)(2,1)}, bf16[3,96,1024]{2,1,0:T(8,128)(2,1)S(1)}, u32[]{:S(2)}, u32[]{:S(2)}) collective-permute-start(bf16[3,96,1024]{2,1,0:T(8,128)(2,1)} %get-tuple-element.94), channel_id=1, source_target_pairs={{0,1},{1,2},{2,3},{3,0},{4,5},{5,6},{6,7},{7,4},{8,9},{9,10},{10,1... | collective-permute-start | bytes 1769480 | tf_op jit(solution)/shard_map/ppermute | solution.py:374
  68.4 2.2 %shard_map.89.refs_9_.refs_4_ = bf16[4,96,768]{2,1,0:T(8,128)(2,1)} custom-call(f32[4,96,256]{2,1,0:T(8,128)} %shard_map.88.refs_0_, f32[4,96,256]{2,1,0:T(8,128)} %copy-done.14, bf16[96,1536]{1,0:T(8,128)(2,1)} %get-tuple-element.110.refs_0_.refs_2_.refs_1_, bf16[96,1536]{1,0:T(8,128)(2,1)} %collective-permute-done.3.refs_1_.refs_3_.refs_2_, ...), custom_call_target="tpu_custom_call" | custom-call | flops 1 | bytes 1 | tf_op jit(solution)/shard_map/pallas_call | solution.py:154
  70.6 17.8 %collective-permute-done.12.refs_4_.refs_7_ = bf16[3,96,1024]{2,1,0:T(8,128)(2,1)S(1)} collective-permute-done((bf16[3,96,1024]{2,1,0:T(8,128)(2,1)}, bf16[3,96,1024]{2,1,0:T(8,128)(2,1)S(1)}, u32[]{:S(2)}, u32[]{:S(2)}) %collective-permute-start.12) | collective-permute-done | bytes 589856 | tf_op jit(solution)/shard_map/ppermute | solution.py:374
  88.5 0.8 copy-done.10
  89.3 0.8 copy-done.11
  90.1 0.8 copy-done.12
  90.9 2.4 %collective-permute-start.31 = (bf16[4,96,768]{2,1,0:T(8,128)(2,1)}, bf16[4,96,768]{2,1,0:T(8,128)(2,1)S(1)}, u32[]{:S(2)}, u32[]{:S(2)}) collective-permute-start(bf16[4,96,768]{2,1,0:T(8,128)(2,1)} %shard_map.89.refs_9_.refs_4_), channel_id=1, source_target_pairs={{0,24},{8,16},{16,8},{24,0},{1,25},{9,17},{17,9},{25,1},{2,26},{10... | collective-permute-start | bytes 1769480 | tf_op jit(solution)/shard_map/ppermute | solution.py:371
  94.4 7.2 %shard_map.90 = (f32[4,2,96,128]{3,2,1,0:T(8,128)}, f32[4,2,96,128]{3,2,1,0:T(8,128)}) custom-call(s32[3]{0:T(128)} %pad_add_fusion.refs_0_, bf16[96,1536]{1,0:T(8,128)(2,1)} %get-tuple-element.110.refs_0_.refs_2_.refs_1_, bf16[96,1536]{1,0:T(8,128)(2,1)} %collective-permute-done.4.refs_2_.refs_4_.refs_3_, ...), custom_call_target="tpu_custom_call" | custom-call | flops 10000000000 | bytes 1 | tf_op jit(solution)/shard_map/pallas_call | solution.py:154
  101.7 2.1 %collective-permute-done.17.refs_4_.refs_8_ = bf16[3,96,1024]{2,1,0:T(8,128)(2,1)S(1)} collective-permute-done((bf16[3,96,1024]{2,1,0:T(8,128)(2,1)}, bf16[3,96,1024]{2,1,0:T(8,128)(2,1)S(1)}, u32[]{:S(2)}, u32[]{:S(2)}) %collective-permute-start.17) | collective-permute-done | bytes 589856 | tf_op jit(solution)/shard_map/ppermute | solution.py:374
  103.8 0.9 copy-done.26
  104.7 7.4 %shard_map.91 = (f32[4,2,96,128]{3,2,1,0:T(8,128)}, f32[4,2,96,128]{3,2,1,0:T(8,128)}) custom-call(s32[3]{0:T(128)} %pad_add_fusion.refs_0_, bf16[96,1536]{1,0:T(8,128)(2,1)} %collective-permute-done.3.refs_1_.refs_3_.refs_2_, bf16[96,1536]{1,0:T(8,128)(2,1)} %copy-done.16, bf16[3,96,1024]{2,1,0:T(8,128)(2,1)} %copy-done.25, ...), custom_call_target="tpu_custom_call" | custom-call | flops 10000000000 | bytes 1 | tf_op jit(solution)/shard_map/pallas_call | solution.py:154
  112.1 0.6 pad_add_fusion.1.refs_0_
  112.8 1.3 collective-permute-done.18
  114.0 1.0 add.109
  115.1 1.6 collective-permute-start.19
  116.7 1.0 collective-permute-start.21
  117.7 1.0 collective-permute-start.20
  118.7 1.1 collective-permute-done.30.refs_11_.refs_6_
  119.8 1.1 collective-permute-done.29.refs_10_.refs_5_
  120.9 0.8 copy-done.6
  121.7 8.9 %shard_map.94 = (bf16[8,64,1024]{2,1,0:T(8,128)(2,1)}, bf16[8,64,1024]{2,1,0:T(8,128)(2,1)}, bf16[8,64,1024]{2,1,0:T(8,128)(2,1)}, bf16[8,64,1024]{2,1,0:T(8,128)(2,1)}) custom-call(s32[4]{0:T(128)} %pad_add_fusion.1.refs_0_, bf16[96,1536]{1,0:T(8,128)(2,1)} %get-tuple-element.110.refs_0_.refs_2_.refs_1_, ...), custom_call_target="tpu_custom_call" | custom-call | flops 10000000000 | bytes 1 | tf_op jit(solution)/shard_map/pallas_call | solution.py:154
  130.6 1.6 collective-permute-start.33
  132.3 1.9 collective-permute-start.32
  134.2 0.7 collective-permute-start.22
  134.9 0.6 stack.61.refs_0_
  135.8 0.6 copy-done.20
  136.5 4.1 %shard_map.92 = (bf16[96,512]{1,0:T(8,128)(2,1)}, bf16[96,512]{1,0:T(8,128)(2,1)}, bf16[96,512]{1,0:T(8,128)(2,1)}, bf16[96,512]{1,0:T(8,128)(2,1)}, bf16[4,96,6...) custom-call(s32[5]{0:T(128)} %stack.61.refs_0_, ...), custom_call_target="tpu_custom_call" | custom-call | flops 1 | bytes 1 | tf_op jit(solution)/shard_map/pallas_call | solution.py:154
  140.6 0.9 collective-permute-start.23
  141.5 1.4 collective-permute-start.24
  142.9 1.3 collective-permute-start.25
  144.2 14.8 %collective-permute-done.23.refs_1_ = bf16[4,96,64]{2,1,0:T(8,128)(2,1)S(1)} collective-permute-done((bf16[4,96,64]{2,1,0:T(8,128)(2,1)}, bf16[4,96,64]{2,1,0:T(8,128)(2,1)S(1)}, u32[]{:S(2)}, u32[]{:S(2)}) %collective-permute-start.23) | collective-permute-done | bytes 49184 | tf_op jit(solution)/shard_map/ppermute | solution.py:371
  159.0 3.8 %collective-permute-done.24.refs_2_ = bf16[4,96,64]{2,1,0:T(8,128)(2,1)S(1)} collective-permute-done((bf16[4,96,64]{2,1,0:T(8,128)(2,1)}, bf16[4,96,64]{2,1,0:T(8,128)(2,1)S(1)}, u32[]{:S(2)}, u32[]{:S(2)}) %collective-permute-start.24) | collective-permute-done | bytes 49184 | tf_op jit(solution)/shard_map/ppermute | solution.py:371
  163.7 1.2 collective-permute-start.26
  164.9 2.3 %collective-permute-start.27 = (bf16[96,512]{1,0:T(8,128)(2,1)}, bf16[96,512]{1,0:T(8,128)(2,1)S(1)}, u32[]{:S(2)}, u32[]{:S(2)}) collective-permute-start(bf16[96,512]{1,0:T(8,128)(2,1)} %get-tuple-element.132), channel_id=1, source_target_pairs={{0,2},{1,3},{2,0},{3,1},{4,6},{5,7},{6,4},{7,5},{8,10},{9,11},{10,... | collective-permute-start | bytes 294920 | tf_op jit(solution)/shard_map/ppermute | solution.py:374
  167.3 3.9 %shard_map.95 = f32[8,64,512]{2,1,0:T(8,128)} custom-call(bf16[4,96,64]{2,1,0:T(8,128)(2,1)} %get-tuple-element.152.refs_0_, bf16[4,96,64]{2,1,0:T(8,128)(2,1)} %copy-done.21, bf16[4,96,64]{2,1,0:T(8,128)(2,1)} %copy-done.22, bf16[4,96,64]{2,1,0:T(8,128)(2,1)} %copy-done.23, bf16[4,96,768]{2,1,0:T(8,128)(2,1)} %shard_map.89.refs_9_.refs_4_, ...), custom_call_target="tpu_custom_call" | custom-call | flops 1 | bytes 1 | tf_op jit(solution)/shard_map/pallas_call | solution.py:154
  171.2 5.9 %collective-permute-done.27.refs_7_ = bf16[96,512]{1,0:T(8,128)(2,1)S(1)} collective-permute-done((bf16[96,512]{1,0:T(8,128)(2,1)}, bf16[96,512]{1,0:T(8,128)(2,1)S(1)}, u32[]{:S(2)}, u32[]{:S(2)}) %collective-permute-start.27) | collective-permute-done | bytes 98336 | tf_op jit(solution)/shard_map/ppermute | solution.py:374
  177.0 0.6 copy-done.18
  177.7 2.8 %shard_map.93 = bf16[256,512]{1,0:T(8,128)(2,1)} custom-call(f32[256,512]{1,0:T(8,128)} %get-tuple-element.100.refs_0_, f32[256,512]{1,0:T(8,128)} %copy-done.10, f32[256,512]{1,0:T(8,128)} %copy-done.11, f32[256,512]{1,0:T(8,128)} %copy-done.12, bf16[384,256]{1,0:T(8,128)(2,1)} %get-tuple-element.104.refs_4_, bf16[96,512]{1,0:T(8,128)(2,1)} %get-tuple-element.130.refs_5_, ...), custom_call_target="tpu_custom_call" | custom-call | flops 1 | bytes 1 | tf_op jit(solution)/shard_map/pallas_call | solution.py:154
  180.5 1.0 broadcast_in_dim.3
  182.0 3.7 %collective-permute-done.34 = bf16[8,64,1024]{2,1,0:T(8,128)(2,1)} collective-permute-done((bf16[8,64,1024]{2,1,0:T(8,128)(2,1)}, bf16[8,64,1024]{2,1,0:T(8,128)(2,1)}, u32[]{:S(2)}, u32[]{:S(2)}) %collective-permute-start.34) | collective-permute-done | bytes 1048608 | tf_op jit(solution)/shard_map/ppermute | solution.py:497
  185.7 1.5 convert_dynamic-update-slice_fusion.1
  187.2 1.6 collective-permute-done.35
  189.1 3.4 %copy-done = f32[8,64,4096]{2,1,0:T(8,128)} copy-done((f32[8,64,4096]{2,1,0:T(8,128)}, f32[8,64,4096]{2,1,0:T(8,128)S(1)}, u32[]{:S(2)}) %copy-start) | copy-done | bytes 8388632
  (92 shorter events, 5.7 us)
Async XLA Ops:
  4.0 16.5 %collective-permute-start = (bf16[272,1024]{1,0:T(8,128)(2,1)S(1)}, bf16[272,1024]{1,0:T(8,128)(2,1)S(1)}, u32[]{:S(2)}, u32[]{:S(2)}) collective-permute-start(bf16[272,1024]{1,0:T(8,128)(2,1)S(1)} %get-tuple-element.79), channel_id=1, source_target_pairs={{0,8},{8,0},{16,24},{24,16},{1,9},{9,1},{17,25},{25,17},{2,10},{10... | collective-permute-start | bytes 1671176 | tf_op jit(solution)/shard_map/ppermute | solution.py:371
  7.0 27.7 %collective-permute-start.1 = (bf16[272,1024]{1,0:T(8,128)(2,1)S(1)}, bf16[272,1024]{1,0:T(8,128)(2,1)S(1)}, u32[]{:S(2)}, u32[]{:S(2)}) collective-permute-start(bf16[272,1024]{1,0:T(8,128)(2,1)S(1)} %get-tuple-element.80), channel_id=1, source_target_pairs={{0,16},{8,24},{16,0},{24,8},{1,17},{9,25},{17,1},{25,9},{2,18},{10... | collective-permute-start | bytes 1671176 | tf_op jit(solution)/shard_map/ppermute | solution.py:371
  8.5 26.2 %collective-permute-start.2 = (bf16[272,1024]{1,0:T(8,128)(2,1)S(1)}, bf16[272,1024]{1,0:T(8,128)(2,1)S(1)}, u32[]{:S(2)}, u32[]{:S(2)}) collective-permute-start(bf16[272,1024]{1,0:T(8,128)(2,1)S(1)} %get-tuple-element.81), channel_id=1, source_target_pairs={{0,24},{8,16},{16,8},{24,0},{1,25},{9,17},{17,9},{25,1},{2,26},{10... | collective-permute-start | bytes 1671176 | tf_op jit(solution)/shard_map/ppermute | solution.py:371
  11.3 20.3 %collective-permute-start.3 = (bf16[96,1536]{1,0:T(8,128)(2,1)}, bf16[96,1536]{1,0:T(8,128)(2,1)}, u32[]{:S(2)}, u32[]{:S(2)}) collective-permute-start(bf16[96,1536]{1,0:T(8,128)(2,1)} %get-tuple-element.83), channel_id=1, source_target_pairs={{0,1},{1,2},{2,3},{3,0},{4,5},{5,6},{6,7},{7,4},{8,9},{9,10},{10,1... | collective-permute-start | bytes 884744 | tf_op jit(solution)/shard_map/ppermute | solution.py:374
  13.4 21.3 %collective-permute-start.4 = (bf16[96,1536]{1,0:T(8,128)(2,1)}, bf16[96,1536]{1,0:T(8,128)(2,1)}, u32[]{:S(2)}, u32[]{:S(2)}) collective-permute-start(bf16[96,1536]{1,0:T(8,128)(2,1)} %get-tuple-element.84), channel_id=1, source_target_pairs={{0,2},{1,3},{2,0},{3,1},{4,6},{5,7},{6,4},{7,5},{8,10},{9,11},{10,... | collective-permute-start | bytes 884744 | tf_op jit(solution)/shard_map/ppermute | solution.py:374
  20.5 18.1 %copy-start.1 = (bf16[272,1024]{1,0:T(8,128)(2,1)}, bf16[272,1024]{1,0:T(8,128)(2,1)S(1)}, u32[]{:S(2)}) copy-start(bf16[272,1024]{1,0:T(8,128)(2,1)S(1)} %collective-permute-done.refs_1_.refs_2_) | copy-start | bytes 1671172
  20.5 14.8 %collective-permute-start.5 = (bf16[96,1536]{1,0:T(8,128)(2,1)}, bf16[96,1536]{1,0:T(8,128)(2,1)S(1)}, u32[]{:S(2)}, u32[]{:S(2)}) collective-permute-start(bf16[96,1536]{1,0:T(8,128)(2,1)} %get-tuple-element.86), channel_id=1, source_target_pairs={{0,3},{1,0},{2,1},{3,2},{4,7},{5,4},{6,5},{7,6},{8,11},{9,8},{10,9... | collective-permute-start | bytes 884744 | tf_op jit(solution)/shard_map/ppermute | solution.py:374
  34.7 4.4 %copy-start.2 = (bf16[272,1024]{1,0:T(8,128)(2,1)}, bf16[272,1024]{1,0:T(8,128)(2,1)S(1)}, u32[]{:S(2)}) copy-start(bf16[272,1024]{1,0:T(8,128)(2,1)S(1)} %collective-permute-done.1.refs_2_.refs_3_) | copy-start | bytes 1671172
  34.7 4.4 %copy-start.3 = (bf16[272,1024]{1,0:T(8,128)(2,1)}, bf16[272,1024]{1,0:T(8,128)(2,1)S(1)}, u32[]{:S(2)}) copy-start(bf16[272,1024]{1,0:T(8,128)(2,1)S(1)} %collective-permute-done.2.refs_3_.refs_4_) | copy-start | bytes 1671172
  35.3 24.6 %copy-start.16 = (bf16[96,1536]{1,0:T(8,128)(2,1)}, bf16[96,1536]{1,0:T(8,128)(2,1)S(1)}, u32[]{:S(2)}) copy-start(bf16[96,1536]{1,0:T(8,128)(2,1)S(1)} %collective-permute-done.5.refs_3_.refs_5_.refs_2_.refs_4_) | copy-start | bytes 884740
  35.3 24.5 %collective-permute-start.13 = (bf16[8,256,1024]{2,1,0:T(8,128)(2,1)}, bf16[8,256,1024]{2,1,0:T(8,128)(2,1)}, u32[]{:S(2)}, u32[]{:S(2)}) collective-permute-start(bf16[8,256,1024]{2,1,0:T(8,128)(2,1)} %constant_dynamic-slice_fusion.1), channel_id=1, source_target_pairs={{0,4},{8,12},{20,16},{28,24},{1,5},{9,13},{21,17},{29,25},{2,6},{1... | collective-permute-start | bytes 12582920 | tf_op jit(solution)/shard_map/ppermute | solution.py:412
  38.6 10.4 %collective-permute-start.6 = (bf16[272,1024]{1,0:T(8,128)(2,1)S(1)}, bf16[272,1024]{1,0:T(8,128)(2,1)S(1)}, u32[]{:S(2)}, u32[]{:S(2)}) collective-permute-start(bf16[272,1024]{1,0:T(8,128)(2,1)S(1)} %collective-permute-done.refs_1_.refs_2_), channel_id=1, source_target_pairs={{0,4},{4,0},{1,5},{5,1},{2,6},{6,2},{3,7},{7,3},{8,12},{12,8},{9,1... | collective-permute-start | bytes 1671176 | tf_op jit(solution)/shard_map/ppermute | solution.py:377
  38.6 10.4 %collective-permute-start.7 = (bf16[272,1024]{1,0:T(8,128)(2,1)S(1)}, bf16[272,1024]{1,0:T(8,128)(2,1)S(1)}, u32[]{:S(2)}, u32[]{:S(2)}) collective-permute-start(bf16[272,1024]{1,0:T(8,128)(2,1)S(1)} %collective-permute-done.1.refs_2_.refs_3_), channel_id=1, source_target_pairs={{0,4},{4,0},{1,5},{5,1},{2,6},{6,2},{3,7},{7,3},{8,12},{12,8},{9,1... | collective-permute-start | bytes 1671176 | tf_op jit(solution)/shard_map/ppermute | solution.py:377
  39.1 9.9 %collective-permute-start.8 = (bf16[272,1024]{1,0:T(8,128)(2,1)S(1)}, bf16[272,1024]{1,0:T(8,128)(2,1)S(1)}, u32[]{:S(2)}, u32[]{:S(2)}) collective-permute-start(bf16[272,1024]{1,0:T(8,128)(2,1)S(1)} %collective-permute-done.2.refs_3_.refs_4_), channel_id=1, source_target_pairs={{0,4},{4,0},{1,5},{5,1},{2,6},{6,2},{3,7},{7,3},{8,12},{12,8},{9,1... | collective-permute-start | bytes 1671176 | tf_op jit(solution)/shard_map/ppermute | solution.py:377
  43.1 45.3 %collective-permute-start.12 = (bf16[3,96,1024]{2,1,0:T(8,128)(2,1)}, bf16[3,96,1024]{2,1,0:T(8,128)(2,1)S(1)}, u32[]{:S(2)}, u32[]{:S(2)}) collective-permute-start(bf16[3,96,1024]{2,1,0:T(8,128)(2,1)} %get-tuple-element.95), channel_id=1, source_target_pairs={{0,2},{1,3},{2,0},{3,1},{4,6},{5,7},{6,4},{7,5},{8,10},{9,11},{10,... | collective-permute-start | bytes 1769480 | tf_op jit(solution)/shard_map/ppermute | solution.py:374
  49.0 0.8 copy-start.7
  49.0 1.0 copy-start.8
  49.0 1.2 copy-start.9
  56.3 32.2 %collective-permute-start.9 = (f32[256,512]{1,0:T(8,128)}, f32[256,512]{1,0:T(8,128)S(1)}, u32[]{:S(2)}, u32[]{:S(2)}) collective-permute-start(f32[256,512]{1,0:T(8,128)} %get-tuple-element.101), channel_id=1, source_target_pairs={{0,8},{8,0},{16,24},{24,16},{1,9},{9,1},{17,25},{25,17},{2,10},{10... | collective-permute-start | bytes 1572872 | tf_op jit(solution)/shard_map/ppermute | solution.py:371
  57.8 30.6 %collective-permute-start.10 = (f32[256,512]{1,0:T(8,128)}, f32[256,512]{1,0:T(8,128)S(1)}, u32[]{:S(2)}, u32[]{:S(2)}) collective-permute-start(f32[256,512]{1,0:T(8,128)} %get-tuple-element.102), channel_id=1, source_target_pairs={{0,16},{8,24},{16,0},{24,8},{1,17},{9,25},{17,1},{25,9},{2,18},{10... | collective-permute-start | bytes 1572872 | tf_op jit(solution)/shard_map/ppermute | solution.py:371
  59.8 30.2 %collective-permute-start.11 = (f32[256,512]{1,0:T(8,128)}, f32[256,512]{1,0:T(8,128)S(1)}, u32[]{:S(2)}, u32[]{:S(2)}) collective-permute-start(f32[256,512]{1,0:T(8,128)} %get-tuple-element.103), channel_id=1, source_target_pairs={{0,24},{8,16},{16,8},{24,0},{1,25},{9,17},{17,9},{25,1},{2,26},{10... | collective-permute-start | bytes 1572872 | tf_op jit(solution)/shard_map/ppermute | solution.py:371
  63.3 2.0 %collective-permute-start.14 = (f32[4,96,256]{2,1,0:T(8,128)}, f32[4,96,256]{2,1,0:T(8,128)S(1)}, u32[]{:S(2)}, u32[]{:S(2)}) collective-permute-start(f32[4,96,256]{2,1,0:T(8,128)} %shard_map.88.refs_0_), channel_id=1, source_target_pairs={{0,4},{4,0},{1,5},{5,1},{2,6},{6,2},{3,7},{7,3},{8,12},{12,8},{9,1... | collective-permute-start | bytes 1179656 | tf_op jit(solution)/shard_map/ppermute | solution.py:377
  65.3 3.1 %copy-start.14 = (f32[4,96,256]{2,1,0:T(8,128)}, f32[4,96,256]{2,1,0:T(8,128)S(1)}, u32[]{:S(2)}) copy-start(f32[4,96,256]{2,1,0:T(8,128)S(1)} %collective-permute-done.14.refs_1_) | copy-start | bytes 1179652
  65.3 36.3 %collective-permute-start.16 = (bf16[3,96,1024]{2,1,0:T(8,128)(2,1)}, bf16[3,96,1024]{2,1,0:T(8,128)(2,1)S(1)}, u32[]{:S(2)}, u32[]{:S(2)}) collective-permute-start(bf16[3,96,1024]{2,1,0:T(8,128)(2,1)} %get-tuple-element.94), channel_id=1, source_target_pairs={{0,1},{1,2},{2,3},{3,0},{4,5},{5,6},{6,7},{7,4},{8,9},{9,10},{10,1... | collective-permute-start | bytes 1769480 | tf_op jit(solution)/shard_map/ppermute | solution.py:374
  88.4 5.9 %copy-start.24 = (bf16[3,96,1024]{2,1,0:T(8,128)(2,1)}, bf16[3,96,1024]{2,1,0:T(8,128)(2,1)S(1)}, u32[]{:S(2)}) copy-start(bf16[3,96,1024]{2,1,0:T(8,128)(2,1)S(1)} %collective-permute-done.12.refs_4_.refs_7_) | copy-start | bytes 1769476
  88.4 15.4 %collective-permute-start.17 = (bf16[3,96,1024]{2,1,0:T(8,128)(2,1)}, bf16[3,96,1024]{2,1,0:T(8,128)(2,1)S(1)}, u32[]{:S(2)}, u32[]{:S(2)}) collective-permute-start(bf16[3,96,1024]{2,1,0:T(8,128)(2,1)} %get-tuple-element.96), channel_id=1, source_target_pairs={{0,3},{1,0},{2,1},{3,2},{4,7},{5,4},{6,5},{7,6},{8,11},{9,8},{10,9... | collective-permute-start | bytes 1769480 | tf_op jit(solution)/shard_map/ppermute | solution.py:374
  88.4 0.8 copy-start.10
  89.3 0.8 copy-start.11
  90.1 0.8 copy-start.12
  90.9 26.8 %collective-permute-start.31 = (bf16[4,96,768]{2,1,0:T(8,128)(2,1)}, bf16[4,96,768]{2,1,0:T(8,128)(2,1)S(1)}, u32[]{:S(2)}, u32[]{:S(2)}) collective-permute-start(bf16[4,96,768]{2,1,0:T(8,128)(2,1)} %shard_map.89.refs_9_.refs_4_), channel_id=1, source_target_pairs={{0,24},{8,16},{16,8},{24,0},{1,25},{9,17},{17,9},{25,1},{2,26},{10... | collective-permute-start | bytes 1769480 | tf_op jit(solution)/shard_map/ppermute | solution.py:371
  93.3 26.5 %collective-permute-start.30 = (bf16[4,96,768]{2,1,0:T(8,128)(2,1)}, bf16[4,96,768]{2,1,0:T(8,128)(2,1)S(1)}, u32[]{:S(2)}, u32[]{:S(2)}) collective-permute-start(bf16[4,96,768]{2,1,0:T(8,128)(2,1)} %shard_map.89.refs_9_.refs_4_), channel_id=1, source_target_pairs={{0,16},{8,24},{16,0},{24,8},{1,17},{9,25},{17,1},{25,9},{2,18},{10... | collective-permute-start | bytes 1769480 | tf_op jit(solution)/shard_map/ppermute | solution.py:371
  93.8 27.0 %collective-permute-start.29 = (bf16[4,96,768]{2,1,0:T(8,128)(2,1)}, bf16[4,96,768]{2,1,0:T(8,128)(2,1)S(1)}, u32[]{:S(2)}, u32[]{:S(2)}) collective-permute-start(bf16[4,96,768]{2,1,0:T(8,128)(2,1)} %shard_map.89.refs_9_.refs_4_), channel_id=1, source_target_pairs={{0,8},{8,0},{16,24},{24,16},{1,9},{9,1},{17,25},{25,17},{2,10},{10... | collective-permute-start | bytes 1769480 | tf_op jit(solution)/shard_map/ppermute | solution.py:371
  101.6 2.2 %copy-start.25 = (bf16[3,96,1024]{2,1,0:T(8,128)(2,1)}, bf16[3,96,1024]{2,1,0:T(8,128)(2,1)S(1)}, u32[]{:S(2)}) copy-start(bf16[3,96,1024]{2,1,0:T(8,128)(2,1)S(1)} %collective-permute-done.16.refs_3_.refs_6_) | copy-start | bytes 1769476
  101.6 11.1 %collective-permute-start.15 = (f32[4,2,96,128]{3,2,1,0:T(8,128)}, f32[4,2,96,128]{3,2,1,0:T(8,128)S(1)}, u32[]{:S(2)}, u32[]{:S(2)}) collective-permute-start(f32[4,2,96,128]{3,2,1,0:T(8,128)} %get-tuple-element.118), channel_id=1, source_target_pairs={{0,4},{4,0},{1,5},{5,1},{2,6},{6,2},{3,7},{7,3},{8,12},{12,8},{9,1... | collective-permute-start | bytes 1179656 | tf_op jit(solution)/shard_map/ppermute | solution.py:377
  103.8 0.9 copy-start.26
  104.7 8.1 %copy-start.15 = (f32[4,2,96,128]{3,2,1,0:T(8,128)S(1)}, f32[4,2,96,128]{3,2,1,0:T(8,128)}, u32[]{:S(2)}) copy-start(f32[4,2,96,128]{3,2,1,0:T(8,128)} %get-tuple-element.117) | copy-start | bytes 1179652
  112.0 2.0 %collective-permute-start.18 = (f32[4,2,96,128]{3,2,1,0:T(8,128)}, f32[4,2,96,128]{3,2,1,0:T(8,128)S(1)}, u32[]{:S(2)}, u32[]{:S(2)}) collective-permute-start(f32[4,2,96,128]{3,2,1,0:T(8,128)} %get-tuple-element.122), channel_id=1, source_target_pairs={{0,4},{4,0},{1,5},{5,1},{2,6},{6,2},{3,7},{7,3},{8,12},{12,8},{9,1... | collective-permute-start | bytes 1179656 | tf_op jit(solution)/shard_map/ppermute | solution.py:377
  115.1 15.5 %collective-permute-start.19 = (f32[4,96,128]{2,1,0:T(8,128)S(1)}, f32[4,96,128]{2,1,0:T(8,128)S(1)}, u32[]{:S(2)}, u32[]{:S(2)}) collective-permute-start(f32[4,96,128]{2,1,0:T(8,128)S(1)} %get-tuple-element.157), channel_id=1, source_target_pairs={{0,8},{8,0},{16,24},{24,16},{1,9},{9,1},{17,25},{25,17},{2,10},{10... | collective-permute-start | bytes 589832 | tf_op jit(solution)/shard_map/ppermute | solution.py:371
  116.7 13.9 %collective-permute-start.21 = (f32[4,96,128]{2,1,0:T(8,128)S(1)}, f32[4,96,128]{2,1,0:T(8,128)S(1)}, u32[]{:S(2)}, u32[]{:S(2)}) collective-permute-start(f32[4,96,128]{2,1,0:T(8,128)S(1)} %get-tuple-element.158), channel_id=1, source_target_pairs={{0,24},{8,16},{16,8},{24,0},{1,25},{9,17},{17,9},{25,1},{2,26},{10... | collective-permute-start | bytes 589832 | tf_op jit(solution)/shard_map/ppermute | solution.py:371
  117.7 3.2 %copy-start.4 = (bf16[4,96,768]{2,1,0:T(8,128)(2,1)}, bf16[4,96,768]{2,1,0:T(8,128)(2,1)S(1)}, u32[]{:S(2)}) copy-start(bf16[4,96,768]{2,1,0:T(8,128)(2,1)S(1)} %collective-permute-done.31.refs_12_.refs_7_) | copy-start | bytes 1769476
  117.7 12.9 %collective-permute-start.20 = (f32[4,96,128]{2,1,0:T(8,128)S(1)}, f32[4,96,128]{2,1,0:T(8,128)S(1)}, u32[]{:S(2)}, u32[]{:S(2)}) collective-permute-start(f32[4,96,128]{2,1,0:T(8,128)S(1)} %get-tuple-element.159), channel_id=1, source_target_pairs={{0,16},{8,24},{16,0},{24,8},{1,17},{9,25},{17,1},{25,9},{2,18},{10... | collective-permute-start | bytes 589832 | tf_op jit(solution)/shard_map/ppermute | solution.py:371
  119.8 1.1 copy-start.5
  120.9 0.8 copy-start.6
  130.6 32.2 %collective-permute-start.33 = (bf16[8,64,1024]{2,1,0:T(8,128)(2,1)}, bf16[8,64,1024]{2,1,0:T(8,128)(2,1)S(1)}, u32[]{:S(2)}, u32[]{:S(2)}) collective-permute-start(bf16[8,64,1024]{2,1,0:T(8,128)(2,1)} %get-tuple-element.147), channel_id=1, source_target_pairs={{0,8},{4,24},{8,0},{12,16},{16,12},{20,28},{24,4},{28,20},{1,9},{5... | collective-permute-start | bytes 3145736 | tf_op jit(solution)/shard_map/ppermute | solution.py:497
  132.3 30.6 %collective-permute-start.32 = (bf16[8,64,1024]{2,1,0:T(8,128)(2,1)}, bf16[8,64,1024]{2,1,0:T(8,128)(2,1)S(1)}, u32[]{:S(2)}, u32[]{:S(2)}) collective-permute-start(bf16[8,64,1024]{2,1,0:T(8,128)(2,1)} %get-tuple-element.145), channel_id=1, source_target_pairs={{0,0},{4,16},{8,8},{12,24},{16,4},{20,20},{24,12},{28,28},{1,1},{5... | collective-permute-start | bytes 3145736 | tf_op jit(solution)/shard_map/ppermute | solution.py:497
  134.2 1.6 copy-start.13
  134.2 1.6 collective-permute-start.22
  135.8 0.6 copy-start.20
  140.6 18.3 %collective-permute-start.23 = (bf16[4,96,64]{2,1,0:T(8,128)(2,1)}, bf16[4,96,64]{2,1,0:T(8,128)(2,1)S(1)}, u32[]{:S(2)}, u32[]{:S(2)}) collective-permute-start(bf16[4,96,64]{2,1,0:T(8,128)(2,1)} %get-tuple-element.127), channel_id=1, source_target_pairs={{0,8},{8,0},{16,24},{24,16},{1,9},{9,1},{17,25},{25,17},{2,10},{10... | collective-permute-start | bytes 147464 | tf_op jit(solution)/shard_map/ppermute | solution.py:371
  141.5 21.3 %collective-permute-start.24 = (bf16[4,96,64]{2,1,0:T(8,128)(2,1)}, bf16[4,96,64]{2,1,0:T(8,128)(2,1)S(1)}, u32[]{:S(2)}, u32[]{:S(2)}) collective-permute-start(bf16[4,96,64]{2,1,0:T(8,128)(2,1)} %get-tuple-element.128), channel_id=1, source_target_pairs={{0,16},{8,24},{16,0},{24,8},{1,17},{9,25},{17,1},{25,9},{2,18},{10... | collective-permute-start | bytes 147464 | tf_op jit(solution)/shard_map/ppermute | solution.py:371
  142.9 19.9 %collective-permute-start.25 = (bf16[4,96,64]{2,1,0:T(8,128)(2,1)}, bf16[4,96,64]{2,1,0:T(8,128)(2,1)S(1)}, u32[]{:S(2)}, u32[]{:S(2)}) collective-permute-start(bf16[4,96,64]{2,1,0:T(8,128)(2,1)} %get-tuple-element.129), channel_id=1, source_target_pairs={{0,24},{8,16},{16,8},{24,0},{1,25},{9,17},{17,9},{25,1},{2,26},{10... | collective-permute-start | bytes 147464 | tf_op jit(solution)/shard_map/ppermute | solution.py:371
  159.0 8.3 %copy-start.21 = (bf16[4,96,64]{2,1,0:T(8,128)(2,1)}, bf16[4,96,64]{2,1,0:T(8,128)(2,1)S(1)}, u32[]{:S(2)}) copy-start(bf16[4,96,64]{2,1,0:T(8,128)(2,1)S(1)} %collective-permute-done.23.refs_1_) | copy-start | bytes 147460
  162.8 0.6 copy-start.22
  162.8 0.7 copy-start.23
  162.8 22.9 %collective-permute-start.34 = (bf16[8,64,1024]{2,1,0:T(8,128)(2,1)}, bf16[8,64,1024]{2,1,0:T(8,128)(2,1)}, u32[]{:S(2)}, u32[]{:S(2)}) collective-permute-start(bf16[8,64,1024]{2,1,0:T(8,128)(2,1)} %get-tuple-element.149), channel_id=1, source_target_pairs={{0,16},{4,0},{8,24},{12,8},{16,20},{20,4},{24,28},{28,12},{1,17},{... | collective-permute-start | bytes 3145736 | tf_op jit(solution)/shard_map/ppermute | solution.py:497
  163.5 25.3 %collective-permute-start.35 = (bf16[8,64,1024]{2,1,0:T(8,128)(2,1)}, bf16[8,64,1024]{2,1,0:T(8,128)(2,1)S(1)}, u32[]{:S(2)}, u32[]{:S(2)}) collective-permute-start(bf16[8,64,1024]{2,1,0:T(8,128)(2,1)} %get-tuple-element.151), channel_id=1, source_target_pairs={{0,24},{4,8},{8,16},{12,0},{16,28},{20,12},{24,20},{28,4},{1,25},{... | collective-permute-start | bytes 3145736 | tf_op jit(solution)/shard_map/ppermute | solution.py:497
  163.7 7.5 %collective-permute-start.26 = (bf16[96,512]{1,0:T(8,128)(2,1)}, bf16[96,512]{1,0:T(8,128)(2,1)S(1)}, u32[]{:S(2)}, u32[]{:S(2)}) collective-permute-start(bf16[96,512]{1,0:T(8,128)(2,1)} %get-tuple-element.131), channel_id=1, source_target_pairs={{0,3},{1,0},{2,1},{3,2},{4,7},{5,4},{6,5},{7,6},{8,11},{9,8},{10,9... | collective-permute-start | bytes 294920 | tf_op jit(solution)/shard_map/ppermute | solution.py:374
  164.9 12.1 %collective-permute-start.27 = (bf16[96,512]{1,0:T(8,128)(2,1)}, bf16[96,512]{1,0:T(8,128)(2,1)S(1)}, u32[]{:S(2)}, u32[]{:S(2)}) collective-permute-start(bf16[96,512]{1,0:T(8,128)(2,1)} %get-tuple-element.132), channel_id=1, source_target_pairs={{0,2},{1,3},{2,0},{3,1},{4,6},{5,7},{6,4},{7,5},{8,10},{9,11},{10,... | collective-permute-start | bytes 294920 | tf_op jit(solution)/shard_map/ppermute | solution.py:374
  167.3 9.8 %collective-permute-start.28 = (bf16[96,512]{1,0:T(8,128)(2,1)}, bf16[96,512]{1,0:T(8,128)(2,1)S(1)}, u32[]{:S(2)}, u32[]{:S(2)}) collective-permute-start(bf16[96,512]{1,0:T(8,128)(2,1)} %get-tuple-element.133), channel_id=1, source_target_pairs={{0,1},{1,2},{2,3},{3,0},{4,5},{5,6},{6,7},{7,4},{8,9},{9,10},{10,1... | collective-permute-start | bytes 294920 | tf_op jit(solution)/shard_map/ppermute | solution.py:374
  171.1 5.9 %copy-start.17 = (bf16[96,512]{1,0:T(8,128)(2,1)}, bf16[96,512]{1,0:T(8,128)(2,1)S(1)}, u32[]{:S(2)}) copy-start(bf16[96,512]{1,0:T(8,128)(2,1)S(1)} %collective-permute-done.26.refs_6_) | copy-start | bytes 294916
  177.0 0.6 copy-start.18
  177.0 0.7 copy-start.19
  189.1 3.4 %copy-start = (f32[8,64,4096]{2,1,0:T(8,128)}, f32[8,64,4096]{2,1,0:T(8,128)S(1)}, u32[]{:S(2)}) copy-start(f32[8,64,4096]{2,1,0:T(8,128)S(1)} %convert_dynamic-update-slice_fusion) | copy-start | bytes 25165828
